TPU v7x, 32 devices: a whole 2x2x4 slice. The times are simulated.
32 devices in a mesh: dp: 16 (over z, y, core), expert: 2 (over x).
Axes of the slice: x: 2, y: 2, z: 4, core: 2. Of those that a mesh axis runs over, the one named last changes fastest.
Arguments:
- hidden_in: bfloat16 [2, 16384, 768], P(None, ('dp', 'expert')), may hold values from -6 to 6
- out_grad: bfloat16 [2, 16384, 768], P(None, ('dp', 'expert')), may hold values from -6 to 6
- places: int32 [2, 16, 1024], P(None, 'dp'), may hold values from 0 to 1023, as said below
- lengths: int32 [2, 16, 2], P(None, 'dp'), may hold values from 0 to 1024, as said below
- routes: int32 [2, 16384, 1], P(None, ('dp', 'expert')), may hold values from 0 to 1; in each aligned block of 512 rows (0 to 511, 512 to 1023, ..., all dimensions but the last counted through in order) at most 272 rows name the same one
- norm1_gain: bfloat16 [768], P('dp'), may hold values from 0.5 to 1.5
- w_query: bfloat16 [768, 768], P('dp'), may hold values from -0.21875 to 0.21875
- w_key: bfloat16 [768, 768], P('dp'), may hold values from -0.21875 to 0.21875
- w_value: bfloat16 [768, 768], P('dp'), may hold values from -0.21875 to 0.21875
- w_output: bfloat16 [768, 768], P('dp'), may hold values from -1.75 to 1.75
- rel_table: bfloat16 [32, 12], P('dp'), may hold values from -4 to 4
- norm2_gain: bfloat16 [768], P('dp'), may hold values from 0.5 to 1.5
- w_router: bfloat16 [768, 2], P('dp'), may hold values from -0.15625 to 0.15625
- w_in: bfloat16 [2, 768, 3072], P('expert', 'dp'), may hold values from -0.21875 to 0.21875
- w_out: bfloat16 [2, 3072, 768], P('expert', 'dp'), may hold values from -0.625 to 0.625
Outputs:
- layer_out: bfloat16 [2, 16384, 768], P(None, ('dp', 'expert'))
- in_grad: float32 [2, 16384, 768], P(None, ('dp', 'expert'))
- norm1_gain_grad: float32 [768], P('dp')
- w_query_grad: float32 [768, 768], P('dp')
- w_key_grad: float32 [768, 768], P('dp')
- w_value_grad: float32 [768, 768], P('dp')
- w_output_grad: float32 [768, 768], P('dp')
- rel_table_grad: float32 [32, 12], P('dp')
- norm2_gain_grad: float32 [768], P('dp')
- w_router_grad: float32 [768, 2], P('dp')
- w_in_grad: float32 [2, 768, 3072], P('expert', 'dp')
- w_out_grad: float32 [2, 3072, 768], P('expert', 'dp')
Inputs may be any that keep to these rules, and one draw needn't show every extreme that they name: `routes`: in each aligned block of 512 rows (one device's tokens of one micro-batch) no expert is named more than 272 times, and in some blocks one is named exactly 272 times. `places`: for each micro-batch and group the entries are a permutation of the packed positions; rows k of the 2 devices of a group hold the positions k * 2 to k * 2 + 1 in some order. Each row sums to 1024; lengths may be 0; in each draw one length is exactly 1024.
All inputs are finite; a program needn't handle non-finite values.
Results may differ from a plain program's by a relative error of at most 0.028.
Values may be sent and summed in bfloat16 or wider, within the bound.
No kernel may reach another device: no remote copies, remote signals or barrier semaphores. Data moves between devices by JAX's collectives and lax.ppermute only.
A program may use at most 176 MiB of HBM per device.

v0:
```python
import jax
import jax.numpy as jnp
from jax import lax
from jax.sharding import PartitionSpec as P

bucket_edges = (1, 2, 3, 4, 5, 6, 7, 8, 12, 16, 23, 32, 46, 64, 91)
epsilon = 1e-06
masked_score = -1000000000.0
precise = lax.Precision.HIGHEST


def norm_rows(rows, gain):
    mean_square = jnp.mean(rows * rows, axis=-1, keepdims=True)
    return rows * lax.rsqrt(mean_square + epsilon) * gain


def gelu_tanh(values):
    return jax.nn.gelu(values, approximate=True)


def bucket_ids(query_pos, key_pos):
    offset = key_pos[None, :] - query_pos[:, None]
    distance = jnp.abs(offset)
    levels = jnp.zeros(offset.shape, jnp.int32)
    for edge_value in bucket_edges:
        levels = levels + (distance >= edge_value).astype(jnp.int32)
    return levels + 16 * (offset > 0).astype(jnp.int32)


def segment_ids(positions, lengths_row):
    seq_ends = jnp.cumsum(lengths_row)[:-1]
    return jnp.sum((positions[:, None] >= seq_ends[None, :]).astype(jnp.int32), axis=1)


def softmax_rows(scores):
    row_max = jnp.max(scores, axis=-1, keepdims=True)
    shifted = jnp.exp(scores - row_max)
    return shifted / jnp.sum(shifted, axis=-1, keepdims=True)


def bucket_onehot(bucket_grid, bucket_count):
    bucket_range = jnp.arange(bucket_count, dtype=jnp.int32)[:, None, None]
    return (bucket_grid[None] == bucket_range).astype(jnp.bfloat16)


def bias_of(table_full, onehot):
    return jnp.einsum("kab,kh->hab", onehot, table_full, preferred_element_type=jnp.float32)


def table_grad(grad_scores, onehot):
    return jnp.einsum("hab,kab->kh", grad_scores, onehot, preferred_element_type=jnp.float32)


def accumulate(total, term):
    if total is None:
        return term
    return total + term


def fetch_dense(
    gain_first,
    query_shard,
    key_shard,
    value_shard,
    output_shard,
    table_shard,
    gain_second,
    router_shard,
):
    return (
        lax.all_gather(gain_first, "dp", axis=0, tiled=True),
        lax.all_gather(query_shard, "dp", axis=0, tiled=True),
        lax.all_gather(key_shard, "dp", axis=0, tiled=True),
        lax.all_gather(value_shard, "dp", axis=0, tiled=True),
        lax.all_gather(output_shard, "dp", axis=0, tiled=True),
        lax.all_gather(table_shard, "dp", axis=0, tiled=True),
        lax.all_gather(gain_second, "dp", axis=0, tiled=True),
        lax.all_gather(router_shard, "dp", axis=0, tiled=True),
    )


def fetch_experts(inner_shard, outer_shard):
    return (
        lax.all_gather(inner_shard, "dp", axis=1, tiled=True),
        lax.all_gather(outer_shard, "dp", axis=1, tiled=True),
    )


def on_device(
    hidden_in,
    out_grad,
    places,
    lengths,
    routes,
    norm1_gain,
    w_query,
    w_key,
    w_value,
    w_output,
    rel_table,
    norm2_gain,
    w_router,
    w_in,
    w_out,
):
    micro_count = hidden_in.shape[0]
    tok_rows = hidden_in.shape[1]
    model_width = hidden_in.shape[2]
    head_count = rel_table.shape[1]
    head_dim = model_width // head_count
    buckets_all = rel_table.shape[0] * lax.axis_size("dp")
    experts = w_router.shape[1]
    ff_width = w_in.shape[2]
    capacity = max(2, tok_rows * 17 // (experts * 16))
    score_scale = head_dim ** (-0.5)
    column = lax.axis_index("expert")
    float32 = jnp.float32
    bfloat = jnp.bfloat16
    grad_gain_one = None
    grad_wq = None
    grad_wk = None
    grad_wv = None
    grad_wo = None
    grad_table = None
    grad_gain_two = None
    grad_router = None
    grad_inner = None
    grad_outer = None
    layer_rows = []
    input_rows = []
    for batch_idx in range(micro_count):
        dense_full = fetch_dense(
            norm1_gain, w_query, w_key, w_value, w_output, rel_table, norm2_gain, w_router
        )
        expert_full = fetch_experts(w_in, w_out)
        gain_one, query_w, key_w, value_w, output_w, table_w, gain_two, router_w = dense_full
        inner_w = expert_full[0][0]
        outer_w = expert_full[1][0]
        gain_one_f = gain_one.astype(float32)
        gain_two_f = gain_two.astype(float32)
        tokens_f = hidden_in[batch_idx].astype(float32)
        normed_one = norm_rows(tokens_f, gain_one_f).astype(bfloat)
        queries = jnp.dot(normed_one, query_w, preferred_element_type=float32).astype(bfloat)
        keys_own = jnp.dot(normed_one, key_w, preferred_element_type=float32).astype(bfloat)
        values_own = jnp.dot(normed_one, value_w, preferred_element_type=float32).astype(bfloat)
        keys_all, values_all = (
            lax.all_gather(keys_own, "expert", axis=0, tiled=True),
            lax.all_gather(values_own, "expert", axis=0, tiled=True),
        )
        key_rows = keys_all.shape[0]
        key_pos = places[batch_idx, 0]
        query_pos = lax.dynamic_slice_in_dim(key_pos, column * tok_rows, tok_rows)
        seq_row = lengths[batch_idx, 0]
        segment_own = segment_ids(query_pos, seq_row)
        segment_all = segment_ids(key_pos, seq_row)
        same_seq = segment_own[:, None] == segment_all[None, :]
        bucket_table = bucket_onehot(bucket_ids(query_pos, key_pos), buckets_all)
        query_heads = queries.reshape(tok_rows, head_count, head_dim)
        key_heads = keys_all.reshape(key_rows, head_count, head_dim)
        value_heads = values_all.reshape(key_rows, head_count, head_dim)

        def masked_scores():
            raw_scores = jnp.einsum(
                "ahd,bhd->hab", query_heads, key_heads, preferred_element_type=float32
            ) * score_scale + bias_of(table_w, bucket_table)
            return jnp.where(same_seq[None], raw_scores, masked_score)

        scores = masked_scores()
        row_max = jnp.max(scores, axis=-1, keepdims=True)
        log_total = row_max + jnp.log(jnp.sum(jnp.exp(scores - row_max), axis=-1, keepdims=True))
        attn_probs = jnp.exp(scores - log_total)
        attended = (
            jnp.einsum(
                "hab,bhd->ahd",
                attn_probs.astype(bfloat),
                value_heads,
                preferred_element_type=float32,
            )
            .reshape(tok_rows, model_width)
            .astype(bfloat)
        )
        attn_out = jnp.dot(attended, output_w, preferred_element_type=float32)
        resid_mid = tokens_f + attn_out
        normed_two = norm_rows(resid_mid, gain_two_f).astype(bfloat)
        logits = jnp.dot(normed_two, router_w, preferred_element_type=float32)
        gate_all = softmax_rows(logits)
        chosen = routes[batch_idx, :, 0]
        picked = chosen[:, None] == jnp.arange(experts, dtype=jnp.int32)[None, :]
        gate_prob = jnp.sum(jnp.where(picked, gate_all, 0.0), axis=1)
        counts = picked.astype(jnp.int32)
        slot_idx = jnp.sum((jnp.cumsum(counts, axis=0) - counts) * counts, axis=1)
        target = chosen * capacity + slot_idx
        route_mat = (
            jnp.arange(experts * capacity, dtype=jnp.int32)[:, None] == target[None, :]
        ).astype(bfloat)
        outgoing = (
            jnp.dot(route_mat, normed_two, preferred_element_type=float32)
            .astype(bfloat)
            .reshape(experts, capacity, model_width)
        )
        arrived = lax.all_to_all(outgoing, "expert", split_axis=0, concat_axis=0, tiled=True)
        senders = arrived.shape[0]
        slots_here = arrived.shape[1]
        flat_rows = arrived.reshape(senders * slots_here, model_width)
        pre_act = jnp.dot(flat_rows, inner_w, preferred_element_type=float32)
        hidden = gelu_tanh(pre_act).astype(bfloat)
        produced = jnp.dot(hidden, outer_w, preferred_element_type=float32).astype(bfloat)
        returned = lax.all_to_all(
            produced.reshape(senders, slots_here, model_width),
            "expert",
            split_axis=0,
            concat_axis=0,
            tiled=True,
        )
        returned, arrived, pre_kept = (
            returned,
            arrived,
            pre_act.reshape(senders, slots_here, ff_width),
        )
        expert_back = jnp.einsum(
            "st,sd->td",
            route_mat,
            returned.reshape(experts * capacity, model_width),
            preferred_element_type=float32,
        )
        layer_rows.append((resid_mid + gate_prob[:, None] * expert_back).astype(bfloat))
        grad_output = out_grad[batch_idx].astype(float32)
        grad_gate = jnp.sum(grad_output * expert_back, axis=1)
        grad_expert = (gate_prob[:, None] * grad_output).astype(bfloat)
        grad_slots = (
            jnp.dot(route_mat, grad_expert, preferred_element_type=float32)
            .astype(bfloat)
            .reshape(experts, capacity, model_width)
        )
        grad_arrived = lax.all_to_all(grad_slots, "expert", split_axis=0, concat_axis=0, tiled=True)
        slot_rows = grad_arrived.shape[0] * grad_arrived.shape[1]
        grad_produced = grad_arrived.reshape(slot_rows, model_width)
        flat_pre = pre_kept.reshape(slot_rows, ff_width)
        hidden_again, gelu_back = jax.vjp(gelu_tanh, flat_pre)
        hidden_low = hidden_again.astype(bfloat)
        grad_outer = accumulate(
            grad_outer,
            jnp.einsum("rf,rd->fd", hidden_low, grad_produced, preferred_element_type=float32),
        )
        grad_hidden = jnp.einsum(
            "rd,fd->rf", grad_produced, outer_w, preferred_element_type=float32
        )
        grad_pre = gelu_back(grad_hidden)[0].astype(bfloat)
        flat_in = arrived.reshape(slot_rows, model_width)
        grad_inner = accumulate(
            grad_inner, jnp.einsum("rd,rf->df", flat_in, grad_pre, preferred_element_type=float32)
        )
        grad_sent = jnp.einsum(
            "rf,df->rd", grad_pre, inner_w, preferred_element_type=float32
        ).astype(bfloat)
        grad_home = lax.all_to_all(
            grad_sent.reshape(grad_arrived.shape), "expert", split_axis=0, concat_axis=0, tiled=True
        )
        grad_normed = jnp.einsum(
            "st,sd->td",
            route_mat,
            grad_home.reshape(experts * capacity, model_width),
            preferred_element_type=float32,
        )
        picked_f = jnp.where(picked, 1.0, 0.0)
        grad_logits = (grad_gate * gate_prob)[:, None] * (picked_f - gate_all)
        router_f = router_w.astype(float32)
        grad_normed = grad_normed + jnp.dot(grad_logits, router_f.T, precision=precise)
        grad_router = accumulate(
            grad_router, jnp.dot(normed_two.astype(float32).T, grad_logits, precision=precise)
        )
        renormed, norm_back = jax.vjp(norm_rows, resid_mid, gain_two_f)
        grad_resid, grad_gain = norm_back(grad_normed)
        grad_gain_two = accumulate(grad_gain_two, grad_gain)
        grad_mid = grad_output + grad_resid
        grad_attn = grad_mid.astype(bfloat)
        grad_wo = accumulate(
            grad_wo, jnp.einsum("ad,ae->de", attended, grad_attn, preferred_element_type=float32)
        )
        grad_attended = jnp.einsum(
            "ae,de->ad", grad_attn, output_w, preferred_element_type=float32
        ).astype(bfloat)
        grad_heads = grad_attended.reshape(tok_rows, head_count, head_dim)
        scores_again = masked_scores()
        probs_again = jnp.exp(scores_again - log_total)
        grad_probs = jnp.einsum(
            "ahd,bhd->hab", grad_heads, value_heads, preferred_element_type=float32
        )
        row_dot = jnp.sum(probs_again * grad_probs, axis=-1, keepdims=True)
        grad_scores = (probs_again * (grad_probs - row_dot)).astype(bfloat)
        grad_queries = (
            jnp.einsum(
                "hab,bhd->ahd", grad_scores, key_heads, preferred_element_type=float32
            ).reshape(tok_rows, model_width)
            * score_scale
        ).astype(bfloat)
        grad_table = accumulate(grad_table, table_grad(grad_scores, bucket_table))
        grad_values = jnp.einsum(
            "hab,ahd->bhd", probs_again.astype(bfloat), grad_heads, preferred_element_type=float32
        ).reshape(key_rows, model_width)
        grad_keys = (
            jnp.einsum(
                "hab,ahd->bhd", grad_scores, query_heads, preferred_element_type=float32
            ).reshape(key_rows, model_width)
            * score_scale
        )
        keys_sum, values_sum = (
            lax.psum_scatter(
                grad_keys.astype(jnp.bfloat16), "expert", scatter_dimension=0, tiled=True
            ).astype(jnp.float32),
            lax.psum_scatter(
                grad_values.astype(jnp.bfloat16), "expert", scatter_dimension=0, tiled=True
            ).astype(jnp.float32),
        )
        keys_low = keys_sum.astype(bfloat)
        values_low = values_sum.astype(bfloat)
        grad_wq = accumulate(
            grad_wq,
            jnp.einsum("ad,ae->de", normed_one, grad_queries, preferred_element_type=float32),
        )
        grad_wk = accumulate(
            grad_wk, jnp.einsum("ad,ae->de", normed_one, keys_low, preferred_element_type=float32)
        )
        grad_wv = accumulate(
            grad_wv, jnp.einsum("ad,ae->de", normed_one, values_low, preferred_element_type=float32)
        )
        grad_normed_one = jnp.einsum(
            "ae,de->ad", grad_queries, query_w, preferred_element_type=float32
        )
        grad_normed_one = grad_normed_one + jnp.einsum(
            "ae,de->ad", keys_low, key_w, preferred_element_type=float32
        )
        grad_normed_one = grad_normed_one + jnp.einsum(
            "ae,de->ad", values_low, value_w, preferred_element_type=float32
        )
        renormed_one, first_back = jax.vjp(norm_rows, tokens_f, gain_one_f)
        grad_tokens, grad_gain_first = first_back(grad_normed_one)
        grad_gain_one = accumulate(grad_gain_one, grad_gain_first)
        input_rows.append(grad_mid + grad_tokens)
    part_gain_one, part_wq, part_wk, part_wv, part_wo, part_table, part_gain_two, part_router = (
        lax.psum_scatter(
            grad_gain_one.astype(jnp.bfloat16), "dp", scatter_dimension=0, tiled=True
        ).astype(jnp.float32),
        lax.psum_scatter(
            grad_wq.astype(jnp.bfloat16), "dp", scatter_dimension=0, tiled=True
        ).astype(jnp.float32),
        lax.psum_scatter(
            grad_wk.astype(jnp.bfloat16), "dp", scatter_dimension=0, tiled=True
        ).astype(jnp.float32),
        lax.psum_scatter(
            grad_wv.astype(jnp.bfloat16), "dp", scatter_dimension=0, tiled=True
        ).astype(jnp.float32),
        lax.psum_scatter(
            grad_wo.astype(jnp.bfloat16), "dp", scatter_dimension=0, tiled=True
        ).astype(jnp.float32),
        lax.psum_scatter(
            grad_table.astype(jnp.bfloat16), "dp", scatter_dimension=0, tiled=True
        ).astype(jnp.float32),
        lax.psum_scatter(
            grad_gain_two.astype(jnp.bfloat16), "dp", scatter_dimension=0, tiled=True
        ).astype(jnp.float32),
        lax.psum_scatter(
            grad_router.astype(jnp.bfloat16), "dp", scatter_dimension=0, tiled=True
        ).astype(jnp.float32),
    )
    sum_gain_one, sum_wq, sum_wk, sum_wv, sum_wo, sum_table, sum_gain_two, sum_router = (
        lax.psum(part_gain_one.astype(jnp.bfloat16), "expert").astype(jnp.float32),
        lax.psum(part_wq.astype(jnp.bfloat16), "expert").astype(jnp.float32),
        lax.psum(part_wk.astype(jnp.bfloat16), "expert").astype(jnp.float32),
        lax.psum(part_wv.astype(jnp.bfloat16), "expert").astype(jnp.float32),
        lax.psum(part_wo.astype(jnp.bfloat16), "expert").astype(jnp.float32),
        lax.psum(part_table.astype(jnp.bfloat16), "expert").astype(jnp.float32),
        lax.psum(part_gain_two.astype(jnp.bfloat16), "expert").astype(jnp.float32),
        lax.psum(part_router.astype(jnp.bfloat16), "expert").astype(jnp.float32),
    )
    inner_part, outer_part = (
        lax.psum_scatter(
            grad_inner[None].astype(jnp.bfloat16), "dp", scatter_dimension=1, tiled=True
        ).astype(jnp.float32),
        lax.psum_scatter(
            grad_outer[None].astype(jnp.bfloat16), "dp", scatter_dimension=1, tiled=True
        ).astype(jnp.float32),
    )
    return (
        jnp.stack(layer_rows),
        jnp.stack(input_rows),
        sum_gain_one,
        sum_wq,
        sum_wk,
        sum_wv,
        sum_wo,
        sum_table,
        sum_gain_two,
        sum_router,
        inner_part,
        outer_part,
    )


def solution(mesh):
    return jax.shard_map(
        on_device,
        mesh=mesh,
        in_specs=(
            P(None, ("dp", "expert"), None),
            P(None, ("dp", "expert"), None),
            P(None, "dp", None),
            P(None, "dp", None),
            P(None, ("dp", "expert"), None),
            P("dp"),
            P("dp", None),
            P("dp", None),
            P("dp", None),
            P("dp", None),
            P("dp", None),
            P("dp"),
            P("dp", None),
            P("expert", "dp", None),
            P("expert", "dp", None),
        ),
        out_specs=(
            P(None, ("dp", "expert"), None),
            P(None, ("dp", "expert"), None),
            P("dp"),
            P("dp", None),
            P("dp", None),
            P("dp", None),
            P("dp", None),
            P("dp", None),
            P("dp"),
            P("dp", None),
            P("expert", "dp", None),
            P("expert", "dp", None),
        ),
        check_vma=False,
    )
```

profile of v0, /device:TPU:0, one launch (start us, length us, event | category | flops | bytes accessed | tf_op | source)
XLA Modules:
  0.0 1132.6 jit_solution(10793893675216077602)
XLA Ops:
  13.1 35.2 %all-reduce.6 = (bf16[768]{0:T(1024)(128)(2,1)S(1)}, bf16[768]{0:T(1024)(128)(2,1)S(1)}) all-reduce(bf16[768]{0:T(1024)(128)(2,1)S(1)} %dynamic-update-slice, bf16[768]{0:T(1024)(128)(2,1)S(1)} %dynamic-update-slice.1), channel_id=1, replica_groups=mesh['dp'=16,'expert'=2] {'dp'}, use_global_device_ids=true, to_apply=%add | all-reduce | flops 1536 | bytes 6144
  54.8 36.2 %all-gather.13.cloned.1.call-done = bf16[768,768]{1,0:T(8,128)(2,1)} async-done(((bf16[48,768]{1,0:T(8,128)(2,1)}), bf16[768,768]{1,0:T(8,128)(2,1)}) %all-gather.13.cloned.1.call-update) | async-done | bytes 1179664 | tf_op jit(solution)/shard_map/all_gather | solution.py:74
  114.3 19.3 %all-gather = bf16[16,2,12]{2,1,0:T(2,128)(2,1)S(1)} all-gather(bf16[1,2,12]{2,1,0:T(2,128)(2,1)S(1)} %bitcast.412), channel_id=1, replica_groups=mesh['dp'=16,'expert'=2] {'dp'}, dimensions={0}, use_global_device_ids=true | all-gather | bytes 816 | tf_op jit(solution)/shard_map/all_gather | solution.py:76
  133.6 17.5 %all-gather.1 = bf16[16,48,2]{1,2,0:T(2,128)(2,1)S(1)} all-gather(bf16[1,48,2]{1,2,0:T(2,128)(2,1)S(1)} %bitcast.413), channel_id=1, replica_groups=mesh['dp'=16,'expert'=2] {'dp'}, dimensions={0}, use_global_device_ids=true | all-gather | bytes 3264 | tf_op jit(solution)/shard_map/all_gather | solution.py:78
  151.2 16.7 %fusion.3 = f32[512,1024,12]{1,2,0:T(8,128)} fusion(bf16[32,12,1]{1,0,2:T(8,128)(2,1)S(1)} %bitcast.396, s32[512,1024]{1,0:T(8,128)} %select_add_fusion.1), kind=kOutput, calls=%fused_computation.5 | convolution fusion | flops 419430400 | bytes 27263744 | tf_op jit(solution)/shard_map/kab,kh->hab/dot_general | solution.py:47
  167.9 16.2 %fusion.1 = f32[512,1024,12]{1,2,0:T(8,128)} fusion(bf16[32,12,1]{1,0,2:T(8,128)(2,1)S(1)} %bitcast.397, s32[512,1024]{1,0:T(8,128)S(1)} %copy-done.15), kind=kOutput, calls=%fused_computation.2 | convolution fusion | flops 419430400 | bytes 27263744 | tf_op jit(solution)/shard_map/kab,kh->hab/dot_general | solution.py:47
  197.4 31.1 %fusion.232 = (f32[12,512]{1,0:T(8,128)S(1)}, f32[12,512,1024]{2,1,0:T(8,128)}) fusion(f32[512,1024,12]{1,2,0:T(8,128)} %fusion.3, bf16[512,12,64]{0,2,1:T(8,128)(2,1)} %bitcast.355, bf16[1024,12,64]{0,2,1:T(8,128)(2,1)} %bitcast.349, pred[512,1024]{1,0:T(8,128)(4,1)S(1)} %broadcast_compare_fusion.1), kind=kOutput, calls=%fused_computation.304 | convolution fusion | flops 830466048 | bytes 53239808 | tf_op jit(solution)/shard_map/ahd,bhd->hab/dot_general | solution.py:163
  260.3 24.4 %all-gather.29.cloned.1.call-done = bf16[1024,768]{1,0:T(8,128)(2,1)} async-done(((bf16[512,768]{1,0:T(8,128)(2,1)}), bf16[1024,768]{1,0:T(8,128)(2,1)}) %all-gather.29.cloned.1.call-update) | async-done | bytes 1572880 | tf_op jit(solution)/shard_map/all_gather | solution.py:148
  287.3 29.1 %fusion.233 = (f32[12,512]{1,0:T(8,128)S(1)}, f32[12,512,1024]{2,1,0:T(8,128)}) fusion(f32[512,1024,12]{1,2,0:T(8,128)} %fusion.1, bf16[512,12,64]{0,2,1:T(8,128)(2,1)S(1)} %bitcast.353, bf16[1024,12,64]{0,2,1:T(8,128)(2,1)} %bitcast.351, pred[512,1024]{1,0:T(8,128)(4,1)S(1)} %broadcast_compare_fusion), kind=kOutput, calls=%fused_computation.305 | convolution fusion | flops 830466048 | bytes 53239808 | tf_op jit(solution)/shard_map/ahd,bhd->hab/dot_general | solution.py:163
  377.1 17.5 %all-gather.27.cloned.1.call-done = bf16[1,3072,768]{2,1,0:T(8,128)(2,1)} async-done(((bf16[1,192,768]{2,1,0:T(8,128)(2,1)}), bf16[1,3072,768]{2,1,0:T(8,128)(2,1)}) %all-gather.27.cloned.1.call-update) | async-done | bytes 4718608 | tf_op jit(solution)/shard_map/all_gather | solution.py:85
  505.3 11.9 %fusion.102 = bf16[12,64,1024]{2,1,0:T(8,128)(2,1)} fusion(bf16[512,12,64]{0,2,1:T(8,128)(2,1)} %bitcast.361, f32[12,512,1024]{2,1,0:T(8,128)} %get-tuple-element.62, f32[12,512]{1,0:T(8,128)S(1)} %log_add_fusion.1), kind=kOutput, calls=%fused_computation.141 | convolution fusion | flops 818675712 | bytes 27549696 | tf_op jit(solution)/shard_map/hab,ahd->bhd/dot_general | solution.py:298
  536.3 16.2 %multiply_reduce_fusion.1 = (f32[12,512]{1,0:T(8,128)S(1)}, f32[12,512,1024]{2,1,0:T(8,128)}) fusion(f32[12,512,1024]{2,1,0:T(8,128)} %get-tuple-element.62, f32[12,512]{1,0:T(8,128)S(1)} %log_add_fusion.1, bf16[512,12,64]{0,2,1:T(8,128)(2,1)} %bitcast.362, bf16[1024,12,64]{0,2,1:T(8,128)(2,1)S(1)} %bitcast.348), kind=kOutput, calls=%fused_computation.17 | convolution fusion | flops 824174592 | bytes 52740096 | tf_op jit(solution)/shard_map/ahd,bhd->hab/dot_general | solution.py:286
  552.5 16.8 %multiply_convert_fusion.1 = bf16[12,512,1024]{2,1,0:T(8,128)(2,1)S(1)} fusion(f32[12,512,1024]{2,1,0:T(8,128)} %get-tuple-element.76, f32[12,512,1024]{2,1,0:T(8,128)} %get-tuple-element.62, f32[12,512]{1,0:T(8,128)S(1)} %get-tuple-element.75, f32[12,512]{1,0:T(8,128)S(1)} %log_add_fusion.1), kind=kLoop, calls=%fused_computation.16 | loop fusion | flops 25165824 | bytes 62963712 | tf_op jit(solution)/shard_map/convert_element_type | solution.py:290
  575.7 16.4 %multiply_reduce_fusion = (f32[12,512]{1,0:T(8,128)S(1)}, f32[12,512,1024]{2,1,0:T(8,128)}) fusion(f32[12,512,1024]{2,1,0:T(8,128)} %get-tuple-element.66, f32[12,512]{1,0:T(8,128)S(1)} %log_add_fusion, bf16[512,12,64]{0,2,1:T(8,128)(2,1)} %bitcast.360, bf16[1024,12,64]{0,2,1:T(8,128)(2,1)S(1)} %bitcast.346), kind=kOutput, calls=%fused_computation.15 | convolution fusion | flops 824174592 | bytes 52740096 | tf_op jit(solution)/shard_map/ahd,bhd->hab/dot_general | solution.py:286
  592.1 16.7 %multiply_convert_fusion = bf16[12,512,1024]{2,1,0:T(8,128)(2,1)S(1)} fusion(f32[12,512,1024]{2,1,0:T(8,128)} %get-tuple-element.78, f32[12,512,1024]{2,1,0:T(8,128)} %get-tuple-element.66, f32[12,512]{1,0:T(8,128)S(1)} %get-tuple-element.77, f32[12,512]{1,0:T(8,128)S(1)} %log_add_fusion), kind=kLoop, calls=%fused_computation.14 | loop fusion | flops 25165824 | bytes 62963712 | tf_op jit(solution)/shard_map/convert_element_type | solution.py:290
  672.1 28.3 %reduce-scatter.28.cloned.1.call-done = bf16[48,768]{1,0:T(8,128)(2,1)} async-done(((bf16[768,768]{1,0:T(8,128)(2,1)}), bf16[48,768]{1,0:T(8,128)(2,1)}) %reduce-scatter.28.cloned.1.call-update) | async-done | bytes 73744 | tf_op jit(solution)/shard_map/reduce_scatter | solution.py:353
  700.4 60.6 %reduce-scatter.22.cloned.1.call-done = bf16[48,768]{1,0:T(8,128)(2,1)} async-done(((bf16[768,768]{1,0:T(8,128)(2,1)}), bf16[48,768]{1,0:T(8,128)(2,1)}) %reduce-scatter.22.cloned.1.call-update) | async-done | bytes 73744 | tf_op jit(solution)/shard_map/reduce_scatter | solution.py:344
  761.0 60.6 %reduce-scatter.26.cloned.1.call-done = bf16[48,768]{1,0:T(8,128)(2,1)} async-done(((bf16[768,768]{1,0:T(8,128)(2,1)}), bf16[48,768]{1,0:T(8,128)(2,1)}) %reduce-scatter.26.cloned.1.call-update) | async-done | bytes 73744 | tf_op jit(solution)/shard_map/reduce_scatter | solution.py:350
  821.6 61.1 %reduce-scatter.24.cloned.1.call-done = bf16[48,768]{1,0:T(8,128)(2,1)} async-done(((bf16[768,768]{1,0:T(8,128)(2,1)}), bf16[48,768]{1,0:T(8,128)(2,1)}) %reduce-scatter.24.cloned.1.call-update) | async-done | bytes 73744 | tf_op jit(solution)/shard_map/reduce_scatter | solution.py:347
  882.8 12.9 %fusion.45 = bf16[1,3072,768]{2,1,0:T(8,128)(2,1)} fusion(f32[3072,768]{1,0:T(8,128)} %fusion.226, bf16[544,768]{1,0:T(8,128)(2,1)} %bitcast.376, f32[544,3072]{1,0:T(8,128)} %fusion.40), kind=kOutput, calls=%fused_computation.65 | convolution fusion | flops 2586673152 | bytes 21676032 | tf_op jit(solution)/shard_map/rf,rd->fd/dot_general | solution.py:243
  917.2 16.0 %fusion.148 = f32[32,12]{1,0:T(8,128)S(1)} fusion(bf16[12,512,1024]{2,1,0:T(8,128)(2,1)} %copy-done, s32[512,1024]{1,0:T(8,128)S(1)} %copy-done.17), kind=kOutput, calls=%fused_computation.202 | convolution fusion | flops 419430400 | bytes 14681600 | tf_op jit(solution)/shard_map/hab,kab->kh/dot_general | solution.py:51
  933.2 15.2 %fusion.157 = bf16[32,12]{1,0:T(8,128)(2,1)S(1)} fusion(f32[32,12]{1,0:T(8,128)S(1)} %fusion.148, bf16[12,512,1024]{2,1,0:T(8,128)(2,1)S(1)} %bitcast.344, s32[512,1024]{1,0:T(8,128)S(1)} %copy-done.16), kind=kOutput, calls=%fused_computation.205 | convolution fusion | flops 419431168 | bytes 14682368 | tf_op jit(solution)/shard_map/hab,kab->kh/dot_general | solution.py:51
  958.0 58.3 %all-reduce.5 = (bf16[768]{0:T(1024)(128)(2,1)S(1)}, bf16[32,12]{1,0:T(8,128)(2,1)S(1)}, bf16[768]{0:T(1024)(128)(2,1)S(1)}) all-reduce(bf16[768]{0:T(1024)(128)(2,1)S(1)} %get-tuple-element.83, bf16[32,12]{1,0:T(8,128)(2,1)S(1)} %fusion.157, bf16[768]{0:T(1024)(128)(2,1)S(1)} %get-tuple-element.82), channel_id=6, replica_groups=mesh['dp'=16,'expert'=2] {'dp'}, use_global_device_ids=true, to_apply=%region_36.37.clone | all-reduce | flops 1920 | bytes 7680
  1046.6 77.2 %reduce-scatter.30.cloned.1.call-done = bf16[1,48,3072]{2,1,0:T(8,128)(2,1)} async-done(((bf16[1,768,3072]{2,1,0:T(8,128)(2,1)}), bf16[1,48,3072]{2,1,0:T(8,128)(2,1)}) %reduce-scatter.30.cloned.1.call-update) | async-done | bytes 294928 | tf_op jit(solution)/shard_map/reduce_scatter | solution.py:377
  (365 shorter events, 403.5 us)
Async XLA Ops:
  7.2 44.3 %all-gather.19.cloned.1.call-start = ((), (), s32[]{:S(2)}) async-start(), calls=%async_computation.22 | async-start | bytes 1253376 | tf_op jit(solution)/shard_map/all_gather | solution.py:73
  7.9 83.1 %all-gather.13.cloned.1.call-start = ((), (), s32[]{:S(2)}) async-start(), calls=%async_computation.19 | async-start | bytes 1253376 | tf_op jit(solution)/shard_map/all_gather | solution.py:74
  8.7 176.2 %all-gather.17.cloned.1.call-start = ((), (), s32[]{:S(2)}) async-start(), calls=%async_computation.21 | async-start | bytes 1253376 | tf_op jit(solution)/shard_map/all_gather | solution.py:72
  9.4 185.5 %all-gather.21.cloned.1.call-start = ((), (), s32[]{:S(2)}) async-start(), calls=%async_computation.23 | async-start | bytes 2359296 | tf_op jit(solution)/shard_map/all_gather | solution.py:147
  54.8 185.2 %all-gather.15.cloned.1.call-start = ((), (), s32[]{:S(2)}) async-start(), calls=%async_computation.20 | async-start | bytes 2359296 | tf_op jit(solution)/shard_map/all_gather | solution.py:148
  94.0 160.2 %all-gather.23.cloned.1.call-start = ((), (), s32[]{:S(2)}) async-start(), calls=%async_computation.24 | async-start | bytes 1253376 | tf_op jit(solution)/shard_map/all_gather | solution.py:75
  94.6 163.1 %all-gather.31.cloned.1.call-start = ((), (), s32[]{:S(2)}) async-start(), calls=%async_computation.28 | async-start | bytes 2359296 | tf_op jit(solution)/shard_map/all_gather | solution.py:147
  97.8 186.9 %all-gather.29.cloned.1.call-start = ((), (), s32[]{:S(2)}) async-start(), calls=%async_computation.27 | async-start | bytes 2359296 | tf_op jit(solution)/shard_map/all_gather | solution.py:148
  100.8 261.0 %all-gather.25.cloned.1.call-start = ((), (), s32[]{:S(2)}) async-start(), calls=%async_computation.25 | async-start | bytes 5013504 | tf_op jit(solution)/shard_map/all_gather | solution.py:84
  101.6 293.1 %all-gather.27.cloned.1.call-start = ((), (), s32[]{:S(2)}) async-start(), calls=%async_computation.26 | async-start | bytes 5013504 | tf_op jit(solution)/shard_map/all_gather | solution.py:85
  373.5 36.4 %all-to-all-start = ((bf16[2,272,768]{2,1,0:T(8,128)(2,1)}), bf16[2,272,768]{2,1,0:T(8,128)(2,1)S(1)}, u32[]{:S(2)}, u32[]{:S(2)}) async-start(bf16[2,272,768]{2,1,0:T(8,128)(2,1)} %bitcast.379), calls=%async_computation | async-start | bytes 1671168 | tf_op jit(solution)/shard_map/all_to_all | solution.py:201
  429.5 20.1 %all-to-all-start.3 = ((bf16[2,272,768]{2,1,0:T(8,128)(2,1)}), bf16[2,272,768]{2,1,0:T(8,128)(2,1)S(1)}, u32[]{:S(2)}, u32[]{:S(2)}) async-start(bf16[2,272,768]{2,1,0:T(8,128)(2,1)} %bitcast.381), calls=%async_computation.3 | async-start | bytes 1671168 | tf_op jit(solution)/shard_map/all_to_all | solution.py:208
  486.1 154.8 %reduce-scatter.16.cloned.1.call-start = ((), (), s32[]{:S(2)}) async-start(), calls=%async_computation.30 | async-start | bytes 2359296 | tf_op jit(solution)/shard_map/reduce_scatter | solution.py:311
  517.3 127.2 %reduce-scatter.20.cloned.1.call-start = ((), (), s32[]{:S(2)}) async-start(), calls=%async_computation.32 | async-start | bytes 2359296 | tf_op jit(solution)/shard_map/reduce_scatter | solution.py:311
  534.9 113.6 %reduce-scatter.14.cloned.1.call-start = ((), (), s32[]{:S(2)}) async-start(), calls=%async_computation.29 | async-start | bytes 2359296 | tf_op jit(solution)/shard_map/reduce_scatter | solution.py:308
  574.3 77.7 %reduce-scatter.18.cloned.1.call-start = ((), (), s32[]{:S(2)}) async-start(), calls=%async_computation.31 | async-start | bytes 2359296 | tf_op jit(solution)/shard_map/reduce_scatter | solution.py:308
  613.8 86.6 %reduce-scatter.28.cloned.1.call-start = ((), (), s32[]{:S(2)}) async-start(), calls=%async_computation.36 | async-start | bytes 1253376 | tf_op jit(solution)/shard_map/reduce_scatter | solution.py:353
  617.9 143.1 %reduce-scatter.22.cloned.1.call-start = ((), (), s32[]{:S(2)}) async-start(), calls=%async_computation.33 | async-start | bytes 1253376 | tf_op jit(solution)/shard_map/reduce_scatter | solution.py:344
  640.9 180.6 %reduce-scatter.26.cloned.1.call-start = ((), (), s32[]{:S(2)}) async-start(), calls=%async_computation.35 | async-start | bytes 1253376 | tf_op jit(solution)/shard_map/reduce_scatter | solution.py:350
  648.4 234.2 %reduce-scatter.24.cloned.1.call-start = ((), (), s32[]{:S(2)}) async-start(), calls=%async_computation.34 | async-start | bytes 1253376 | tf_op jit(solution)/shard_map/reduce_scatter | solution.py:347
  656.0 292.4 %reduce-scatter.34.cloned.1.call-start = ((), (), s32[]{:S(2)}) async-start(), calls=%async_computation.39 | async-start | bytes 208896
  660.5 368.2 %all-reduce.11.cloned.1.call-start = ((), (), s32[]{:S(2)}) async-start(), calls=%async_computation.40 | async-start | bytes 589824 | tf_op jit(solution)/shard_map/psum | solution.py:368
  882.7 162.1 %reduce-scatter.32.cloned.1.call-start = ((), (), s32[]{:S(2)}) async-start(), calls=%async_computation.38 | async-start | bytes 5013504 | tf_op jit(solution)/shard_map/reduce_scatter | solution.py:380
  895.7 228.0 %reduce-scatter.30.cloned.1.call-start = ((), (), s32[]{:S(2)}) async-start(), calls=%async_computation.37 | async-start | bytes 5013504 | tf_op jit(solution)/shard_map/reduce_scatter | solution.py:377
  (80 other events, 1231.0 us)
Sparse Core Ops, SparseCore 0:
  10.3 41.1 all-gather.18
  53.8 37.1 all-gather.12
  93.3 37.3 all-gather.16
  132.1 26.2 all-gather.20
  160.4 27.1 all-gather.14
  189.8 38.3 all-gather.22
  229.7 26.1 all-gather.30
  257.4 27.2 all-gather.28
  287.0 53.3 all-gather.24
  342.5 52.1 all-gather.26
  517.4 23.7 reduce-scatter.15
  543.4 26.0 reduce-scatter.19
  574.5 23.9 reduce-scatter.13
  614.0 24.8 reduce-scatter.17
  642.3 58.0 reduce-scatter.27
  703.9 57.0 reduce-scatter.21
  764.5 57.0 reduce-scatter.25
  825.6 57.0 reduce-scatter.23
  886.8 52.7 reduce-scatter.33
  941.9 23.1 all-reduce.10
  968.9 75.8 reduce-scatter.31
  1049.1 74.5 reduce-scatter.29
where the time goes:
time: 1140 us; the launch traced here: 1130 us
  matrix products  411 us (36%)
  waiting for transfers between devices  405 us (36%)
  blocking collectives  135 us (12%)
  other arithmetic  92.7 us (8%)
  local copies, waits for them, and re-layouts  36.1 us (3%)
  starting transfers between devices  35 us (3%)
  between operations  17.6 us (2%)
    unnamed x2, blocking collectives  93.5 us
    reduce_scatter x1, waiting for transfers between devices, on_device(): lax.psum_scatter(grad_inner[None].astype(jnp.bfloat16), 'dp', scatter_dim...  77.2 us
    reduce_scatter x1, waiting for transfers between devices, on_device(): lax.psum_scatter(grad_wk.astype(jnp.bfloat16), 'dp', scatter_dimension=0,...  61.1 us
    reduce_scatter x1, waiting for transfers between devices, on_device(): lax.psum_scatter(grad_wq.astype(jnp.bfloat16), 'dp', scatter_dimension=0,...  60.6 us
    reduce_scatter x1, waiting for transfers between devices, on_device(): lax.psum_scatter(grad_wv.astype(jnp.bfloat16), 'dp', scatter_dimension=0,...  60.6 us
    dot_general x2, matrix products, masked_scores(): jnp.einsum('ahd,bhd->hab', query_heads, key_heads, preferred_element_type...  60.2 us
    all_gather x1, waiting for transfers between devices, fetch_dense(): lax.all_gather(value_shard, 'dp', axis=0, tiled=True)  36.2 us
    convert_element_type x2, other arithmetic, on_device(): grad_scores = (probs_again * (grad_probs - row_dot)).astype(bfloat)  33.5 us
  transfers between devices with their start and end apart: 30, of which 15 were waited for; matrix products, arithmetic and copies ran while one was open for 44% of the time, Pallas kernels for 0%

commit v1 on v0

v1 whole, which is shorter than its diff:
```python
import functools

import jax
import jax.numpy as jnp
from jax import lax
from jax.experimental import pallas as pl
from jax.experimental.pallas import tpu as pltpu
from jax.sharding import PartitionSpec as P

bucket_edges = (1, 2, 3, 4, 5, 6, 7, 8, 12, 16, 23, 32, 46, 64, 91)
levels_all = len(bucket_edges) + 1
epsilon = 1e-06
masked_score = -1000000000.0
precise = lax.Precision.HIGHEST
float32 = jnp.float32
bfloat = jnp.bfloat16
tile = 128
vmem_bytes = 56 * 1024 * 1024


def params():
    return pltpu.CompilerParams(vmem_limit_bytes=vmem_bytes)


def dot_nn(left, right):
    return lax.dot_general(left, right, (((1,), (0,)), ((), ())), preferred_element_type=float32)


def dot_nt(left, right):
    return lax.dot_general(left, right, (((1,), (1,)), ((), ())), preferred_element_type=float32)


def dot_tn(left, right):
    return lax.dot_general(left, right, (((0,), (0,)), ((), ())), preferred_element_type=float32)


def norm_rows(rows, gain):
    mean_square = jnp.mean(rows * rows, axis=-1, keepdims=True)
    return rows * lax.rsqrt(mean_square + epsilon) * gain


def norm_back(rows, gain, grad):
    scale = lax.rsqrt(jnp.mean(rows * rows, axis=-1, keepdims=True) + epsilon)
    unit = rows * scale
    weighted = grad * gain
    inner = jnp.mean(weighted * unit, axis=-1, keepdims=True)
    return scale * (weighted - unit * inner), grad * unit


def bucket_of(offset):
    distance = jnp.abs(offset)
    levels = jnp.zeros(offset.shape, jnp.int32)
    for edge_value in bucket_edges:
        levels = levels + (distance >= edge_value).astype(jnp.int32)
    return levels + levels_all * (offset > 0).astype(jnp.int32)


def near_shift(tiles):
    return min(1, tiles - 1)


def bias_kernel(stride, reach, table_ref, out_ref):
    row = lax.broadcasted_iota(jnp.int32, (tile, tile), 0)
    lane = lax.broadcasted_iota(jnp.int32, (tile, tile), 1)
    heads = out_ref.shape[0]
    for shift in range(-reach, reach + 1):
        for step in range(2 * stride - 1):
            ids = bucket_of(stride * (tile * shift + lane - row) + step - (stride - 1))
            columns = slice((shift + reach) * tile, (shift + reach + 1) * tile)
            for head in range(heads):
                values = jnp.broadcast_to(table_ref[head : head + 1, :], (tile, tile))
                out_ref[head, step, :, columns] = jnp.take_along_axis(values, ids, axis=1)


def bias_tiles(table, stride, tiles):
    heads = table.shape[1]
    reach = near_shift(tiles)
    lanes = jnp.pad(table.astype(float32).T, ((0, 0), (0, tile - table.shape[0])))
    return pl.pallas_call(
        functools.partial(bias_kernel, stride, reach),
        out_shape=jax.ShapeDtypeStruct(
            (heads, 2 * stride - 1, tile, (2 * reach + 1) * tile), float32
        ),
        compiler_params=params(),
        name="bias_tiles",
    )(lanes)


def attend_kernel(
    stride, head_dim, far_ref, q_ref, k_ref, v_ref, info_ref, bias_ref, probs_ref, out_ref
):
    pair = pl.program_id(0)
    rows_all = q_ref.shape[0]
    tiles = rows_all // tile
    reach = near_shift(tiles)
    per = tile // head_dim
    lane = lax.broadcasted_iota(jnp.int32, (tile, tile), 1)
    for block in range(tiles):
        rows = slice(block * tile, (block + 1) * tile)
        place = info_ref[rows, 0:1]
        low = info_ref[rows, 1:2]
        high = info_ref[rows, 2:3]
        queries = q_ref[rows, :]
        joined = None
        for sub in range(per):
            head = pair * per + sub
            inside = (lane >= sub * head_dim) & (lane < (sub + 1) * head_dim)
            own = jnp.where(inside, queries, jnp.zeros_like(queries))
            raw = dot_nt(own, k_ref[...])
            pieces = []
            top = None
            for part in range(stride):
                for col in range(tiles):
                    start = part * rows_all + col * tile
                    piece = raw[:, start : start + tile]
                    shift = col - block
                    if shift < -reach:
                        piece = piece + far_ref[0, head]
                    elif shift > reach:
                        piece = piece + far_ref[1, head]
                    else:
                        columns = slice((shift + reach) * tile, (shift + reach + 1) * tile)
                        bias = bias_ref[sub, part + stride - 1, :, columns]
                        for other in range(1, stride):
                            bias = jnp.where(
                                place == other,
                                bias_ref[sub, part - other + stride - 1, :, columns],
                                bias,
                            )
                        piece = piece + bias
                    position = stride * (col * tile + lane) + part
                    piece = jnp.where(
                        (position >= low) & (position < high), piece, masked_score
                    )
                    pieces.append(piece)
                    top = piece if top is None else jnp.maximum(top, piece)
            row_max = jnp.max(top, axis=-1, keepdims=True)
            total = None
            for idx, piece in enumerate(pieces):
                pieces[idx] = jnp.exp(piece - row_max)
                total = pieces[idx] if total is None else total + pieces[idx]
            inverse = 1.0 / jnp.sum(total, axis=-1, keepdims=True)
            low_probs = jnp.concatenate(
                [(piece * inverse).astype(bfloat) for piece in pieces], axis=1
            )
            probs_ref[sub, rows, :] = low_probs
            result = dot_nn(low_probs, v_ref[...])
            joined = result if joined is None else jnp.where(inside, result, joined)
        out_ref[rows, :] = joined.astype(bfloat)


def attend(queries, keys, values, info, bias, far, head_dim, stride):
    rows_all, width = queries.shape
    keys_all = keys.shape[0]
    per = tile // head_dim
    heads = width // head_dim
    return pl.pallas_call(
        functools.partial(attend_kernel, stride, head_dim),
        grid=(width // tile,),
        in_specs=[
            pl.BlockSpec(memory_space=pltpu.SMEM),
            pl.BlockSpec((rows_all, tile), lambda i: (0, i)),
            pl.BlockSpec((keys_all, tile), lambda i: (0, i)),
            pl.BlockSpec((keys_all, tile), lambda i: (0, i)),
            pl.BlockSpec(info.shape, lambda i: (0, 0)),
            pl.BlockSpec((per,) + bias.shape[1:], lambda i: (i, 0, 0, 0)),
        ],
        out_specs=[
            pl.BlockSpec((per, rows_all, keys_all), lambda i: (i, 0, 0)),
            pl.BlockSpec((rows_all, tile), lambda i: (0, i)),
        ],
        out_shape=[
            jax.ShapeDtypeStruct((heads, rows_all, keys_all), bfloat),
            jax.ShapeDtypeStruct((rows_all, width), bfloat),
        ],
        compiler_params=params(),
        cost_estimate=pl.CostEstimate(
            flops=16 * rows_all * keys_all * width,
            bytes_accessed=2 * heads * rows_all * keys_all,
            transcendentals=heads * rows_all * keys_all,
        ),
        name="attend",
    )(far, queries, keys, values, info, bias)


def attend_back_kernel(
    stride,
    head_dim,
    scale,
    probs_ref,
    grad_ref,
    out_ref,
    q_ref,
    k_ref,
    v_ref,
    info_ref,
    dq_ref,
    dk_ref,
    dv_ref,
    dbias_ref,
    dfar_ref,
    ds_ref,
):
    rows_all = q_ref.shape[0]
    tiles = rows_all // tile
    reach = near_shift(tiles)
    per = tile // head_dim
    lane = lax.broadcasted_iota(jnp.int32, (tile, tile), 1)
    queries_t = q_ref[...].T
    grads_t = grad_ref[...].T
    dbias_ref[...] = jnp.zeros_like(dbias_ref)
    dfar_ref[...] = jnp.zeros_like(dfar_ref)
    dk_parts = []
    dv_parts = []
    for sub in range(per):
        inside = (lane >= sub * head_dim) & (lane < (sub + 1) * head_dim)
        for block in range(tiles):
            rows = slice(block * tile, (block + 1) * tile)
            place = info_ref[rows, 0:1]
            grads = grad_ref[rows, :]
            own = jnp.where(inside, grads, jnp.zeros_like(grads))
            row_dot = jnp.sum(
                own.astype(float32) * out_ref[rows, :].astype(float32), axis=-1, keepdims=True
            )
            raw = dot_nt(own, v_ref[...])
            pieces = []
            for part in range(stride):
                for col in range(tiles):
                    start = part * rows_all + col * tile
                    piece = probs_ref[sub, rows, start : start + tile].astype(float32) * (
                        raw[:, start : start + tile] - row_dot
                    )
                    shift = col - block
                    if shift < -reach:
                        dfar_ref[sub, 0] += piece
                    elif shift > reach:
                        dfar_ref[sub, 1] += piece
                    else:
                        columns = slice((shift + reach) * tile, (shift + reach + 1) * tile)
                        for other in range(stride):
                            dbias_ref[sub, part - other + stride - 1, :, columns] += jnp.where(
                                place == other, piece, 0.0
                            )
                    pieces.append(piece.astype(bfloat))
            low_grads = jnp.concatenate(pieces, axis=1)
            ds_ref[rows, :] = low_grads
            result = dot_nn(low_grads, k_ref[...]) * scale
            if sub == 0:
                dq_ref[rows, :] = result.astype(bfloat)
            else:
                dq_ref[rows, :] = jnp.where(inside, result.astype(bfloat), dq_ref[rows, :])
        dims = slice(sub * head_dim, (sub + 1) * head_dim)
        dk_parts.append(dot_nn(queries_t[dims, :], ds_ref[...]))
        dv_parts.append(dot_nn(grads_t[dims, :], probs_ref[sub]))
    dk_ref[...] = jnp.concatenate(dk_parts, axis=0).T.astype(bfloat)
    dv_ref[...] = jnp.concatenate(dv_parts, axis=0).T.astype(bfloat)


def attend_back(probs, grads, outs, queries, keys, values, info, head_dim, stride, bias_shape):
    rows_all, width = queries.shape
    keys_all = keys.shape[0]
    per = tile // head_dim
    heads = width // head_dim
    row_spec = pl.BlockSpec((rows_all, tile), lambda i: (0, i))
    key_spec = pl.BlockSpec((keys_all, tile), lambda i: (0, i))
    return pl.pallas_call(
        functools.partial(attend_back_kernel, stride, head_dim, head_dim ** (-0.5)),
        grid=(width // tile,),
        in_specs=[
            pl.BlockSpec((per, rows_all, keys_all), lambda i: (i, 0, 0)),
            row_spec,
            row_spec,
            row_spec,
            key_spec,
            key_spec,
            pl.BlockSpec(info.shape, lambda i: (0, 0)),
        ],
        out_specs=[
            row_spec,
            key_spec,
            key_spec,
            pl.BlockSpec((per,) + bias_shape[1:], lambda i: (i, 0, 0, 0)),
            pl.BlockSpec((per, 2, tile, tile), lambda i: (i, 0, 0, 0)),
        ],
        out_shape=[
            jax.ShapeDtypeStruct((rows_all, width), bfloat),
            jax.ShapeDtypeStruct((keys_all, width), bfloat),
            jax.ShapeDtypeStruct((keys_all, width), bfloat),
            jax.ShapeDtypeStruct(bias_shape, float32),
            jax.ShapeDtypeStruct((heads, 2, tile, tile), float32),
        ],
        scratch_shapes=[pltpu.VMEM((rows_all, keys_all), bfloat)],
        compiler_params=params(),
        cost_estimate=pl.CostEstimate(
            flops=32 * rows_all * keys_all * width,
            bytes_accessed=2 * heads * rows_all * keys_all,
            transcendentals=0,
        ),
        name="attend_back",
    )(probs, grads, outs, queries, keys, values, info)


def expert_kernel(
    count, slots, width, chunk, inner_ref, outer_ref, *refs
):
    blocks = refs[:count]
    results = refs[count : 2 * count]
    hidden_ref, grad_pre_ref, rows_ref, grads_ref, sum_ref, back_ref = refs[2 * count :]
    turn = pl.program_id(0)

    @pl.when(turn == 0)
    def _():
        for idx in range(count):
            rows = slice(idx * slots, (idx + 1) * slots)
            rows_ref[rows, :] = blocks[idx][:, :width]
            grads_ref[rows, :] = blocks[idx][:, width:]

    inner = inner_ref[...].reshape(width, width)
    outer = outer_ref[...].reshape(width, width)
    rows = rows_ref[...]
    grads = grads_ref[...]
    root = 0.7978845608028654
    for start in range(0, width, chunk):
        columns = slice(start, start + chunk)
        pre = dot_nn(rows, inner[:, columns])
        grad_hidden = dot_nt(grads, outer[columns, :])
        square = pre * pre
        curve = jnp.tanh(root * pre * (1.0 + 0.044715 * square))
        half = 0.5 * (1.0 + curve)
        slope = half + (0.5 * root) * pre * (1.0 - curve * curve) * (1.0 + 0.134145 * square)
        hidden_ref[:, columns] = (pre * half).astype(bfloat)
        grad_pre_ref[:, columns] = (grad_hidden * slope).astype(bfloat)
    product = dot_nn(hidden_ref[...], outer)
    product_back = dot_nt(grad_pre_ref[...], inner)

    @pl.when(turn == 0)
    def _():
        sum_ref[...] = product
        back_ref[...] = product_back

    @pl.when(turn > 0)
    def _():
        sum_ref[...] += product
        back_ref[...] += product_back

    @pl.when(turn == pl.num_programs(0) - 1)
    def _():
        for idx in range(count):
            span = slice(idx * slots, (idx + 1) * slots)
            results[idx][:, :width] = sum_ref[span, :].astype(bfloat)
            results[idx][:, width:] = back_ref[span, :].astype(bfloat)


def run_expert(weights, blocks, width):
    (inner, inner_spec), (outer, outer_spec), turns = weights
    count = len(blocks)
    slots = blocks[0].shape[0]
    total = count * slots
    whole = pl.BlockSpec((slots, 2 * width), lambda i: (0, 0))
    chunk = pl.BlockSpec((total, width), lambda i: (0, i))
    outs = pl.pallas_call(
        functools.partial(expert_kernel, count, slots, width, 256),
        grid=(turns,),
        in_specs=[inner_spec, outer_spec] + [whole] * count,
        out_specs=[whole] * count + [chunk, chunk],
        out_shape=[jax.ShapeDtypeStruct((slots, 2 * width), bfloat)] * count
        + [jax.ShapeDtypeStruct((total, turns * width), bfloat)] * 2,
        scratch_shapes=[
            pltpu.VMEM((total, width), bfloat),
            pltpu.VMEM((total, width), bfloat),
            pltpu.VMEM((total, width), float32),
            pltpu.VMEM((total, width), float32),
        ],
        compiler_params=params(),
        cost_estimate=pl.CostEstimate(
            flops=8 * total * width * width * turns,
            bytes_accessed=4 * width * width * turns,
            transcendentals=total * width * turns,
        ),
        name="run_expert",
    )(inner, outer, *blocks)
    return outs[:count], outs[count], outs[count + 1]


def expert_grad_kernel(batches, count, slots, width, second, *refs):
    groups = [refs[idx * count : (idx + 1) * count] for idx in range(batches)]
    wide = refs[batches * count : batches * count + batches]
    out_ref, rows_ref = refs[-2], refs[-1]
    half = slice(width, 2 * width) if second else slice(0, width)

    @pl.when(pl.program_id(0) == 0)
    def _():
        for batch in range(batches):
            for idx in range(count):
                start = (batch * count + idx) * slots
                rows_ref[start : start + slots, :] = groups[batch][idx][:, half]

    total = None
    span = count * slots
    for batch in range(batches):
        rows = rows_ref[batch * span : (batch + 1) * span, :]
        if second:
            term = dot_tn(wide[batch][...], rows)
        else:
            term = dot_tn(rows, wide[batch][...])
        total = term if total is None else total + term
    out_ref[...] = total.astype(bfloat).reshape(out_ref.shape)


def expert_grad(groups, wide, width, second, out_shape, out_spec, buffer=None):
    batches = len(groups)
    count = len(groups[0])
    slots = groups[0][0].shape[0]
    total = count * slots
    turns = wide[0].shape[1] // width
    kernel = functools.partial(expert_grad_kernel, batches, count, slots, width, second)
    in_specs = [pl.BlockSpec((slots, 2 * width), lambda i: (0, 0))] * (batches * count)
    in_specs = in_specs + [pl.BlockSpec((total, width), lambda i: (0, i))] * batches
    operands = [block for group in groups for block in group] + list(wide)
    aliases = {}
    body = kernel
    if buffer is not None:
        in_specs = [pl.BlockSpec(memory_space=pl.ANY)] + in_specs
        operands = [buffer] + operands
        aliases = {0: 0}

        def body(*refs):
            kernel(*refs[1:])

    return pl.pallas_call(
        body,
        grid=(turns,),
        in_specs=in_specs,
        out_specs=out_spec,
        out_shape=jax.ShapeDtypeStruct(out_shape, bfloat),
        scratch_shapes=[pltpu.VMEM((batches * total, width), bfloat)],
        input_output_aliases=aliases,
        compiler_params=params(),
        cost_estimate=pl.CostEstimate(
            flops=2 * batches * total * width * width * turns,
            bytes_accessed=4 * width * width * turns,
            transcendentals=0,
        ),
        name="expert_grad_outer" if second else "expert_grad_inner",
    )(*operands)


def on_device(
    hidden_in,
    out_grad,
    places,
    lengths,
    routes,
    norm1_gain,
    w_query,
    w_key,
    w_value,
    w_output,
    rel_table,
    norm2_gain,
    w_router,
    w_in,
    w_out,
):
    batches, rows_own, width = hidden_in.shape
    heads = rel_table.shape[1]
    head_dim = width // heads
    scale = head_dim ** (-0.5)
    shards = lax.axis_size("dp")
    members = lax.axis_size("expert")
    me = lax.axis_index("expert")
    experts = w_router.shape[1]
    hidden_width = w_in.shape[2]
    turns = hidden_width // width
    tiles = rows_own // tile
    depth = width // shards
    depth_out = hidden_width // shards
    table_rows = rel_table.shape[0]
    capacity = max(2, rows_own * 17 // (experts * 16))
    slots = -(-capacity // 16) * 16

    def around(step):
        return [(idx, (idx + step) % members) for idx in range(members)]

    hidden_from = [hidden_in] + [
        lax.ppermute(hidden_in, "expert", around(step)) for step in range(1, members)
    ]

    small = jnp.concatenate(
        [
            norm1_gain.reshape(-1),
            norm2_gain.reshape(-1),
            w_router.reshape(-1),
            rel_table.reshape(-1),
        ]
    )
    small_used = small.shape[0]
    small_rows = -(-small_used // width)
    small_pad = -(-small_rows // 16) * 16
    small = jnp.pad(small, (0, small_pad * width - small_used)).reshape(small_pad, width)
    first = lax.all_gather(
        jnp.concatenate([w_query, w_key, w_value, small], axis=0), "dp", axis=0, tiled=False
    )
    inner_parts = [w_in[0, :, idx * width : (idx + 1) * width] for idx in range(turns)]
    second_own = jnp.concatenate(inner_parts + [w_out[0], w_output], axis=0)
    second_own, _ = lax.optimization_barrier((second_own, first))
    second = lax.all_gather(second_own, "dp", axis=0, tiled=False)

    query_w = first[:, :depth].reshape(width, width)
    key_w = first[:, depth : 2 * depth].reshape(width, width)
    value_w = first[:, 2 * depth : 3 * depth].reshape(width, width)
    small_all = first[:, 3 * depth :].reshape(shards, small_pad * width)
    gain_one = small_all[:, :depth].reshape(width).astype(float32)
    gain_two = small_all[:, depth : 2 * depth].reshape(width).astype(float32)
    router_end = 2 * depth + depth * experts
    router_w = small_all[:, 2 * depth : router_end].reshape(width, experts)
    table = small_all[:, router_end:small_used].reshape(shards * table_rows, heads)
    output_w = second[:, turns * depth + depth_out :].reshape(width, width)

    direct = depth % 16 == 0 and turns * depth == depth_out and shards % turns == 0
    if direct:
        group = shards // turns
        inner_spec = pl.BlockSpec((shards, depth, width), lambda i: (0, i, 0))
        outer_spec = pl.BlockSpec((group, depth_out, width), lambda i: (i, 1, 0))
        weights = ((second, inner_spec), (second, outer_spec), turns)
    else:
        inner_w = second[:, : turns * depth].reshape(shards, turns, depth, width)
        inner_w = jnp.transpose(inner_w, (1, 0, 2, 3)).reshape(turns, width, width)
        outer_w = second[:, turns * depth : turns * depth + depth_out].reshape(
            turns, width, width
        )
        plain = pl.BlockSpec((1, width, width), lambda i: (i, 0, 0))
        weights = ((inner_w, plain), (outer_w, plain), turns)

    places_in = places[:, 0].reshape(batches, members, rows_own)
    offsets = places_in - members * jnp.arange(rows_own, dtype=jnp.int32)[None, None]
    offset_from = [
        jnp.take(offsets, jnp.mod(me - step, members), axis=1) for step in range(members)
    ]

    def by_place(parts):
        ordered = []
        for place in range(members):
            rows = parts[0]
            for step in range(1, members):
                rows = jnp.where((offset_from[step] == place)[..., None], parts[step], rows)
            ordered.append(rows)
        return jnp.concatenate(ordered, axis=1)

    def of_member(ordered, batch, step):
        rows = ordered[:rows_own]
        for place in range(1, members):
            rows = jnp.where(
                (offset_from[step][batch] == place)[:, None],
                ordered[place * rows_own : (place + 1) * rows_own],
                rows,
            )
        return rows

    ends = jnp.cumsum(lengths[:, 0], axis=-1)[:, :-1]
    position_own = offset_from[0] + members * jnp.arange(rows_own, dtype=jnp.int32)[None]
    past = position_own[:, :, None] >= ends[:, None, :]
    low = jnp.max(jnp.where(past, ends[:, None, :], 0), axis=-1)
    high = jnp.min(jnp.where(past, members * rows_own, ends[:, None, :]), axis=-1)
    info = jnp.stack([offset_from[0], low, high], axis=-1)
    info = jnp.pad(info, ((0, 0), (0, 0), (0, 5)))

    chosen = routes[:, :, 0]
    picked = chosen[:, :, None] == jnp.arange(experts, dtype=jnp.int32)
    counts = picked.astype(jnp.int32)
    slot = jnp.sum((jnp.cumsum(counts, axis=1) - counts) * counts, axis=2)
    target = jnp.mod(chosen - me, members) * slots + slot
    dispatch = (
        jnp.arange(members * slots, dtype=jnp.int32)[None, :, None] == target[:, None, :]
    ).astype(bfloat)

    ordered_in = by_place(hidden_from)
    ordered_f = ordered_in.astype(float32)
    own_f = hidden_in.astype(float32)
    normed_all = norm_rows(ordered_f, gain_one).astype(bfloat)
    normed_own = norm_rows(own_f, gain_one).astype(bfloat)
    flat_all = normed_all.reshape(batches * members * rows_own, width)
    flat_own = normed_own.reshape(batches * rows_own, width)
    queries = (dot_nn(flat_own, query_w).astype(bfloat) * bfloat(scale)).reshape(
        batches, rows_own, width
    )
    keys = dot_nn(flat_all, key_w).astype(bfloat).reshape(batches, members * rows_own, width)
    values = dot_nn(flat_all, value_w).astype(bfloat).reshape(batches, members * rows_own, width)
    bias = bias_tiles(table, members, tiles)
    table_f = table.astype(float32)
    far = jnp.stack([table_f[levels_all - 1], table_f[2 * levels_all - 1]])

    probs = []
    attended = []
    resid_mid = []
    normed_two = []
    gate_all = []
    gate = []
    blocks = []
    for batch in range(batches):
        kept, joined = attend(
            queries[batch], keys[batch], values[batch], info[batch], bias, far, head_dim, members
        )
        probs.append(kept)
        attended.append(joined)
        mid = own_f[batch] + dot_nn(joined, output_w)
        normed = norm_rows(mid, gain_two).astype(bfloat)
        logits = dot_nn(normed, router_w)
        shifted = jnp.exp(logits - jnp.max(logits, axis=-1, keepdims=True))
        router_probs = shifted / jnp.sum(shifted, axis=-1, keepdims=True)
        gate_own = jnp.sum(jnp.where(picked[batch], router_probs, 0.0), axis=1, keepdims=True)
        grad_expert = (gate_own * out_grad[batch].astype(float32)).astype(bfloat)
        outgoing = dot_nn(
            dispatch[batch], jnp.concatenate([normed, grad_expert], axis=1)
        ).astype(bfloat)
        received = [outgoing[:slots]]
        for step in range(1, members):
            received.append(
                lax.ppermute(
                    outgoing[step * slots : (step + 1) * slots], "expert", around(step)
                )
            )
        resid_mid.append(mid)
        normed_two.append(normed)
        gate_all.append(router_probs)
        gate.append(gate_own)
        blocks.append(received)

    returned = []
    hidden = []
    grad_pre = []
    for batch in range(batches):
        results, hidden_rows, grad_rows = run_expert(weights, blocks[batch], width)
        hidden.append(hidden_rows)
        grad_pre.append(grad_rows)
        back = [results[0]]
        for step in range(1, members):
            back.append(lax.ppermute(results[step], "expert", around(-step)))
        returned.append(jnp.concatenate(back, axis=0))

    if direct:
        buffer_shape = (shards, turns * depth + depth_out, width)
        buffer = expert_grad(
            blocks,
            grad_pre,
            width,
            False,
            buffer_shape,
            pl.BlockSpec((shards, depth, width), lambda i: (0, i, 0)),
        )
        buffer = expert_grad(
            blocks,
            hidden,
            width,
            True,
            buffer_shape,
            pl.BlockSpec((group, depth_out, width), lambda i: (i, 1, 0)),
            buffer,
        )
    else:
        plain_shape = (turns, width, width)
        inner_g = expert_grad(blocks, grad_pre, width, False, plain_shape, plain)
        outer_g = expert_grad(blocks, hidden, width, True, plain_shape, plain)
        inner_g = jnp.transpose(inner_g.reshape(turns, shards, depth, width), (1, 0, 2, 3))
        buffer = jnp.concatenate(
            [
                inner_g.reshape(shards, turns * depth, width),
                outer_g.reshape(shards, depth_out, width),
            ],
            axis=1,
        )
    expert_sum = lax.psum_scatter(buffer, "dp", scatter_dimension=0, tiled=False)

    layer_rows = []
    input_rows = []
    grad_attn_rows = []
    grad_q_rows = []
    grad_k_rows = []
    grad_v_rows = []
    grad_gain_one = 0.0
    grad_gain_two = 0.0
    grad_router = 0.0
    grad_bias = 0.0
    grad_far = 0.0
    router_f = router_w.astype(float32)
    for batch in range(batches):
        home = dot_tn(dispatch[batch], returned[batch])
        expert_back = home[:, :width]
        grad_output = out_grad[batch].astype(float32)
        layer_rows.append((resid_mid[batch] + gate[batch] * expert_back).astype(bfloat))
        grad_gate = jnp.sum(grad_output * expert_back, axis=1, keepdims=True)
        grad_logits = (grad_gate * gate[batch]) * (
            jnp.where(picked[batch], 1.0, 0.0) - gate_all[batch]
        )
        grad_normed = home[:, width:] + lax.dot_general(
            grad_logits, router_f, (((1,), (1,)), ((), ())), precision=precise
        )
        grad_router = grad_router + lax.dot_general(
            normed_two[batch].astype(float32),
            grad_logits,
            (((0,), (0,)), ((), ())),
            precision=precise,
        )
        grad_resid, gain_terms = norm_back(resid_mid[batch], gain_two, grad_normed)
        grad_gain_two = grad_gain_two + jnp.sum(gain_terms, axis=0)
        grad_mid = grad_output + grad_resid
        grad_attn = grad_mid.astype(bfloat)
        grad_attn_rows.append(grad_attn)
        grad_attended = dot_nt(grad_attn, output_w).astype(bfloat)
        grad_q, grad_k, grad_v, bias_terms, far_terms = attend_back(
            probs[batch],
            grad_attended,
            attended[batch],
            queries[batch],
            keys[batch],
            values[batch],
            info[batch],
            head_dim,
            members,
            bias.shape,
        )
        grad_q_rows.append(grad_q)
        grad_k_rows.append(grad_k)
        grad_v_rows.append(grad_v)
        grad_bias = grad_bias + bias_terms
        grad_far = grad_far + far_terms
        grad_ordered = dot_nt(grad_k, key_w) + dot_nt(grad_v, value_w)
        grad_own = dot_nt(grad_q, query_w)
        home_rows = of_member(grad_ordered, batch, 0)
        for step in range(1, members):
            sent = of_member(grad_ordered, batch, step).astype(bfloat)
            home_rows = home_rows + lax.ppermute(sent, "expert", around(-step)).astype(float32)
        grad_tokens, _ = norm_back(own_f[batch], gain_one, grad_own + home_rows)
        input_rows.append(grad_mid + grad_tokens)
        _, terms_all = norm_back(ordered_f[batch], gain_one, grad_ordered)
        _, terms_own = norm_back(own_f[batch], gain_one, grad_own)
        grad_gain_one = grad_gain_one + jnp.sum(terms_all, axis=0) + jnp.sum(terms_own, axis=0)

    def flat(rows):
        return jnp.concatenate(rows, axis=0)

    grad_wo = dot_tn(flat(attended), flat(grad_attn_rows))
    grad_wq = dot_tn(flat_own, flat(grad_q_rows))
    grad_wk = dot_tn(flat_all, flat(grad_k_rows))
    grad_wv = dot_tn(flat_all, flat(grad_v_rows))

    steps = 2 * members - 1
    reach = near_shift(tiles)
    shape = (steps, tile, (2 * reach + 1) * tile)
    delta = (
        members
        * (
            lax.broadcasted_iota(jnp.int32, shape, 2)
            - reach * tile
            - lax.broadcasted_iota(jnp.int32, shape, 1)
        )
        + lax.broadcasted_iota(jnp.int32, shape, 0)
        - (members - 1)
    )
    buckets = shards * table_rows
    onehot = (
        bucket_of(delta)[None] == jnp.arange(buckets, dtype=jnp.int32)[:, None, None, None]
    ).astype(bfloat)
    grad_table = jnp.einsum(
        "hsab,ksab->kh", grad_bias.astype(bfloat), onehot, preferred_element_type=float32
    )
    far_sum = jnp.sum(grad_far, axis=(2, 3))
    grad_table = grad_table.at[levels_all - 1].add(far_sum[:, 0])
    grad_table = grad_table.at[2 * levels_all - 1].add(far_sum[:, 1])

    small_grad = jnp.concatenate(
        [
            grad_gain_one.reshape(shards, depth),
            grad_gain_two.reshape(shards, depth),
            grad_router.reshape(shards, depth * experts),
            grad_table.reshape(shards, table_rows * heads),
        ],
        axis=1,
    )
    small_grad = jnp.pad(small_grad, ((0, 0), (0, small_pad * width - small_used)))
    dense = jnp.concatenate(
        [
            grad_wq.astype(bfloat).reshape(shards, depth, width),
            grad_wk.astype(bfloat).reshape(shards, depth, width),
            grad_wv.astype(bfloat).reshape(shards, depth, width),
            grad_wo.astype(bfloat).reshape(shards, depth, width),
            small_grad.astype(bfloat).reshape(shards, small_pad, width),
        ],
        axis=1,
    )
    dense, _ = lax.optimization_barrier((dense, expert_sum))
    dense_part = lax.psum_scatter(dense, "dp", scatter_dimension=0, tiled=False)
    dense_sum = dense_part.astype(float32)
    for step in range(1, members):
        dense_sum = dense_sum + lax.ppermute(dense_part, "expert", around(step)).astype(float32)

    expert_f = expert_sum.astype(float32)
    inner_sum = jnp.concatenate(
        [expert_f[idx * depth : (idx + 1) * depth] for idx in range(turns)], axis=1
    )[None]
    outer_sum = expert_f[turns * depth :][None]
    small_sum = dense_sum[4 * depth :].reshape(-1)
    return (
        jnp.stack(layer_rows),
        jnp.stack(input_rows),
        small_sum[:depth],
        dense_sum[:depth],
        dense_sum[depth : 2 * depth],
        dense_sum[2 * depth : 3 * depth],
        dense_sum[3 * depth : 4 * depth],
        small_sum[router_end:small_used].reshape(table_rows, heads),
        small_sum[depth : 2 * depth],
        small_sum[2 * depth : router_end].reshape(depth, experts),
        inner_sum,
        outer_sum,
    )


def solution(mesh):
    return jax.shard_map(
        on_device,
        mesh=mesh,
        in_specs=(
            P(None, ("dp", "expert"), None),
            P(None, ("dp", "expert"), None),
            P(None, "dp", None),
            P(None, "dp", None),
            P(None, ("dp", "expert"), None),
            P("dp"),
            P("dp", None),
            P("dp", None),
            P("dp", None),
            P("dp", None),
            P("dp", None),
            P("dp"),
            P("dp", None),
            P("expert", "dp", None),
            P("expert", "dp", None),
        ),
        out_specs=(
            P(None, ("dp", "expert"), None),
            P(None, ("dp", "expert"), None),
            P("dp"),
            P("dp", None),
            P("dp", None),
            P("dp", None),
            P("dp", None),
            P("dp", None),
            P("dp"),
            P("dp", None),
            P("expert", "dp", None),
            P("expert", "dp", None),
        ),
        check_vma=False,
    )
```

time: 1140 us -> 617 us (0.54)
  matrix products: 411 us -> 59.2 us
  Pallas kernels: 0 us -> 171 us
  waiting for transfers between devices: 405 us -> 252 us
  blocking collectives: 135 us -> 0 us
  other arithmetic: 92.7 us -> 48.5 us
  starting transfers between devices: 35 us -> 9.33 us
  local copies, waits for them, and re-layouts: 36.1 us -> 52.1 us
    dot_general x66 -> x28, matrix products: 411 us -> 59.2 us  [the longest x8 20.3 us: dot_nt(): lax.dot_general(left, right, (((1,), (1,)), ((), ())), preferred_element_...]
    pallas_call x0 -> x9, Pallas kernels: none -> 171 us  [the longest x2 58.2 us: attend(): pl.pallas_call(functools.partial(attend_kernel, stride, head_dim), grid=(...]
    reduce_scatter x10 -> x2, waiting for transfers between devices: 298 us -> 147 us  [the longest x1 96.2 us: on_device(): lax.psum_scatter(buffer, 'dp', scatter_dimension=0, tiled=False)]
    unnamed x2 -> x0, blocking collectives: 93.5 us -> none
    ppermute x0 -> x8, waiting for transfers between devices: none -> 56.1 us  [the longest x1 26 us: on_device(): lax.ppermute(hidden_in, 'expert', around(step))]
    all_gather x2 -> x0, blocking collectives: 36.8 us -> none  [the longest x1 19.3 us: fetch_dense(): lax.all_gather(table_shard, 'dp', axis=0, tiled=True)]
    all_to_all x8 -> x0, starting transfers between devices: 33.1 us -> none  [the longest x2 8.67 us: on_device(): lax.all_to_all(grad_sent.reshape(grad_arrived.shape), 'expert', split_axi...]
    all_gather x10 -> x2, waiting for transfers between devices: 79.6 us -> 48 us  [the longest x1 48 us: on_device(): lax.all_gather(jnp.concatenate([w_query, w_key, w_value, small], axis=0),...]
  transfers between devices with their start and end apart: 30 -> 12, of which waited for: 15 -> 7; matrix products, arithmetic and copies ran while one was open for 44% -> 15% of each run, Pallas kernels for 0% -> 21%
where the time goes in v1:
time: 617 us; the launch traced here: 607 us
  waiting for transfers between devices  252 us (41%)
  Pallas kernels  171 us (28%)
  matrix products  59.2 us (10%)
  local copies, waits for them, and re-layouts  52.1 us (8%)
  other arithmetic  48.5 us (8%)
  between operations  15.1 us (2%)
  starting transfers between devices  9.33 us (2%)
    reduce_scatter x1, waiting for transfers between devices, on_device(): lax.psum_scatter(buffer, 'dp', scatter_dimension=0, tiled=False)  96.2 us
    pallas_call x2, Pallas kernels, attend(): pl.pallas_call(functools.partial(attend_kernel, stride, head_dim), grid=(...  58.2 us
    reduce_scatter x1, waiting for transfers between devices, on_device(): dense_part = lax.psum_scatter(dense, 'dp', scatter_dimension=0, tiled=False)  51.2 us
    all_gather x1, waiting for transfers between devices, on_device(): lax.all_gather(jnp.concatenate([w_query, w_key, w_value, small], axis=0),...  48 us
    pallas_call x2, Pallas kernels, attend_back(): pl.pallas_call(functools.partial(attend_back_kernel, stride, head_dim, he...  44.3 us
    pallas_call x2, Pallas kernels, run_expert(): pl.pallas_call(functools.partial(expert_kernel, count, slots, width, 256)...  35.4 us
    ppermute x1, waiting for transfers between devices, on_device(): lax.ppermute(hidden_in, 'expert', around(step))  26 us
    pallas_call x2, Pallas kernels, expert_grad(): pl.pallas_call(body, grid=(turns,), in_specs=in_specs, out_specs=out_spec...  24.4 us
  transfers between devices with their start and end apart: 12, of which 7 were waited for; matrix products, arithmetic and copies ran while one was open for 15% of the time, Pallas kernels for 21%

profile of v1, /device:TPU:0, one launch (start us, length us, event | category | flops | bytes accessed | tf_op | source)
XLA Modules:
  0.0 606.7 jit_solution(11798159899735562719)
XLA Ops:
  15.2 48.0 %all-gather.5.cloned.1.call-done = bf16[2560,768]{1,0:T(8,128)(2,1)} async-done(((bf16[160,768]{1,0:T(8,128)(2,1)}), bf16[2560,768]{1,0:T(8,128)(2,1)}) %all-gather.5.cloned.1.call-update) | async-done | bytes 3932176 | tf_op jit(solution)/shard_map/all_gather | solution.py:501
  74.0 26.0 %collective-permute-done = bf16[2,512,768]{2,1,0:T(8,128)(2,1)} collective-permute-done((bf16[2,512,768]{2,1,0:T(8,128)(2,1)S(1)}, bf16[2,512,768]{2,1,0:T(8,128)(2,1)}, u32[]{:S(2)}, u32[]{:S(2)}) %collective-permute-start) | collective-permute-done | bytes 1572896 | tf_op jit(solution)/shard_map/ppermute | solution.py:486
  114.6 8.6 %bias_tiles.1.bias_ref = f32[12,3,128,384]{3,2,1,0:T(8,128)} custom-call(f32[12,128]{1,0:T(8,128)} %pad.23.table_ref), custom_call_target="tpu_custom_call" | custom-call | tf_op jit(solution)/shard_map/bias_tiles/pallas_call | solution.py:79
  141.1 28.9 %attend.3 = (bf16[12,512,1024]{2,1,0:T(8,128)(2,1)}, bf16[512,768]{1,0:T(8,128)(2,1)}) custom-call(f32[2,12]{1,0:T(2,128)} %pad_maximum_fusion.3.far_ref, bf16[512,768]{1,0:T(8,128)(2,1)} %get-tuple-element.220.q_ref, bf16[1024,768]{1,0:T(8,128)(2,1)} %get-tuple-element.260.k_ref, bf16[1024,768]{1,0:T(8,128)(2,1)} %get-tuple-element.206.v_ref, ...), custom_call_target="tpu_custom_call" | custom-call | flops 6442450944 | bytes 12582912 | tf_op jit(solution)/shard_map/attend/pallas_call | solution.py:157
  170.0 29.3 %attend.2 = (bf16[12,512,1024]{2,1,0:T(8,128)(2,1)}, bf16[512,768]{1,0:T(8,128)(2,1)}) custom-call(f32[2,12]{1,0:T(2,128)} %pad_maximum_fusion.3.far_ref, bf16[512,768]{1,0:T(8,128)(2,1)} %get-tuple-element.219.q_ref, bf16[1024,768]{1,0:T(8,128)(2,1)} %get-tuple-element.261.k_ref, bf16[1024,768]{1,0:T(8,128)(2,1)} %get-tuple-element.205.v_ref, ...), custom_call_target="tpu_custom_call" | custom-call | flops 6442450944 | bytes 12582912 | tf_op jit(solution)/shard_map/attend/pallas_call | solution.py:157
  214.4 17.4 %collective-permute-done.3.refs_1_.refs_3_.refs_4_ = bf16[272,1536]{1,0:T(8,128)(2,1)S(1)} collective-permute-done((bf16[272,1536]{1,0:T(8,128)(2,1)S(1)}, bf16[272,1536]{1,0:T(8,128)(2,1)S(1)}, u32[]{:S(2)}, u32[]{:S(2)}) %collective-permute-start.3) | collective-permute-done | bytes 835616 | tf_op jit(solution)/shard_map/ppermute | solution.py:619
  232.8 17.6 %run_expert.3 = (bf16[272,1536]{1,0:T(8,128)(2,1)}, bf16[272,1536]{1,0:T(8,128)(2,1)}, bf16[544,3072]{1,0:T(8,128)(2,1)}, bf16[544,3072]{1,0:T(8,128)(2,1)}) custom-call(bf16[16,432,768]{2,1,0:T(8,128)(2,1)} %bitcast.269, bf16[16,432,768]{2,1,0:T(8,128)(2,1)} %bitcast.270, bf16[272,1536]{1,0:T(8,128)(2,1)} %get-tuple-element.214.refs_0_.refs_2_.refs_3_, ...), custom_call_target="tpu_custom_call" | custom-call | flops 10267656192 | bytes 9437184 | tf_op jit(solution)/shard_map/run_expert/pallas_call | solution.py:361
  251.6 17.9 %run_expert.2 = (bf16[272,1536]{1,0:T(8,128)(2,1)}, bf16[272,1536]{1,0:T(8,128)(2,1)}, bf16[544,3072]{1,0:T(8,128)(2,1)}, bf16[544,3072]{1,0:T(8,128)(2,1)}) custom-call(bf16[16,432,768]{2,1,0:T(8,128)(2,1)} %bitcast.271, bf16[16,432,768]{2,1,0:T(8,128)(2,1)} %bitcast.272, bf16[272,1536]{1,0:T(8,128)(2,1)} %get-tuple-element.212.refs_0_.refs_1_, ...), custom_call_target="tpu_custom_call" | custom-call | flops 10267656192 | bytes 9437184 | tf_op jit(solution)/shard_map/run_expert/pallas_call | solution.py:361
  275.4 11.5 %collective-permute-done.2 = bf16[272,1536]{1,0:T(8,128)(2,1)S(1)} collective-permute-done((bf16[272,1536]{1,0:T(8,128)(2,1)}, bf16[272,1536]{1,0:T(8,128)(2,1)S(1)}, u32[]{:S(2)}, u32[]{:S(2)}) %collective-permute-start.2) | collective-permute-done | bytes 835616 | tf_op jit(solution)/shard_map/ppermute | solution.py:638
  297.9 22.0 %attend_back.2 = (bf16[512,768]{1,0:T(8,128)(2,1)}, bf16[1024,768]{1,0:T(8,128)(2,1)}, bf16[1024,768]{1,0:T(8,128)(2,1)}, f32[12,3,128,384]{3,2,1,0:T(8,128)}, f32[12,2,128,128]{3,2,1,0:T(8,128)}) custom-call(bf16[12,512,1024]{2,1,0:T(8,128)(2,1)} %get-tuple-element.68.probs_ref, bf16[512,768]{1,0:T(8,128)(2,1)} %convolution_convert_fusion.6.grad_ref, ...), custom_call_target="tpu_custom_call" | custom-call | flops 12884901888 | bytes 12582912 | tf_op jit(solution)/shard_map/attend_back/pallas_call | solution.py:266
  319.9 3.3 fusion.158
  323.2 3.5 multiply_reduce_fusion.3
  328.5 22.4 %attend_back.3 = (bf16[512,768]{1,0:T(8,128)(2,1)}, bf16[1024,768]{1,0:T(8,128)(2,1)}, bf16[1024,768]{1,0:T(8,128)(2,1)}, f32[12,3,128,384]{3,2,1,0:T(8,128)}, f32[12,2,128,128]{3,2,1,0:T(8,128)}) custom-call(bf16[12,512,1024]{2,1,0:T(8,128)(2,1)} %get-tuple-element.72.probs_ref, bf16[512,768]{1,0:T(8,128)(2,1)} %convolution_convert_fusion.5.grad_ref, ...), custom_call_target="tpu_custom_call" | custom-call | flops 12884901888 | bytes 12582912 | tf_op jit(solution)/shard_map/attend_back/pallas_call | solution.py:266
  350.9 3.3 fusion.160
  354.5 3.7 fusion.45
  358.3 3.8 fusion.42
  371.4 6.3 %add_convert_fusion = bf16[12,3,128,384]{3,2,1,0:T(8,128)(2,1)S(1)} fusion(f32[12,3,128,384]{3,2,1,0:T(8,128)} %get-tuple-element.76, f32[12,3,128,384]{3,2,1,0:T(8,128)} %get-tuple-element.77), kind=kLoop, calls=%fused_computation.3 | loop fusion | flops 3538944 | bytes 17694720 | tf_op jit(solution)/shard_map/convert_element_type | solution.py:765
  377.8 5.5 fusion.59
  397.5 4.3 multiply_reduce_fusion.9
  403.0 12.2 %expert_grad_inner.1.refs_0_ = bf16[16,384,768]{2,1,0:T(8,128)(2,1)} custom-call(bf16[272,1536]{1,0:T(8,128)(2,1)} %get-tuple-element.212.refs_0_.refs_1_, bf16[272,1536]{1,0:T(8,128)(2,1)} %collective-permute-done.1.refs_1_.refs_2_, bf16[272,1536]{1,0:T(8,128)(2,1)} %get-tuple-element.214.refs_0_.refs_2_.refs_3_, bf16[272,1536]{1,0:T(8,128)(2,1)} %copy-done.26, ...), custom_call_target="tpu_custom_call" | custom-call | flops 5133828096 | bytes 9437184 | tf_op jit(solution)/shard_map/expert_grad_inner/pallas_call | solution.py:430
  415.2 12.1 %expert_grad_outer.1 = bf16[16,384,768]{2,1,0:T(8,128)(2,1)} custom-call(bf16[16,384,768]{2,1,0:T(8,128)(2,1)} %expert_grad_inner.1.refs_0_, bf16[272,1536]{1,0:T(8,128)(2,1)} %get-tuple-element.212.refs_0_.refs_1_, bf16[272,1536]{1,0:T(8,128)(2,1)} %collective-permute-done.1.refs_1_.refs_2_, ...), custom_call_target="tpu_custom_call", output_to_operand_aliasing={{}: (0, {})} | custom-call | flops 5133828096 | bytes 9437184 | tf_op jit(solution)/shard_map/expert_grad_outer/pallas_call | solution.py:430
  430.9 51.2 %reduce-scatter.5.cloned.1.call-done = bf16[1,208,768]{2,1,0:T(8,128)(2,1)} async-done(((bf16[16,208,768]{2,1,0:T(8,128)(2,1)}), bf16[1,208,768]{2,1,0:T(8,128)(2,1)}) %reduce-scatter.5.cloned.1.call-update) | async-done | bytes 319504 | tf_op jit(solution)/shard_map/reduce_scatter | solution.py:792
  483.6 5.4 add_bitcast_fusion.1
  500.9 96.2 %reduce-scatter.3.cloned.1.call-done = bf16[1,384,768]{2,1,0:T(8,128)(2,1)} async-done(((bf16[16,384,768]{2,1,0:T(8,128)(2,1)}), bf16[1,384,768]{2,1,0:T(8,128)(2,1)}) %reduce-scatter.3.cloned.1.call-update) | async-done | bytes 589840 | tf_op jit(solution)/shard_map/reduce_scatter | solution.py:672
  (327 shorter events, 131.1 us)
Async XLA Ops:
  7.2 56.0 %copy-start.9 = (bf16[2,512,768]{2,1,0:T(8,128)(2,1)S(1)}, bf16[2,512,768]{2,1,0:T(8,128)(2,1)}, u32[]{:S(2)}) copy-start(bf16[2,512,768]{2,1,0:T(8,128)(2,1)} %param.21) | copy-start | bytes 4718596
  7.2 57.6 %copy-start.62 = (s32[2,1,1024]{2,1,0:T(1,128)S(1)}, s32[2,1,1024]{2,1,0:T(1,128)}, u32[]{:S(2)}) copy-start(s32[2,1,1024]{2,1,0:T(1,128)} %param.23) | copy-start | bytes 24580
  7.2 57.6 %copy-start.65 = (s32[2,1,2]{2,1,0:T(1,128)S(1)}, s32[2,1,2]{2,1,0:T(1,128)}, u32[]{:S(2)}) copy-start(s32[2,1,2]{2,1,0:T(1,128)} %param.24) | copy-start | bytes 52
  7.2 55.9 %all-gather.5.cloned.1.call-start = ((), (), s32[]{:S(2)}) async-start(), calls=%async_computation.4 | async-start | bytes 4177920 | tf_op jit(solution)/shard_map/all_gather | solution.py:501
  11.5 54.1 %copy-start.54 = (s32[2,512,1]{1,2,0:T(1,128)S(1)}, s32[2,512,1]{1,2,0:T(1,128)}, u32[]{:S(2)}) copy-start(s32[2,512,1]{1,2,0:T(1,128)} %param.25) | copy-start | bytes 12292
  11.5 187.8 %all-gather.7.cloned.1.call-start = ((), (), s32[]{:S(2)}) async-start(), calls=%async_computation.5 | async-start | bytes 11280384 | tf_op jit(solution)/shard_map/all_gather | solution.py:507
  15.2 48.0 %copy-start.39 = (bf16[432,768]{1,0:T(8,128)(2,1)}, bf16[432,768]{1,0:T(8,128)(2,1)S(1)}, u32[]{:S(2)}) copy-start(bf16[432,768]{1,0:T(8,128)(2,1)S(1)} %constant_dynamic-update-slice_fusion) | copy-start | bytes 1990660
  63.2 418.9 %reduce-scatter.5.cloned.1.call-start = ((), (), s32[]{:S(2)}) async-start(), calls=%async_computation.3 | async-start | bytes 5431296 | tf_op jit(solution)/shard_map/reduce_scatter | solution.py:792
  63.2 36.7 %collective-permute-start = (bf16[2,512,768]{2,1,0:T(8,128)(2,1)S(1)}, bf16[2,512,768]{2,1,0:T(8,128)(2,1)}, u32[]{:S(2)}, u32[]{:S(2)}) collective-permute-start(bf16[2,512,768]{2,1,0:T(8,128)(2,1)S(1)} %copy-done.9), channel_id=1, source_target_pairs={{0,1},{1,0},{2,3},{3,2},{4,5},{5,4},{6,7},{7,6},{8,9},{9,8},{10,11... | collective-permute-start | bytes 4718600 | tf_op jit(solution)/shard_map/ppermute | solution.py:486
  71.0 29.0 %copy-start.10 = (bf16[2,512,768]{2,1,0:T(8,128)(2,1)S(1)}, bf16[2,512,768]{2,1,0:T(8,128)(2,1)}, u32[]{:S(2)}) copy-start(bf16[2,512,768]{2,1,0:T(8,128)(2,1)} %param.21) | copy-start | bytes 4718596
  114.6 8.6 %copy-start.56 = (f32[16,48]{1,0:T(8,128)S(1)}, f32[16,48]{1,0:T(8,128)}, u32[]{:S(2)}) copy-start(f32[16,48]{1,0:T(8,128)} %get-tuple-element.232) | copy-start | bytes 9220
  114.6 8.7 %copy-start.59 = (bf16[16,96]{1,0:T(8,128)(2,1)S(1)}, bf16[16,96]{1,0:T(8,128)(2,1)}, u32[]{:S(2)}) copy-start(bf16[16,96]{1,0:T(8,128)(2,1)} %slice.368) | copy-start | bytes 9220
  114.6 9.5 %copy-start.58 = (f32[2,512]{1,0:T(2,128)S(1)}, f32[2,512]{1,0:T(2,128)}, u32[]{:S(2)}) copy-start(f32[2,512]{1,0:T(2,128)} %add_rsqrt_fusion.3) | copy-start | bytes 12292
  210.3 21.5 %collective-permute-start.3 = (bf16[272,1536]{1,0:T(8,128)(2,1)S(1)}, bf16[272,1536]{1,0:T(8,128)(2,1)S(1)}, u32[]{:S(2)}, u32[]{:S(2)}) collective-permute-start(bf16[272,1536]{1,0:T(8,128)(2,1)S(1)} %get-tuple-element.213), channel_id=1, source_target_pairs={{0,1},{1,0},{2,3},{3,2},{4,5},{5,4},{6,7},{7,6},{8,9},{9,8},{10,11... | collective-permute-start | bytes 2506760 | tf_op jit(solution)/shard_map/ppermute | solution.py:619
  213.7 37.9 %collective-permute-start.1 = (bf16[272,1536]{1,0:T(8,128)(2,1)S(1)}, bf16[272,1536]{1,0:T(8,128)(2,1)}, u32[]{:S(2)}, u32[]{:S(2)}) collective-permute-start(bf16[272,1536]{1,0:T(8,128)(2,1)S(1)} %get-tuple-element.211), channel_id=1, source_target_pairs={{0,1},{1,0},{2,3},{3,2},{4,5},{5,4},{6,7},{7,6},{8,9},{9,8},{10,11... | collective-permute-start | bytes 2506760 | tf_op jit(solution)/shard_map/ppermute | solution.py:619
  250.3 22.3 %collective-permute-start.4 = (bf16[272,1536]{1,0:T(8,128)(2,1)}, bf16[272,1536]{1,0:T(8,128)(2,1)}, u32[]{:S(2)}, u32[]{:S(2)}) collective-permute-start(bf16[272,1536]{1,0:T(8,128)(2,1)} %get-tuple-element.67), channel_id=1, source_target_pairs={{0,1},{1,0},{2,3},{3,2},{4,5},{5,4},{6,7},{7,6},{8,9},{9,8},{10,11... | collective-permute-start | bytes 2506760 | tf_op jit(solution)/shard_map/ppermute | solution.py:638
  251.6 18.7 %slice-start = ((s8[6291456]{0:T(1024)(128)(4,1)}), s8[4194304]{0:T(1024)(128)(4,1)S(1)}, s32[]{:S(2)}) async-start(s8[6291456]{0:T(1024)(128)(4,1)} %bitcast.236), calls=%async_computation.6 | async-start | bytes 8388608
  251.6 18.7 %slice-start.1 = ((s8[6291456]{0:T(1024)(128)(4,1)}), s8[2097152]{0:T(1024)(128)(4,1)S(1)}, s32[]{:S(2)}) async-start(s8[6291456]{0:T(1024)(128)(4,1)} %bitcast.236), calls=%async_computation.7 | async-start | bytes 4194304
  269.5 17.4 %collective-permute-start.2 = (bf16[272,1536]{1,0:T(8,128)(2,1)}, bf16[272,1536]{1,0:T(8,128)(2,1)S(1)}, u32[]{:S(2)}, u32[]{:S(2)}) collective-permute-start(bf16[272,1536]{1,0:T(8,128)(2,1)} %get-tuple-element.64), channel_id=1, source_target_pairs={{0,1},{1,0},{2,3},{3,2},{4,5},{5,4},{6,7},{7,6},{8,9},{9,8},{10,11... | collective-permute-start | bytes 2506760 | tf_op jit(solution)/shard_map/ppermute | solution.py:638
  272.6 14.3 %copy-start.71 = (bf16[272,1536]{1,0:T(8,128)(2,1)S(1)}, bf16[272,1536]{1,0:T(8,128)(2,1)}, u32[]{:S(2)}) copy-start(bf16[272,1536]{1,0:T(8,128)(2,1)} %get-tuple-element.63) | copy-start | bytes 2506756
  365.1 31.1 %collective-permute-start.6 = (bf16[512,768]{1,0:T(8,128)(2,1)}, bf16[512,768]{1,0:T(8,128)(2,1)}, u32[]{:S(2)}, u32[]{:S(2)}) collective-permute-start(bf16[512,768]{1,0:T(8,128)(2,1)} %select_convert_fusion), channel_id=1, source_target_pairs={{0,1},{1,0},{2,3},{3,2},{4,5},{5,4},{6,7},{7,6},{8,9},{9,8},{10,11... | collective-permute-start | bytes 2359304 | tf_op jit(solution)/shard_map/ppermute | solution.py:732
  366.7 30.8 %collective-permute-start.5 = (bf16[512,768]{1,0:T(8,128)(2,1)}, bf16[512,768]{1,0:T(8,128)(2,1)}, u32[]{:S(2)}, u32[]{:S(2)}) collective-permute-start(bf16[512,768]{1,0:T(8,128)(2,1)} %select_convert_fusion.1), channel_id=1, source_target_pairs={{0,1},{1,0},{2,3},{3,2},{4,5},{5,4},{6,7},{7,6},{8,9},{9,8},{10,11... | collective-permute-start | bytes 2359304 | tf_op jit(solution)/shard_map/ppermute | solution.py:732
  402.9 194.1 %reduce-scatter.3.cloned.1.call-start = ((), (), s32[]{:S(2)}) async-start(), calls=%async_computation.2 | async-start | bytes 10027008 | tf_op jit(solution)/shard_map/reduce_scatter | solution.py:672
  482.1 8.8 %collective-permute-start.7 = (bf16[208,768]{1,0:T(8,128)(2,1)}, bf16[208,768]{1,0:T(8,128)(2,1)S(1)}, u32[]{:S(2)}, u32[]{:S(2)}) collective-permute-start(bf16[208,768]{1,0:T(8,128)(2,1)} %bitcast.267), channel_id=1, source_target_pairs={{0,1},{1,0},{2,3},{3,2},{4,5},{5,4},{6,7},{7,6},{8,9},{9,8},{10,11... | collective-permute-start | bytes 958472 | tf_op jit(solution)/shard_map/ppermute | solution.py:795
  (64 other events, 189.6 us)
Sparse Core Ops, SparseCore 0:
  11.6 51.4 all-gather.4
  65.4 87.7 all-gather.6
  403.0 79.0 reduce-scatter.4
  486.6 110.3 reduce-scatter.2

commit v2 on v1

--- a/solution.py
+++ b/solution.py
@@ -86,101 +86,166 @@
     )(lanes)
 
 
+def project_kernel(scale, rows_ref, gain_ref, weight_ref, normed_ref, q_ref, k_ref, v_ref):
+    width = rows_ref.shape[1]
+    span = q_ref.shape[1]
+    depth = weight_ref.shape[1] // 3
+    normed = norm_rows(rows_ref[...].astype(float32), gain_ref[...]).astype(bfloat)
+    normed_ref[...] = normed
+    for idx, out_ref in enumerate((q_ref, k_ref, v_ref)):
+        weight = weight_ref[:, idx * depth : (idx + 1) * depth, :].reshape(width, span)
+        product = dot_nn(normed, weight).astype(bfloat)
+        out_ref[...] = product * bfloat(scale) if idx == 0 else product
+
+
+def project(rows, gain, packed, scale):
+    count, width = rows.shape
+    span = packed.shape[2]
+    step = min(512, count)
+    row_spec = pl.BlockSpec((step, width), lambda i: (i, 0))
+    out_spec = pl.BlockSpec((step, span), lambda i: (i, 0))
+    return pl.pallas_call(
+        functools.partial(project_kernel, scale),
+        grid=(count // step,),
+        in_specs=[
+            row_spec,
+            pl.BlockSpec((1, width), lambda i: (0, 0)),
+            pl.BlockSpec(packed.shape, lambda i: (0, 0, 0)),
+        ],
+        out_specs=[row_spec, out_spec, out_spec, out_spec],
+        out_shape=[jax.ShapeDtypeStruct((count, width), bfloat)]
+        + [jax.ShapeDtypeStruct((count, span), bfloat)] * 3,
+        compiler_params=params(),
+        cost_estimate=pl.CostEstimate(
+            flops=6 * count * width * span, bytes_accessed=4 * count * width, transcendentals=0
+        ),
+        name="project",
+    )(rows, gain, packed)
+
+
+def segment_of(positions, ends):
+    segment = jnp.zeros(positions.shape, jnp.int32)
+    for end in ends:
+        segment = segment + (positions >= end).astype(jnp.int32)
+    return segment
+
+
+def masked_heads(rows, lane, per, head_dim):
+    parts = []
+    for sub in range(per):
+        inside = (lane >= sub * head_dim) & (lane < (sub + 1) * head_dim)
+        parts.append(jnp.where(inside, rows, jnp.zeros_like(rows)))
+    return jnp.concatenate(parts, axis=0)
+
+
+def joined_heads(rows, lane, per, head_dim):
+    joined = rows[:tile]
+    for sub in range(1, per):
+        inside = (lane >= sub * head_dim) & (lane < (sub + 1) * head_dim)
+        joined = jnp.where(inside, rows[sub * tile : (sub + 1) * tile], joined)
+    return joined
+
+
 def attend_kernel(
-    stride, head_dim, far_ref, q_ref, k_ref, v_ref, info_ref, bias_ref, probs_ref, out_ref
+    stride, head_dim, far_ref, ends_ref, q_ref, k_ref, v_ref, bias_ref, probs_ref, out_ref, inv_ref
 ):
     pair = pl.program_id(0)
     rows_all = q_ref.shape[0]
-    tiles = rows_all // tile
+    rows_part = rows_all // stride
+    tiles = rows_part // tile
     reach = near_shift(tiles)
     per = tile // head_dim
     lane = lax.broadcasted_iota(jnp.int32, (tile, tile), 1)
-    for block in range(tiles):
-        rows = slice(block * tile, (block + 1) * tile)
-        place = info_ref[rows, 0:1]
-        low = info_ref[rows, 1:2]
-        high = info_ref[rows, 2:3]
-        queries = q_ref[rows, :]
-        joined = None
-        for sub in range(per):
-            head = pair * per + sub
-            inside = (lane >= sub * head_dim) & (lane < (sub + 1) * head_dim)
-            own = jnp.where(inside, queries, jnp.zeros_like(queries))
-            raw = dot_nt(own, k_ref[...])
-            pieces = []
-            top = None
-            for part in range(stride):
-                for col in range(tiles):
-                    start = part * rows_all + col * tile
-                    piece = raw[:, start : start + tile]
-                    shift = col - block
-                    if shift < -reach:
-                        piece = piece + far_ref[0, head]
-                    elif shift > reach:
-                        piece = piece + far_ref[1, head]
-                    else:
-                        columns = slice((shift + reach) * tile, (shift + reach + 1) * tile)
-                        bias = bias_ref[sub, part + stride - 1, :, columns]
-                        for other in range(1, stride):
-                            bias = jnp.where(
-                                place == other,
-                                bias_ref[sub, part - other + stride - 1, :, columns],
-                                bias,
-                            )
-                        piece = piece + bias
-                    position = stride * (col * tile + lane) + part
-                    piece = jnp.where(
-                        (position >= low) & (position < high), piece, masked_score
-                    )
-                    pieces.append(piece)
-                    top = piece if top is None else jnp.maximum(top, piece)
-            row_max = jnp.max(top, axis=-1, keepdims=True)
-            total = None
-            for idx, piece in enumerate(pieces):
-                pieces[idx] = jnp.exp(piece - row_max)
-                total = pieces[idx] if total is None else total + pieces[idx]
-            inverse = 1.0 / jnp.sum(total, axis=-1, keepdims=True)
-            low_probs = jnp.concatenate(
-                [(piece * inverse).astype(bfloat) for piece in pieces], axis=1
-            )
-            probs_ref[sub, rows, :] = low_probs
-            result = dot_nn(low_probs, v_ref[...])
-            joined = result if joined is None else jnp.where(inside, result, joined)
-        out_ref[rows, :] = joined.astype(bfloat)
-
-
-def attend(queries, keys, values, info, bias, far, head_dim, stride):
-    rows_all, width = queries.shape
-    keys_all = keys.shape[0]
+    ends = [ends_ref[idx] for idx in range(ends_ref.shape[0])]
+    keys_t = k_ref[...].T
+    lane_row = lax.broadcasted_iota(jnp.int32, (1, tile), 1)
+    row_column = lax.broadcasted_iota(jnp.int32, (tile, 1), 0)
+    key_segments = [
+        segment_of(stride * (col * tile + lane_row) + part, ends)
+        for part in range(stride)
+        for col in range(tiles)
+    ]
+    for mine in range(stride):
+        for block in range(tiles):
+            begin = mine * rows_part + block * tile
+            rows = slice(begin, begin + tile)
+            segment = segment_of(stride * (block * tile + row_column) + mine, ends)
+            raw = dot_nn(masked_heads(q_ref[rows, :], lane, per, head_dim), keys_t)
+            stacked = []
+            inverses = []
+            for sub in range(per):
+                head = pair * per + sub
+                pieces = []
+                top = None
+                for part in range(stride):
+                    for col in range(tiles):
+                        start = (part * tiles + col) * tile
+                        piece = raw[sub * tile : (sub + 1) * tile, start : start + tile]
+                        shift = col - block
+                        if shift < -reach:
+                            piece = piece + far_ref[0, head]
+                        elif shift > reach:
+                            piece = piece + far_ref[1, head]
+                        else:
+                            columns = slice((shift + reach) * tile, (shift + reach + 1) * tile)
+                            piece = piece + bias_ref[sub, part - mine + stride - 1, :, columns]
+                        same = key_segments[part * tiles + col] == segment
+                        piece = jnp.where(same, piece, masked_score)
+                        pieces.append(piece)
+                        top = piece if top is None else jnp.maximum(top, piece)
+                row_max = jnp.max(top, axis=-1, keepdims=True)
+                total = None
+                for idx, piece in enumerate(pieces):
+                    piece = jnp.exp(piece - row_max)
+                    total = piece if total is None else total + piece
+                    pieces[idx] = piece.astype(bfloat)
+                kept = jnp.concatenate(pieces, axis=1)
+                probs_ref[sub, rows, :] = kept
+                stacked.append(kept)
+                inverses.append(1.0 / jnp.sum(total, axis=-1, keepdims=True))
+            result = dot_nn(jnp.concatenate(stacked, axis=0), v_ref[...])
+            inverse = jnp.broadcast_to(inverses[0], (tile, tile))
+            for sub in range(1, per):
+                inside = (lane >= sub * head_dim) & (lane < (sub + 1) * head_dim)
+                inverse = jnp.where(inside, inverses[sub], inverse)
+            out_ref[rows, :] = (joined_heads(result, lane, per, head_dim) * inverse).astype(bfloat)
+            inv_ref[rows, :] = inverse
+
+
+def attend(queries, keys, values, ends, bias, far, head_dim, stride):
+    rows_all, span = queries.shape
     per = tile // head_dim
-    heads = width // head_dim
+    heads = span // head_dim
+    row_spec = pl.BlockSpec((rows_all, tile), lambda i: (0, i))
     return pl.pallas_call(
         functools.partial(attend_kernel, stride, head_dim),
-        grid=(width // tile,),
+        grid=(span // tile,),
         in_specs=[
             pl.BlockSpec(memory_space=pltpu.SMEM),
-            pl.BlockSpec((rows_all, tile), lambda i: (0, i)),
-            pl.BlockSpec((keys_all, tile), lambda i: (0, i)),
-            pl.BlockSpec((keys_all, tile), lambda i: (0, i)),
-            pl.BlockSpec(info.shape, lambda i: (0, 0)),
+            pl.BlockSpec(memory_space=pltpu.SMEM),
+            row_spec,
+            row_spec,
+            row_spec,
             pl.BlockSpec((per,) + bias.shape[1:], lambda i: (i, 0, 0, 0)),
         ],
         out_specs=[
-            pl.BlockSpec((per, rows_all, keys_all), lambda i: (i, 0, 0)),
-            pl.BlockSpec((rows_all, tile), lambda i: (0, i)),
+            pl.BlockSpec((per, rows_all, rows_all), lambda i: (i, 0, 0)),
+            row_spec,
+            row_spec,
         ],
         out_shape=[
-            jax.ShapeDtypeStruct((heads, rows_all, keys_all), bfloat),
-            jax.ShapeDtypeStruct((rows_all, width), bfloat),
+            jax.ShapeDtypeStruct((heads, rows_all, rows_all), bfloat),
+            jax.ShapeDtypeStruct((rows_all, span), bfloat),
+            jax.ShapeDtypeStruct((rows_all, span), float32),
         ],
         compiler_params=params(),
         cost_estimate=pl.CostEstimate(
-            flops=16 * rows_all * keys_all * width,
-            bytes_accessed=2 * heads * rows_all * keys_all,
-            transcendentals=heads * rows_all * keys_all,
+            flops=16 * rows_all * rows_all * span,
+            bytes_accessed=2 * heads * rows_all * rows_all,
+            transcendentals=heads * rows_all * rows_all,
         ),
         name="attend",
-    )(far, queries, keys, values, info, bias)
+    )(far, ends, queries, keys, values, bias)
 
 
 def attend_back_kernel(
@@ -190,114 +255,153 @@
     probs_ref,
     grad_ref,
     out_ref,
+    inv_ref,
     q_ref,
     k_ref,
     v_ref,
-    info_ref,
+    after_ref,
     dq_ref,
     dk_ref,
     dv_ref,
     dbias_ref,
     dfar_ref,
     ds_ref,
+    grads_ref,
 ):
     rows_all = q_ref.shape[0]
-    tiles = rows_all // tile
+    rows_part = rows_all // stride
+    tiles = rows_part // tile
     reach = near_shift(tiles)
     per = tile // head_dim
     lane = lax.broadcasted_iota(jnp.int32, (tile, tile), 1)
     queries_t = q_ref[...].T
-    grads_t = grad_ref[...].T
+    values_t = v_ref[...].T
+    grads_ref[...] = (grad_ref[...].astype(float32) * inv_ref[...]).astype(bfloat)
+    grads_t = grads_ref[...].T
     dbias_ref[...] = jnp.zeros_like(dbias_ref)
     dfar_ref[...] = jnp.zeros_like(dfar_ref)
+    for mine in range(stride):
+        for block in range(tiles):
+            begin = mine * rows_part + block * tile
+            rows = slice(begin, begin + tile)
+            own = masked_heads(grads_ref[rows, :], lane, per, head_dim)
+            outs = out_ref[rows, :].astype(float32)
+            raw = dot_nn(own, values_t)
+            stacked = []
+            for sub in range(per):
+                span = slice(sub * tile, (sub + 1) * tile)
+                row_dot = jnp.sum(own[span].astype(float32) * outs, axis=-1, keepdims=True)
+                pieces = []
+                for part in range(stride):
+                    for col in range(tiles):
+                        start = (part * tiles + col) * tile
+                        piece = probs_ref[sub, rows, start : start + tile].astype(float32) * (
+                            raw[span, start : start + tile] - row_dot
+                        )
+                        shift = col - block
+                        if shift < -reach:
+                            dfar_ref[sub, 0] += piece
+                        elif shift > reach:
+                            dfar_ref[sub, 1] += piece
+                        else:
+                            columns = slice((shift + reach) * tile, (shift + reach + 1) * tile)
+                            dbias_ref[sub, part - mine + stride - 1, :, columns] += piece
+                        pieces.append(piece.astype(bfloat))
+                low_grads = jnp.concatenate(pieces, axis=1)
+                ds_ref[sub, rows, :] = low_grads
+                stacked.append(low_grads)
+            result = dot_nn(jnp.concatenate(stacked, axis=0), k_ref[...]) * scale
+            dq_ref[rows, :] = joined_heads(result, lane, per, head_dim).astype(bfloat)
     dk_parts = []
     dv_parts = []
     for sub in range(per):
-        inside = (lane >= sub * head_dim) & (lane < (sub + 1) * head_dim)
-        for block in range(tiles):
-            rows = slice(block * tile, (block + 1) * tile)
-            place = info_ref[rows, 0:1]
-            grads = grad_ref[rows, :]
-            own = jnp.where(inside, grads, jnp.zeros_like(grads))
-            row_dot = jnp.sum(
-                own.astype(float32) * out_ref[rows, :].astype(float32), axis=-1, keepdims=True
-            )
-            raw = dot_nt(own, v_ref[...])
-            pieces = []
-            for part in range(stride):
-                for col in range(tiles):
-                    start = part * rows_all + col * tile
-                    piece = probs_ref[sub, rows, start : start + tile].astype(float32) * (
-                        raw[:, start : start + tile] - row_dot
-                    )
-                    shift = col - block
-                    if shift < -reach:
-                        dfar_ref[sub, 0] += piece
-                    elif shift > reach:
-                        dfar_ref[sub, 1] += piece
-                    else:
-                        columns = slice((shift + reach) * tile, (shift + reach + 1) * tile)
-                        for other in range(stride):
-                            dbias_ref[sub, part - other + stride - 1, :, columns] += jnp.where(
-                                place == other, piece, 0.0
-                            )
-                    pieces.append(piece.astype(bfloat))
-            low_grads = jnp.concatenate(pieces, axis=1)
-            ds_ref[rows, :] = low_grads
-            result = dot_nn(low_grads, k_ref[...]) * scale
-            if sub == 0:
-                dq_ref[rows, :] = result.astype(bfloat)
-            else:
-                dq_ref[rows, :] = jnp.where(inside, result.astype(bfloat), dq_ref[rows, :])
         dims = slice(sub * head_dim, (sub + 1) * head_dim)
-        dk_parts.append(dot_nn(queries_t[dims, :], ds_ref[...]))
+        dk_parts.append(dot_nn(queries_t[dims, :], ds_ref[sub]))
         dv_parts.append(dot_nn(grads_t[dims, :], probs_ref[sub]))
     dk_ref[...] = jnp.concatenate(dk_parts, axis=0).T.astype(bfloat)
     dv_ref[...] = jnp.concatenate(dv_parts, axis=0).T.astype(bfloat)
 
 
-def attend_back(probs, grads, outs, queries, keys, values, info, head_dim, stride, bias_shape):
-    rows_all, width = queries.shape
-    keys_all = keys.shape[0]
+def attend_back(
+    probs, grads, outs, inverse, queries, keys, values, after, head_dim, stride, bias_shape
+):
+    rows_all, span = queries.shape
     per = tile // head_dim
-    heads = width // head_dim
+    heads = span // head_dim
     row_spec = pl.BlockSpec((rows_all, tile), lambda i: (0, i))
-    key_spec = pl.BlockSpec((keys_all, tile), lambda i: (0, i))
     return pl.pallas_call(
         functools.partial(attend_back_kernel, stride, head_dim, head_dim ** (-0.5)),
-        grid=(width // tile,),
-        in_specs=[
-            pl.BlockSpec((per, rows_all, keys_all), lambda i: (i, 0, 0)),
+        grid=(span // tile,),
+        in_specs=[pl.BlockSpec((per, rows_all, rows_all), lambda i: (i, 0, 0))]
+        + [row_spec] * 6
+        + [pl.BlockSpec(memory_space=pl.ANY)],
+        out_specs=[
             row_spec,
             row_spec,
             row_spec,
-            key_spec,
-            key_spec,
-            pl.BlockSpec(info.shape, lambda i: (0, 0)),
-        ],
-        out_specs=[
-            row_spec,
-            key_spec,
-            key_spec,
             pl.BlockSpec((per,) + bias_shape[1:], lambda i: (i, 0, 0, 0)),
             pl.BlockSpec((per, 2, tile, tile), lambda i: (i, 0, 0, 0)),
         ],
-        out_shape=[
-            jax.ShapeDtypeStruct((rows_all, width), bfloat),
-            jax.ShapeDtypeStruct((keys_all, width), bfloat),
-            jax.ShapeDtypeStruct((keys_all, width), bfloat),
+        out_shape=[jax.ShapeDtypeStruct((rows_all, span), bfloat)] * 3
+        + [
             jax.ShapeDtypeStruct(bias_shape, float32),
             jax.ShapeDtypeStruct((heads, 2, tile, tile), float32),
         ],
-        scratch_shapes=[pltpu.VMEM((rows_all, keys_all), bfloat)],
+        scratch_shapes=[
+            pltpu.VMEM((per, rows_all, rows_all), bfloat),
+            pltpu.VMEM((rows_all, tile), bfloat),
+        ],
         compiler_params=params(),
         cost_estimate=pl.CostEstimate(
-            flops=32 * rows_all * keys_all * width,
-            bytes_accessed=2 * heads * rows_all * keys_all,
+            flops=32 * rows_all * rows_all * span,
+            bytes_accessed=2 * heads * rows_all * rows_all,
             transcendentals=0,
         ),
         name="attend_back",
-    )(probs, grads, outs, queries, keys, values, info)
+    )(probs, grads, outs, inverse, queries, keys, values, after)
+
+
+def add_kernel(left_ref, right_ref, after_ref, out_ref):
+    out_ref[...] = (left_ref[...].astype(float32) + right_ref[...].astype(float32)).astype(bfloat)
+
+
+def add_after(left, right, after):
+    return pl.pallas_call(
+        add_kernel,
+        in_specs=[
+            pl.BlockSpec(memory_space=pltpu.VMEM),
+            pl.BlockSpec(memory_space=pltpu.VMEM),
+            pl.BlockSpec(memory_space=pl.ANY),
+        ],
+        out_specs=pl.BlockSpec(memory_space=pltpu.VMEM),
+        out_shape=jax.ShapeDtypeStruct(left.shape, bfloat),
+        compiler_params=params(),
+        name="add_after",
+    )(left, right, after)
+
+
+def order_kernel(count, place_ref, *refs):
+    out_ref = refs[count]
+    for place in range(count):
+        rows = refs[0][0]
+        for step in range(1, count):
+            rows = jnp.where(place_ref[0, :, step : step + 1] == place, refs[step][0], rows)
+        out_ref[0, place] = rows
+
+
+def order_rows(parts, offsets):
+    batches, rows, width = parts[0].shape
+    count = len(parts)
+    part_spec = pl.BlockSpec((1, rows, width), lambda i: (i, 0, 0))
+    return pl.pallas_call(
+        functools.partial(order_kernel, count),
+        grid=(batches,),
+        in_specs=[pl.BlockSpec((1, rows, count), lambda i: (i, 0, 0))] + [part_spec] * count,
+        out_specs=pl.BlockSpec((1, count, rows, width), lambda i: (i, 0, 0, 0)),
+        out_shape=jax.ShapeDtypeStruct((batches, count, rows, width), bfloat),
+        compiler_params=params(),
+        name="order_rows",
+    )(offsets, *parts)
 
 
 def expert_kernel(
@@ -473,14 +577,26 @@
     hidden_width = w_in.shape[2]
     turns = hidden_width // width
     tiles = rows_own // tile
+    rows_group = members * rows_own
     depth = width // shards
     depth_out = hidden_width // shards
     table_rows = rel_table.shape[0]
     capacity = max(2, rows_own * 17 // (experts * 16))
     slots = -(-capacity // 16) * 16
+    per = tile // head_dim
+    heads_own = per * (-(-heads // (per * members)))
+    span = heads_own * head_dim
+    split = width // span
 
     def around(step):
         return [(idx, (idx + step) % members) for idx in range(members)]
+
+    def columns_own(weight):
+        wide = jnp.pad(weight, ((0, 0), (0, members * span - width)))
+        return lax.dynamic_slice_in_dim(wide, me * span, span, axis=1)
+
+    def in_order(parts):
+        return jnp.take(jnp.stack(parts), jnp.mod(me - jnp.arange(members), members), axis=0)
 
     hidden_from = [hidden_in] + [
         lax.ppermute(hidden_in, "expert", around(step)) for step in range(1, members)
@@ -495,35 +611,55 @@
         ]
     )
     small_used = small.shape[0]
-    small_rows = -(-small_used // width)
-    small_pad = -(-small_rows // 16) * 16
-    small = jnp.pad(small, (0, small_pad * width - small_used)).reshape(small_pad, width)
-    first = lax.all_gather(
-        jnp.concatenate([w_query, w_key, w_value, small], axis=0), "dp", axis=0, tiled=False
-    )
+    small_pad = -(-small_used // (16 * span)) * 16
+    small = jnp.pad(small, (0, small_pad * span - small_used)).reshape(small_pad, span)
+    first_own = jnp.concatenate(
+        [columns_own(w_query), columns_own(w_key), columns_own(w_value)]
+        + [w_output[:, idx * span : (idx + 1) * span] for idx in range(split)]
+        + [small],
+        axis=0,
+    )
+    first = lax.all_gather(first_own, "dp", axis=0, tiled=False)
     inner_parts = [w_in[0, :, idx * width : (idx + 1) * width] for idx in range(turns)]
-    second_own = jnp.concatenate(inner_parts + [w_out[0], w_output], axis=0)
+    second_own = jnp.concatenate(inner_parts + [w_out[0]], axis=0)
     second_own, _ = lax.optimization_barrier((second_own, first))
     second = lax.all_gather(second_own, "dp", axis=0, tiled=False)
 
-    query_w = first[:, :depth].reshape(width, width)
-    key_w = first[:, depth : 2 * depth].reshape(width, width)
-    value_w = first[:, 2 * depth : 3 * depth].reshape(width, width)
-    small_all = first[:, 3 * depth :].reshape(shards, small_pad * width)
-    gain_one = small_all[:, :depth].reshape(width).astype(float32)
+    small_start = (3 + split) * depth
+    small_all = first[:, small_start:].reshape(shards, small_pad * span)
+    gain_one = small_all[:, :depth].reshape(1, width).astype(float32)
     gain_two = small_all[:, depth : 2 * depth].reshape(width).astype(float32)
     router_end = 2 * depth + depth * experts
     router_w = small_all[:, 2 * depth : router_end].reshape(width, experts)
     table = small_all[:, router_end:small_used].reshape(shards * table_rows, heads)
-    output_w = second[:, turns * depth + depth_out :].reshape(width, width)
+    output_w = jnp.concatenate(
+        [
+            first[:, (3 + idx) * depth : (4 + idx) * depth].reshape(width, span)
+            for idx in range(split)
+        ],
+        axis=1,
+    )
+    output_wide = jnp.pad(output_w, ((0, members * span - width), (0, 0)))
+    output_parts = [
+        lax.dynamic_slice_in_dim(output_wide, jnp.mod(me - step, members) * span, span, axis=0)
+        for step in range(members)
+    ]
 
     direct = depth % 16 == 0 and turns * depth == depth_out and shards % turns == 0
     if direct:
         group = shards // turns
+        packed = first[:, : 3 * depth]
         inner_spec = pl.BlockSpec((shards, depth, width), lambda i: (0, i, 0))
         outer_spec = pl.BlockSpec((group, depth_out, width), lambda i: (i, 1, 0))
         weights = ((second, inner_spec), (second, outer_spec), turns)
     else:
+        packed = jnp.concatenate(
+            [
+                first[:, idx * depth : (idx + 1) * depth].reshape(1, width, span)
+                for idx in range(3)
+            ],
+            axis=1,
+        )
         inner_w = second[:, : turns * depth].reshape(shards, turns, depth, width)
         inner_w = jnp.transpose(inner_w, (1, 0, 2, 3)).reshape(turns, width, width)
         outer_w = second[:, turns * depth : turns * depth + depth_out].reshape(
@@ -531,21 +667,16 @@
         )
         plain = pl.BlockSpec((1, width, width), lambda i: (i, 0, 0))
         weights = ((inner_w, plain), (outer_w, plain), turns)
+    query_w, key_w, value_w = (
+        first[:, idx * depth : (idx + 1) * depth].reshape(width, span) for idx in range(3)
+    )
 
     places_in = places[:, 0].reshape(batches, members, rows_own)
     offsets = places_in - members * jnp.arange(rows_own, dtype=jnp.int32)[None, None]
     offset_from = [
         jnp.take(offsets, jnp.mod(me - step, members), axis=1) for step in range(members)
     ]
-
-    def by_place(parts):
-        ordered = []
-        for place in range(members):
-            rows = parts[0]
-            for step in range(1, members):
-                rows = jnp.where((offset_from[step] == place)[..., None], parts[step], rows)
-            ordered.append(rows)
-        return jnp.concatenate(ordered, axis=1)
+    ends = jnp.cumsum(lengths[:, 0], axis=-1)[:, :-1]
 
     def of_member(ordered, batch, step):
         rows = ordered[:rows_own]
@@ -557,13 +688,14 @@
             )
         return rows
 
-    ends = jnp.cumsum(lengths[:, 0], axis=-1)[:, :-1]
-    position_own = offset_from[0] + members * jnp.arange(rows_own, dtype=jnp.int32)[None]
-    past = position_own[:, :, None] >= ends[:, None, :]
-    low = jnp.max(jnp.where(past, ends[:, None, :], 0), axis=-1)
-    high = jnp.min(jnp.where(past, members * rows_own, ends[:, None, :]), axis=-1)
-    info = jnp.stack([offset_from[0], low, high], axis=-1)
-    info = jnp.pad(info, ((0, 0), (0, 0), (0, 5)))
+    def by_place(parts, batch):
+        ordered = []
+        for place in range(members):
+            rows = parts[0]
+            for step in range(1, members):
+                rows = jnp.where((offset_from[step][batch] == place)[:, None], parts[step], rows)
+            ordered.append(rows)
+        return jnp.concatenate(ordered, axis=0)
 
     chosen = routes[:, :, 0]
     picked = chosen[:, :, None] == jnp.arange(experts, dtype=jnp.int32)
@@ -574,23 +706,22 @@
         jnp.arange(members * slots, dtype=jnp.int32)[None, :, None] == target[:, None, :]
     ).astype(bfloat)
 
-    ordered_in = by_place(hidden_from)
-    ordered_f = ordered_in.astype(float32)
+    ordered_in = order_rows(hidden_from, jnp.stack(offset_from, axis=-1))
+    flat_in = ordered_in.reshape(batches * rows_group, width)
+    flat_normed, flat_q, flat_k, flat_v = project(flat_in, gain_one, packed, scale)
+    queries = flat_q.reshape(batches, rows_group, span)
+    keys = flat_k.reshape(batches, rows_group, span)
+    values = flat_v.reshape(batches, rows_group, span)
     own_f = hidden_in.astype(float32)
-    normed_all = norm_rows(ordered_f, gain_one).astype(bfloat)
-    normed_own = norm_rows(own_f, gain_one).astype(bfloat)
-    flat_all = normed_all.reshape(batches * members * rows_own, width)
-    flat_own = normed_own.reshape(batches * rows_own, width)
-    queries = (dot_nn(flat_own, query_w).astype(bfloat) * bfloat(scale)).reshape(
-        batches, rows_own, width
-    )
-    keys = dot_nn(flat_all, key_w).astype(bfloat).reshape(batches, members * rows_own, width)
-    values = dot_nn(flat_all, value_w).astype(bfloat).reshape(batches, members * rows_own, width)
-    bias = bias_tiles(table, members, tiles)
-    table_f = table.astype(float32)
+    table_wide = jnp.pad(table, ((0, 0), (0, members * heads_own - heads)))
+    table_own = lax.dynamic_slice_in_dim(table_wide, me * heads_own, heads_own, axis=1)
+    bias = bias_tiles(table_own, members, tiles)
+    table_f = table_own.astype(float32)
     far = jnp.stack([table_f[levels_all - 1], table_f[2 * levels_all - 1]])
 
     probs = []
+    outs = []
+    inverses = []
     attended = []
     resid_mid = []
     normed_two = []
@@ -598,12 +729,23 @@
     gate = []
     blocks = []
     for batch in range(batches):
-        kept, joined = attend(
-            queries[batch], keys[batch], values[batch], info[batch], bias, far, head_dim, members
+        kept, joined, inverse = attend(
+            queries[batch], keys[batch], values[batch], ends[batch], bias, far, head_dim, members
         )
         probs.append(kept)
-        attended.append(joined)
-        mid = own_f[batch] + dot_nn(joined, output_w)
+        outs.append(joined)
+        inverses.append(inverse)
+        head_parts = [of_member(joined, batch, 0)]
+        for step in range(1, members):
+            head_parts.append(
+                lax.ppermute(
+                    of_member(joined, batch, members - step), "expert", around(step)
+                )
+            )
+        attended.append(head_parts)
+        mid = own_f[batch]
+        for part, weight in zip(head_parts, output_parts):
+            mid = mid + dot_nn(part, weight)
         normed = norm_rows(mid, gain_two).astype(bfloat)
         logits = dot_nn(normed, router_w)
         shifted = jnp.exp(logits - jnp.max(logits, axis=-1, keepdims=True))
@@ -672,16 +814,11 @@
     expert_sum = lax.psum_scatter(buffer, "dp", scatter_dimension=0, tiled=False)
 
     layer_rows = []
-    input_rows = []
+    grad_mid_rows = []
     grad_attn_rows = []
-    grad_q_rows = []
-    grad_k_rows = []
-    grad_v_rows = []
-    grad_gain_one = 0.0
+    grad_head_rows = []
     grad_gain_two = 0.0
     grad_router = 0.0
-    grad_bias = 0.0
-    grad_far = 0.0
     router_f = router_w.astype(float32)
     for batch in range(batches):
         home = dot_tn(dispatch[batch], returned[batch])
@@ -704,17 +841,32 @@
         grad_resid, gain_terms = norm_back(resid_mid[batch], gain_two, grad_normed)
         grad_gain_two = grad_gain_two + jnp.sum(gain_terms, axis=0)
         grad_mid = grad_output + grad_resid
+        grad_mid_rows.append(grad_mid)
         grad_attn = grad_mid.astype(bfloat)
         grad_attn_rows.append(grad_attn)
-        grad_attended = dot_nt(grad_attn, output_w).astype(bfloat)
+        parts = [dot_nt(grad_attn, weight).astype(bfloat) for weight in output_parts]
+        from_members = [parts[0]]
+        for step in range(1, members):
+            from_members.append(lax.ppermute(parts[members - step], "expert", around(step)))
+        grad_head_rows.append(by_place(from_members, batch))
+
+    input_rows = []
+    grad_q_rows = []
+    grad_k_rows = []
+    grad_v_rows = []
+    grad_gain_one = 0.0
+    grad_bias = 0.0
+    grad_far = 0.0
+    for batch in range(batches):
         grad_q, grad_k, grad_v, bias_terms, far_terms = attend_back(
             probs[batch],
-            grad_attended,
-            attended[batch],
+            grad_head_rows[batch],
+            outs[batch],
+            inverses[batch],
             queries[batch],
             keys[batch],
             values[batch],
-            info[batch],
+            buffer,
             head_dim,
             members,
             bias.shape,
@@ -724,25 +876,28 @@
         grad_v_rows.append(grad_v)
         grad_bias = grad_bias + bias_terms
         grad_far = grad_far + far_terms
-        grad_ordered = dot_nt(grad_k, key_w) + dot_nt(grad_v, value_w)
-        grad_own = dot_nt(grad_q, query_w)
+        grad_ordered = dot_nt(grad_q, query_w) + dot_nt(grad_k, key_w) + dot_nt(grad_v, value_w)
         home_rows = of_member(grad_ordered, batch, 0)
         for step in range(1, members):
             sent = of_member(grad_ordered, batch, step).astype(bfloat)
             home_rows = home_rows + lax.ppermute(sent, "expert", around(-step)).astype(float32)
-        grad_tokens, _ = norm_back(own_f[batch], gain_one, grad_own + home_rows)
-        input_rows.append(grad_mid + grad_tokens)
-        _, terms_all = norm_back(ordered_f[batch], gain_one, grad_ordered)
-        _, terms_own = norm_back(own_f[batch], gain_one, grad_own)
-        grad_gain_one = grad_gain_one + jnp.sum(terms_all, axis=0) + jnp.sum(terms_own, axis=0)
+        grad_tokens, _ = norm_back(own_f[batch], gain_one, home_rows)
+        input_rows.append(grad_mid_rows[batch] + grad_tokens)
+        rows = slice(batch * rows_group, (batch + 1) * rows_group)
+        _, terms = norm_back(flat_in[rows].astype(float32), gain_one, grad_ordered)
+        grad_gain_one = grad_gain_one + jnp.sum(terms, axis=0)
 
     def flat(rows):
         return jnp.concatenate(rows, axis=0)
 
-    grad_wo = dot_tn(flat(attended), flat(grad_attn_rows))
-    grad_wq = dot_tn(flat_own, flat(grad_q_rows))
-    grad_wk = dot_tn(flat_all, flat(grad_k_rows))
-    grad_wv = dot_tn(flat_all, flat(grad_v_rows))
+    grad_out_parts = [
+        dot_tn(flat([parts[step] for parts in attended]), flat(grad_attn_rows)).astype(bfloat)
+        for step in range(members)
+    ]
+    grad_wo = in_order(grad_out_parts).reshape(members * span, width)[:width]
+    grad_wq = dot_tn(flat_normed, flat(grad_q_rows))
+    grad_wk = dot_tn(flat_normed, flat(grad_k_rows))
+    grad_wv = dot_tn(flat_normed, flat(grad_v_rows))
 
     steps = 2 * members - 1
     reach = near_shift(tiles)
@@ -767,6 +922,9 @@
     far_sum = jnp.sum(grad_far, axis=(2, 3))
     grad_table = grad_table.at[levels_all - 1].add(far_sum[:, 0])
     grad_table = grad_table.at[2 * levels_all - 1].add(far_sum[:, 1])
+    grad_table = lax.dynamic_update_slice_in_dim(
+        jnp.zeros((buckets, members * heads_own), float32), grad_table, me * heads_own, axis=1
+    )[:, :heads]
 
     small_grad = jnp.concatenate(
         [
@@ -777,37 +935,71 @@
         ],
         axis=1,
     )
-    small_grad = jnp.pad(small_grad, ((0, 0), (0, small_pad * width - small_used)))
+    small_grad = jnp.pad(small_grad, ((0, 0), (0, small_pad * span - small_used)))
     dense = jnp.concatenate(
         [
-            grad_wq.astype(bfloat).reshape(shards, depth, width),
-            grad_wk.astype(bfloat).reshape(shards, depth, width),
-            grad_wv.astype(bfloat).reshape(shards, depth, width),
-            grad_wo.astype(bfloat).reshape(shards, depth, width),
-            small_grad.astype(bfloat).reshape(shards, small_pad, width),
-        ],
+            grad_wq.astype(bfloat).reshape(shards, depth, span),
+            grad_wk.astype(bfloat).reshape(shards, depth, span),
+            grad_wv.astype(bfloat).reshape(shards, depth, span),
+        ]
+        + [
+            grad_wo[:, idx * span : (idx + 1) * span].reshape(shards, depth, span)
+            for idx in range(split)
+        ]
+        + [small_grad.astype(bfloat).reshape(shards, small_pad, span)],
         axis=1,
     )
-    dense, _ = lax.optimization_barrier((dense, expert_sum))
-    dense_part = lax.psum_scatter(dense, "dp", scatter_dimension=0, tiled=False)
-    dense_sum = dense_part.astype(float32)
-    for step in range(1, members):
-        dense_sum = dense_sum + lax.ppermute(dense_part, "expert", around(step)).astype(float32)
+
+    line = shards // 4
+    my_shard = lax.axis_index("dp")
+    rows_dense = dense.shape[1]
+    dense = dense.reshape(line, 2, 2, rows_dense, span)
+    odd = my_shard % 2 == 1
+    sent = jnp.where(odd, dense[:, :, 0], dense[:, :, 1])
+    held = jnp.where(odd, dense[:, :, 1], dense[:, :, 0])
+    got = lax.ppermute(sent, "dp", [(idx, idx ^ 1) for idx in range(shards)])
+    dense = (held.astype(float32) + got.astype(float32)).astype(bfloat)
+    odd = (my_shard // 2) % 2 == 1
+    sent = jnp.where(odd, dense[:, 0], dense[:, 1])
+    held = jnp.where(odd, dense[:, 1], dense[:, 0])
+    got = lax.ppermute(sent, "dp", [(idx, idx ^ 2) for idx in range(shards)])
+    dense = add_after(held, got, expert_sum)
+    dense_part = lax.psum_scatter(
+        dense,
+        "dp",
+        scatter_dimension=0,
+        tiled=False,
+        axis_index_groups=[[rest + 4 * idx for idx in range(line)] for rest in range(4)],
+    )
+    parts = [dense_part] + [
+        lax.ppermute(dense_part, "expert", around(step)) for step in range(1, members)
+    ]
+    qkv_parts = in_order([part[: 3 * depth] for part in parts]).astype(float32)
+    qkv_grads = [
+        jnp.concatenate(
+            [qkv_parts[idx, kind * depth : (kind + 1) * depth] for idx in range(members)], axis=1
+        )[:, :width]
+        for kind in range(3)
+    ]
+    rest_sum = sum(part[3 * depth :].astype(float32) for part in parts)
+    out_grad_sum = jnp.concatenate(
+        [rest_sum[idx * depth : (idx + 1) * depth] for idx in range(split)], axis=1
+    )
+    small_sum = rest_sum[split * depth :].reshape(-1)
 
     expert_f = expert_sum.astype(float32)
     inner_sum = jnp.concatenate(
         [expert_f[idx * depth : (idx + 1) * depth] for idx in range(turns)], axis=1
     )[None]
     outer_sum = expert_f[turns * depth :][None]
-    small_sum = dense_sum[4 * depth :].reshape(-1)
     return (
         jnp.stack(layer_rows),
         jnp.stack(input_rows),
         small_sum[:depth],
-        dense_sum[:depth],
-        dense_sum[depth : 2 * depth],
-        dense_sum[2 * depth : 3 * depth],
-        dense_sum[3 * depth : 4 * depth],
+        qkv_grads[0],
+        qkv_grads[1],
+        qkv_grads[2],
+        out_grad_sum,
         small_sum[router_end:small_used].reshape(table_rows, heads),
         small_sum[depth : 2 * depth],
         small_sum[2 * depth : router_end].reshape(depth, experts),

time: 617 us -> 480 us (0.78)
  waiting for transfers between devices: 252 us -> 126 us
  Pallas kernels: 171 us -> 149 us
  other arithmetic: 48.5 us -> 61.1 us
    reduce_scatter x1, waiting for transfers between devices: 96.2 us -> 0.01 us  [on_device(): lax.psum_scatter(buffer, 'dp', scatter_dimension=0, tiled=False)]
    reduce_scatter x1, waiting for transfers between devices: 51.2 us -> 15.3 us  [on_device(): lax.psum_scatter(dense, 'dp', scatter_dimension=0, tiled=False, axis_inde...]
    ppermute x2, waiting for transfers between devices: 1.21 us -> 26.4 us  [on_device(): lax.ppermute(sent, 'expert', around(-step)).astype(float32)]
    pallas_call x2, Pallas kernels: 58.2 us -> 35.7 us  [attend(): pl.pallas_call(functools.partial(attend_kernel, stride, head_dim), grid=(...]
    pallas_call x0 -> x3, Pallas kernels: none -> 15.3 us  [the longest x1 8.61 us: project(): pl.pallas_call(functools.partial(project_kernel, scale), grid=(count // s...]
    ppermute x2, waiting for transfers between devices: 11.5 us -> 0.01 us  [on_device(): back.append(lax.ppermute(results[step], 'expert', around(-step)))]
    pallas_call x2, Pallas kernels: 44.3 us -> 33.3 us  [attend_back(): pl.pallas_call(functools.partial(attend_back_kernel, stride, head_dim, he...]
    select_n x3 -> x6, other arithmetic: 1.96 us -> 9.47 us  [the longest x2 4.3 us: of_member(): jnp.where((offset_from[step][batch] == place)[:, None], ordered[place * r...]
  transfers between devices with their start and end apart: 12 -> 18, of which waited for: 7 -> 8; matrix products, arithmetic and copies ran while one was open for 15% -> 30% of each run, Pallas kernels for 21% -> 31%
where the time goes in v2:
time: 480 us; the launch traced here: 471 us
  Pallas kernels  149 us (31%)
  waiting for transfers between devices  126 us (26%)
  other arithmetic  61.1 us (13%)
  matrix products  53.1 us (11%)
  local copies, waits for them, and re-layouts  52.6 us (11%)
  between operations  15.2 us (3%)
  starting transfers between devices  14 us (3%)
    all_gather x1, waiting for transfers between devices, on_device(): first = lax.all_gather(first_own, 'dp', axis=0, tiled=False)  43.4 us
    pallas_call x2, Pallas kernels, run_expert(): pl.pallas_call(functools.partial(expert_kernel, count, slots, width, 256)...  35.7 us
    pallas_call x2, Pallas kernels, attend(): pl.pallas_call(functools.partial(attend_kernel, stride, head_dim), grid=(...  35.7 us
    pallas_call x2, Pallas kernels, attend_back(): pl.pallas_call(functools.partial(attend_back_kernel, stride, head_dim, he...  33.3 us
    ppermute x2, waiting for transfers between devices, on_device(): lax.ppermute(sent, 'expert', around(-step)).astype(float32)  26.4 us
    pallas_call x2, Pallas kernels, expert_grad(): pl.pallas_call(body, grid=(turns,), in_specs=in_specs, out_specs=out_spec...  23.7 us
    ppermute x1, waiting for transfers between devices, on_device(): lax.ppermute(hidden_in, 'expert', around(step))  21.1 us
    unnamed x169, local copies, waits for them, and re-layouts  20.8 us
  transfers between devices with their start and end apart: 18, of which 8 were waited for; matrix products, arithmetic and copies ran while one was open for 30% of the time, Pallas kernels for 31%

profile of v2, /device:TPU:0, one launch (start us, length us, event | category | flops | bytes accessed | tf_op | source)
XLA Modules:
  0.0 471.2 jit_solution(12875878364144772721)
XLA Ops:
  18.9 43.4 %all-gather.5.cloned.1.call-done = bf16[4096,384]{1,0:T(8,128)(2,1)} async-done(((bf16[256,384]{1,0:T(8,128)(2,1)}), bf16[4096,384]{1,0:T(8,128)(2,1)}) %all-gather.5.cloned.1.call-update) | async-done | bytes 3145744 | tf_op jit(solution)/shard_map/all_gather | solution.py:622
  78.2 21.1 %collective-permute-done.refs_1_ = bf16[2,512,768]{2,1,0:T(8,128)(2,1)} collective-permute-done((bf16[2,512,768]{2,1,0:T(8,128)(2,1)}, bf16[2,512,768]{2,1,0:T(8,128)(2,1)}, u32[]{:S(2)}, u32[]{:S(2)}) %collective-permute-start) | collective-permute-done | bytes 1572896 | tf_op jit(solution)/shard_map/ppermute | solution.py:602
  99.3 4.3 order_rows.1
  106.5 3.3 slice_convert_fusion
  113.0 5.1 %bias_tiles.1.bias_ref = f32[6,3,128,384]{3,2,1,0:T(8,128)} custom-call(f32[6,128]{1,0:T(8,128)} %pad.18.clone.table_ref), custom_call_target="tpu_custom_call" | custom-call | tf_op jit(solution)/shard_map/bias_tiles/pallas_call | solution.py:79
  118.6 8.6 %project.1 = (bf16[2048,768]{1,0:T(8,128)(2,1)}, bf16[2048,384]{1,0:T(8,128)(2,1)}, bf16[2048,384]{1,0:T(8,128)(2,1)}, bf16[2048,384]{1,0:T(8,128)(2,1)}) custom-call(bf16[2048,768]{1,0:T(8,128)(2,1)} %bitcast.249, f32[1,768]{1,0:T(1,128)} %reshape.576.gain_ref, bf16[16,144,384]{2,1,0:T(8,128)(2,1)} %slice.467.weight_ref), custom_call_target="tpu_custom_call" | custom-call | flops 3623878656 | bytes 6291456 | tf_op jit(solution)/shard_map/project/pallas_call | solution.py:107
  127.2 3.1 fusion.151
  132.1 17.7 %attend.3 = (bf16[6,1024,1024]{2,1,0:T(8,128)(2,1)}, bf16[1024,384]{1,0:T(8,128)(2,1)}, f32[1024,384]{1,0:T(8,128)}) custom-call(f32[2,6]{1,0:T(2,128)} %pad_maximum_fusion.13.far_ref, s32[1]{0:T(128)} %bitcast.23.ends_ref, bf16[1024,384]{1,0:T(8,128)(2,1)} %get-tuple-element.232.q_ref, bf16[1024,384]{1,0:T(8,128)(2,1)} %get-tuple-element.283.k_ref, ...), custom_call_target="tpu_custom_call" | custom-call | flops 6442450944 | bytes 12582912 | tf_op jit(solution)/shard_map/attend/pallas_call | solution.py:220
  153.5 18.0 %attend.2 = (bf16[6,1024,1024]{2,1,0:T(8,128)(2,1)}, bf16[1024,384]{1,0:T(8,128)(2,1)}, f32[1024,384]{1,0:T(8,128)}) custom-call(f32[2,6]{1,0:T(2,128)} %pad_maximum_fusion.13.far_ref, s32[1]{0:T(128)} %bitcast.4.ends_ref, bf16[1024,384]{1,0:T(8,128)(2,1)} %get-tuple-element.231.q_ref, bf16[1024,384]{1,0:T(8,128)(2,1)} %get-tuple-element.284.k_ref, ...), custom_call_target="tpu_custom_call" | custom-call | flops 6442450944 | bytes 12582912 | tf_op jit(solution)/shard_map/attend/pallas_call | solution.py:220
  195.9 17.1 %collective-permute-done.5.refs_1_.refs_3_.refs_4_ = bf16[272,1536]{1,0:T(8,128)(2,1)} collective-permute-done((bf16[272,1536]{1,0:T(8,128)(2,1)S(1)}, bf16[272,1536]{1,0:T(8,128)(2,1)}, u32[]{:S(2)}, u32[]{:S(2)}) %collective-permute-start.5) | collective-permute-done | bytes 835616 | tf_op jit(solution)/shard_map/ppermute | solution.py:761
  213.0 17.7 %run_expert.3 = (bf16[272,1536]{1,0:T(8,128)(2,1)}, bf16[272,1536]{1,0:T(8,128)(2,1)}, bf16[544,3072]{1,0:T(8,128)(2,1)}, bf16[544,3072]{1,0:T(8,128)(2,1)}) custom-call(bf16[16,384,768]{2,1,0:T(8,128)(2,1)} %bitcast.282, bf16[16,384,768]{2,1,0:T(8,128)(2,1)} %bitcast.283, bf16[272,1536]{1,0:T(8,128)(2,1)} %get-tuple-element.220.refs_0_.refs_2_.refs_3_, ...), custom_call_target="tpu_custom_call" | custom-call | flops 10267656192 | bytes 9437184 | tf_op jit(solution)/shard_map/run_expert/pallas_call | solution.py:465
  232.2 18.0 %run_expert.2 = (bf16[272,1536]{1,0:T(8,128)(2,1)}, bf16[272,1536]{1,0:T(8,128)(2,1)}, bf16[544,3072]{1,0:T(8,128)(2,1)}, bf16[544,3072]{1,0:T(8,128)(2,1)}) custom-call(bf16[16,384,768]{2,1,0:T(8,128)(2,1)} %bitcast.284, bf16[16,384,768]{2,1,0:T(8,128)(2,1)} %bitcast.285, bf16[272,1536]{1,0:T(8,128)(2,1)} %get-tuple-element.218.refs_0_.refs_1_, ...), custom_call_target="tpu_custom_call" | custom-call | flops 10267656192 | bytes 9437184 | tf_op jit(solution)/shard_map/run_expert/pallas_call | solution.py:465
  250.7 11.9 %expert_grad_inner.1.refs_0_ = bf16[16,384,768]{2,1,0:T(8,128)(2,1)} custom-call(bf16[272,1536]{1,0:T(8,128)(2,1)} %get-tuple-element.218.refs_0_.refs_1_, bf16[272,1536]{1,0:T(8,128)(2,1)} %collective-permute-done.2.refs_1_.refs_2_, bf16[272,1536]{1,0:T(8,128)(2,1)} %get-tuple-element.220.refs_0_.refs_2_.refs_3_, ...), custom_call_target="tpu_custom_call" | custom-call | flops 5133828096 | bytes 9437184 | tf_op jit(solution)/shard_map/expert_grad_inner/pallas_call | solution.py:534
  262.6 11.8 %expert_grad_outer.1.after_ref = bf16[16,384,768]{2,1,0:T(8,128)(2,1)} custom-call(bf16[16,384,768]{2,1,0:T(8,128)(2,1)} %expert_grad_inner.1.refs_0_, bf16[272,1536]{1,0:T(8,128)(2,1)} %get-tuple-element.218.refs_0_.refs_1_, bf16[272,1536]{1,0:T(8,128)(2,1)} %collective-permute-done.2.refs_1_.refs_2_, ...), custom_call_target="tpu_custom_call", output_to_operand_aliasing={{}: (0, {})} | custom-call | flops 5133828096 | bytes 9437184 | tf_op jit(solution)/shard_map/expert_grad_outer/pallas_call | solution.py:534
  274.7 3.1 fusion.12
  312.5 16.5 %attend_back.3 = (bf16[1024,384]{1,0:T(8,128)(2,1)}, bf16[1024,384]{1,0:T(8,128)(2,1)}, bf16[1024,384]{1,0:T(8,128)(2,1)}, f32[6,3,128,384]{3,2,1,0:T(8,128)}, f32[6,2,128,128]{3,2,1,0:T(8,128)}) custom-call(bf16[6,1024,1024]{2,1,0:T(8,128)(2,1)} %get-tuple-element.85.probs_ref, bf16[1024,384]{1,0:T(8,128)(2,1)} %pad_maximum_fusion.7.grad_ref, ...), custom_call_target="tpu_custom_call" | custom-call | flops 12884901888 | bytes 12582912 | tf_op jit(solution)/shard_map/attend_back/pallas_call | solution.py:332
  331.2 16.8 %attend_back.2 = (bf16[1024,384]{1,0:T(8,128)(2,1)}, bf16[1024,384]{1,0:T(8,128)(2,1)}, bf16[1024,384]{1,0:T(8,128)(2,1)}, f32[6,3,128,384]{3,2,1,0:T(8,128)}, f32[6,2,128,128]{3,2,1,0:T(8,128)}) custom-call(bf16[6,1024,1024]{2,1,0:T(8,128)(2,1)} %get-tuple-element.76.probs_ref, bf16[1024,384]{1,0:T(8,128)(2,1)} %pad_maximum_fusion.6.grad_ref, ...), custom_call_target="tpu_custom_call" | custom-call | flops 12884901888 | bytes 12582912 | tf_op jit(solution)/shard_map/attend_back/pallas_call | solution.py:332
  360.9 4.0 add_convert_fusion
  365.0 3.5 fusion.50
  369.5 4.3 fusion.44
  395.1 10.0 %collective-permute-done.10 = bf16[512,768]{1,0:T(8,128)(2,1)S(1)} collective-permute-done((bf16[512,768]{1,0:T(8,128)(2,1)S(1)}, bf16[512,768]{1,0:T(8,128)(2,1)S(1)}, u32[]{:S(2)}, u32[]{:S(2)}) %collective-permute-start.10) | collective-permute-done | bytes 786464 | tf_op jit(solution)/shard_map/ppermute | solution.py:883
  405.1 16.5 %collective-permute-done.8 = bf16[512,768]{1,0:T(8,128)(2,1)S(1)} collective-permute-done((bf16[512,768]{1,0:T(8,128)(2,1)S(1)}, bf16[512,768]{1,0:T(8,128)(2,1)S(1)}, u32[]{:S(2)}, u32[]{:S(2)}) %collective-permute-start.8) | collective-permute-done | bytes 786464 | tf_op jit(solution)/shard_map/ppermute | solution.py:883
  428.4 3.9 add_bitcast_fusion
  435.2 15.3 %reduce-scatter.5.cloned.1.call-done = bf16[1,256,384]{2,1,0:T(8,128)(2,1)} async-done(((bf16[4,256,384]{2,1,0:T(8,128)(2,1)}), bf16[1,256,384]{2,1,0:T(8,128)(2,1)}) %reduce-scatter.5.cloned.1.call-update) | async-done | bytes 196624 | tf_op jit(solution)/shard_map/reduce_scatter | solution.py:967
  (364 shorter events, 161.1 us)
Async XLA Ops:
  7.2 56.7 %copy-start.67 = (s32[2,1,1024]{2,1,0:T(1,128)S(1)}, s32[2,1,1024]{2,1,0:T(1,128)}, u32[]{:S(2)}) copy-start(s32[2,1,1024]{2,1,0:T(1,128)} %param.23) | copy-start | bytes 24580
  7.2 56.8 %copy-start.66 = (s32[2,512,1]{1,2,0:T(1,128)S(1)}, s32[2,512,1]{1,2,0:T(1,128)}, u32[]{:S(2)}) copy-start(s32[2,512,1]{1,2,0:T(1,128)} %param.25) | copy-start | bytes 12292
  7.2 55.1 %all-gather.5.cloned.1.call-start = ((), (), s32[]{:S(2)}) async-start(), calls=%async_computation.4 | async-start | bytes 3342336 | tf_op jit(solution)/shard_map/all_gather | solution.py:622
  14.3 198.8 %all-gather.7.cloned.1.call-start = ((), (), s32[]{:S(2)}) async-start(), calls=%async_computation.5 | async-start | bytes 10027008 | tf_op jit(solution)/shard_map/all_gather | solution.py:626
  18.9 43.5 %copy-start.59 = (bf16[384,768]{1,0:T(8,128)(2,1)}, bf16[384,768]{1,0:T(8,128)(2,1)S(1)}, u32[]{:S(2)}) copy-start(bf16[384,768]{1,0:T(8,128)(2,1)S(1)} %bitcast_dynamic-update-slice_fusion) | copy-start | bytes 1769476
  62.3 363.6 %reduce-scatter.3.cloned.1.call-start = ((), (), s32[]{:S(2)}) async-start(), calls=%async_computation.2 | async-start | bytes 10027008 | tf_op jit(solution)/shard_map/reduce_scatter | solution.py:814
  62.4 36.9 %collective-permute-start = (bf16[2,512,768]{2,1,0:T(8,128)(2,1)}, bf16[2,512,768]{2,1,0:T(8,128)(2,1)}, u32[]{:S(2)}, u32[]{:S(2)}) collective-permute-start(bf16[2,512,768]{2,1,0:T(8,128)(2,1)} %refs_0_.1), channel_id=1, source_target_pairs={{0,1},{1,0},{2,3},{3,2},{4,5},{5,4},{6,7},{7,6},{8,9},{9,8},{10,11... | collective-permute-start | bytes 4718600 | tf_op jit(solution)/shard_map/ppermute | solution.py:602
  151.8 24.5 %copy-start.41 = (bf16[512,384]{1,0:T(8,128)(2,1)}, bf16[512,384]{1,0:T(8,128)(2,1)S(1)}, u32[]{:S(2)}) copy-start(bf16[512,384]{1,0:T(8,128)(2,1)S(1)} %get-tuple-element.248) | copy-start | bytes 1179652
  151.8 29.3 %collective-permute-start.4 = (bf16[512,384]{1,0:T(8,128)(2,1)}, bf16[512,384]{1,0:T(8,128)(2,1)}, u32[]{:S(2)}, u32[]{:S(2)}) collective-permute-start(bf16[512,384]{1,0:T(8,128)(2,1)} %get-tuple-element.247), channel_id=1, source_target_pairs={{0,1},{1,0},{2,3},{3,2},{4,5},{5,4},{6,7},{7,6},{8,9},{9,8},{10,11... | collective-permute-start | bytes 1179656 | tf_op jit(solution)/shard_map/ppermute | solution.py:741
  173.8 9.4 %collective-permute-start.1 = (bf16[512,384]{1,0:T(8,128)(2,1)}, bf16[512,384]{1,0:T(8,128)(2,1)}, u32[]{:S(2)}, u32[]{:S(2)}) collective-permute-start(bf16[512,384]{1,0:T(8,128)(2,1)} %get-tuple-element.245), channel_id=1, source_target_pairs={{0,1},{1,0},{2,3},{3,2},{4,5},{5,4},{6,7},{7,6},{8,9},{9,8},{10,11... | collective-permute-start | bytes 1179656 | tf_op jit(solution)/shard_map/ppermute | solution.py:741
  191.4 21.6 %collective-permute-start.5 = (bf16[272,1536]{1,0:T(8,128)(2,1)S(1)}, bf16[272,1536]{1,0:T(8,128)(2,1)}, u32[]{:S(2)}, u32[]{:S(2)}) collective-permute-start(bf16[272,1536]{1,0:T(8,128)(2,1)S(1)} %get-tuple-element.219), channel_id=1, source_target_pairs={{0,1},{1,0},{2,3},{3,2},{4,5},{5,4},{6,7},{7,6},{8,9},{9,8},{10,11... | collective-permute-start | bytes 2506760 | tf_op jit(solution)/shard_map/ppermute | solution.py:761
  195.4 36.9 %collective-permute-start.2 = (bf16[272,1536]{1,0:T(8,128)(2,1)}, bf16[272,1536]{1,0:T(8,128)(2,1)}, u32[]{:S(2)}, u32[]{:S(2)}) collective-permute-start(bf16[272,1536]{1,0:T(8,128)(2,1)} %get-tuple-element.217), channel_id=1, source_target_pairs={{0,1},{1,0},{2,3},{3,2},{4,5},{5,4},{6,7},{7,6},{8,9},{9,8},{10,11... | collective-permute-start | bytes 2506760 | tf_op jit(solution)/shard_map/ppermute | solution.py:761
  230.7 44.0 %collective-permute-start.6 = (bf16[272,1536]{1,0:T(8,128)(2,1)}, bf16[272,1536]{1,0:T(8,128)(2,1)}, u32[]{:S(2)}, u32[]{:S(2)}) collective-permute-start(bf16[272,1536]{1,0:T(8,128)(2,1)} %get-tuple-element.75), channel_id=1, source_target_pairs={{0,1},{1,0},{2,3},{3,2},{4,5},{5,4},{6,7},{7,6},{8,9},{9,8},{10,11... | collective-permute-start | bytes 2506760 | tf_op jit(solution)/shard_map/ppermute | solution.py:780
  250.2 27.6 %collective-permute-start.3 = (bf16[272,1536]{1,0:T(8,128)(2,1)}, bf16[272,1536]{1,0:T(8,128)(2,1)}, u32[]{:S(2)}, u32[]{:S(2)}) collective-permute-start(bf16[272,1536]{1,0:T(8,128)(2,1)} %get-tuple-element.72), channel_id=1, source_target_pairs={{0,1},{1,0},{2,3},{3,2},{4,5},{5,4},{6,7},{7,6},{8,9},{9,8},{10,11... | collective-permute-start | bytes 2506760 | tf_op jit(solution)/shard_map/ppermute | solution.py:780
  274.5 176.0 %reduce-scatter.5.cloned.1.call-start = ((), (), s32[]{:S(2)}) async-start(), calls=%async_computation.3 | async-start | bytes 983040 | tf_op jit(solution)/shard_map/reduce_scatter | solution.py:967
  292.2 15.0 %collective-permute-start.9 = (bf16[512,384]{1,0:T(8,128)(2,1)}, bf16[512,384]{1,0:T(8,128)(2,1)}, u32[]{:S(2)}, u32[]{:S(2)}) collective-permute-start(bf16[512,384]{1,0:T(8,128)(2,1)} %convolution_convert_fusion.5), channel_id=1, source_target_pairs={{0,1},{1,0},{2,3},{3,2},{4,5},{5,4},{6,7},{7,6},{8,9},{9,8},{10,11... | collective-permute-start | bytes 1179656 | tf_op jit(solution)/shard_map/ppermute | solution.py:850
  293.8 16.1 %collective-permute-start.7 = (bf16[512,384]{1,0:T(8,128)(2,1)}, bf16[512,384]{1,0:T(8,128)(2,1)}, u32[]{:S(2)}, u32[]{:S(2)}) collective-permute-start(bf16[512,384]{1,0:T(8,128)(2,1)} %convolution_convert_fusion.7), channel_id=1, source_target_pairs={{0,1},{1,0},{2,3},{3,2},{4,5},{5,4},{6,7},{7,6},{8,9},{9,8},{10,11... | collective-permute-start | bytes 1179656 | tf_op jit(solution)/shard_map/ppermute | solution.py:850
  381.7 8.7 %collective-permute-start.11 = (bf16[4,2,256,384]{3,2,0,1:T(8,128)(2,1)}, bf16[4,2,256,384]{3,2,0,1:T(8,128)(2,1)}, u32[]{:S(2)}, u32[]{:S(2)}) collective-permute-start(bf16[4,2,256,384]{3,2,0,1:T(8,128)(2,1)} %select_bitcast_fusion), channel_id=1, source_target_pairs={{0,2},{2,0},{4,6},{6,4},{8,10},{10,8},{12,14},{14,12},{16,18},{18,... | collective-permute-start | bytes 4718600 | tf_op jit(solution)/shard_map/ppermute | solution.py:960
  384.7 20.4 %collective-permute-start.10 = (bf16[512,768]{1,0:T(8,128)(2,1)S(1)}, bf16[512,768]{1,0:T(8,128)(2,1)S(1)}, u32[]{:S(2)}, u32[]{:S(2)}) collective-permute-start(bf16[512,768]{1,0:T(8,128)(2,1)S(1)} %select_convert_fusion), channel_id=1, source_target_pairs={{0,1},{1,0},{2,3},{3,2},{4,5},{5,4},{6,7},{7,6},{8,9},{9,8},{10,11... | collective-permute-start | bytes 2359304 | tf_op jit(solution)/shard_map/ppermute | solution.py:883
  388.7 32.9 %collective-permute-start.8 = (bf16[512,768]{1,0:T(8,128)(2,1)S(1)}, bf16[512,768]{1,0:T(8,128)(2,1)S(1)}, u32[]{:S(2)}, u32[]{:S(2)}) collective-permute-start(bf16[512,768]{1,0:T(8,128)(2,1)S(1)} %select_convert_fusion.1), channel_id=1, source_target_pairs={{0,1},{1,0},{2,3},{3,2},{4,5},{5,4},{6,7},{7,6},{8,9},{9,8},{10,11... | collective-permute-start | bytes 2359304 | tf_op jit(solution)/shard_map/ppermute | solution.py:883
  391.6 30.0 %copy-start.6 = (f32[1024,768]{1,0:T(8,128)S(1)}, f32[1024,768]{1,0:T(8,128)}, u32[]{:S(2)}) copy-start(f32[1024,768]{1,0:T(8,128)} %get-tuple-element.201) | copy-start | bytes 9437188
  393.8 27.8 %copy-start.5 = (f32[1024,768]{1,0:T(8,128)S(1)}, f32[1024,768]{1,0:T(8,128)}, u32[]{:S(2)}) copy-start(f32[1024,768]{1,0:T(8,128)} %get-tuple-element.199) | copy-start | bytes 9437188
  394.8 31.1 %collective-permute-start.12 = (bf16[4,256,384]{2,1,0:T(8,128)(2,1)S(1)}, bf16[4,256,384]{2,1,0:T(8,128)(2,1)}, u32[]{:S(2)}, u32[]{:S(2)}) collective-permute-start(bf16[4,256,384]{2,1,0:T(8,128)(2,1)S(1)} %get-tuple-element.223), channel_id=1, source_target_pairs={{0,4},{2,6},{4,0},{6,2},{8,12},{10,14},{12,8},{14,10},{16,20},{18,... | collective-permute-start | bytes 2359304 | tf_op jit(solution)/shard_map/ppermute | solution.py:965
  450.5 5.9 %collective-permute-start.13 = (bf16[256,384]{1,0:T(8,128)(2,1)}, bf16[256,384]{1,0:T(8,128)(2,1)S(1)}, u32[]{:S(2)}, u32[]{:S(2)}) collective-permute-start(bf16[256,384]{1,0:T(8,128)(2,1)} %bitcast.273), channel_id=1, source_target_pairs={{0,1},{1,0},{2,3},{3,2},{4,5},{5,4},{6,7},{7,6},{8,9},{9,8},{10,11... | collective-permute-start | bytes 589832 | tf_op jit(solution)/shard_map/ppermute | solution.py:975
  (67 other events, 218.6 us)
Sparse Core Ops, SparseCore 0:
  14.4 47.8 all-gather.4
  65.2 80.2 all-gather.6
  274.6 109.8 reduce-scatter.2
  428.5 21.9 reduce-scatter.4

commit v3 on v2

--- a/solution.py
+++ b/solution.py
@@ -86,41 +86,502 @@
     )(lanes)
 
 
-def project_kernel(scale, rows_ref, gain_ref, weight_ref, normed_ref, q_ref, k_ref, v_ref):
-    width = rows_ref.shape[1]
-    span = q_ref.shape[1]
-    depth = weight_ref.shape[1] // 3
-    normed = norm_rows(rows_ref[...].astype(float32), gain_ref[...]).astype(bfloat)
+def project_kernel(pairs, scale, rows_ref, gain_ref, weight_ref, normed_ref, out_ref):
+    width = rows_ref.shape[2]
+    depth = weight_ref.shape[1] // pairs
+    lanes = weight_ref.shape[2]
+    normed = norm_rows(rows_ref[0].astype(float32), gain_ref[...]).astype(bfloat)
     normed_ref[...] = normed
-    for idx, out_ref in enumerate((q_ref, k_ref, v_ref)):
-        weight = weight_ref[:, idx * depth : (idx + 1) * depth, :].reshape(width, span)
+    for pair in range(pairs):
+        weight = weight_ref[:, pair * depth : (pair + 1) * depth, :].reshape(width, lanes)
         product = dot_nn(normed, weight).astype(bfloat)
-        out_ref[...] = product * bfloat(scale) if idx == 0 else product
-
-
-def project(rows, gain, packed, scale):
-    count, width = rows.shape
-    span = packed.shape[2]
+        start = pair * lanes
+        out_ref[:, start : start + tile] = product[:, :tile] * bfloat(scale)
+        out_ref[:, start + tile : start + lanes] = product[:, tile:]
+
+
+def project(batch, rows, gain, packed, pairs, scale):
+    _, count, width = rows.shape
+    lanes = packed.shape[2]
+    weight_shape = (packed.shape[0], pairs * width // packed.shape[0], lanes)
     step = min(512, count)
-    row_spec = pl.BlockSpec((step, width), lambda i: (i, 0))
-    out_spec = pl.BlockSpec((step, span), lambda i: (i, 0))
     return pl.pallas_call(
-        functools.partial(project_kernel, scale),
+        functools.partial(project_kernel, pairs, scale),
         grid=(count // step,),
         in_specs=[
-            row_spec,
+            pl.BlockSpec((1, step, width), lambda i: (batch, i, 0)),
             pl.BlockSpec((1, width), lambda i: (0, 0)),
-            pl.BlockSpec(packed.shape, lambda i: (0, 0, 0)),
-        ],
-        out_specs=[row_spec, out_spec, out_spec, out_spec],
-        out_shape=[jax.ShapeDtypeStruct((count, width), bfloat)]
-        + [jax.ShapeDtypeStruct((count, span), bfloat)] * 3,
+            pl.BlockSpec(weight_shape, lambda i: (0, 0, 0)),
+        ],
+        out_specs=[
+            pl.BlockSpec((step, width), lambda i: (i, 0)),
+            pl.BlockSpec((step, pairs * lanes), lambda i: (i, 0)),
+        ],
+        out_shape=[
+            jax.ShapeDtypeStruct((count, width), bfloat),
+            jax.ShapeDtypeStruct((count, pairs * lanes), bfloat),
+        ],
         compiler_params=params(),
         cost_estimate=pl.CostEstimate(
-            flops=6 * count * width * span, bytes_accessed=4 * count * width, transcendentals=0
+            flops=2 * count * width * lanes * pairs,
+            bytes_accessed=6 * count * width,
+            transcendentals=0,
         ),
         name="project",
     )(rows, gain, packed)
+
+
+def count_earlier(picked, first_axis):
+    size = picked.shape[1 - first_axis]
+    row = lax.broadcasted_iota(jnp.int32, (size, size), 0)
+    column = lax.broadcasted_iota(jnp.int32, (size, size), 1)
+    if first_axis == 0:
+        return dot_nn(picked, (row < column).astype(float32).astype(bfloat))
+    return dot_nn((column < row).astype(float32).astype(bfloat), picked)
+
+
+def tables_kernel(
+    members,
+    slots,
+    me_ref,
+    row_ref,
+    column_ref,
+    place_ref,
+    after_ref,
+    carried_ref,
+    send_ref,
+    back_ref,
+    offset_ref,
+    handed_ref,
+):
+    me = me_ref[0]
+    batches, rows = column_ref.shape[0], column_ref.shape[1]
+    names = 128
+    for batch in range(batches):
+        route = row_ref[batch]
+        picked = lax.broadcasted_iota(jnp.int32, (names, rows), 0) == route
+        earlier = count_earlier(picked.astype(float32).astype(bfloat), 0)
+        slot = jnp.sum(jnp.where(picked, earlier, 0.0), axis=0, keepdims=True).astype(jnp.int32)
+        target = jnp.where(route >= me, route - me, route - me + members) * slots + slot
+        index = lax.broadcasted_iota(jnp.int32, (members * slots, rows), 0)
+        send_ref[batch] = (index == target).astype(float32).astype(bfloat)
+
+        route = column_ref[batch]
+        picked = lax.broadcasted_iota(jnp.int32, (rows, names), 1) == route
+        earlier = count_earlier(picked.astype(float32).astype(bfloat), 1)
+        slot = jnp.sum(jnp.where(picked, earlier, 0.0), axis=1, keepdims=True).astype(jnp.int32)
+        target = jnp.where(route >= me, route - me, route - me + members) * slots + slot
+        index = lax.broadcasted_iota(jnp.int32, (rows, members * slots), 1)
+        back_ref[batch] = (index == target).astype(float32).astype(bfloat)
+
+        offsets = place_ref[batch] - members * lax.broadcasted_iota(
+            jnp.int32, (rows, members), 0
+        )
+        lane = lax.broadcasted_iota(jnp.int32, (rows, members), 1)
+        for step in range(members):
+            owner = jnp.where(me >= step, me - step, me - step + members)
+            chosen = jnp.sum(jnp.where(lane == owner, offsets, 0), axis=1, keepdims=True)
+            offset_ref[batch, :, step : step + 1] = chosen
+
+
+def row_tables(me, routes, places, after, carried, members, slots):
+    batches, rows, _ = routes.shape
+    vmem = pl.BlockSpec(memory_space=pltpu.VMEM)
+    return pl.pallas_call(
+        functools.partial(tables_kernel, members, slots),
+        in_specs=[pl.BlockSpec(memory_space=pltpu.SMEM), vmem, vmem, vmem]
+        + [pl.BlockSpec(memory_space=pl.ANY)] * 2,
+        out_specs=[vmem, vmem, vmem, pl.BlockSpec(memory_space=pl.ANY)],
+        out_shape=[
+            jax.ShapeDtypeStruct((batches, members * slots, rows), bfloat),
+            jax.ShapeDtypeStruct((batches, rows, members * slots), bfloat),
+            jax.ShapeDtypeStruct((batches, rows, members), jnp.int32),
+            jax.ShapeDtypeStruct(carried.shape, carried.dtype),
+        ],
+        input_output_aliases={5: 3},
+        compiler_params=params(),
+        name="row_tables",
+    )(
+        me,
+        routes.reshape(batches, 1, rows),
+        routes,
+        jnp.transpose(places, (0, 2, 1)),
+        after,
+        carried,
+    )
+
+
+def member_rows(ordered, offset_ref, step, members):
+    count = ordered.shape[0] // members
+    rows = ordered[:count]
+    for place in range(1, members):
+        rows = jnp.where(
+            offset_ref[0, :, step : step + 1] == place,
+            ordered[place * count : (place + 1) * count],
+            rows,
+        )
+    return rows
+
+
+def middle_kernel(
+    members,
+    experts,
+    me_ref,
+    joined_ref,
+    offset_ref,
+    weight_ref,
+    rows_ref,
+    grad_ref,
+    gain_ref,
+    router_ref,
+    route_ref,
+    send_ref,
+    after_ref,
+    *refs,
+):
+    received = refs[: members - 1]
+    mid_ref, normed_ref, probs_ref = refs[members - 1 : members + 2]
+    out_refs = refs[members + 2 :]
+    me = me_ref[0]
+    span = joined_ref.shape[1]
+    width = rows_ref.shape[2]
+    slots = out_refs[0].shape[0]
+    mid = rows_ref[0].astype(float32)
+    for step in range(members):
+        owner = jnp.where(me >= step, me - step, me - step + members)
+        part = (
+            member_rows(joined_ref[...], offset_ref, 0, members)
+            if step == 0
+            else received[step - 1][...]
+        )
+        mid = mid + dot_nn(part, weight_ref[pl.ds(pl.multiple_of(owner * span, span), span), :])
+    mid_ref[...] = mid
+    normed = norm_rows(mid, gain_ref[...]).astype(bfloat)
+    normed_ref[...] = normed
+    logits = dot_nn(normed, router_ref[...])
+    lane = lax.broadcasted_iota(jnp.int32, logits.shape, 1)
+    logits = jnp.where(lane < experts, logits, -jnp.inf)
+    shifted = jnp.exp(logits - jnp.max(logits, axis=-1, keepdims=True))
+    probs = shifted / jnp.sum(shifted, axis=-1, keepdims=True)
+    probs_ref[...] = probs
+    gate = jnp.sum(jnp.where(lane == route_ref[0], probs, 0.0), axis=1, keepdims=True)
+    grad_expert = (gate * grad_ref[0].astype(float32)).astype(bfloat)
+    tokens = dot_nn(send_ref[0], normed).astype(bfloat)
+    grads = dot_nn(send_ref[0], grad_expert).astype(bfloat)
+    for step in range(members):
+        rows = slice(step * slots, (step + 1) * slots)
+        out_refs[step][:, :width] = tokens[rows]
+        out_refs[step][:, width:] = grads[rows]
+
+
+def middle(
+    batch, me, joined, received, offsets, weight, rows, grads, gain, router, routes, send, after
+):
+    members = offsets.shape[2]
+    experts = members
+    _, count, width = rows.shape
+    slots = send.shape[1] // members
+    row_spec = pl.BlockSpec((1, count, width), lambda i: (batch, 0, 0))
+
+    def full(array):
+        return pl.BlockSpec(array.shape, lambda i: (0,) * array.ndim)
+
+    def own(array):
+        return pl.BlockSpec((1,) + array.shape[1:], lambda i: (batch, 0, 0))
+
+    out_shape = [
+        jax.ShapeDtypeStruct((count, width), float32),
+        jax.ShapeDtypeStruct((count, width), bfloat),
+        jax.ShapeDtypeStruct((count, tile), float32),
+    ] + [jax.ShapeDtypeStruct((slots, 2 * width), bfloat)] * members
+    outs = pl.pallas_call(
+        functools.partial(middle_kernel, members, experts),
+        grid=(1,),
+        in_specs=[
+            pl.BlockSpec(memory_space=pltpu.SMEM),
+            full(joined),
+            own(offsets),
+            full(weight),
+            row_spec,
+            row_spec,
+            full(gain),
+            full(router),
+            own(routes),
+            own(send),
+            pl.BlockSpec(memory_space=pl.ANY),
+        ]
+        + [full(part) for part in received],
+        out_specs=[full(shape) for shape in out_shape],
+        out_shape=out_shape,
+        compiler_params=params(),
+        cost_estimate=pl.CostEstimate(
+            flops=6 * count * width * width, bytes_accessed=12 * count * width, transcendentals=0
+        ),
+        name="middle",
+    )(me, joined, offsets, weight, rows, grads, gain, router, routes, send, after, *received)
+    return outs[0], outs[1], outs[2], list(outs[3:])
+
+
+def second_kernel(
+    members,
+    experts,
+    aliased,
+    me_ref,
+    back_ref,
+    mid_ref,
+    normed_ref,
+    probs_ref,
+    grad_ref,
+    route_ref,
+    gain_ref,
+    router_ref,
+    weight_ref,
+    *refs,
+):
+    returned = refs[:members]
+    outs = refs[members + aliased :]
+    layer_ref, grad_mid_ref, grad_attn_ref, gain_out_ref, router_out_ref = outs[:5]
+    part_refs = outs[5:]
+    me = me_ref[0]
+    width = mid_ref.shape[1]
+    span = part_refs[0].shape[1]
+    blocks = jnp.concatenate([ref[...] for ref in returned], axis=0)
+    home = dot_nn(back_ref[0], blocks)
+    expert_back = home[:, :width]
+    mid = mid_ref[...]
+    gain = gain_ref[...]
+    grads = grad_ref[0].astype(float32)
+    probs = probs_ref[...]
+    lane = lax.broadcasted_iota(jnp.int32, probs.shape, 1)
+    picked = lane == route_ref[0]
+    gate = jnp.sum(jnp.where(picked, probs, 0.0), axis=1, keepdims=True)
+    layer_ref[0] = (mid + gate * expert_back).astype(bfloat)
+    grad_gate = jnp.sum(grads * expert_back, axis=1, keepdims=True)
+    grad_logits = (grad_gate * gate) * (jnp.where(picked, 1.0, 0.0) - probs)
+    grad_logits = jnp.where(lane < experts, grad_logits, 0.0)
+    grad_normed = home[:, width:]
+    for name in range(experts):
+        grad_normed = grad_normed + grad_logits[:, name : name + 1] * router_ref[name : name + 1, :]
+    upper = grad_logits.astype(bfloat)
+    lower = (grad_logits - upper.astype(float32)).astype(bfloat)
+    normed = normed_ref[...]
+    router_out_ref[...] = dot_tn(upper, normed) + dot_tn(lower, normed)
+    grad_resid, terms = norm_back(mid, gain, grad_normed)
+    gain_out_ref[...] = jnp.sum(terms, axis=0, keepdims=True)
+    grad_mid = grads + grad_resid
+    grad_mid_ref[...] = grad_mid
+    grad_attn = grad_mid.astype(bfloat)
+    grad_attn_ref[...] = grad_attn
+    for step in range(members):
+        owner = jnp.where(me >= step, me - step, me - step + members)
+        rows = weight_ref[pl.ds(pl.multiple_of(owner * span, span), span), :]
+        part_refs[step][...] = dot_nt(grad_attn, rows).astype(bfloat)
+
+
+def second_back(
+    batch,
+    batches,
+    me,
+    returned,
+    back,
+    mid,
+    normed,
+    probs,
+    grads,
+    routes,
+    gain,
+    router,
+    weight,
+    members,
+    span,
+    layer,
+):
+    count, width = mid.shape
+    grad_spec = pl.BlockSpec((1, count, width), lambda i: (batch, 0, 0))
+
+    def full(array):
+        return pl.BlockSpec(array.shape, lambda i: (0,) * array.ndim)
+
+    def own(array):
+        return pl.BlockSpec((1,) + array.shape[1:], lambda i: (batch, 0, 0))
+
+    rest = [
+        jax.ShapeDtypeStruct((count, width), float32),
+        jax.ShapeDtypeStruct((count, width), bfloat),
+        jax.ShapeDtypeStruct((1, width), float32),
+        jax.ShapeDtypeStruct((tile, width), float32),
+    ] + [jax.ShapeDtypeStruct((count, span), bfloat)] * members
+    aliased = 0 if layer is None else 1
+    outs = pl.pallas_call(
+        functools.partial(second_kernel, members, members, aliased),
+        grid=(1,),
+        in_specs=[
+            pl.BlockSpec(memory_space=pltpu.SMEM),
+            own(back),
+            full(mid),
+            full(normed),
+            full(probs),
+            grad_spec,
+            own(routes),
+            full(gain),
+            full(router),
+            full(weight),
+        ]
+        + [full(part) for part in returned]
+        + [pl.BlockSpec(memory_space=pl.ANY)] * aliased,
+        out_specs=[grad_spec] + [full(shape) for shape in rest],
+        out_shape=[jax.ShapeDtypeStruct((batches, count, width), bfloat)] + rest,
+        input_output_aliases={10 + members: 0} if aliased else {},
+        compiler_params=params(),
+        cost_estimate=pl.CostEstimate(
+            flops=6 * count * width * width, bytes_accessed=12 * count * width, transcendentals=0
+        ),
+        name="second_back",
+    )(
+        me,
+        back,
+        mid,
+        normed,
+        probs,
+        grads,
+        routes,
+        gain,
+        router,
+        weight,
+        *returned,
+        *([] if layer is None else [layer]),
+    )
+    return outs[0], outs[1], outs[2], outs[3], outs[4], list(outs[5:])
+
+
+def first_kernel(
+    members, pairs, grads_ref, weight_ref, rows_ref, gain_ref, offset_ref, gain_out_ref, *out_refs
+):
+    width = rows_ref.shape[2]
+    depth = weight_ref.shape[1] // pairs
+    lanes = weight_ref.shape[2]
+    total = None
+    for pair in range(pairs):
+        weight = weight_ref[:, pair * depth : (pair + 1) * depth, :].reshape(width, lanes)
+        term = dot_nt(grads_ref[:, pair * lanes : (pair + 1) * lanes], weight)
+        total = term if total is None else total + term
+    rows = rows_ref[0].astype(float32)
+    scale = lax.rsqrt(jnp.mean(rows * rows, axis=-1, keepdims=True) + epsilon)
+    gain_out_ref[...] = jnp.sum(total * rows * scale, axis=0, keepdims=True)
+    for step in range(members):
+        out_refs[step][...] = member_rows(total, offset_ref, step, members).astype(
+            out_refs[step].dtype
+        )
+
+
+def first_back(batch, grads, packed, pairs, rows, gain, offsets):
+    members = offsets.shape[2]
+    _, count, width = rows.shape
+    lanes = packed.shape[2]
+    weight_shape = (packed.shape[0], pairs * width // packed.shape[0], lanes)
+    own = jax.ShapeDtypeStruct((count // members, width), float32)
+    sent = jax.ShapeDtypeStruct((count // members, width), bfloat)
+    out_shape = [jax.ShapeDtypeStruct((1, width), float32), own] + [sent] * (members - 1)
+
+    def full(array):
+        return pl.BlockSpec(array.shape, lambda i: (0,) * len(array.shape))
+
+    outs = pl.pallas_call(
+        functools.partial(first_kernel, members, pairs),
+        grid=(1,),
+        in_specs=[
+            full(grads),
+            pl.BlockSpec(weight_shape, lambda i: (0, 0, 0)),
+            pl.BlockSpec((1, count, width), lambda i: (batch, 0, 0)),
+            full(gain),
+            pl.BlockSpec((1,) + offsets.shape[1:], lambda i: (batch, 0, 0)),
+        ],
+        out_specs=[full(shape) for shape in out_shape],
+        out_shape=out_shape,
+        compiler_params=params(),
+        cost_estimate=pl.CostEstimate(
+            flops=2 * count * width * lanes * pairs,
+            bytes_accessed=8 * count * width,
+            transcendentals=0,
+        ),
+        name="first_back",
+    )(grads, packed, rows, gain, offsets)
+    return outs[0], outs[1], list(outs[2:])
+
+
+def finish_kernel(received, own_ref, rows_ref, gain_ref, mid_ref, *refs):
+    total = own_ref[...]
+    for ref in refs[:received]:
+        total = total + ref[...].astype(float32)
+    grad, _ = norm_back(rows_ref[0].astype(float32), gain_ref[...], total)
+    refs[-1][0] = mid_ref[...] + grad
+
+
+def finish(batch, own, received, rows, gain, mid, buffer):
+    batches, count, width = rows.shape
+    row_spec = pl.BlockSpec((1, count, width), lambda i: (batch, 0, 0))
+
+    def full(array):
+        return pl.BlockSpec(array.shape, lambda i: (0,) * array.ndim)
+
+    operands = [own, rows, gain, mid] + received
+    in_specs = [full(own), row_spec, full(gain), full(mid)] + [full(part) for part in received]
+    aliases = {}
+    if buffer is not None:
+        aliases = {len(operands): 0}
+        operands.append(buffer)
+        in_specs.append(pl.BlockSpec(memory_space=pl.ANY))
+    return pl.pallas_call(
+        functools.partial(finish_kernel, len(received)),
+        grid=(1,),
+        in_specs=in_specs,
+        out_specs=row_spec,
+        out_shape=jax.ShapeDtypeStruct((batches, count, width), float32),
+        input_output_aliases=aliases,
+        compiler_params=params(),
+        name="finish",
+    )(*operands)
+
+
+def dense_kernel(batches, *refs):
+    out_ref = refs[-1]
+    total = None
+    for batch in range(batches):
+        term = dot_tn(refs[batch][...], refs[batches + batch][...])
+        total = term if total is None else total + term
+    out_ref[...] = total.astype(bfloat).reshape(out_ref.shape)
+
+
+def dense_grad(left, right, lanes, shards, direct):
+    batches = len(left)
+    count, width = left[0].shape
+    blocks = right[0].shape[1] // lanes
+    depth = width // shards
+    if direct:
+        out_shape = (shards, blocks * depth, lanes)
+        out_spec = pl.BlockSpec((shards, depth, lanes), lambda i: (0, i, 0))
+    else:
+        out_shape = (blocks, width, lanes)
+        out_spec = pl.BlockSpec((1, width, lanes), lambda i: (i, 0, 0))
+    out = pl.pallas_call(
+        functools.partial(dense_kernel, batches),
+        grid=(blocks,),
+        in_specs=[pl.BlockSpec((count, width), lambda i: (0, 0))] * batches
+        + [pl.BlockSpec((count, lanes), lambda i: (0, i))] * batches,
+        out_specs=out_spec,
+        out_shape=jax.ShapeDtypeStruct(out_shape, bfloat),
+        compiler_params=params(),
+        cost_estimate=pl.CostEstimate(
+            flops=2 * batches * count * width * lanes * blocks,
+            bytes_accessed=2 * batches * count * width,
+            transcendentals=0,
+        ),
+        name="dense_grad",
+    )(*left, *right)
+    if not direct:
+        out = jnp.transpose(out.reshape(blocks, shards, depth, lanes), (1, 0, 2, 3))
+        out = out.reshape(shards, blocks * depth, lanes)
+    return out
 
 
 def segment_of(positions, ends):
@@ -147,7 +608,18 @@
 
 
 def attend_kernel(
-    stride, head_dim, far_ref, ends_ref, q_ref, k_ref, v_ref, bias_ref, probs_ref, out_ref, inv_ref
+    stride,
+    head_dim,
+    far_ref,
+    ends_ref,
+    q_ref,
+    k_ref,
+    v_ref,
+    bias_ref,
+    after_ref,
+    probs_ref,
+    out_ref,
+    inv_ref,
 ):
     pair = pl.program_id(0)
     rows_all = q_ref.shape[0]
@@ -212,8 +684,14 @@
             inv_ref[rows, :] = inverse
 
 
-def attend(queries, keys, values, ends, bias, far, head_dim, stride):
-    rows_all, span = queries.shape
+def kind_specs(rows_all):
+    return [
+        pl.BlockSpec((rows_all, tile), lambda i, kind=kind: (0, 3 * i + kind)) for kind in range(3)
+    ]
+
+
+def attend(qkv, ends, bias, far, after, head_dim, stride):
+    rows_all, span = qkv.shape[0], qkv.shape[1] // 3
     per = tile // head_dim
     heads = span // head_dim
     row_spec = pl.BlockSpec((rows_all, tile), lambda i: (0, i))
@@ -223,10 +701,9 @@
         in_specs=[
             pl.BlockSpec(memory_space=pltpu.SMEM),
             pl.BlockSpec(memory_space=pltpu.SMEM),
-            row_spec,
-            row_spec,
-            row_spec,
+            *kind_specs(rows_all),
             pl.BlockSpec((per,) + bias.shape[1:], lambda i: (i, 0, 0, 0)),
+            pl.BlockSpec(memory_space=pl.ANY),
         ],
         out_specs=[
             pl.BlockSpec((per, rows_all, rows_all), lambda i: (i, 0, 0)),
@@ -245,7 +722,7 @@
             transcendentals=heads * rows_all * rows_all,
         ),
         name="attend",
-    )(far, ends, queries, keys, values, bias)
+    )(far, ends, qkv, qkv, qkv, bias, after)
 
 
 def attend_back_kernel(
@@ -260,9 +737,7 @@
     k_ref,
     v_ref,
     after_ref,
-    dq_ref,
-    dk_ref,
-    dv_ref,
+    dqkv_ref,
     dbias_ref,
     dfar_ref,
     ds_ref,
@@ -311,21 +786,19 @@
                 ds_ref[sub, rows, :] = low_grads
                 stacked.append(low_grads)
             result = dot_nn(jnp.concatenate(stacked, axis=0), k_ref[...]) * scale
-            dq_ref[rows, :] = joined_heads(result, lane, per, head_dim).astype(bfloat)
+            dqkv_ref[rows, :tile] = joined_heads(result, lane, per, head_dim).astype(bfloat)
     dk_parts = []
     dv_parts = []
     for sub in range(per):
         dims = slice(sub * head_dim, (sub + 1) * head_dim)
         dk_parts.append(dot_nn(queries_t[dims, :], ds_ref[sub]))
         dv_parts.append(dot_nn(grads_t[dims, :], probs_ref[sub]))
-    dk_ref[...] = jnp.concatenate(dk_parts, axis=0).T.astype(bfloat)
-    dv_ref[...] = jnp.concatenate(dv_parts, axis=0).T.astype(bfloat)
-
-
-def attend_back(
-    probs, grads, outs, inverse, queries, keys, values, after, head_dim, stride, bias_shape
-):
-    rows_all, span = queries.shape
+    dqkv_ref[:, tile : 2 * tile] = jnp.concatenate(dk_parts, axis=0).T.astype(bfloat)
+    dqkv_ref[:, 2 * tile :] = jnp.concatenate(dv_parts, axis=0).T.astype(bfloat)
+
+
+def attend_back(probs, grads, outs, inverse, qkv, after, head_dim, stride, bias_shape):
+    rows_all, span = outs.shape
     per = tile // head_dim
     heads = span // head_dim
     row_spec = pl.BlockSpec((rows_all, tile), lambda i: (0, i))
@@ -333,17 +806,16 @@
         functools.partial(attend_back_kernel, stride, head_dim, head_dim ** (-0.5)),
         grid=(span // tile,),
         in_specs=[pl.BlockSpec((per, rows_all, rows_all), lambda i: (i, 0, 0))]
-        + [row_spec] * 6
+        + [row_spec] * 3
+        + kind_specs(rows_all)
         + [pl.BlockSpec(memory_space=pl.ANY)],
         out_specs=[
-            row_spec,
-            row_spec,
-            row_spec,
+            pl.BlockSpec((rows_all, 3 * tile), lambda i: (0, i)),
             pl.BlockSpec((per,) + bias_shape[1:], lambda i: (i, 0, 0, 0)),
             pl.BlockSpec((per, 2, tile, tile), lambda i: (i, 0, 0, 0)),
         ],
-        out_shape=[jax.ShapeDtypeStruct((rows_all, span), bfloat)] * 3
-        + [
+        out_shape=[
+            jax.ShapeDtypeStruct((rows_all, 3 * span), bfloat),
             jax.ShapeDtypeStruct(bias_shape, float32),
             jax.ShapeDtypeStruct((heads, 2, tile, tile), float32),
         ],
@@ -358,30 +830,36 @@
             transcendentals=0,
         ),
         name="attend_back",
-    )(probs, grads, outs, inverse, queries, keys, values, after)
-
-
-def add_kernel(left_ref, right_ref, after_ref, out_ref):
-    out_ref[...] = (left_ref[...].astype(float32) + right_ref[...].astype(float32)).astype(bfloat)
-
-
-def add_after(left, right, after):
+    )(probs, grads, outs, inverse, qkv, qkv, qkv, after)
+
+
+def add_kernel(after_ref, *refs):
+    out_ref = refs[-1]
+    start = 0
+    for left_ref, right_ref in zip(refs[:-1:2], refs[1:-1:2]):
+        rows = left_ref.shape[1]
+        out_ref[:, start : start + rows] = (
+            left_ref[...].astype(float32) + right_ref[...].astype(float32)
+        ).astype(bfloat)
+        start += rows
+
+
+def add_after(after, *operands):
+    vmem = pl.BlockSpec(memory_space=pltpu.VMEM)
+    outer, _, lanes = operands[0].shape
+    rows = sum(operand.shape[1] for operand in operands[::2])
     return pl.pallas_call(
         add_kernel,
-        in_specs=[
-            pl.BlockSpec(memory_space=pltpu.VMEM),
-            pl.BlockSpec(memory_space=pltpu.VMEM),
-            pl.BlockSpec(memory_space=pl.ANY),
-        ],
-        out_specs=pl.BlockSpec(memory_space=pltpu.VMEM),
-        out_shape=jax.ShapeDtypeStruct(left.shape, bfloat),
+        in_specs=[pl.BlockSpec(memory_space=pl.ANY)] + [vmem] * len(operands),
+        out_specs=vmem,
+        out_shape=jax.ShapeDtypeStruct((outer, rows, lanes), bfloat),
         compiler_params=params(),
         name="add_after",
-    )(left, right, after)
+    )(after, *operands)
 
 
 def order_kernel(count, place_ref, *refs):
-    out_ref = refs[count]
+    out_ref = refs[count + 1]
     for place in range(count):
         rows = refs[0][0]
         for step in range(1, count):
@@ -389,23 +867,32 @@
         out_ref[0, place] = rows
 
 
-def order_rows(parts, offsets):
+def order_rows(parts, offsets, carried):
     batches, rows, width = parts[0].shape
     count = len(parts)
     part_spec = pl.BlockSpec((1, rows, width), lambda i: (i, 0, 0))
     return pl.pallas_call(
         functools.partial(order_kernel, count),
         grid=(batches,),
-        in_specs=[pl.BlockSpec((1, rows, count), lambda i: (i, 0, 0))] + [part_spec] * count,
-        out_specs=pl.BlockSpec((1, count, rows, width), lambda i: (i, 0, 0, 0)),
-        out_shape=jax.ShapeDtypeStruct((batches, count, rows, width), bfloat),
+        in_specs=[pl.BlockSpec((1, rows, count), lambda i: (i, 0, 0))]
+        + [part_spec] * count
+        + [pl.BlockSpec(memory_space=pl.ANY)],
+        out_specs=[
+            pl.BlockSpec((1, count, rows, width), lambda i: (i, 0, 0, 0)),
+            pl.BlockSpec(memory_space=pl.ANY),
+        ],
+        out_shape=[
+            jax.ShapeDtypeStruct((batches, count, rows, width), bfloat),
+            jax.ShapeDtypeStruct(carried.shape, carried.dtype),
+        ],
+        input_output_aliases={count + 1: 1},
         compiler_params=params(),
         name="order_rows",
-    )(offsets, *parts)
+    )(offsets, *parts, carried)
 
 
 def expert_kernel(
-    count, slots, width, chunk, inner_ref, outer_ref, *refs
+    count, slots, width, chunk, inner_ref, outer_ref, after_ref, *refs
 ):
     blocks = refs[:count]
     results = refs[count : 2 * count]
@@ -455,7 +942,7 @@
             results[idx][:, width:] = back_ref[span, :].astype(bfloat)
 
 
-def run_expert(weights, blocks, width):
+def run_expert(weights, blocks, width, after):
     (inner, inner_spec), (outer, outer_spec), turns = weights
     count = len(blocks)
     slots = blocks[0].shape[0]
@@ -465,7 +952,7 @@
     outs = pl.pallas_call(
         functools.partial(expert_kernel, count, slots, width, 256),
         grid=(turns,),
-        in_specs=[inner_spec, outer_spec] + [whole] * count,
+        in_specs=[inner_spec, outer_spec, pl.BlockSpec(memory_space=pl.ANY)] + [whole] * count,
         out_specs=[whole] * count + [chunk, chunk],
         out_shape=[jax.ShapeDtypeStruct((slots, 2 * width), bfloat)] * count
         + [jax.ShapeDtypeStruct((total, turns * width), bfloat)] * 2,
@@ -482,7 +969,7 @@
             transcendentals=total * width * turns,
         ),
         name="run_expert",
-    )(inner, outer, *blocks)
+    )(inner, outer, after, *blocks)
     return outs[:count], outs[count], outs[count + 1]
 
 
@@ -586,7 +1073,10 @@
     per = tile // head_dim
     heads_own = per * (-(-heads // (per * members)))
     span = heads_own * head_dim
-    split = width // span
+    pairs = span // tile
+    lanes = 3 * tile
+    split = width // lanes
+    me_row = me.reshape(1)
 
     def around(step):
         return [(idx, (idx + step) % members) for idx in range(members)]
@@ -596,7 +1086,13 @@
         return lax.dynamic_slice_in_dim(wide, me * span, span, axis=1)
 
     def in_order(parts):
-        return jnp.take(jnp.stack(parts), jnp.mod(me - jnp.arange(members), members), axis=0)
+        if members == 2:
+            return [
+                jnp.where(me == 0, parts[0], parts[1]),
+                jnp.where(me == 0, parts[1], parts[0]),
+            ]
+        stacked = jnp.stack(parts)
+        return [stacked[jnp.mod(me - idx, members)] for idx in range(members)]
 
     hidden_from = [hidden_in] + [
         lax.ppermute(hidden_in, "expert", around(step)) for step in range(1, members)
@@ -611,52 +1107,60 @@
         ]
     )
     small_used = small.shape[0]
-    small_pad = -(-small_used // (16 * span)) * 16
-    small = jnp.pad(small, (0, small_pad * span - small_used)).reshape(small_pad, span)
+    small_pad = -(-small_used // (16 * lanes)) * 16
+    small = jnp.pad(small, (0, small_pad * lanes - small_used)).reshape(small_pad, lanes)
+    kinds = [columns_own(weight) for weight in (w_query, w_key, w_value)]
     first_own = jnp.concatenate(
-        [columns_own(w_query), columns_own(w_key), columns_own(w_value)]
-        + [w_output[:, idx * span : (idx + 1) * span] for idx in range(split)]
+        [
+            jnp.concatenate([kind[:, idx * tile : (idx + 1) * tile] for kind in kinds], axis=1)
+            for idx in range(pairs)
+        ]
+        + [w_output[:, idx * lanes : (idx + 1) * lanes] for idx in range(split)]
         + [small],
         axis=0,
     )
     first = lax.all_gather(first_own, "dp", axis=0, tiled=False)
     inner_parts = [w_in[0, :, idx * width : (idx + 1) * width] for idx in range(turns)]
     second_own = jnp.concatenate(inner_parts + [w_out[0]], axis=0)
-    second_own, _ = lax.optimization_barrier((second_own, first))
+    places_in = places[:, 0].reshape(batches, members, rows_own)
+    dispatch, collect, offsets, second_own = row_tables(
+        me_row, routes, places_in, hidden_from[-1], second_own, members, slots
+    )
     second = lax.all_gather(second_own, "dp", axis=0, tiled=False)
-
-    small_start = (3 + split) * depth
-    small_all = first[:, small_start:].reshape(shards, small_pad * span)
+    ends = jnp.cumsum(lengths[:, 0], axis=-1)[:, :-1]
+    ordered_in, first = order_rows(hidden_from, offsets, first)
+    ordered_in = ordered_in.reshape(batches, rows_group, width)
+
+    small_start = (pairs + split) * depth
+    small_all = first[:, small_start:].reshape(shards, small_pad * lanes)
     gain_one = small_all[:, :depth].reshape(1, width).astype(float32)
-    gain_two = small_all[:, depth : 2 * depth].reshape(width).astype(float32)
+    gain_two = small_all[:, depth : 2 * depth].reshape(1, width).astype(float32)
     router_end = 2 * depth + depth * experts
     router_w = small_all[:, 2 * depth : router_end].reshape(width, experts)
     table = small_all[:, router_end:small_used].reshape(shards * table_rows, heads)
+    router_wide = jnp.pad(router_w, ((0, 0), (0, tile - experts)))
+    router_t = router_w.astype(float32).T
     output_w = jnp.concatenate(
         [
-            first[:, (3 + idx) * depth : (4 + idx) * depth].reshape(width, span)
+            first[:, (pairs + idx) * depth : (pairs + idx + 1) * depth].reshape(width, lanes)
             for idx in range(split)
         ],
         axis=1,
     )
-    output_wide = jnp.pad(output_w, ((0, members * span - width), (0, 0)))
-    output_parts = [
-        lax.dynamic_slice_in_dim(output_wide, jnp.mod(me - step, members) * span, span, axis=0)
-        for step in range(members)
-    ]
+    output_w = jnp.pad(output_w, ((0, members * span - width), (0, 0)))
 
     direct = depth % 16 == 0 and turns * depth == depth_out and shards % turns == 0
     if direct:
         group = shards // turns
-        packed = first[:, : 3 * depth]
+        packed = first
         inner_spec = pl.BlockSpec((shards, depth, width), lambda i: (0, i, 0))
         outer_spec = pl.BlockSpec((group, depth_out, width), lambda i: (i, 1, 0))
         weights = ((second, inner_spec), (second, outer_spec), turns)
     else:
         packed = jnp.concatenate(
             [
-                first[:, idx * depth : (idx + 1) * depth].reshape(1, width, span)
-                for idx in range(3)
+                first[:, idx * depth : (idx + 1) * depth].reshape(1, width, lanes)
+                for idx in range(pairs)
             ],
             axis=1,
         )
@@ -667,118 +1171,92 @@
         )
         plain = pl.BlockSpec((1, width, width), lambda i: (i, 0, 0))
         weights = ((inner_w, plain), (outer_w, plain), turns)
-    query_w, key_w, value_w = (
-        first[:, idx * depth : (idx + 1) * depth].reshape(width, span) for idx in range(3)
-    )
-
-    places_in = places[:, 0].reshape(batches, members, rows_own)
-    offsets = places_in - members * jnp.arange(rows_own, dtype=jnp.int32)[None, None]
-    offset_from = [
-        jnp.take(offsets, jnp.mod(me - step, members), axis=1) for step in range(members)
-    ]
-    ends = jnp.cumsum(lengths[:, 0], axis=-1)[:, :-1]
-
-    def of_member(ordered, batch, step):
-        rows = ordered[:rows_own]
-        for place in range(1, members):
-            rows = jnp.where(
-                (offset_from[step][batch] == place)[:, None],
-                ordered[place * rows_own : (place + 1) * rows_own],
-                rows,
-            )
-        return rows
-
-    def by_place(parts, batch):
-        ordered = []
-        for place in range(members):
-            rows = parts[0]
-            for step in range(1, members):
-                rows = jnp.where((offset_from[step][batch] == place)[:, None], parts[step], rows)
-            ordered.append(rows)
-        return jnp.concatenate(ordered, axis=0)
-
-    chosen = routes[:, :, 0]
-    picked = chosen[:, :, None] == jnp.arange(experts, dtype=jnp.int32)
-    counts = picked.astype(jnp.int32)
-    slot = jnp.sum((jnp.cumsum(counts, axis=1) - counts) * counts, axis=2)
-    target = jnp.mod(chosen - me, members) * slots + slot
-    dispatch = (
-        jnp.arange(members * slots, dtype=jnp.int32)[None, :, None] == target[:, None, :]
-    ).astype(bfloat)
-
-    ordered_in = order_rows(hidden_from, jnp.stack(offset_from, axis=-1))
-    flat_in = ordered_in.reshape(batches * rows_group, width)
-    flat_normed, flat_q, flat_k, flat_v = project(flat_in, gain_one, packed, scale)
-    queries = flat_q.reshape(batches, rows_group, span)
-    keys = flat_k.reshape(batches, rows_group, span)
-    values = flat_v.reshape(batches, rows_group, span)
-    own_f = hidden_in.astype(float32)
+
     table_wide = jnp.pad(table, ((0, 0), (0, members * heads_own - heads)))
     table_own = lax.dynamic_slice_in_dim(table_wide, me * heads_own, heads_own, axis=1)
     bias = bias_tiles(table_own, members, tiles)
     table_f = table_own.astype(float32)
     far = jnp.stack([table_f[levels_all - 1], table_f[2 * levels_all - 1]])
 
+    def send_rows(batch, ordered):
+        arrived = []
+        for step in range(1, members):
+            rows = ordered[:rows_own]
+            for place in range(1, members):
+                rows = jnp.where(
+                    offsets[batch, :, members - step : members - step + 1] == place,
+                    ordered[place * rows_own : (place + 1) * rows_own],
+                    rows,
+                )
+            arrived.append(lax.ppermute(rows, "expert", around(step)))
+        return arrived
+
+    normed_one = []
+    qkv = []
     probs = []
     outs = []
     inverses = []
-    attended = []
+    arrived_heads = []
     resid_mid = []
     normed_two = []
-    gate_all = []
-    gate = []
+    router_probs = []
     blocks = []
+    after = table
     for batch in range(batches):
+        normed, packed_rows = project(batch, ordered_in, gain_one, packed, pairs, scale)
+        normed_one.append(normed)
+        qkv.append(packed_rows)
         kept, joined, inverse = attend(
-            queries[batch], keys[batch], values[batch], ends[batch], bias, far, head_dim, members
+            packed_rows, ends[batch], bias, far, after, head_dim, members
         )
         probs.append(kept)
         outs.append(joined)
         inverses.append(inverse)
-        head_parts = [of_member(joined, batch, 0)]
-        for step in range(1, members):
-            head_parts.append(
-                lax.ppermute(
-                    of_member(joined, batch, members - step), "expert", around(step)
-                )
-            )
-        attended.append(head_parts)
-        mid = own_f[batch]
-        for part, weight in zip(head_parts, output_parts):
-            mid = mid + dot_nn(part, weight)
-        normed = norm_rows(mid, gain_two).astype(bfloat)
-        logits = dot_nn(normed, router_w)
-        shifted = jnp.exp(logits - jnp.max(logits, axis=-1, keepdims=True))
-        router_probs = shifted / jnp.sum(shifted, axis=-1, keepdims=True)
-        gate_own = jnp.sum(jnp.where(picked[batch], router_probs, 0.0), axis=1, keepdims=True)
-        grad_expert = (gate_own * out_grad[batch].astype(float32)).astype(bfloat)
-        outgoing = dot_nn(
-            dispatch[batch], jnp.concatenate([normed, grad_expert], axis=1)
-        ).astype(bfloat)
-        received = [outgoing[:slots]]
-        for step in range(1, members):
-            received.append(
-                lax.ppermute(
-                    outgoing[step * slots : (step + 1) * slots], "expert", around(step)
-                )
-            )
+        heads_in = send_rows(batch, joined)
+        arrived_heads.append(heads_in)
+        mid, normed, chances, outgoing = middle(
+            batch,
+            me_row,
+            joined,
+            heads_in,
+            offsets,
+            output_w,
+            hidden_in,
+            out_grad,
+            gain_two,
+            router_wide,
+            routes,
+            dispatch,
+            blocks[-1][-1] if blocks else table,
+        )
+        after = outgoing[-1]
+        blocks.append(
+            [outgoing[0]]
+            + [
+                lax.ppermute(outgoing[step], "expert", around(step))
+                for step in range(1, members)
+            ]
+        )
         resid_mid.append(mid)
         normed_two.append(normed)
-        gate_all.append(router_probs)
-        gate.append(gate_own)
-        blocks.append(received)
+        router_probs.append(chances)
 
     returned = []
     hidden = []
     grad_pre = []
     for batch in range(batches):
-        results, hidden_rows, grad_rows = run_expert(weights, blocks[batch], width)
+        results, hidden_rows, grad_rows = run_expert(
+            weights, blocks[batch], width, hidden[-1] if hidden else table
+        )
         hidden.append(hidden_rows)
         grad_pre.append(grad_rows)
-        back = [results[0]]
-        for step in range(1, members):
-            back.append(lax.ppermute(results[step], "expert", around(-step)))
-        returned.append(jnp.concatenate(back, axis=0))
+        returned.append(
+            [results[0]]
+            + [
+                lax.ppermute(results[step], "expert", around(-step))
+                for step in range(1, members)
+            ]
+        )
 
     if direct:
         buffer_shape = (shards, turns * depth + depth_out, width)
@@ -813,91 +1291,112 @@
         )
     expert_sum = lax.psum_scatter(buffer, "dp", scatter_dimension=0, tiled=False)
 
-    layer_rows = []
-    grad_mid_rows = []
-    grad_attn_rows = []
-    grad_head_rows = []
+    line = shards // 4
+    my_shard = lax.axis_index("dp")
+
+    def by_core_and_y(dense):
+        dense = dense.reshape((line, 2, 2) + dense.shape[1:])
+        odd = my_shard % 2 == 1
+        sent = jnp.where(odd, dense[:, :, 0], dense[:, :, 1])
+        held = jnp.where(odd, dense[:, :, 1], dense[:, :, 0])
+        got = lax.ppermute(sent, "dp", [(idx, idx ^ 1) for idx in range(shards)])
+        dense = (held.astype(float32) + got.astype(float32)).astype(bfloat)
+        odd = (my_shard // 2) % 2 == 1
+        sent = jnp.where(odd, dense[:, 0], dense[:, 1])
+        held = jnp.where(odd, dense[:, 1], dense[:, 0])
+        return held, lax.ppermute(sent, "dp", [(idx, idx ^ 2) for idx in range(shards)])
+
+    layer = None
+    grad_mid = []
+    grad_attn = []
+    grad_heads = []
     grad_gain_two = 0.0
     grad_router = 0.0
-    router_f = router_w.astype(float32)
     for batch in range(batches):
-        home = dot_tn(dispatch[batch], returned[batch])
-        expert_back = home[:, :width]
-        grad_output = out_grad[batch].astype(float32)
-        layer_rows.append((resid_mid[batch] + gate[batch] * expert_back).astype(bfloat))
-        grad_gate = jnp.sum(grad_output * expert_back, axis=1, keepdims=True)
-        grad_logits = (grad_gate * gate[batch]) * (
-            jnp.where(picked[batch], 1.0, 0.0) - gate_all[batch]
-        )
-        grad_normed = home[:, width:] + lax.dot_general(
-            grad_logits, router_f, (((1,), (1,)), ((), ())), precision=precise
-        )
-        grad_router = grad_router + lax.dot_general(
-            normed_two[batch].astype(float32),
-            grad_logits,
-            (((0,), (0,)), ((), ())),
-            precision=precise,
-        )
-        grad_resid, gain_terms = norm_back(resid_mid[batch], gain_two, grad_normed)
-        grad_gain_two = grad_gain_two + jnp.sum(gain_terms, axis=0)
-        grad_mid = grad_output + grad_resid
-        grad_mid_rows.append(grad_mid)
-        grad_attn = grad_mid.astype(bfloat)
-        grad_attn_rows.append(grad_attn)
-        parts = [dot_nt(grad_attn, weight).astype(bfloat) for weight in output_parts]
-        from_members = [parts[0]]
-        for step in range(1, members):
-            from_members.append(lax.ppermute(parts[members - step], "expert", around(step)))
-        grad_head_rows.append(by_place(from_members, batch))
-
-    input_rows = []
-    grad_q_rows = []
-    grad_k_rows = []
-    grad_v_rows = []
+        layer, mid, attn, gain_terms, router_terms, parts = second_back(
+            batch,
+            batches,
+            me_row,
+            returned[batch],
+            collect,
+            resid_mid[batch],
+            normed_two[batch],
+            router_probs[batch],
+            out_grad,
+            routes,
+            gain_two,
+            router_t,
+            output_w,
+            members,
+            span,
+            layer,
+        )
+        grad_mid.append(mid)
+        grad_attn.append(attn)
+        grad_gain_two = grad_gain_two + gain_terms
+        grad_router = grad_router + router_terms[:experts]
+        from_members = [parts[0]] + [
+            lax.ppermute(parts[members - step], "expert", around(step))
+            for step in range(1, members)
+        ]
+        ordered = []
+        for place in range(members):
+            rows = from_members[0]
+            for step in range(1, members):
+                rows = jnp.where(
+                    offsets[batch, :, step : step + 1] == place, from_members[step], rows
+                )
+            ordered.append(rows)
+        grad_heads.append(jnp.concatenate(ordered, axis=0))
+
+    grad_qkv = []
     grad_gain_one = 0.0
     grad_bias = 0.0
     grad_far = 0.0
+    in_grad = None
     for batch in range(batches):
-        grad_q, grad_k, grad_v, bias_terms, far_terms = attend_back(
+        grads, bias_terms, far_terms = attend_back(
             probs[batch],
-            grad_head_rows[batch],
+            grad_heads[batch],
             outs[batch],
             inverses[batch],
-            queries[batch],
-            keys[batch],
-            values[batch],
+            qkv[batch],
             buffer,
             head_dim,
             members,
             bias.shape,
         )
-        grad_q_rows.append(grad_q)
-        grad_k_rows.append(grad_k)
-        grad_v_rows.append(grad_v)
+        grad_qkv.append(grads)
         grad_bias = grad_bias + bias_terms
         grad_far = grad_far + far_terms
-        grad_ordered = dot_nt(grad_q, query_w) + dot_nt(grad_k, key_w) + dot_nt(grad_v, value_w)
-        home_rows = of_member(grad_ordered, batch, 0)
-        for step in range(1, members):
-            sent = of_member(grad_ordered, batch, step).astype(bfloat)
-            home_rows = home_rows + lax.ppermute(sent, "expert", around(-step)).astype(float32)
-        grad_tokens, _ = norm_back(own_f[batch], gain_one, home_rows)
-        input_rows.append(grad_mid_rows[batch] + grad_tokens)
-        rows = slice(batch * rows_group, (batch + 1) * rows_group)
-        _, terms = norm_back(flat_in[rows].astype(float32), gain_one, grad_ordered)
-        grad_gain_one = grad_gain_one + jnp.sum(terms, axis=0)
-
-    def flat(rows):
-        return jnp.concatenate(rows, axis=0)
-
-    grad_out_parts = [
-        dot_tn(flat([parts[step] for parts in attended]), flat(grad_attn_rows)).astype(bfloat)
-        for step in range(members)
+        gain_terms, own_rows, sent = first_back(
+            batch, grads, packed, pairs, ordered_in, gain_one, offsets
+        )
+        grad_gain_one = grad_gain_one + gain_terms
+        received = [
+            lax.ppermute(rows, "expert", around(-step)) for step, rows in enumerate(sent, 1)
+        ]
+        in_grad = finish(
+            batch, own_rows, received, hidden_in, gain_one, grad_mid[batch], in_grad
+        )
+
+    def own_rows_of(batch):
+        joined = outs[batch]
+        rows = joined[:rows_own]
+        for place in range(1, members):
+            rows = jnp.where(
+                offsets[batch, :, 0:1] == place,
+                joined[place * rows_own : (place + 1) * rows_own],
+                rows,
+            )
+        return rows
+
+    attended = [
+        jnp.concatenate(in_order([own_rows_of(batch)] + arrived_heads[batch]), axis=1)[:, :width]
+        for batch in range(batches)
     ]
-    grad_wo = in_order(grad_out_parts).reshape(members * span, width)[:width]
-    grad_wq = dot_tn(flat_normed, flat(grad_q_rows))
-    grad_wk = dot_tn(flat_normed, flat(grad_k_rows))
-    grad_wv = dot_tn(flat_normed, flat(grad_v_rows))
+    early = by_core_and_y(dense_grad(attended, grad_attn, lanes, shards, direct))
+    grad_dense = dense_grad(normed_one, grad_qkv, lanes, shards, direct)
 
     steps = 2 * members - 1
     reach = near_shift(tiles)
@@ -930,42 +1429,16 @@
         [
             grad_gain_one.reshape(shards, depth),
             grad_gain_two.reshape(shards, depth),
-            grad_router.reshape(shards, depth * experts),
+            grad_router.T.reshape(shards, depth * experts),
             grad_table.reshape(shards, table_rows * heads),
         ],
         axis=1,
     )
-    small_grad = jnp.pad(small_grad, ((0, 0), (0, small_pad * span - small_used)))
-    dense = jnp.concatenate(
-        [
-            grad_wq.astype(bfloat).reshape(shards, depth, span),
-            grad_wk.astype(bfloat).reshape(shards, depth, span),
-            grad_wv.astype(bfloat).reshape(shards, depth, span),
-        ]
-        + [
-            grad_wo[:, idx * span : (idx + 1) * span].reshape(shards, depth, span)
-            for idx in range(split)
-        ]
-        + [small_grad.astype(bfloat).reshape(shards, small_pad, span)],
-        axis=1,
-    )
-
-    line = shards // 4
-    my_shard = lax.axis_index("dp")
-    rows_dense = dense.shape[1]
-    dense = dense.reshape(line, 2, 2, rows_dense, span)
-    odd = my_shard % 2 == 1
-    sent = jnp.where(odd, dense[:, :, 0], dense[:, :, 1])
-    held = jnp.where(odd, dense[:, :, 1], dense[:, :, 0])
-    got = lax.ppermute(sent, "dp", [(idx, idx ^ 1) for idx in range(shards)])
-    dense = (held.astype(float32) + got.astype(float32)).astype(bfloat)
-    odd = (my_shard // 2) % 2 == 1
-    sent = jnp.where(odd, dense[:, 0], dense[:, 1])
-    held = jnp.where(odd, dense[:, 1], dense[:, 0])
-    got = lax.ppermute(sent, "dp", [(idx, idx ^ 2) for idx in range(shards)])
-    dense = add_after(held, got, expert_sum)
+    small_grad = jnp.pad(small_grad, ((0, 0), (0, small_pad * lanes - small_used)))
+    small_grad = small_grad.astype(bfloat).reshape(shards, small_pad, lanes)
+    late = by_core_and_y(jnp.concatenate([grad_dense, small_grad], axis=1))
     dense_part = lax.psum_scatter(
-        dense,
+        add_after(expert_sum, *late, *early),
         "dp",
         scatter_dimension=0,
         tiled=False,
@@ -974,18 +1447,29 @@
     parts = [dense_part] + [
         lax.ppermute(dense_part, "expert", around(step)) for step in range(1, members)
     ]
-    qkv_parts = in_order([part[: 3 * depth] for part in parts]).astype(float32)
+    qkv_parts = [
+        part.astype(float32) for part in in_order([part[: pairs * depth] for part in parts])
+    ]
     qkv_grads = [
         jnp.concatenate(
-            [qkv_parts[idx, kind * depth : (kind + 1) * depth] for idx in range(members)], axis=1
+            [
+                part[pair * depth : (pair + 1) * depth, kind * tile : (kind + 1) * tile]
+                for part in qkv_parts
+                for pair in range(pairs)
+            ],
+            axis=1,
         )[:, :width]
         for kind in range(3)
     ]
-    rest_sum = sum(part[3 * depth :].astype(float32) for part in parts)
+    rest_sum = sum(part[pairs * depth :].astype(float32) for part in parts)
     out_grad_sum = jnp.concatenate(
-        [rest_sum[idx * depth : (idx + 1) * depth] for idx in range(split)], axis=1
+        [
+            rest_sum[small_pad + idx * depth : small_pad + (idx + 1) * depth]
+            for idx in range(split)
+        ],
+        axis=1,
     )
-    small_sum = rest_sum[split * depth :].reshape(-1)
+    small_sum = rest_sum[:small_pad].reshape(-1)
 
     expert_f = expert_sum.astype(float32)
     inner_sum = jnp.concatenate(
@@ -993,8 +1477,8 @@
     )[None]
     outer_sum = expert_f[turns * depth :][None]
     return (
-        jnp.stack(layer_rows),
-        jnp.stack(input_rows),
+        layer,
+        in_grad,
         small_sum[:depth],
         qkv_grads[0],
         qkv_grads[1],

time: 480 us -> 426 us (0.89)
  Pallas kernels: 149 us -> 219 us
  matrix products: 53.1 us -> 3.55 us
  other arithmetic: 61.1 us -> 30.6 us
  waiting for transfers between devices: 126 us -> 102 us
  local copies, waits for them, and re-layouts: 52.6 us -> 33.7 us
    pallas_call x2 -> x14, Pallas kernels: 11 us -> 83.8 us  [the longest x2 15.6 us: second_back(): pl.pallas_call(functools.partial(second_kernel, members, members, aliased...]
    dot_general x29 -> x0, matrix products: 49.6 us -> none  [the longest x7 18.2 us: dot_tn(): lax.dot_general(left, right, (((0,), (0,)), ((), ())), preferred_element_...]
    all_gather x1, waiting for transfers between devices: 43.4 us -> 2.1 us  [on_device(): first = lax.all_gather(first_own, 'dp', axis=0, tiled=False)]
    reduce_scatter x1, waiting for transfers between devices: 15.3 us -> 0.01 us  [on_device(): lax.psum_scatter(add_after(expert_sum, *late, *early), 'dp', scatter_dime...]
    ppermute x10 -> x12, waiting for transfers between devices: 43.9 us -> 58.1 us  [the longest x2 20.8 us: on_device(): lax.ppermute(results[step], 'expert', around(-step))]
    another operation x13 -> x2, other arithmetic: 14.1 us -> 1.4 us  [the longest x3 7.75 us: on_device(): jnp.stack(input_rows)]
    convert_element_type x11 -> x4, other arithmetic: 13.2 us -> 2.97 us  [the longest x2 2.86 us: by_core_and_y(): dense = (held.astype(float32) + got.astype(float32)).astype(bfloat)]
    ppermute x1, waiting for transfers between devices: 21.1 us -> 31 us  [on_device(): lax.ppermute(hidden_in, 'expert', around(step))]
  transfers between devices with their start and end apart: 18 -> 20, of which waited for: 8 -> 12; matrix products, arithmetic and copies ran while one was open for 30% -> 11% of each run, Pallas kernels for 31% -> 42%
where the time goes in v3:
time: 426 us; the launch traced here: 422 us
  Pallas kernels  219 us (51%)
  waiting for transfers between devices  102 us (24%)
  local copies, waits for them, and re-layouts  33.7 us (8%)
  other arithmetic  30.6 us (7%)
  starting transfers between devices  18.1 us (4%)
  between operations  14.9 us (3%)
    pallas_call x2, Pallas kernels, run_expert(): pl.pallas_call(functools.partial(expert_kernel, count, slots, width, 256)...  35.6 us
    pallas_call x2, Pallas kernels, attend(): pl.pallas_call(functools.partial(attend_kernel, stride, head_dim), grid=(...  35.2 us
    pallas_call x2, Pallas kernels, attend_back(): pl.pallas_call(functools.partial(attend_back_kernel, stride, head_dim, he...  32.5 us
    ppermute x1, waiting for transfers between devices, on_device(): lax.ppermute(hidden_in, 'expert', around(step))  31 us
    pallas_call x2, Pallas kernels, expert_grad(): pl.pallas_call(body, grid=(turns,), in_specs=in_specs, out_specs=out_spec...  23.7 us
    ppermute x2, waiting for transfers between devices, on_device(): lax.ppermute(results[step], 'expert', around(-step))  20.8 us
    unnamed x88, local copies, waits for them, and re-layouts  16.4 us
    pallas_call x2, Pallas kernels, second_back(): pl.pallas_call(functools.partial(second_kernel, members, members, aliased...  15.6 us
  transfers between devices with their start and end apart: 20, of which 12 were waited for; matrix products, arithmetic and copies ran while one was open for 11% of the time, Pallas kernels for 42%

profile of v3, /device:TPU:0, one launch (start us, length us, event | category | flops | bytes accessed | tf_op | source)
XLA Modules:
  0.0 421.8 jit_solution(6747409298640888365)
XLA Ops:
  20.2 31.0 %collective-permute-done.after_ref.refs_1_ = bf16[2,512,768]{2,1,0:T(8,128)(2,1)S(1)} collective-permute-done((bf16[2,512,768]{2,1,0:T(8,128)(2,1)}, bf16[2,512,768]{2,1,0:T(8,128)(2,1)S(1)}, u32[]{:S(2)}, u32[]{:S(2)}) %collective-permute-start) | collective-permute-done | bytes 1572896 | tf_op jit(solution)/shard_map/ppermute | solution.py:1098
  67.9 5.0 %bias_tiles.1.bias_ref = f32[6,3,128,384]{3,2,1,0:T(8,128)} custom-call(f32[6,128]{1,0:T(8,128)} %pad.22.clone.table_ref), custom_call_target="tpu_custom_call" | custom-call | tf_op jit(solution)/shard_map/bias_tiles/pallas_call | solution.py:79
  73.5 5.8 %project.3 = (bf16[1024,768]{1,0:T(8,128)(2,1)}, bf16[1024,1152]{1,0:T(8,128)(2,1)}) custom-call(bf16[2,1024,768]{2,1,0:T(8,128)(2,1)} %bitcast.78, f32[1,768]{1,0:T(1,128)} %reshape.326.gain_ref, bf16[16,256,384]{2,1,0:T(8,128)(2,1)} %get-tuple-element.98.weight_ref), custom_call_target="tpu_custom_call" | custom-call | flops 1811939328 | bytes 4718592 | tf_op jit(solution)/shard_map/project/pallas_call | solution.py:108
  79.4 17.7 %attend.2 = (bf16[6,1024,1024]{2,1,0:T(8,128)(2,1)}, bf16[1024,384]{1,0:T(8,128)(2,1)}, f32[1024,384]{1,0:T(8,128)}) custom-call(f32[2,6]{1,0:T(2,128)} %pad_maximum_fusion.7.far_ref, s32[1]{0:T(128)} %bitcast.13.ends_ref, bf16[1024,1152]{1,0:T(8,128)(2,1)} %get-tuple-element.101.q_ref.k_ref.v_ref, bf16[1024,1152]{1,0:T(8,128)(2,1)} %get-tuple-element.101.q_ref.k_ref.v_ref, ...), custom_call_target="tpu_custom_call" | custom-call | flops 6442450944 | bytes 12582912 | tf_op jit(solution)/shard_map/attend/pallas_call | solution.py:698
  104.1 6.0 %project.2 = (bf16[1024,768]{1,0:T(8,128)(2,1)}, bf16[1024,1152]{1,0:T(8,128)(2,1)}) custom-call(bf16[2,1024,768]{2,1,0:T(8,128)(2,1)} %bitcast.79, f32[1,768]{1,0:T(1,128)} %reshape.326.gain_ref, bf16[16,256,384]{2,1,0:T(8,128)(2,1)} %get-tuple-element.98.weight_ref), custom_call_target="tpu_custom_call" | custom-call | flops 1811939328 | bytes 4718592 | tf_op jit(solution)/shard_map/project/pallas_call | solution.py:108
  110.9 6.2 %middle.2 = (f32[512,768]{1,0:T(8,128)}, bf16[512,768]{1,0:T(8,128)(2,1)}, f32[512,128]{1,0:T(8,128)}, bf16[272,1536]{1,0:T(8,128)(2,1)}, bf16[272,1536]{1,0:T(8,128)(2,1)}) custom-call(s32[1]{0:T(128)} %bitcast.me_ref, bf16[1024,384]{1,0:T(8,128)(2,1)} %get-tuple-element.102.joined_ref.out_ref, s32[2,512,2]{2,1,0:T(8,128)} %get-tuple-element.97.place_ref.offset_ref, ...), custom_call_target="tpu_custom_call" | custom-call | flops 1811939328 | bytes 4718592 | tf_op jit(solution)/shard_map/middle/pallas_call | solution.py:297
  118.1 17.6 %attend.3 = (bf16[6,1024,1024]{2,1,0:T(8,128)(2,1)}, bf16[1024,384]{1,0:T(8,128)(2,1)}, f32[1024,384]{1,0:T(8,128)}) custom-call(f32[2,6]{1,0:T(2,128)} %pad_maximum_fusion.7.far_ref, s32[1]{0:T(128)} %bitcast.10.ends_ref, bf16[1024,1152]{1,0:T(8,128)(2,1)} %get-tuple-element.100.q_ref.k_ref.v_ref, bf16[1024,1152]{1,0:T(8,128)(2,1)} %get-tuple-element.100.q_ref.k_ref.v_ref, ...), custom_call_target="tpu_custom_call" | custom-call | flops 6442450944 | bytes 12582912 | tf_op jit(solution)/shard_map/attend/pallas_call | solution.py:698
  138.1 9.3 %collective-permute-done.3.refs_0_ = bf16[512,384]{1,0:T(8,128)(2,1)S(1)} collective-permute-done((bf16[512,384]{1,0:T(8,128)(2,1)S(1)}, bf16[512,384]{1,0:T(8,128)(2,1)S(1)}, u32[]{:S(2)}, u32[]{:S(2)}) %collective-permute-start.3) | collective-permute-done | bytes 393248 | tf_op jit(solution)/shard_map/ppermute | solution.py:1191
  149.0 6.2 %middle.3 = (f32[512,768]{1,0:T(8,128)}, bf16[512,768]{1,0:T(8,128)(2,1)}, f32[512,128]{1,0:T(8,128)}, bf16[272,1536]{1,0:T(8,128)(2,1)}, bf16[272,1536]{1,0:T(8,128)(2,1)}) custom-call(s32[1]{0:T(128)} %bitcast.me_ref, bf16[1024,384]{1,0:T(8,128)(2,1)} %get-tuple-element.105.joined_ref.out_ref, s32[2,512,2]{2,1,0:T(8,128)} %get-tuple-element.97.place_ref.offset_ref, ...), custom_call_target="tpu_custom_call" | custom-call | flops 1811939328 | bytes 4718592 | tf_op jit(solution)/shard_map/middle/pallas_call | solution.py:297
  156.9 18.0 %run_expert.2 = (bf16[272,1536]{1,0:T(8,128)(2,1)}, bf16[272,1536]{1,0:T(8,128)(2,1)}, bf16[544,3072]{1,0:T(8,128)(2,1)}, bf16[544,3072]{1,0:T(8,128)(2,1)}) custom-call(bf16[16,384,768]{2,1,0:T(8,128)(2,1)} %bitcast.99, bf16[16,384,768]{2,1,0:T(8,128)(2,1)} %bitcast.100, bf16[32,12]{1,0:T(8,128)(2,1)} %copy-done.26, ...), custom_call_target="tpu_custom_call" | custom-call | flops 10267656192 | bytes 9437184 | tf_op jit(solution)/shard_map/run_expert/pallas_call | solution.py:952
  175.8 17.6 %run_expert.3 = (bf16[272,1536]{1,0:T(8,128)(2,1)}, bf16[272,1536]{1,0:T(8,128)(2,1)}, bf16[544,3072]{1,0:T(8,128)(2,1)}, bf16[544,3072]{1,0:T(8,128)(2,1)}) custom-call(bf16[16,384,768]{2,1,0:T(8,128)(2,1)} %bitcast.101, bf16[16,384,768]{2,1,0:T(8,128)(2,1)} %bitcast.102, bf16[544,3072]{1,0:T(8,128)(2,1)} %get-tuple-element.111.after_ref.refs_5_, ...), custom_call_target="tpu_custom_call" | custom-call | flops 10267656192 | bytes 9437184 | tf_op jit(solution)/shard_map/run_expert/pallas_call | solution.py:952
  193.4 11.9 %expert_grad_inner.1.refs_0_ = bf16[16,384,768]{2,1,0:T(8,128)(2,1)} custom-call(bf16[272,1536]{1,0:T(8,128)(2,1)} %get-tuple-element.110.refs_0_.refs_1_, bf16[272,1536]{1,0:T(8,128)(2,1)} %copy-done, bf16[272,1536]{1,0:T(8,128)(2,1)} %get-tuple-element.112.refs_0_.refs_2_.refs_3_, bf16[272,1536]{1,0:T(8,128)(2,1)} %copy-done.5, ...), custom_call_target="tpu_custom_call" | custom-call | flops 5133828096 | bytes 9437184 | tf_op jit(solution)/shard_map/expert_grad_inner/pallas_call | solution.py:1021
  205.3 11.9 %expert_grad_outer.1.after_ref = bf16[16,384,768]{2,1,0:T(8,128)(2,1)} custom-call(bf16[16,384,768]{2,1,0:T(8,128)(2,1)} %expert_grad_inner.1.refs_0_, bf16[272,1536]{1,0:T(8,128)(2,1)} %get-tuple-element.110.refs_0_.refs_1_, bf16[272,1536]{1,0:T(8,128)(2,1)} %copy-done, ...), custom_call_target="tpu_custom_call", output_to_operand_aliasing={{}: (0, {})} | custom-call | flops 5133828096 | bytes 9437184 | tf_op jit(solution)/shard_map/expert_grad_outer/pallas_call | solution.py:1021
  225.3 13.9 %collective-permute-done.6.refs_1_ = bf16[272,1536]{1,0:T(8,128)(2,1)S(1)} collective-permute-done((bf16[272,1536]{1,0:T(8,128)(2,1)}, bf16[272,1536]{1,0:T(8,128)(2,1)S(1)}, u32[]{:S(2)}, u32[]{:S(2)}) %collective-permute-start.6) | collective-permute-done | bytes 835616 | tf_op jit(solution)/shard_map/ppermute | solution.py:1256
  240.1 7.8 %second_back.2 = (bf16[2,512,768]{2,1,0:T(8,128)(2,1)}, f32[512,768]{1,0:T(8,128)}, bf16[512,768]{1,0:T(8,128)(2,1)}, f32[1,768]{1,0:T(1,128)}, f32[128,768]{1,0...) custom-call(s32[1]{0:T(128)} %bitcast.me_ref, bf16[2,512,544]{2,1,0:T(8,128)(2,1)} %get-tuple-element.96.back_ref, ...), custom_call_target="tpu_custom_call" | custom-call | flops 1811939328 | bytes 4718592 | tf_op jit(solution)/shard_map/second_back/pallas_call | solution.py:415
  247.9 6.9 %collective-permute-done.5.refs_1_ = bf16[272,1536]{1,0:T(8,128)(2,1)S(1)} collective-permute-done((bf16[272,1536]{1,0:T(8,128)(2,1)}, bf16[272,1536]{1,0:T(8,128)(2,1)S(1)}, u32[]{:S(2)}, u32[]{:S(2)}) %collective-permute-start.5) | collective-permute-done | bytes 835616 | tf_op jit(solution)/shard_map/ppermute | solution.py:1256
  255.7 7.9 %second_back.3 = (bf16[2,512,768]{2,1,0:T(8,128)(2,1)}, f32[512,768]{1,0:T(8,128)}, bf16[512,768]{1,0:T(8,128)(2,1)}, f32[1,768]{1,0:T(1,128)}, f32[128,768]{1,0...) custom-call(s32[1]{0:T(128)} %bitcast.me_ref, ...), custom_call_target="tpu_custom_call", output_to_operand_aliasing={{0}: (12, {})} | custom-call | flops 1811939328 | bytes 4718592 | tf_op jit(solution)/shard_map/second_back/pallas_call | solution.py:415
  282.3 16.0 %attend_back.2 = (bf16[1024,1152]{1,0:T(8,128)(2,1)}, f32[6,3,128,384]{3,2,1,0:T(8,128)}, f32[6,2,128,128]{3,2,1,0:T(8,128)}) custom-call(bf16[6,1024,1024]{2,1,0:T(8,128)(2,1)} %get-tuple-element.123.probs_ref, bf16[1024,384]{1,0:T(8,128)(2,1)} %pad_maximum_fusion.2.grad_ref, bf16[1024,384]{1,0:T(8,128)(2,1)} %get-tuple-element.105.joined_ref.out_ref, ...), custom_call_target="tpu_custom_call" | custom-call | flops 12884901888 | bytes 12582912 | tf_op jit(solution)/shard_map/attend_back/pallas_call | solution.py:805
  298.3 16.4 %attend_back.3 = (bf16[1024,1152]{1,0:T(8,128)(2,1)}, f32[6,3,128,384]{3,2,1,0:T(8,128)}, f32[6,2,128,128]{3,2,1,0:T(8,128)}) custom-call(bf16[6,1024,1024]{2,1,0:T(8,128)(2,1)} %get-tuple-element.134.probs_ref, bf16[1024,384]{1,0:T(8,128)(2,1)} %pad_maximum_fusion.3.grad_ref, bf16[1024,384]{1,0:T(8,128)(2,1)} %get-tuple-element.102.joined_ref.out_ref, ...), custom_call_target="tpu_custom_call" | custom-call | flops 12884901888 | bytes 12582912 | tf_op jit(solution)/shard_map/attend_back/pallas_call | solution.py:805
  322.9 7.3 %first_back.2 = (f32[1,768]{1,0:T(1,128)}, f32[512,768]{1,0:T(8,128)}, bf16[512,768]{1,0:T(8,128)(2,1)}) custom-call(bf16[1024,1152]{1,0:T(8,128)(2,1)} %get-tuple-element.130.grads_ref.refs_3_, bf16[16,256,384]{2,1,0:T(8,128)(2,1)} %get-tuple-element.98.weight_ref, bf16[2,1024,768]{2,1,0:T(8,128)(2,1)} %bitcast.80, f32[1,768]{1,0:T(1,128)} %reshape.326.gain_ref, ...), custom_call_target="tpu_custom_call" | custom-call | flops 1811939328 | bytes 6291456 | tf_op jit(solution)/shard_map/first_back/pallas_call | solution.py:489
  330.2 7.3 %first_back.3 = (f32[1,768]{1,0:T(1,128)}, f32[512,768]{1,0:T(8,128)}, bf16[512,768]{1,0:T(8,128)(2,1)}) custom-call(bf16[1024,1152]{1,0:T(8,128)(2,1)} %get-tuple-element.138.grads_ref.refs_2_, bf16[16,256,384]{2,1,0:T(8,128)(2,1)} %get-tuple-element.98.weight_ref, bf16[2,1024,768]{2,1,0:T(8,128)(2,1)} %bitcast.81, f32[1,768]{1,0:T(1,128)} %reshape.326.gain_ref, ...), custom_call_target="tpu_custom_call" | custom-call | flops 1811939328 | bytes 6291456 | tf_op jit(solution)/shard_map/first_back/pallas_call | solution.py:489
  338.4 9.0 %dense_grad.2 = bf16[16,144,384]{2,1,0:T(8,128)(2,1)} custom-call(bf16[1024,768]{1,0:T(8,128)(2,1)} %get-tuple-element.142.refs_0_, bf16[1024,768]{1,0:T(8,128)(2,1)} %get-tuple-element.143.refs_1_, bf16[1024,1152]{1,0:T(8,128)(2,1)} %get-tuple-element.138.grads_ref.refs_2_, bf16[1024,1152]{1,0:T(8,128)(2,1)} %get-tuple-element.130.grads_ref.refs_3_), custom_call_target="tpu_custom_call" | custom-call | flops 3623878656 | bytes 3145728 | tf_op jit(solution)/shard_map/dense_grad/pallas_call | solution.py:566
  362.5 14.8 %collective-permute-done.14.refs_3_ = bf16[4,96,384]{2,1,0:T(8,128)(2,1)S(1)} collective-permute-done((bf16[4,96,384]{2,1,0:T(8,128)(2,1)S(1)}, bf16[4,96,384]{2,1,0:T(8,128)(2,1)S(1)}, u32[]{:S(2)}, u32[]{:S(2)}) %collective-permute-start.14) | collective-permute-done | bytes 294944 | tf_op jit(solution)/shard_map/ppermute | solution.py:1307
  386.3 10.3 %collective-permute-done.8.refs_0_ = bf16[512,768]{1,0:T(8,128)(2,1)S(1)} collective-permute-done((bf16[512,768]{1,0:T(8,128)(2,1)S(1)}, bf16[512,768]{1,0:T(8,128)(2,1)S(1)}, u32[]{:S(2)}, u32[]{:S(2)}) %collective-permute-start.8) | collective-permute-done | bytes 786464 | tf_op jit(solution)/shard_map/ppermute | solution.py:1377
  (220 shorter events, 125.2 us)
Async XLA Ops:
  7.2 13.0 %copy-start.23 = (bf16[1,192,768]{2,1,0:T(8,128)(2,1)S(1)}, bf16[1,192,768]{2,1,0:T(8,128)(2,1)}, u32[]{:S(2)}) copy-start(bf16[1,192,768]{2,1,0:T(8,128)(2,1)} %param.33) | copy-start | bytes 884740
  7.2 54.6 %all-gather.5.cloned.1.call-start = ((), (), s32[]{:S(2)}) async-start(), calls=%async_computation.4 | async-start | bytes 3342336 | tf_op jit(solution)/shard_map/all_gather | solution.py:1122
  13.6 143.3 %all-gather.7.cloned.1.call-start = ((), (), s32[]{:S(2)}) async-start(), calls=%async_computation.5 | async-start | bytes 10027008 | tf_op jit(solution)/shard_map/all_gather | solution.py:1129
  13.6 37.6 %collective-permute-start = (bf16[2,512,768]{2,1,0:T(8,128)(2,1)}, bf16[2,512,768]{2,1,0:T(8,128)(2,1)S(1)}, u32[]{:S(2)}, u32[]{:S(2)}) collective-permute-start(bf16[2,512,768]{2,1,0:T(8,128)(2,1)} %rows_ref.7), channel_id=1, source_target_pairs={{0,1},{1,0},{2,3},{3,2},{4,5},{5,4},{6,7},{7,6},{8,9},{9,8},{10,11... | collective-permute-start | bytes 4718600 | tf_op jit(solution)/shard_map/ppermute | solution.py:1098
  20.2 31.0 %copy-start.6 = (bf16[384,768]{1,0:T(8,128)(2,1)}, bf16[384,768]{1,0:T(8,128)(2,1)S(1)}, u32[]{:S(2)}) copy-start(bf16[384,768]{1,0:T(8,128)(2,1)S(1)} %bitcast_dynamic-update-slice_fusion.carried_ref) | copy-start | bytes 1769476
  56.9 320.4 %reduce-scatter.3.cloned.1.call-start = ((), (), s32[]{:S(2)}) async-start(), calls=%async_computation.2 | async-start | bytes 10027008 | tf_op jit(solution)/shard_map/reduce_scatter | solution.py:1292
  98.3 11.9 %collective-permute-start.1 = (bf16[512,384]{1,0:T(8,128)(2,1)S(1)}, bf16[512,384]{1,0:T(8,128)(2,1)S(1)}, u32[]{:S(2)}, u32[]{:S(2)}) collective-permute-start(bf16[512,384]{1,0:T(8,128)(2,1)S(1)} %broadcast_select_fusion.7), channel_id=1, source_target_pairs={{0,1},{1,0},{2,3},{3,2},{4,5},{5,4},{6,7},{7,6},{8,9},{9,8},{10,11... | collective-permute-start | bytes 1179656 | tf_op jit(solution)/shard_map/ppermute | solution.py:1191
  117.1 30.2 %collective-permute-start.2 = (bf16[272,1536]{1,0:T(8,128)(2,1)}, bf16[272,1536]{1,0:T(8,128)(2,1)S(1)}, u32[]{:S(2)}, u32[]{:S(2)}) collective-permute-start(bf16[272,1536]{1,0:T(8,128)(2,1)} %get-tuple-element.104.after_ref), channel_id=1, source_target_pairs={{0,1},{1,0},{2,3},{3,2},{4,5},{5,4},{6,7},{7,6},{8,9},{9,8},{10,11... | collective-permute-start | bytes 2506760 | tf_op jit(solution)/shard_map/ppermute | solution.py:1236
  136.9 10.4 %collective-permute-start.3 = (bf16[512,384]{1,0:T(8,128)(2,1)S(1)}, bf16[512,384]{1,0:T(8,128)(2,1)S(1)}, u32[]{:S(2)}, u32[]{:S(2)}) collective-permute-start(bf16[512,384]{1,0:T(8,128)(2,1)S(1)} %broadcast_select_fusion.5), channel_id=1, source_target_pairs={{0,1},{1,0},{2,3},{3,2},{4,5},{5,4},{6,7},{7,6},{8,9},{9,8},{10,11... | collective-permute-start | bytes 1179656 | tf_op jit(solution)/shard_map/ppermute | solution.py:1191
  155.2 19.6 %collective-permute-start.4 = (bf16[272,1536]{1,0:T(8,128)(2,1)}, bf16[272,1536]{1,0:T(8,128)(2,1)S(1)}, u32[]{:S(2)}, u32[]{:S(2)}) collective-permute-start(bf16[272,1536]{1,0:T(8,128)(2,1)} %get-tuple-element.113), channel_id=1, source_target_pairs={{0,1},{1,0},{2,3},{3,2},{4,5},{5,4},{6,7},{7,6},{8,9},{9,8},{10,11... | collective-permute-start | bytes 2506760 | tf_op jit(solution)/shard_map/ppermute | solution.py:1236
  217.2 185.6 %reduce-scatter.5.cloned.1.call-start = ((), (), s32[]{:S(2)}) async-start(), calls=%async_computation.3 | async-start | bytes 983040 | tf_op jit(solution)/shard_map/reduce_scatter | solution.py:1440
  217.4 21.8 %collective-permute-start.6 = (bf16[272,1536]{1,0:T(8,128)(2,1)}, bf16[272,1536]{1,0:T(8,128)(2,1)S(1)}, u32[]{:S(2)}, u32[]{:S(2)}) collective-permute-start(bf16[272,1536]{1,0:T(8,128)(2,1)} %get-tuple-element.120), channel_id=1, source_target_pairs={{0,1},{1,0},{2,3},{3,2},{4,5},{5,4},{6,7},{7,6},{8,9},{9,8},{10,11... | collective-permute-start | bytes 2506760 | tf_op jit(solution)/shard_map/ppermute | solution.py:1256
  222.2 32.6 %collective-permute-start.5 = (bf16[272,1536]{1,0:T(8,128)(2,1)}, bf16[272,1536]{1,0:T(8,128)(2,1)S(1)}, u32[]{:S(2)}, u32[]{:S(2)}) collective-permute-start(bf16[272,1536]{1,0:T(8,128)(2,1)} %get-tuple-element.115), channel_id=1, source_target_pairs={{0,1},{1,0},{2,3},{3,2},{4,5},{5,4},{6,7},{7,6},{8,9},{9,8},{10,11... | collective-permute-start | bytes 2506760 | tf_op jit(solution)/shard_map/ppermute | solution.py:1256
  263.6 12.3 %collective-permute-start.7 = (bf16[512,384]{1,0:T(8,128)(2,1)}, bf16[512,384]{1,0:T(8,128)(2,1)S(1)}, u32[]{:S(2)}, u32[]{:S(2)}) collective-permute-start(bf16[512,384]{1,0:T(8,128)(2,1)} %get-tuple-element.124), channel_id=1, source_target_pairs={{0,1},{1,0},{2,3},{3,2},{4,5},{5,4},{6,7},{7,6},{8,9},{9,8},{10,11... | collective-permute-start | bytes 1179656 | tf_op jit(solution)/shard_map/ppermute | solution.py:1339
  264.6 16.5 %collective-permute-start.9 = (bf16[512,384]{1,0:T(8,128)(2,1)S(1)}, bf16[512,384]{1,0:T(8,128)(2,1)S(1)}, u32[]{:S(2)}, u32[]{:S(2)}) collective-permute-start(bf16[512,384]{1,0:T(8,128)(2,1)S(1)} %copy-done.34), channel_id=1, source_target_pairs={{0,1},{1,0},{2,3},{3,2},{4,5},{5,4},{6,7},{7,6},{8,9},{9,8},{10,11... | collective-permute-start | bytes 1179656 | tf_op jit(solution)/shard_map/ppermute | solution.py:1339
  298.3 16.5 %copy-start.16 = (f32[6,2,128,128]{3,2,1,0:T(8,128)S(1)}, f32[6,2,128,128]{3,2,1,0:T(8,128)}, u32[]{:S(2)}) copy-start(f32[6,2,128,128]{3,2,1,0:T(8,128)} %get-tuple-element.153) | copy-start | bytes 2359300
  298.3 17.8 %copy-start.4 = (f32[6,3,128,384]{3,2,1,0:T(8,128)S(1)}, f32[6,3,128,384]{3,2,1,0:T(8,128)}, u32[]{:S(2)}) copy-start(f32[6,3,128,384]{3,2,1,0:T(8,128)} %get-tuple-element.151) | copy-start | bytes 10616836
  350.2 5.0 %collective-permute-start.11 = (bf16[4,2,160,384]{3,2,0,1:T(8,128)(2,1)}, bf16[4,2,160,384]{3,2,0,1:T(8,128)(2,1)}, u32[]{:S(2)}, u32[]{:S(2)}) collective-permute-start(bf16[4,2,160,384]{3,2,0,1:T(8,128)(2,1)} %select_bitcast_fusion), channel_id=1, source_target_pairs={{0,2},{2,0},{4,6},{6,4},{8,10},{10,8},{12,14},{14,12},{16,18},{18,... | collective-permute-start | bytes 2949128 | tf_op jit(solution)/shard_map/ppermute | solution.py:1302
  351.1 2.9 collective-permute-start.13
  357.7 19.6 %collective-permute-start.12 = (bf16[4,160,384]{2,1,0:T(8,128)(2,1)S(1)}, bf16[4,160,384]{2,1,0:T(8,128)(2,1)S(1)}, u32[]{:S(2)}, u32[]{:S(2)}) collective-permute-start(bf16[4,160,384]{2,1,0:T(8,128)(2,1)S(1)} %get-tuple-element.224), channel_id=1, source_target_pairs={{0,4},{2,6},{4,0},{6,2},{8,12},{10,14},{12,8},{14,10},{16,20},{18,... | collective-permute-start | bytes 1474568 | tf_op jit(solution)/shard_map/ppermute | solution.py:1307
  358.5 18.8 %collective-permute-start.14 = (bf16[4,96,384]{2,1,0:T(8,128)(2,1)S(1)}, bf16[4,96,384]{2,1,0:T(8,128)(2,1)S(1)}, u32[]{:S(2)}, u32[]{:S(2)}) collective-permute-start(bf16[4,96,384]{2,1,0:T(8,128)(2,1)S(1)} %get-tuple-element.230), channel_id=1, source_target_pairs={{0,4},{2,6},{4,0},{6,2},{8,12},{10,14},{12,8},{14,10},{16,20},{18,... | collective-permute-start | bytes 884744 | tf_op jit(solution)/shard_map/ppermute | solution.py:1307
  360.5 20.7 %collective-permute-start.10 = (bf16[512,768]{1,0:T(8,128)(2,1)}, bf16[512,768]{1,0:T(8,128)(2,1)S(1)}, u32[]{:S(2)}, u32[]{:S(2)}) collective-permute-start(bf16[512,768]{1,0:T(8,128)(2,1)} %get-tuple-element.141), channel_id=1, source_target_pairs={{0,1},{1,0},{2,3},{3,2},{4,5},{5,4},{6,7},{7,6},{8,9},{9,8},{10,11... | collective-permute-start | bytes 2359304 | tf_op jit(solution)/shard_map/ppermute | solution.py:1377
  361.2 35.4 %collective-permute-start.8 = (bf16[512,768]{1,0:T(8,128)(2,1)S(1)}, bf16[512,768]{1,0:T(8,128)(2,1)S(1)}, u32[]{:S(2)}, u32[]{:S(2)}) collective-permute-start(bf16[512,768]{1,0:T(8,128)(2,1)S(1)} %copy-done.33), channel_id=1, source_target_pairs={{0,1},{1,0},{2,3},{3,2},{4,5},{5,4},{6,7},{7,6},{8,9},{9,8},{10,11... | collective-permute-start | bytes 2359304 | tf_op jit(solution)/shard_map/ppermute | solution.py:1377
  402.7 5.9 %collective-permute-start.15 = (bf16[256,384]{1,0:T(8,128)(2,1)}, bf16[256,384]{1,0:T(8,128)(2,1)S(1)}, u32[]{:S(2)}, u32[]{:S(2)}) collective-permute-start(bf16[256,384]{1,0:T(8,128)(2,1)} %bitcast.94), channel_id=1, source_target_pairs={{0,1},{1,0},{2,3},{3,2},{4,5},{5,4},{6,7},{7,6},{8,9},{9,8},{10,11... | collective-permute-start | bytes 589832 | tf_op jit(solution)/shard_map/ppermute | solution.py:1448
  (31 other events, 108.5 us)
Sparse Core Ops, SparseCore 0:
  13.7 48.1 all-gather.4
  64.7 80.2 all-gather.6
  217.3 110.1 reduce-scatter.2
  380.8 21.0 reduce-scatter.4

commit v4 on v3

--- a/solution.py
+++ b/solution.py
@@ -336,6 +336,7 @@
     gain_ref,
     router_ref,
     weight_ref,
+    after_ref,
     *refs,
 ):
     returned = refs[:members]
@@ -394,6 +395,7 @@
     weight,
     members,
     span,
+    after,
     layer,
 ):
     count, width = mid.shape
@@ -426,12 +428,13 @@
             full(gain),
             full(router),
             full(weight),
+            pl.BlockSpec(memory_space=pl.ANY),
         ]
         + [full(part) for part in returned]
         + [pl.BlockSpec(memory_space=pl.ANY)] * aliased,
         out_specs=[grad_spec] + [full(shape) for shape in rest],
         out_shape=[jax.ShapeDtypeStruct((batches, count, width), bfloat)] + rest,
-        input_output_aliases={10 + members: 0} if aliased else {},
+        input_output_aliases={11 + members: 0} if aliased else {},
         compiler_params=params(),
         cost_estimate=pl.CostEstimate(
             flops=6 * count * width * width, bytes_accessed=12 * count * width, transcendentals=0
@@ -448,6 +451,7 @@
         gain,
         router,
         weight,
+        after,
         *returned,
         *([] if layer is None else [layer]),
     )
@@ -455,9 +459,15 @@
 
 
 def first_kernel(
-    members, pairs, grads_ref, weight_ref, rows_ref, gain_ref, offset_ref, gain_out_ref, *out_refs
+    members,
+    pairs,
+    grads_ref,
+    weight_ref,
+    offset_ref,
+    after_ref,
+    *out_refs,
 ):
-    width = rows_ref.shape[2]
+    width = out_refs[0].shape[1]
     depth = weight_ref.shape[1] // pairs
     lanes = weight_ref.shape[2]
     total = None
@@ -465,23 +475,20 @@
         weight = weight_ref[:, pair * depth : (pair + 1) * depth, :].reshape(width, lanes)
         term = dot_nt(grads_ref[:, pair * lanes : (pair + 1) * lanes], weight)
         total = term if total is None else total + term
-    rows = rows_ref[0].astype(float32)
-    scale = lax.rsqrt(jnp.mean(rows * rows, axis=-1, keepdims=True) + epsilon)
-    gain_out_ref[...] = jnp.sum(total * rows * scale, axis=0, keepdims=True)
     for step in range(members):
         out_refs[step][...] = member_rows(total, offset_ref, step, members).astype(
             out_refs[step].dtype
         )
 
 
-def first_back(batch, grads, packed, pairs, rows, gain, offsets):
+def first_back(batch, grads, packed, pairs, width, offsets, after):
     members = offsets.shape[2]
-    _, count, width = rows.shape
+    count = grads.shape[0]
     lanes = packed.shape[2]
     weight_shape = (packed.shape[0], pairs * width // packed.shape[0], lanes)
     own = jax.ShapeDtypeStruct((count // members, width), float32)
     sent = jax.ShapeDtypeStruct((count // members, width), bfloat)
-    out_shape = [jax.ShapeDtypeStruct((1, width), float32), own] + [sent] * (members - 1)
+    out_shape = [own] + [sent] * (members - 1)
 
     def full(array):
         return pl.BlockSpec(array.shape, lambda i: (0,) * len(array.shape))
@@ -492,9 +499,8 @@
         in_specs=[
             full(grads),
             pl.BlockSpec(weight_shape, lambda i: (0, 0, 0)),
-            pl.BlockSpec((1, count, width), lambda i: (batch, 0, 0)),
-            full(gain),
             pl.BlockSpec((1,) + offsets.shape[1:], lambda i: (batch, 0, 0)),
+            pl.BlockSpec(memory_space=pl.ANY),
         ],
         out_specs=[full(shape) for shape in out_shape],
         out_shape=out_shape,
@@ -505,8 +511,8 @@
             transcendentals=0,
         ),
         name="first_back",
-    )(grads, packed, rows, gain, offsets)
-    return outs[0], outs[1], list(outs[2:])
+    )(grads, packed, offsets, after)
+    return outs[0], list(outs[1:])
 
 
 def finish_kernel(received, own_ref, rows_ref, gain_ref, mid_ref, *refs):
@@ -543,16 +549,28 @@
     )(*operands)
 
 
-def dense_kernel(batches, *refs):
-    out_ref = refs[-1]
+def dense_kernel(batches, weighted, after_ref, *refs):
+    out_ref = refs[2 * batches + weighted]
     total = None
     for batch in range(batches):
         term = dot_tn(refs[batch][...], refs[batches + batch][...])
         total = term if total is None else total + term
     out_ref[...] = total.astype(bfloat).reshape(out_ref.shape)
-
-
-def dense_grad(left, right, lanes, shards, direct):
+    if weighted:
+        sum_ref = refs[-1]
+        weight = refs[2 * batches][...].reshape(total.shape).astype(float32)
+        term = jnp.sum(total * weight, axis=1, keepdims=True)
+
+        @pl.when(pl.program_id(0) == 0)
+        def _():
+            sum_ref[...] = term
+
+        @pl.when(pl.program_id(0) > 0)
+        def _():
+            sum_ref[...] += term
+
+
+def dense_grad(left, right, lanes, shards, direct, after, packed=None):
     batches = len(left)
     count, width = left[0].shape
     blocks = right[0].shape[1] // lanes
@@ -563,13 +581,21 @@
     else:
         out_shape = (blocks, width, lanes)
         out_spec = pl.BlockSpec((1, width, lanes), lambda i: (i, 0, 0))
-    out = pl.pallas_call(
-        functools.partial(dense_kernel, batches),
+    weighted = 0 if packed is None else 1
+    outs = pl.pallas_call(
+        functools.partial(dense_kernel, batches, weighted),
         grid=(blocks,),
-        in_specs=[pl.BlockSpec((count, width), lambda i: (0, 0))] * batches
-        + [pl.BlockSpec((count, lanes), lambda i: (0, i))] * batches,
-        out_specs=out_spec,
-        out_shape=jax.ShapeDtypeStruct(out_shape, bfloat),
+        in_specs=[pl.BlockSpec(memory_space=pl.ANY)]
+        + [pl.BlockSpec((count, width), lambda i: (0, 0))] * batches
+        + [pl.BlockSpec((count, lanes), lambda i: (0, i))] * batches
+        + (
+            [pl.BlockSpec((packed.shape[0], width // packed.shape[0], lanes), lambda i: (0, i, 0))]
+            if weighted
+            else []
+        ),
+        out_specs=[out_spec] + [pl.BlockSpec((width, 1), lambda i: (0, 0))] * weighted,
+        out_shape=[jax.ShapeDtypeStruct(out_shape, bfloat)]
+        + [jax.ShapeDtypeStruct((width, 1), float32)] * weighted,
         compiler_params=params(),
         cost_estimate=pl.CostEstimate(
             flops=2 * batches * count * width * lanes * blocks,
@@ -577,11 +603,12 @@
             transcendentals=0,
         ),
         name="dense_grad",
-    )(*left, *right)
+    )(after, *left, *right, *([packed] if weighted else []))
+    out = outs[0]
     if not direct:
         out = jnp.transpose(out.reshape(blocks, shards, depth, lanes), (1, 0, 2, 3))
         out = out.reshape(shards, blocks * depth, lanes)
-    return out
+    return (out, outs[1]) if weighted else out
 
 
 def segment_of(positions, ends):
@@ -729,20 +756,19 @@
     stride,
     head_dim,
     scale,
+    carried,
     probs_ref,
-    grad_ref,
     out_ref,
     inv_ref,
     q_ref,
     k_ref,
     v_ref,
+    offset_ref,
     after_ref,
-    dqkv_ref,
-    dbias_ref,
-    dfar_ref,
-    ds_ref,
-    grads_ref,
+    *refs,
 ):
+    grad_refs = refs[:stride]
+    dqkv_ref, dbias_ref, dfar_ref, ds_ref, grads_ref = refs[-5:]
     rows_all = q_ref.shape[0]
     rows_part = rows_all // stride
     tiles = rows_part // tile
@@ -751,10 +777,19 @@
     lane = lax.broadcasted_iota(jnp.int32, (tile, tile), 1)
     queries_t = q_ref[...].T
     values_t = v_ref[...].T
-    grads_ref[...] = (grad_ref[...].astype(float32) * inv_ref[...]).astype(bfloat)
+    for place in range(stride):
+        span = slice(place * rows_part, (place + 1) * rows_part)
+        rows = grad_refs[0][...]
+        for step in range(1, stride):
+            rows = jnp.where(offset_ref[0, :, step : step + 1] == place, grad_refs[step][...], rows)
+        grads_ref[span, :] = (rows.astype(float32) * inv_ref[span, :]).astype(bfloat)
     grads_t = grads_ref[...].T
-    dbias_ref[...] = jnp.zeros_like(dbias_ref)
-    dfar_ref[...] = jnp.zeros_like(dfar_ref)
+    if carried:
+        dbias_ref[...] = refs[stride][...]
+        dfar_ref[...] = refs[stride + 1][...]
+    else:
+        dbias_ref[...] = jnp.zeros_like(dbias_ref)
+        dfar_ref[...] = jnp.zeros_like(dfar_ref)
     for mine in range(stride):
         for block in range(tiles):
             begin = mine * rows_part + block * tile
@@ -797,23 +832,31 @@
     dqkv_ref[:, 2 * tile :] = jnp.concatenate(dv_parts, axis=0).T.astype(bfloat)
 
 
-def attend_back(probs, grads, outs, inverse, qkv, after, head_dim, stride, bias_shape):
+def attend_back(
+    batch, probs, grads, outs, inverse, qkv, offsets, after, sums, head_dim, stride, bias_shape
+):
     rows_all, span = outs.shape
     per = tile // head_dim
     heads = span // head_dim
     row_spec = pl.BlockSpec((rows_all, tile), lambda i: (0, i))
+    part_spec = pl.BlockSpec((rows_all // stride, tile), lambda i: (0, i))
+    sum_specs = [
+        pl.BlockSpec((per,) + bias_shape[1:], lambda i: (i, 0, 0, 0)),
+        pl.BlockSpec((per, 2, tile, tile), lambda i: (i, 0, 0, 0)),
+    ]
+    carried = len(sums) > 0
+    first = 8 + stride
     return pl.pallas_call(
-        functools.partial(attend_back_kernel, stride, head_dim, head_dim ** (-0.5)),
+        functools.partial(attend_back_kernel, stride, head_dim, head_dim ** (-0.5), carried),
         grid=(span // tile,),
         in_specs=[pl.BlockSpec((per, rows_all, rows_all), lambda i: (i, 0, 0))]
-        + [row_spec] * 3
+        + [row_spec] * 2
         + kind_specs(rows_all)
-        + [pl.BlockSpec(memory_space=pl.ANY)],
-        out_specs=[
-            pl.BlockSpec((rows_all, 3 * tile), lambda i: (0, i)),
-            pl.BlockSpec((per,) + bias_shape[1:], lambda i: (i, 0, 0, 0)),
-            pl.BlockSpec((per, 2, tile, tile), lambda i: (i, 0, 0, 0)),
-        ],
+        + [pl.BlockSpec((1,) + offsets.shape[1:], lambda i: (batch, 0, 0))]
+        + [pl.BlockSpec(memory_space=pl.ANY)]
+        + [part_spec] * stride
+        + (sum_specs if carried else []),
+        out_specs=[pl.BlockSpec((rows_all, 3 * tile), lambda i: (0, i))] + sum_specs,
         out_shape=[
             jax.ShapeDtypeStruct((rows_all, 3 * span), bfloat),
             jax.ShapeDtypeStruct(bias_shape, float32),
@@ -823,6 +866,7 @@
             pltpu.VMEM((per, rows_all, rows_all), bfloat),
             pltpu.VMEM((rows_all, tile), bfloat),
         ],
+        input_output_aliases={first: 1, first + 1: 2} if carried else {},
         compiler_params=params(),
         cost_estimate=pl.CostEstimate(
             flops=32 * rows_all * rows_all * span,
@@ -830,7 +874,7 @@
             transcendentals=0,
         ),
         name="attend_back",
-    )(probs, grads, outs, inverse, qkv, qkv, qkv, after)
+    )(probs, outs, inverse, qkv, qkv, qkv, offsets, after, *grads, *sums)
 
 
 def add_kernel(after_ref, *refs):
@@ -998,7 +1042,7 @@
     out_ref[...] = total.astype(bfloat).reshape(out_ref.shape)
 
 
-def expert_grad(groups, wide, width, second, out_shape, out_spec, buffer=None):
+def expert_grad(groups, wide, width, second, out_shape, out_spec, after, buffer=None):
     batches = len(groups)
     count = len(groups[0])
     slots = groups[0][0].shape[0]
@@ -1009,14 +1053,16 @@
     in_specs = in_specs + [pl.BlockSpec((total, width), lambda i: (0, i))] * batches
     operands = [block for group in groups for block in group] + list(wide)
     aliases = {}
-    body = kernel
+    carried = [after]
     if buffer is not None:
-        in_specs = [pl.BlockSpec(memory_space=pl.ANY)] + in_specs
-        operands = [buffer] + operands
+        carried = [buffer, after]
         aliases = {0: 0}
-
-        def body(*refs):
-            kernel(*refs[1:])
+    skipped = len(carried)
+    in_specs = [pl.BlockSpec(memory_space=pl.ANY)] * skipped + in_specs
+    operands = carried + operands
+
+    def body(*refs):
+        kernel(*refs[skipped:])
 
     return pl.pallas_call(
         body,
@@ -1267,6 +1313,7 @@
             False,
             buffer_shape,
             pl.BlockSpec((shards, depth, width), lambda i: (0, i, 0)),
+            returned[0][-1],
         )
         buffer = expert_grad(
             blocks,
@@ -1275,12 +1322,17 @@
             True,
             buffer_shape,
             pl.BlockSpec((group, depth_out, width), lambda i: (i, 1, 0)),
+            returned[0][-1],
             buffer,
         )
     else:
         plain_shape = (turns, width, width)
-        inner_g = expert_grad(blocks, grad_pre, width, False, plain_shape, plain)
-        outer_g = expert_grad(blocks, hidden, width, True, plain_shape, plain)
+        inner_g = expert_grad(
+            blocks, grad_pre, width, False, plain_shape, plain, returned[0][-1]
+        )
+        outer_g = expert_grad(
+            blocks, hidden, width, True, plain_shape, plain, returned[0][-1]
+        )
         inner_g = jnp.transpose(inner_g.reshape(turns, shards, depth, width), (1, 0, 2, 3))
         buffer = jnp.concatenate(
             [
@@ -1294,17 +1346,23 @@
     line = shards // 4
     my_shard = lax.axis_index("dp")
 
-    def by_core_and_y(dense):
+    def by_core(dense):
         dense = dense.reshape((line, 2, 2) + dense.shape[1:])
         odd = my_shard % 2 == 1
         sent = jnp.where(odd, dense[:, :, 0], dense[:, :, 1])
         held = jnp.where(odd, dense[:, :, 1], dense[:, :, 0])
-        got = lax.ppermute(sent, "dp", [(idx, idx ^ 1) for idx in range(shards)])
-        dense = (held.astype(float32) + got.astype(float32)).astype(bfloat)
+        return held, lax.ppermute(sent, "dp", [(idx, idx ^ 1) for idx in range(shards)])
+
+    def by_y(core_parts):
+        held, got = core_parts
         odd = (my_shard // 2) % 2 == 1
-        sent = jnp.where(odd, dense[:, 0], dense[:, 1])
-        held = jnp.where(odd, dense[:, 1], dense[:, 0])
-        return held, lax.ppermute(sent, "dp", [(idx, idx ^ 2) for idx in range(shards)])
+
+        def half(idx):
+            return held[:, idx].astype(float32) + got[:, idx].astype(float32)
+
+        sent = jnp.where(odd, half(0), half(1)).astype(bfloat)
+        kept = jnp.where(odd, half(1), half(0)).astype(bfloat)
+        return kept, lax.ppermute(sent, "dp", [(idx, idx ^ 2) for idx in range(shards)])
 
     layer = None
     grad_mid = []
@@ -1329,6 +1387,7 @@
             output_w,
             members,
             span,
+            returned[-1][-1] if batch == 0 else buffer,
             layer,
         )
         grad_mid.append(mid)
@@ -1339,46 +1398,7 @@
             lax.ppermute(parts[members - step], "expert", around(step))
             for step in range(1, members)
         ]
-        ordered = []
-        for place in range(members):
-            rows = from_members[0]
-            for step in range(1, members):
-                rows = jnp.where(
-                    offsets[batch, :, step : step + 1] == place, from_members[step], rows
-                )
-            ordered.append(rows)
-        grad_heads.append(jnp.concatenate(ordered, axis=0))
-
-    grad_qkv = []
-    grad_gain_one = 0.0
-    grad_bias = 0.0
-    grad_far = 0.0
-    in_grad = None
-    for batch in range(batches):
-        grads, bias_terms, far_terms = attend_back(
-            probs[batch],
-            grad_heads[batch],
-            outs[batch],
-            inverses[batch],
-            qkv[batch],
-            buffer,
-            head_dim,
-            members,
-            bias.shape,
-        )
-        grad_qkv.append(grads)
-        grad_bias = grad_bias + bias_terms
-        grad_far = grad_far + far_terms
-        gain_terms, own_rows, sent = first_back(
-            batch, grads, packed, pairs, ordered_in, gain_one, offsets
-        )
-        grad_gain_one = grad_gain_one + gain_terms
-        received = [
-            lax.ppermute(rows, "expert", around(-step)) for step, rows in enumerate(sent, 1)
-        ]
-        in_grad = finish(
-            batch, own_rows, received, hidden_in, gain_one, grad_mid[batch], in_grad
-        )
+        grad_heads.append(from_members)
 
     def own_rows_of(batch):
         joined = outs[batch]
@@ -1395,8 +1415,53 @@
         jnp.concatenate(in_order([own_rows_of(batch)] + arrived_heads[batch]), axis=1)[:, :width]
         for batch in range(batches)
     ]
-    early = by_core_and_y(dense_grad(attended, grad_attn, lanes, shards, direct))
-    grad_dense = dense_grad(normed_one, grad_qkv, lanes, shards, direct)
+    early_core = by_core(
+        dense_grad(attended, grad_attn, lanes, shards, direct, grad_heads[0][-1])
+    )
+    early = by_y(early_core)
+    grad_qkv = []
+    sums = []
+    for batch in range(batches):
+        grads, *sums = attend_back(
+            batch,
+            probs[batch],
+            grad_heads[batch],
+            outs[batch],
+            inverses[batch],
+            qkv[batch],
+            offsets,
+            buffer if batch == 0 else early_core[1],
+            sums,
+            head_dim,
+            members,
+            bias.shape,
+        )
+        grad_qkv.append(grads)
+    grad_bias, grad_far = sums
+    grad_dense, weighted = dense_grad(
+        normed_one, grad_qkv, lanes, shards, direct, early[1], packed
+    )
+    grad_gain_one = weighted[:, 0] / gain_one[0]
+    late_core = by_core(grad_dense)
+    late = by_y(late_core)
+
+    in_grad = None
+    for batch in range(batches):
+        own_rows, sent = first_back(
+            batch,
+            grad_qkv[batch],
+            packed,
+            pairs,
+            width,
+            offsets,
+            late_core[1] if batch == 0 else late[1],
+        )
+        received = [
+            lax.ppermute(rows, "expert", around(-step)) for step, rows in enumerate(sent, 1)
+        ]
+        in_grad = finish(
+            batch, own_rows, received, hidden_in, gain_one, grad_mid[batch], in_grad
+        )
 
     steps = 2 * members - 1
     reach = near_shift(tiles)
@@ -1436,9 +1501,9 @@
     )
     small_grad = jnp.pad(small_grad, ((0, 0), (0, small_pad * lanes - small_used)))
     small_grad = small_grad.astype(bfloat).reshape(shards, small_pad, lanes)
-    late = by_core_and_y(jnp.concatenate([grad_dense, small_grad], axis=1))
+    little = by_y(by_core(small_grad))
     dense_part = lax.psum_scatter(
-        add_after(expert_sum, *late, *early),
+        add_after(expert_sum, *late, *little, *early),
         "dp",
         scatter_dimension=0,
         tiled=False,

time: 426 us -> 403 us (0.946)
  waiting for transfers between devices: 102 us -> 76.2 us
  other arithmetic: 30.6 us -> 21.8 us
  local copies, waits for them, and re-layouts: 33.7 us -> 39.5 us
    ppermute x4 -> x6, waiting for transfers between devices: 17.1 us -> 4.56 us  [the longest x3 3.75 us: by_y(): lax.ppermute(sent, 'dp', [(idx, idx ^ 2) for idx in range(shards)])]
    ppermute x2, waiting for transfers between devices: 20.8 us -> 12.7 us  [on_device(): lax.ppermute(results[step], 'expert', around(-step))]
    ppermute x2, waiting for transfers between devices: 6.1 us -> 0.01 us  [on_device(): lax.ppermute(parts[members - step], 'expert', around(step))]
    unnamed x88 -> x84, local copies, waits for them, and re-layouts: 16.4 us -> 18.5 us
  transfers between devices with their start and end apart: 20 -> 22, of which waited for: 12 -> 11; matrix products, arithmetic and copies ran while one was open for 11% -> 10% of each run, Pallas kernels for 42% -> 50%
where the time goes in v4:
time: 403 us; the launch traced here: 399 us
  Pallas kernels  222 us (55%)
  waiting for transfers between devices  76.2 us (19%)
  local copies, waits for them, and re-layouts  39.5 us (10%)
  starting transfers between devices  21.9 us (5%)
  other arithmetic  21.8 us (5%)
  between operations  14.8 us (4%)
    pallas_call x2, Pallas kernels, run_expert(): pl.pallas_call(functools.partial(expert_kernel, count, slots, width, 256)...  35.5 us
    pallas_call x2, Pallas kernels, attend(): pl.pallas_call(functools.partial(attend_kernel, stride, head_dim), grid=(...  35.3 us
    pallas_call x2, Pallas kernels, attend_back(): pl.pallas_call(functools.partial(attend_back_kernel, stride, head_dim, he...  35.1 us
    ppermute x1, waiting for transfers between devices, on_device(): lax.ppermute(hidden_in, 'expert', around(step))  31 us
    pallas_call x2, Pallas kernels, expert_grad(): pl.pallas_call(body, grid=(turns,), in_specs=in_specs, out_specs=out_spec...  23.7 us
    unnamed x84, local copies, waits for them, and re-layouts  18.5 us
    pallas_call x2, Pallas kernels, second_back(): pl.pallas_call(functools.partial(second_kernel, members, members, aliased...  16.7 us
    pallas_call x2, Pallas kernels, dense_grad(): pl.pallas_call(functools.partial(dense_kernel, batches, weighted), grid=(...  14.5 us
  transfers between devices with their start and end apart: 22, of which 11 were waited for; matrix products, arithmetic and copies ran while one was open for 10% of the time, Pallas kernels for 50%

profile of v4, /device:TPU:0, one launch (start us, length us, event | category | flops | bytes accessed | tf_op | source)
XLA Modules:
  0.0 399.3 jit_solution(4537595443970965313)
XLA Ops:
  20.2 31.0 %collective-permute-done.after_ref.refs_1_ = bf16[2,512,768]{2,1,0:T(8,128)(2,1)S(1)} collective-permute-done((bf16[2,512,768]{2,1,0:T(8,128)(2,1)}, bf16[2,512,768]{2,1,0:T(8,128)(2,1)S(1)}, u32[]{:S(2)}, u32[]{:S(2)}) %collective-permute-start) | collective-permute-done | bytes 1572896 | tf_op jit(solution)/shard_map/ppermute | solution.py:1144
  52.4 4.5 %row_tables.1 = (bf16[2,544,512]{2,1,0:T(8,128)(2,1)}, bf16[2,512,544]{2,1,0:T(8,128)(2,1)}, s32[2,512,2]{2,1,0:T(8,128)}, bf16[384,768]{1,0:T(8,128)(2,1)}) custom-call(s32[1]{0:T(128)} %bitcast.me_ref, s32[2,1,512]{2,1,0:T(1,128)} %bitcast.100, s32[2,512,1]{2,1,0:T(8,128)} %copy.119.column_ref.route_ref, ...), custom_call_target="tpu_custom_call", output_to_operand_aliasing={{3}: (5, {})} | custom-call | tf_op jit(solution)/shard_map/row_tables/pallas_call | solution.py:190
  67.9 5.0 %bias_tiles.1.bias_ref = f32[6,3,128,384]{3,2,1,0:T(8,128)} custom-call(f32[6,128]{1,0:T(8,128)} %pad.22.clone.table_ref), custom_call_target="tpu_custom_call" | custom-call | tf_op jit(solution)/shard_map/bias_tiles/pallas_call | solution.py:79
  73.5 5.8 %project.3 = (bf16[1024,768]{1,0:T(8,128)(2,1)}, bf16[1024,1152]{1,0:T(8,128)(2,1)}) custom-call(bf16[2,1024,768]{2,1,0:T(8,128)(2,1)} %bitcast.106, f32[1,768]{1,0:T(1,128)} %reshape.333.gain_ref, bf16[16,256,384]{2,1,0:T(8,128)(2,1)} %get-tuple-element.98.weight_ref.refs_4_), custom_call_target="tpu_custom_call" | custom-call | flops 1811939328 | bytes 4718592 | tf_op jit(solution)/shard_map/project/pallas_call | solution.py:108
  79.3 17.6 %attend.2 = (bf16[6,1024,1024]{2,1,0:T(8,128)(2,1)}, bf16[1024,384]{1,0:T(8,128)(2,1)}, f32[1024,384]{1,0:T(8,128)}) custom-call(f32[2,6]{1,0:T(2,128)} %pad_maximum_fusion.4.far_ref, s32[1]{0:T(128)} %bitcast.13.ends_ref, bf16[1024,1152]{1,0:T(8,128)(2,1)} %get-tuple-element.101.q_ref.k_ref.v_ref, bf16[1024,1152]{1,0:T(8,128)(2,1)} %get-tuple-element.101.q_ref.k_ref.v_ref, ...), custom_call_target="tpu_custom_call" | custom-call | flops 6442450944 | bytes 12582912 | tf_op jit(solution)/shard_map/attend/pallas_call | solution.py:725
  104.0 6.1 %project.2 = (bf16[1024,768]{1,0:T(8,128)(2,1)}, bf16[1024,1152]{1,0:T(8,128)(2,1)}) custom-call(bf16[2,1024,768]{2,1,0:T(8,128)(2,1)} %bitcast.107, f32[1,768]{1,0:T(1,128)} %reshape.333.gain_ref, bf16[16,256,384]{2,1,0:T(8,128)(2,1)} %get-tuple-element.98.weight_ref.refs_4_), custom_call_target="tpu_custom_call" | custom-call | flops 1811939328 | bytes 4718592 | tf_op jit(solution)/shard_map/project/pallas_call | solution.py:108
  110.9 6.3 %middle.2 = (f32[512,768]{1,0:T(8,128)}, bf16[512,768]{1,0:T(8,128)(2,1)}, f32[512,128]{1,0:T(8,128)}, bf16[272,1536]{1,0:T(8,128)(2,1)}, bf16[272,1536]{1,0:T(8,128)(2,1)}) custom-call(s32[1]{0:T(128)} %bitcast.me_ref, bf16[1024,384]{1,0:T(8,128)(2,1)} %get-tuple-element.102.joined_ref.out_ref, s32[2,512,2]{2,1,0:T(8,128)} %get-tuple-element.97.place_ref.offset_ref, ...), custom_call_target="tpu_custom_call" | custom-call | flops 1811939328 | bytes 4718592 | tf_op jit(solution)/shard_map/middle/pallas_call | solution.py:297
  118.0 17.7 %attend.3 = (bf16[6,1024,1024]{2,1,0:T(8,128)(2,1)}, bf16[1024,384]{1,0:T(8,128)(2,1)}, f32[1024,384]{1,0:T(8,128)}) custom-call(f32[2,6]{1,0:T(2,128)} %pad_maximum_fusion.4.far_ref, s32[1]{0:T(128)} %bitcast.10.ends_ref, bf16[1024,1152]{1,0:T(8,128)(2,1)} %get-tuple-element.100.q_ref.k_ref.v_ref, bf16[1024,1152]{1,0:T(8,128)(2,1)} %get-tuple-element.100.q_ref.k_ref.v_ref, ...), custom_call_target="tpu_custom_call" | custom-call | flops 6442450944 | bytes 12582912 | tf_op jit(solution)/shard_map/attend/pallas_call | solution.py:725
  138.1 9.2 %collective-permute-done.3.refs_0_ = bf16[512,384]{1,0:T(8,128)(2,1)S(1)} collective-permute-done((bf16[512,384]{1,0:T(8,128)(2,1)S(1)}, bf16[512,384]{1,0:T(8,128)(2,1)S(1)}, u32[]{:S(2)}, u32[]{:S(2)}) %collective-permute-start.3) | collective-permute-done | bytes 393248 | tf_op jit(solution)/shard_map/ppermute | solution.py:1237
  149.0 6.2 %middle.3 = (f32[512,768]{1,0:T(8,128)}, bf16[512,768]{1,0:T(8,128)(2,1)}, f32[512,128]{1,0:T(8,128)}, bf16[272,1536]{1,0:T(8,128)(2,1)}, bf16[272,1536]{1,0:T(8,128)(2,1)}) custom-call(s32[1]{0:T(128)} %bitcast.me_ref, bf16[1024,384]{1,0:T(8,128)(2,1)} %get-tuple-element.105.joined_ref.out_ref, s32[2,512,2]{2,1,0:T(8,128)} %get-tuple-element.97.place_ref.offset_ref, ...), custom_call_target="tpu_custom_call" | custom-call | flops 1811939328 | bytes 4718592 | tf_op jit(solution)/shard_map/middle/pallas_call | solution.py:297
  157.0 18.0 %run_expert.2 = (bf16[272,1536]{1,0:T(8,128)(2,1)}, bf16[272,1536]{1,0:T(8,128)(2,1)}, bf16[544,3072]{1,0:T(8,128)(2,1)}, bf16[544,3072]{1,0:T(8,128)(2,1)}) custom-call(bf16[16,384,768]{2,1,0:T(8,128)(2,1)} %bitcast.102, bf16[16,384,768]{2,1,0:T(8,128)(2,1)} %bitcast.103, bf16[32,12]{1,0:T(8,128)(2,1)} %copy-done.25, ...), custom_call_target="tpu_custom_call" | custom-call | flops 10267656192 | bytes 9437184 | tf_op jit(solution)/shard_map/run_expert/pallas_call | solution.py:996
  176.2 17.5 %run_expert.3 = (bf16[272,1536]{1,0:T(8,128)(2,1)}, bf16[272,1536]{1,0:T(8,128)(2,1)}, bf16[544,3072]{1,0:T(8,128)(2,1)}, bf16[544,3072]{1,0:T(8,128)(2,1)}) custom-call(bf16[16,384,768]{2,1,0:T(8,128)(2,1)} %bitcast.104, bf16[16,384,768]{2,1,0:T(8,128)(2,1)} %bitcast.105, bf16[544,3072]{1,0:T(8,128)(2,1)} %get-tuple-element.115.after_ref.refs_6_, ...), custom_call_target="tpu_custom_call" | custom-call | flops 10267656192 | bytes 9437184 | tf_op jit(solution)/shard_map/run_expert/pallas_call | solution.py:996
  195.4 11.9 %expert_grad_inner.1.refs_0_ = bf16[16,384,768]{2,1,0:T(8,128)(2,1)} custom-call(bf16[272,1536]{1,0:T(8,128)(2,1)} %copy-done, bf16[272,1536]{1,0:T(8,128)(2,1)} %get-tuple-element.110.refs_0_.refs_1_.refs_2_, bf16[272,1536]{1,0:T(8,128)(2,1)} %copy-done.1, bf16[272,1536]{1,0:T(8,128)(2,1)} %get-tuple-element.112.refs_0_.refs_3_.refs_4_, ...), custom_call_target="tpu_custom_call" | custom-call | flops 5133828096 | bytes 9437184 | tf_op jit(solution)/shard_map/expert_grad_inner/pallas_call | solution.py:1067
  207.3 11.8 %expert_grad_outer.1.after_ref = bf16[16,384,768]{2,1,0:T(8,128)(2,1)} custom-call(bf16[16,384,768]{2,1,0:T(8,128)(2,1)} %expert_grad_inner.1.refs_0_, bf16[272,1536]{1,0:T(8,128)(2,1)} %copy-done, bf16[272,1536]{1,0:T(8,128)(2,1)} %get-tuple-element.110.refs_0_.refs_1_.refs_2_, bf16[272,1536]{1,0:T(8,128)(2,1)} %copy-done.1, ...), custom_call_target="tpu_custom_call", output_to_operand_aliasing={{}: (0, {})} | custom-call | flops 5133828096 | bytes 9437184 | tf_op jit(solution)/shard_map/expert_grad_outer/pallas_call | solution.py:1067
  226.2 11.9 %collective-permute-done.6.after_ref.refs_1_ = bf16[272,1536]{1,0:T(8,128)(2,1)S(1)} collective-permute-done((bf16[272,1536]{1,0:T(8,128)(2,1)}, bf16[272,1536]{1,0:T(8,128)(2,1)S(1)}, u32[]{:S(2)}, u32[]{:S(2)}) %collective-permute-start.6) | collective-permute-done | bytes 835616 | tf_op jit(solution)/shard_map/ppermute | solution.py:1302
  238.9 8.1 %second_back.2 = (bf16[2,512,768]{2,1,0:T(8,128)(2,1)}, f32[512,768]{1,0:T(8,128)}, bf16[512,768]{1,0:T(8,128)(2,1)}, f32[1,768]{1,0:T(1,128)}, f32[128,768]{1,0...) custom-call(s32[1]{0:T(128)} %bitcast.me_ref, bf16[2,512,544]{2,1,0:T(8,128)(2,1)} %get-tuple-element.96.back_ref, ...), custom_call_target="tpu_custom_call" | custom-call | flops 1811939328 | bytes 4718592 | tf_op jit(solution)/shard_map/second_back/pallas_call | solution.py:417
  248.7 8.6 %second_back.3 = (bf16[2,512,768]{2,1,0:T(8,128)(2,1)}, f32[512,768]{1,0:T(8,128)}, bf16[512,768]{1,0:T(8,128)(2,1)}, f32[1,768]{1,0:T(1,128)}, f32[128,768]{1,0...) custom-call(s32[1]{0:T(128)} %bitcast.me_ref, ...), custom_call_target="tpu_custom_call", output_to_operand_aliasing={{0}: (13, {})} | custom-call | flops 1811939328 | bytes 4718592 | tf_op jit(solution)/shard_map/second_back/pallas_call | solution.py:417
  260.2 4.7 %dense_grad.2 = bf16[16,96,384]{2,1,0:T(8,128)(2,1)} custom-call(bf16[512,384]{1,0:T(8,128)(2,1)} %copy-done.18, bf16[512,768]{1,0:T(8,128)(2,1)} %pad_maximum_fusion.1.refs_0_, bf16[512,768]{1,0:T(8,128)(2,1)} %pad_maximum_fusion.2.refs_1_, bf16[512,768]{1,0:T(8,128)(2,1)} %get-tuple-element.129.refs_2_, bf16[512,768]{1,0:T(8,128)(2,1)} %get-tuple-element.130.refs_3_), custom_call_target="tpu_custom_call" | custom-call | flops 1207959552 | bytes 1572864 | tf_op jit(solution)/shard_map/dense_grad/pallas_call | solution.py:585
  266.5 17.2 %attend_back.2 = (bf16[1024,1152]{1,0:T(8,128)(2,1)}, f32[6,3,128,384]{3,2,1,0:T(8,128)}, f32[6,2,128,128]{3,2,1,0:T(8,128)}) custom-call(bf16[6,1024,1024]{2,1,0:T(8,128)(2,1)} %get-tuple-element.133.probs_ref, bf16[1024,384]{1,0:T(8,128)(2,1)} %get-tuple-element.102.joined_ref.out_ref, f32[1024,384]{1,0:T(8,128)} %get-tuple-element.134.inv_ref, ...), custom_call_target="tpu_custom_call" | custom-call | flops 12884901888 | bytes 12582912 | tf_op jit(solution)/shard_map/attend_back/pallas_call | solution.py:849
  286.3 17.9 %attend_back.3 = (bf16[1024,1152]{1,0:T(8,128)(2,1)}, f32[6,3,128,384]{3,2,1,0:T(8,128)}, f32[6,2,128,128]{3,2,1,0:T(8,128)}) custom-call(bf16[6,1024,1024]{2,1,0:T(8,128)(2,1)} %get-tuple-element.126.probs_ref, bf16[1024,384]{1,0:T(8,128)(2,1)} %get-tuple-element.105.joined_ref.out_ref, ...), custom_call_target="tpu_custom_call", output_to_operand_aliasing={{1}: (10, {}), {2}: (11, {})} | custom-call | flops 12884901888 | bytes 12582912 | tf_op jit(solution)/shard_map/attend_back/pallas_call | solution.py:849
  311.3 9.8 %dense_grad.3 = (bf16[16,144,384]{2,1,0:T(8,128)(2,1)}, f32[768,1]{1,0:T(8,128)}) custom-call(bf16[4,96,384]{2,1,0:T(8,128)(2,1)} %collective-permute-done.10.after_ref.refs_5_, bf16[1024,768]{1,0:T(8,128)(2,1)} %get-tuple-element.139.refs_0_, bf16[1024,768]{1,0:T(8,128)(2,1)} %get-tuple-element.140.refs_1_, ...), custom_call_target="tpu_custom_call" | custom-call | flops 3623878656 | bytes 3145728 | tf_op jit(solution)/shard_map/dense_grad/pallas_call | solution.py:585
  329.7 6.3 %first_back.3 = (f32[512,768]{1,0:T(8,128)}, bf16[512,768]{1,0:T(8,128)(2,1)}) custom-call(bf16[1024,1152]{1,0:T(8,128)(2,1)} %get-tuple-element.141.refs_2_.grads_ref, bf16[16,256,384]{2,1,0:T(8,128)(2,1)} %get-tuple-element.98.weight_ref.refs_4_, s32[2,512,2]{2,1,0:T(8,128)} %get-tuple-element.97.place_ref.offset_ref, bf16[4,2,144,384]{3,2,1,0:T(8,128)(2,1)} %copy.132.after_ref), custom_call_target="tpu_custom_call" | custom-call | flops 1811939328 | bytes 6291456 | tf_op jit(solution)/shard_map/first_back/pallas_call | solution.py:496
  339.9 6.3 %first_back.2 = (f32[512,768]{1,0:T(8,128)}, bf16[512,768]{1,0:T(8,128)(2,1)}) custom-call(bf16[1024,1152]{1,0:T(8,128)(2,1)} %get-tuple-element.138.refs_3_.grads_ref, bf16[16,256,384]{2,1,0:T(8,128)(2,1)} %get-tuple-element.98.weight_ref.refs_4_, s32[2,512,2]{2,1,0:T(8,128)} %get-tuple-element.97.place_ref.offset_ref, bf16[4,144,384]{2,1,0:T(8,128)(2,1)} %copy-done.17), custom_call_target="tpu_custom_call" | custom-call | flops 1811939328 | bytes 6291456 | tf_op jit(solution)/shard_map/first_back/pallas_call | solution.py:496
  361.7 11.4 %collective-permute-done.13.refs_0_ = bf16[512,768]{1,0:T(8,128)(2,1)S(1)} collective-permute-done((bf16[512,768]{1,0:T(8,128)(2,1)}, bf16[512,768]{1,0:T(8,128)(2,1)S(1)}, u32[]{:S(2)}, u32[]{:S(2)}) %collective-permute-start.13) | collective-permute-done | bytes 786464 | tf_op jit(solution)/shard_map/ppermute | solution.py:1460
  (220 shorter events, 113.6 us)
Async XLA Ops:
  7.2 54.7 %all-gather.5.cloned.1.call-start = ((), (), s32[]{:S(2)}) async-start(), calls=%async_computation.4 | async-start | bytes 3342336 | tf_op jit(solution)/shard_map/all_gather | solution.py:1168
  13.6 143.4 %all-gather.7.cloned.1.call-start = ((), (), s32[]{:S(2)}) async-start(), calls=%async_computation.5 | async-start | bytes 10027008 | tf_op jit(solution)/shard_map/all_gather | solution.py:1175
  13.6 37.6 %collective-permute-start = (bf16[2,512,768]{2,1,0:T(8,128)(2,1)}, bf16[2,512,768]{2,1,0:T(8,128)(2,1)S(1)}, u32[]{:S(2)}, u32[]{:S(2)}) collective-permute-start(bf16[2,512,768]{2,1,0:T(8,128)(2,1)} %rows_ref.7), channel_id=1, source_target_pairs={{0,1},{1,0},{2,3},{3,2},{4,5},{5,4},{6,7},{7,6},{8,9},{9,8},{10,11... | collective-permute-start | bytes 4718600 | tf_op jit(solution)/shard_map/ppermute | solution.py:1144
  20.2 31.0 %copy-start.7 = (bf16[384,768]{1,0:T(8,128)(2,1)}, bf16[384,768]{1,0:T(8,128)(2,1)S(1)}, u32[]{:S(2)}) copy-start(bf16[384,768]{1,0:T(8,128)(2,1)S(1)} %bitcast_dynamic-update-slice_fusion.carried_ref) | copy-start | bytes 1769476
  56.9 296.0 %reduce-scatter.3.cloned.1.call-start = ((), (), s32[]{:S(2)}) async-start(), calls=%async_computation.2 | async-start | bytes 10027008 | tf_op jit(solution)/shard_map/reduce_scatter | solution.py:1344
  66.2 34.9 %copy-start.23 = (bf16[2,8,16,384]{3,1,2,0:T(8,128)(2,1)}, bf16[2,8,16,384]{3,1,2,0:T(8,128)(2,1)S(1)}, u32[]{:S(2)}) copy-start(bf16[2,8,16,384]{3,1,2,0:T(8,128)(2,1)S(1)} %copy.150) | copy-start | bytes 589828
  98.2 11.9 %collective-permute-start.1 = (bf16[512,384]{1,0:T(8,128)(2,1)S(1)}, bf16[512,384]{1,0:T(8,128)(2,1)S(1)}, u32[]{:S(2)}, u32[]{:S(2)}) collective-permute-start(bf16[512,384]{1,0:T(8,128)(2,1)S(1)} %broadcast_select_fusion.3), channel_id=1, source_target_pairs={{0,1},{1,0},{2,3},{3,2},{4,5},{5,4},{6,7},{7,6},{8,9},{9,8},{10,11... | collective-permute-start | bytes 1179656 | tf_op jit(solution)/shard_map/ppermute | solution.py:1237
  117.1 30.2 %collective-permute-start.2 = (bf16[272,1536]{1,0:T(8,128)(2,1)}, bf16[272,1536]{1,0:T(8,128)(2,1)S(1)}, u32[]{:S(2)}, u32[]{:S(2)}) collective-permute-start(bf16[272,1536]{1,0:T(8,128)(2,1)} %get-tuple-element.104.after_ref), channel_id=1, source_target_pairs={{0,1},{1,0},{2,3},{3,2},{4,5},{5,4},{6,7},{7,6},{8,9},{9,8},{10,11... | collective-permute-start | bytes 2506760 | tf_op jit(solution)/shard_map/ppermute | solution.py:1282
  136.9 10.5 %collective-permute-start.3 = (bf16[512,384]{1,0:T(8,128)(2,1)S(1)}, bf16[512,384]{1,0:T(8,128)(2,1)S(1)}, u32[]{:S(2)}, u32[]{:S(2)}) collective-permute-start(bf16[512,384]{1,0:T(8,128)(2,1)S(1)} %broadcast_select_fusion.2), channel_id=1, source_target_pairs={{0,1},{1,0},{2,3},{3,2},{4,5},{5,4},{6,7},{7,6},{8,9},{9,8},{10,11... | collective-permute-start | bytes 1179656 | tf_op jit(solution)/shard_map/ppermute | solution.py:1237
  155.2 20.1 %collective-permute-start.5 = (bf16[272,1536]{1,0:T(8,128)(2,1)}, bf16[272,1536]{1,0:T(8,128)(2,1)S(1)}, u32[]{:S(2)}, u32[]{:S(2)}) collective-permute-start(bf16[272,1536]{1,0:T(8,128)(2,1)} %get-tuple-element.113), channel_id=1, source_target_pairs={{0,1},{1,0},{2,3},{3,2},{4,5},{5,4},{6,7},{7,6},{8,9},{9,8},{10,11... | collective-permute-start | bytes 2506760 | tf_op jit(solution)/shard_map/ppermute | solution.py:1282
  175.0 19.5 %collective-permute-start.4 = (bf16[272,1536]{1,0:T(8,128)(2,1)}, bf16[272,1536]{1,0:T(8,128)(2,1)S(1)}, u32[]{:S(2)}, u32[]{:S(2)}) collective-permute-start(bf16[272,1536]{1,0:T(8,128)(2,1)} %get-tuple-element.111), channel_id=1, source_target_pairs={{0,1},{1,0},{2,3},{3,2},{4,5},{5,4},{6,7},{7,6},{8,9},{9,8},{10,11... | collective-permute-start | bytes 2506760 | tf_op jit(solution)/shard_map/ppermute | solution.py:1302
  219.2 160.1 %reduce-scatter.5.cloned.1.call-start = ((), (), s32[]{:S(2)}) async-start(), calls=%async_computation.3 | async-start | bytes 983040 | tf_op jit(solution)/shard_map/reduce_scatter | solution.py:1505
  219.4 18.7 %collective-permute-start.6 = (bf16[272,1536]{1,0:T(8,128)(2,1)}, bf16[272,1536]{1,0:T(8,128)(2,1)S(1)}, u32[]{:S(2)}, u32[]{:S(2)}) collective-permute-start(bf16[272,1536]{1,0:T(8,128)(2,1)} %get-tuple-element.119), channel_id=1, source_target_pairs={{0,1},{1,0},{2,3},{3,2},{4,5},{5,4},{6,7},{7,6},{8,9},{9,8},{10,11... | collective-permute-start | bytes 2506760 | tf_op jit(solution)/shard_map/ppermute | solution.py:1302
  247.1 12.4 %collective-permute-start.7 = (bf16[512,384]{1,0:T(8,128)(2,1)}, bf16[512,384]{1,0:T(8,128)(2,1)S(1)}, u32[]{:S(2)}, u32[]{:S(2)}) collective-permute-start(bf16[512,384]{1,0:T(8,128)(2,1)} %get-tuple-element.128), channel_id=1, source_target_pairs={{0,1},{1,0},{2,3},{3,2},{4,5},{5,4},{6,7},{7,6},{8,9},{9,8},{10,11... | collective-permute-start | bytes 1179656 | tf_op jit(solution)/shard_map/ppermute | solution.py:1398
  257.3 28.3 %collective-permute-start.9 = (bf16[512,384]{1,0:T(8,128)(2,1)}, bf16[512,384]{1,0:T(8,128)(2,1)S(1)}, u32[]{:S(2)}, u32[]{:S(2)}) collective-permute-start(bf16[512,384]{1,0:T(8,128)(2,1)} %get-tuple-element.132), channel_id=1, source_target_pairs={{0,1},{1,0},{2,3},{3,2},{4,5},{5,4},{6,7},{7,6},{8,9},{9,8},{10,11... | collective-permute-start | bytes 1179656 | tf_op jit(solution)/shard_map/ppermute | solution.py:1398
  266.4 17.3 %collective-permute-start.8 = (bf16[4,2,96,384]{3,2,0,1:T(8,128)(2,1)S(1)}, bf16[4,2,96,384]{3,2,0,1:T(8,128)(2,1)S(1)}, u32[]{:S(2)}, u32[]{:S(2)}) collective-permute-start(bf16[4,2,96,384]{3,2,0,1:T(8,128)(2,1)S(1)} %get-tuple-element.227), channel_id=1, source_target_pairs={{0,2},{2,0},{4,6},{6,4},{8,10},{10,8},{12,14},{14,12},{16,18},{18,... | collective-permute-start | bytes 1769480 | tf_op jit(solution)/shard_map/ppermute | solution.py:1354
  284.7 26.6 %collective-permute-start.10 = (bf16[4,96,384]{2,1,0:T(8,128)(2,1)}, bf16[4,96,384]{2,1,0:T(8,128)(2,1)}, u32[]{:S(2)}, u32[]{:S(2)}) collective-permute-start(bf16[4,96,384]{2,1,0:T(8,128)(2,1)} %get-tuple-element.225), channel_id=1, source_target_pairs={{0,4},{2,6},{4,0},{6,2},{8,12},{10,14},{12,8},{14,10},{16,20},{18,... | collective-permute-start | bytes 884744 | tf_op jit(solution)/shard_map/ppermute | solution.py:1365
  322.9 2.7 collective-permute-start.11
  326.7 12.4 %collective-permute-start.12 = (bf16[4,144,384]{2,1,0:T(8,128)(2,1)S(1)}, bf16[4,144,384]{2,1,0:T(8,128)(2,1)S(1)}, u32[]{:S(2)}, u32[]{:S(2)}) collective-permute-start(bf16[4,144,384]{2,1,0:T(8,128)(2,1)S(1)} %get-tuple-element.211), channel_id=1, source_target_pairs={{0,4},{2,6},{4,0},{6,2},{8,12},{10,14},{12,8},{14,10},{16,20},{18,... | collective-permute-start | bytes 1327112 | tf_op jit(solution)/shard_map/ppermute | solution.py:1365
  328.6 19.6 %collective-permute-start.15 = (bf16[4,2,16,384]{3,2,0,1:T(8,128)(2,1)S(1)}, bf16[4,2,16,384]{3,2,0,1:T(8,128)(2,1)S(1)}, u32[]{:S(2)}, u32[]{:S(2)}) collective-permute-start(bf16[4,2,16,384]{3,2,0,1:T(8,128)(2,1)S(1)} %get-tuple-element.253), channel_id=1, source_target_pairs={{0,2},{2,0},{4,6},{6,4},{8,10},{10,8},{12,14},{14,12},{16,18},{18,... | collective-permute-start | bytes 294920 | tf_op jit(solution)/shard_map/ppermute | solution.py:1354
  336.0 20.6 %collective-permute-start.14 = (bf16[512,768]{1,0:T(8,128)(2,1)}, bf16[512,768]{1,0:T(8,128)(2,1)S(1)}, u32[]{:S(2)}, u32[]{:S(2)}) collective-permute-start(bf16[512,768]{1,0:T(8,128)(2,1)} %get-tuple-element.148), channel_id=1, source_target_pairs={{0,1},{1,0},{2,3},{3,2},{4,5},{5,4},{6,7},{7,6},{8,9},{9,8},{10,11... | collective-permute-start | bytes 2359304 | tf_op jit(solution)/shard_map/ppermute | solution.py:1460
  346.2 27.0 %collective-permute-start.13 = (bf16[512,768]{1,0:T(8,128)(2,1)}, bf16[512,768]{1,0:T(8,128)(2,1)S(1)}, u32[]{:S(2)}, u32[]{:S(2)}) collective-permute-start(bf16[512,768]{1,0:T(8,128)(2,1)} %get-tuple-element.145), channel_id=1, source_target_pairs={{0,1},{1,0},{2,3},{3,2},{4,5},{5,4},{6,7},{7,6},{8,9},{9,8},{10,11... | collective-permute-start | bytes 2359304 | tf_op jit(solution)/shard_map/ppermute | solution.py:1460
  348.8 4.1 %collective-permute-start.16 = (bf16[4,16,384]{2,1,0:T(8,128)(2,1)S(1)}, bf16[4,16,384]{2,1,0:T(8,128)(2,1)S(1)}, u32[]{:S(2)}, u32[]{:S(2)}) collective-permute-start(bf16[4,16,384]{2,1,0:T(8,128)(2,1)S(1)} %get-tuple-element.250), channel_id=1, source_target_pairs={{0,4},{2,6},{4,0},{6,2},{8,12},{10,14},{12,8},{14,10},{16,20},{18,... | collective-permute-start | bytes 147464 | tf_op jit(solution)/shard_map/ppermute | solution.py:1365
  379.3 6.9 %collective-permute-start.17 = (bf16[256,384]{1,0:T(8,128)(2,1)}, bf16[256,384]{1,0:T(8,128)(2,1)S(1)}, u32[]{:S(2)}, u32[]{:S(2)}) collective-permute-start(bf16[256,384]{1,0:T(8,128)(2,1)} %bitcast.97), channel_id=1, source_target_pairs={{0,1},{1,0},{2,3},{3,2},{4,5},{5,4},{6,7},{7,6},{8,9},{9,8},{10,11... | collective-permute-start | bytes 589832 | tf_op jit(solution)/shard_map/ppermute | solution.py:1513
  (31 other events, 93.0 us)
Sparse Core Ops, SparseCore 0:
  13.7 48.1 all-gather.4
  64.7 80.2 all-gather.6
  219.3 115.8 reduce-scatter.2
  356.1 22.0 reduce-scatter.4

commit v5 on v4

--- a/solution.py
+++ b/solution.py
@@ -315,7 +315,7 @@
         out_shape=out_shape,
         compiler_params=params(),
         cost_estimate=pl.CostEstimate(
-            flops=6 * count * width * width, bytes_accessed=12 * count * width, transcendentals=0
+            flops=48 * count * width * width, bytes_accessed=12 * count * width, transcendentals=0
         ),
         name="middle",
     )(me, joined, offsets, weight, rows, grads, gain, router, routes, send, after, *received)
@@ -549,56 +549,49 @@
     )(*operands)
 
 
-def dense_kernel(batches, weighted, after_ref, *refs):
+def dense_kernel(batches, weighted, blocks, after_ref, *refs):
     out_ref = refs[2 * batches + weighted]
-    total = None
-    for batch in range(batches):
-        term = dot_tn(refs[batch][...], refs[batches + batch][...])
-        total = term if total is None else total + term
-    out_ref[...] = total.astype(bfloat).reshape(out_ref.shape)
+    left = jnp.concatenate([ref[...] for ref in refs[:batches]], axis=0)
+    right = jnp.concatenate([ref[...] for ref in refs[batches : 2 * batches]], axis=0)
+    total = dot_tn(left, right)
+    depth = out_ref.shape[1] // blocks
+    lanes = out_ref.shape[2]
+    term = None
+    for block in range(blocks):
+        part = total[:, block * lanes : (block + 1) * lanes]
+        rows = slice(block * depth, (block + 1) * depth)
+        out_ref[:, rows, :] = part.astype(bfloat).reshape(out_ref.shape[0], depth, lanes)
+        if weighted:
+            weight = refs[2 * batches][:, rows, :].reshape(part.shape).astype(float32)
+            term = part * weight if term is None else term + part * weight
     if weighted:
-        sum_ref = refs[-1]
-        weight = refs[2 * batches][...].reshape(total.shape).astype(float32)
-        term = jnp.sum(total * weight, axis=1, keepdims=True)
-
-        @pl.when(pl.program_id(0) == 0)
-        def _():
-            sum_ref[...] = term
-
-        @pl.when(pl.program_id(0) > 0)
-        def _():
-            sum_ref[...] += term
+        refs[-1][...] = jnp.sum(term, axis=1, keepdims=True)
 
 
 def dense_grad(left, right, lanes, shards, direct, after, packed=None):
     batches = len(left)
     count, width = left[0].shape
-    blocks = right[0].shape[1] // lanes
+    columns = right[0].shape[1]
+    blocks = columns // lanes
     depth = width // shards
-    if direct:
-        out_shape = (shards, blocks * depth, lanes)
-        out_spec = pl.BlockSpec((shards, depth, lanes), lambda i: (0, i, 0))
-    else:
-        out_shape = (blocks, width, lanes)
-        out_spec = pl.BlockSpec((1, width, lanes), lambda i: (i, 0, 0))
+    steps = 2 if direct and width % (2 * tile) == 0 and shards % 2 == 0 else 1
+    outer = shards // steps if direct else 1
+    inner = depth if direct else width
     weighted = 0 if packed is None else 1
     outs = pl.pallas_call(
-        functools.partial(dense_kernel, batches, weighted),
-        grid=(blocks,),
+        functools.partial(dense_kernel, batches, weighted, blocks),
+        grid=(steps,),
         in_specs=[pl.BlockSpec(memory_space=pl.ANY)]
-        + [pl.BlockSpec((count, width), lambda i: (0, 0))] * batches
-        + [pl.BlockSpec((count, lanes), lambda i: (0, i))] * batches
-        + (
-            [pl.BlockSpec((packed.shape[0], width // packed.shape[0], lanes), lambda i: (0, i, 0))]
-            if weighted
-            else []
-        ),
-        out_specs=[out_spec] + [pl.BlockSpec((width, 1), lambda i: (0, 0))] * weighted,
-        out_shape=[jax.ShapeDtypeStruct(out_shape, bfloat)]
+        + [pl.BlockSpec((count, width // steps), lambda i: (0, i))] * batches
+        + [pl.BlockSpec((count, columns), lambda i: (0, 0))] * batches
+        + [pl.BlockSpec((outer, blocks * inner, lanes), lambda i: (i, 0, 0))] * weighted,
+        out_specs=[pl.BlockSpec((outer, blocks * inner, lanes), lambda i: (i, 0, 0))]
+        + [pl.BlockSpec((width // steps, 1), lambda i: (i, 0))] * weighted,
+        out_shape=[jax.ShapeDtypeStruct((outer * steps, blocks * inner, lanes), bfloat)]
         + [jax.ShapeDtypeStruct((width, 1), float32)] * weighted,
         compiler_params=params(),
         cost_estimate=pl.CostEstimate(
-            flops=2 * batches * count * width * lanes * blocks,
+            flops=2 * batches * count * width * columns,
             bytes_accessed=2 * batches * count * width,
             transcendentals=0,
         ),
@@ -936,7 +929,7 @@
 
 
 def expert_kernel(
-    count, slots, width, chunk, inner_ref, outer_ref, after_ref, *refs
+    count, slots, width, inner_ref, outer_ref, after_ref, *refs
 ):
     blocks = refs[:count]
     results = refs[count : 2 * count]
@@ -955,16 +948,14 @@
     rows = rows_ref[...]
     grads = grads_ref[...]
     root = 0.7978845608028654
-    for start in range(0, width, chunk):
-        columns = slice(start, start + chunk)
-        pre = dot_nn(rows, inner[:, columns])
-        grad_hidden = dot_nt(grads, outer[columns, :])
-        square = pre * pre
-        curve = jnp.tanh(root * pre * (1.0 + 0.044715 * square))
-        half = 0.5 * (1.0 + curve)
-        slope = half + (0.5 * root) * pre * (1.0 - curve * curve) * (1.0 + 0.134145 * square)
-        hidden_ref[:, columns] = (pre * half).astype(bfloat)
-        grad_pre_ref[:, columns] = (grad_hidden * slope).astype(bfloat)
+    pre = dot_nn(rows, inner)
+    grad_hidden = dot_nt(grads, outer)
+    square = pre * pre
+    curve = jnp.tanh(root * pre * (1.0 + 0.044715 * square))
+    half = 0.5 * (1.0 + curve)
+    slope = half + (0.5 * root) * pre * (1.0 - curve * curve) * (1.0 + 0.134145 * square)
+    hidden_ref[...] = (pre * half).astype(bfloat)
+    grad_pre_ref[...] = (grad_hidden * slope).astype(bfloat)
     product = dot_nn(hidden_ref[...], outer)
     product_back = dot_nt(grad_pre_ref[...], inner)
 
@@ -994,7 +985,7 @@
     whole = pl.BlockSpec((slots, 2 * width), lambda i: (0, 0))
     chunk = pl.BlockSpec((total, width), lambda i: (0, i))
     outs = pl.pallas_call(
-        functools.partial(expert_kernel, count, slots, width, 256),
+        functools.partial(expert_kernel, count, slots, width),
         grid=(turns,),
         in_specs=[inner_spec, outer_spec, pl.BlockSpec(memory_space=pl.ANY)] + [whole] * count,
         out_specs=[whole] * count + [chunk, chunk],
@@ -1030,15 +1021,9 @@
                 start = (batch * count + idx) * slots
                 rows_ref[start : start + slots, :] = groups[batch][idx][:, half]
 
-    total = None
-    span = count * slots
-    for batch in range(batches):
-        rows = rows_ref[batch * span : (batch + 1) * span, :]
-        if second:
-            term = dot_tn(wide[batch][...], rows)
-        else:
-            term = dot_tn(rows, wide[batch][...])
-        total = term if total is None else total + term
+    rows = rows_ref[...]
+    columns = jnp.concatenate([ref[...] for ref in wide], axis=0)
+    total = dot_tn(columns, rows) if second else dot_tn(rows, columns)
     out_ref[...] = total.astype(bfloat).reshape(out_ref.shape)
 
 
@@ -1247,24 +1232,29 @@
     normed_two = []
     router_probs = []
     blocks = []
-    after = table
     for batch in range(batches):
         normed, packed_rows = project(batch, ordered_in, gain_one, packed, pairs, scale)
         normed_one.append(normed)
         qkv.append(packed_rows)
         kept, joined, inverse = attend(
-            packed_rows, ends[batch], bias, far, after, head_dim, members
+            packed_rows,
+            ends[batch],
+            bias,
+            far,
+            arrived_heads[-1][-1] if arrived_heads else table,
+            head_dim,
+            members,
         )
         probs.append(kept)
         outs.append(joined)
         inverses.append(inverse)
-        heads_in = send_rows(batch, joined)
-        arrived_heads.append(heads_in)
+        arrived_heads.append(send_rows(batch, joined))
+    for batch in range(batches):
         mid, normed, chances, outgoing = middle(
             batch,
             me_row,
-            joined,
-            heads_in,
+            outs[batch],
+            arrived_heads[batch],
             offsets,
             output_w,
             hidden_in,
@@ -1273,9 +1263,8 @@
             router_wide,
             routes,
             dispatch,
-            blocks[-1][-1] if blocks else table,
-        )
-        after = outgoing[-1]
+            outs[-1],
+        )
         blocks.append(
             [outgoing[0]]
             + [
@@ -1322,7 +1311,7 @@
             True,
             buffer_shape,
             pl.BlockSpec((group, depth_out, width), lambda i: (i, 1, 0)),
-            returned[0][-1],
+            returned[-1][-1],
             buffer,
         )
     else:
@@ -1387,7 +1376,7 @@
             output_w,
             members,
             span,
-            returned[-1][-1] if batch == 0 else buffer,
+            buffer,
             layer,
         )
         grad_mid.append(mid)

time: 403 us -> 395 us (0.980)
  Pallas kernels: 222 us -> 217 us
    ppermute x2, waiting for transfers between devices: 0.01 us -> 10.5 us  [on_device(): lax.ppermute(outgoing[step], 'expert', around(step))]
    ppermute x2, waiting for transfers between devices: 12.7 us -> 6.16 us  [on_device(): lax.ppermute(results[step], 'expert', around(-step))]
    ppermute x2, waiting for transfers between devices: 9.23 us -> 3.64 us  [send_rows(): arrived.append(lax.ppermute(rows, 'expert', around(step)))]
    unnamed x84 -> x82, local copies, waits for them, and re-layouts: 18.5 us -> 18.3 us
  transfers between devices with their start and end apart: 22 -> 22, of which waited for: 11 -> 11; matrix products, arithmetic and copies ran while one was open for 10% -> 10% of each run, Pallas kernels for 50% -> 53%
where the time goes in v5:
time: 395 us; the launch traced here: 391 us
  Pallas kernels  217 us (55%)
  waiting for transfers between devices  76.2 us (19%)
  local copies, waits for them, and re-layouts  38.7 us (10%)
  other arithmetic  21.7 us (5%)
  starting transfers between devices  19.8 us (5%)
  between operations  14.8 us (4%)
    pallas_call x2, Pallas kernels, attend(): pl.pallas_call(functools.partial(attend_kernel, stride, head_dim), grid=(...  35.5 us
    pallas_call x2, Pallas kernels, attend_back(): pl.pallas_call(functools.partial(attend_back_kernel, stride, head_dim, he...  35.1 us
    pallas_call x2, Pallas kernels, run_expert(): pl.pallas_call(functools.partial(expert_kernel, count, slots, width), gri...  33.7 us
    ppermute x1, waiting for transfers between devices, on_device(): lax.ppermute(hidden_in, 'expert', around(step))  31 us
    pallas_call x2, Pallas kernels, expert_grad(): pl.pallas_call(body, grid=(turns,), in_specs=in_specs, out_specs=out_spec...  21.4 us
    unnamed x82, local copies, waits for them, and re-layouts  18.3 us
    pallas_call x2, Pallas kernels, second_back(): pl.pallas_call(functools.partial(second_kernel, members, members, aliased...  17.3 us
    pallas_call x2, Pallas kernels, dense_grad(): pl.pallas_call(functools.partial(dense_kernel, batches, weighted, blocks)...  13.1 us
  transfers between devices with their start and end apart: 22, of which 11 were waited for; matrix products, arithmetic and copies ran while one was open for 10% of the time, Pallas kernels for 53%

profile of v5, /device:TPU:0, one launch (start us, length us, event | category | flops | bytes accessed | tf_op | source)
XLA Modules:
  0.0 391.4 jit_solution(14618886679061283849)
XLA Ops:
  20.2 31.0 %collective-permute-done.after_ref.refs_1_ = bf16[2,512,768]{2,1,0:T(8,128)(2,1)S(1)} collective-permute-done((bf16[2,512,768]{2,1,0:T(8,128)(2,1)}, bf16[2,512,768]{2,1,0:T(8,128)(2,1)S(1)}, u32[]{:S(2)}, u32[]{:S(2)}) %collective-permute-start) | collective-permute-done | bytes 1572896 | tf_op jit(solution)/shard_map/ppermute | solution.py:1129
  52.4 4.5 %row_tables.1 = (bf16[2,544,512]{2,1,0:T(8,128)(2,1)}, bf16[2,512,544]{2,1,0:T(8,128)(2,1)}, s32[2,512,2]{2,1,0:T(8,128)}, bf16[384,768]{1,0:T(8,128)(2,1)}) custom-call(s32[1]{0:T(128)} %bitcast.me_ref, s32[2,1,512]{2,1,0:T(1,128)} %bitcast.100, s32[2,512,1]{2,1,0:T(8,128)} %copy.119.column_ref.route_ref, ...), custom_call_target="tpu_custom_call", output_to_operand_aliasing={{3}: (5, {})} | custom-call | tf_op jit(solution)/shard_map/row_tables/pallas_call | solution.py:190
  67.9 5.0 %bias_tiles.1.bias_ref = f32[6,3,128,384]{3,2,1,0:T(8,128)} custom-call(f32[6,128]{1,0:T(8,128)} %pad.22.clone.table_ref), custom_call_target="tpu_custom_call" | custom-call | tf_op jit(solution)/shard_map/bias_tiles/pallas_call | solution.py:79
  73.5 5.8 %project.3 = (bf16[1024,768]{1,0:T(8,128)(2,1)}, bf16[1024,1152]{1,0:T(8,128)(2,1)}) custom-call(bf16[2,1024,768]{2,1,0:T(8,128)(2,1)} %bitcast.106, f32[1,768]{1,0:T(1,128)} %reshape.333.gain_ref, bf16[16,256,384]{2,1,0:T(8,128)(2,1)} %get-tuple-element.98.weight_ref.refs_4_), custom_call_target="tpu_custom_call" | custom-call | flops 1811939328 | bytes 4718592 | tf_op jit(solution)/shard_map/project/pallas_call | solution.py:108
  79.3 17.6 %attend.2 = (bf16[6,1024,1024]{2,1,0:T(8,128)(2,1)}, bf16[1024,384]{1,0:T(8,128)(2,1)}, f32[1024,384]{1,0:T(8,128)}) custom-call(f32[2,6]{1,0:T(2,128)} %pad_maximum_fusion.4.far_ref, s32[1]{0:T(128)} %bitcast.13.ends_ref, bf16[1024,1152]{1,0:T(8,128)(2,1)} %get-tuple-element.101.q_ref.k_ref.v_ref, bf16[1024,1152]{1,0:T(8,128)(2,1)} %get-tuple-element.101.q_ref.k_ref.v_ref, ...), custom_call_target="tpu_custom_call" | custom-call | flops 6442450944 | bytes 12582912 | tf_op jit(solution)/shard_map/attend/pallas_call | solution.py:718
  103.9 5.9 %project.2 = (bf16[1024,768]{1,0:T(8,128)(2,1)}, bf16[1024,1152]{1,0:T(8,128)(2,1)}) custom-call(bf16[2,1024,768]{2,1,0:T(8,128)(2,1)} %bitcast.107, f32[1,768]{1,0:T(1,128)} %reshape.333.gain_ref, bf16[16,256,384]{2,1,0:T(8,128)(2,1)} %get-tuple-element.98.weight_ref.refs_4_), custom_call_target="tpu_custom_call" | custom-call | flops 1811939328 | bytes 4718592 | tf_op jit(solution)/shard_map/project/pallas_call | solution.py:108
  110.5 17.9 %attend.3 = (bf16[6,1024,1024]{2,1,0:T(8,128)(2,1)}, bf16[1024,384]{1,0:T(8,128)(2,1)}, f32[1024,384]{1,0:T(8,128)}) custom-call(f32[2,6]{1,0:T(2,128)} %pad_maximum_fusion.4.far_ref, s32[1]{0:T(128)} %bitcast.10.ends_ref, bf16[1024,1152]{1,0:T(8,128)(2,1)} %get-tuple-element.100.q_ref.k_ref.v_ref, bf16[1024,1152]{1,0:T(8,128)(2,1)} %get-tuple-element.100.q_ref.k_ref.v_ref, ...), custom_call_target="tpu_custom_call" | custom-call | flops 6442450944 | bytes 12582912 | tf_op jit(solution)/shard_map/attend/pallas_call | solution.py:718
  130.9 6.3 %middle.3 = (f32[512,768]{1,0:T(8,128)}, bf16[512,768]{1,0:T(8,128)(2,1)}, f32[512,128]{1,0:T(8,128)}, bf16[272,1536]{1,0:T(8,128)(2,1)}, bf16[272,1536]{1,0:T(8,128)(2,1)}) custom-call(s32[1]{0:T(128)} %bitcast.me_ref, bf16[1024,384]{1,0:T(8,128)(2,1)} %get-tuple-element.102.joined_ref.out_ref, s32[2,512,2]{2,1,0:T(8,128)} %get-tuple-element.97.place_ref.offset_ref, ...), custom_call_target="tpu_custom_call" | custom-call | flops 14495514624 | bytes 4718592 | tf_op jit(solution)/shard_map/middle/pallas_call | solution.py:297
  142.5 6.4 %middle.2 = (f32[512,768]{1,0:T(8,128)}, bf16[512,768]{1,0:T(8,128)(2,1)}, f32[512,128]{1,0:T(8,128)}, bf16[272,1536]{1,0:T(8,128)(2,1)}, bf16[272,1536]{1,0:T(8,128)(2,1)}) custom-call(s32[1]{0:T(128)} %bitcast.me_ref, bf16[1024,384]{1,0:T(8,128)(2,1)} %get-tuple-element.103.joined_ref.after_ref.out_ref, ...), custom_call_target="tpu_custom_call" | custom-call | flops 14495514624 | bytes 4718592 | tf_op jit(solution)/shard_map/middle/pallas_call | solution.py:297
  149.1 10.5 %collective-permute-done.3.refs_1_.refs_2_.refs_3_ = bf16[272,1536]{1,0:T(8,128)(2,1)S(1)} collective-permute-done((bf16[272,1536]{1,0:T(8,128)(2,1)}, bf16[272,1536]{1,0:T(8,128)(2,1)S(1)}, u32[]{:S(2)}, u32[]{:S(2)}) %collective-permute-start.3) | collective-permute-done | bytes 835616 | tf_op jit(solution)/shard_map/ppermute | solution.py:1271
  160.6 17.1 %run_expert.2 = (bf16[272,1536]{1,0:T(8,128)(2,1)}, bf16[272,1536]{1,0:T(8,128)(2,1)}, bf16[544,3072]{1,0:T(8,128)(2,1)}, bf16[544,3072]{1,0:T(8,128)(2,1)}) custom-call(bf16[16,384,768]{2,1,0:T(8,128)(2,1)} %bitcast.102, bf16[16,384,768]{2,1,0:T(8,128)(2,1)} %bitcast.103, bf16[32,12]{1,0:T(8,128)(2,1)} %copy-done.25, ...), custom_call_target="tpu_custom_call" | custom-call | flops 10267656192 | bytes 9437184 | tf_op jit(solution)/shard_map/run_expert/pallas_call | solution.py:987
  178.8 16.6 %run_expert.3 = (bf16[272,1536]{1,0:T(8,128)(2,1)}, bf16[272,1536]{1,0:T(8,128)(2,1)}, bf16[544,3072]{1,0:T(8,128)(2,1)}, bf16[544,3072]{1,0:T(8,128)(2,1)}) custom-call(bf16[16,384,768]{2,1,0:T(8,128)(2,1)} %bitcast.104, bf16[16,384,768]{2,1,0:T(8,128)(2,1)} %bitcast.105, bf16[544,3072]{1,0:T(8,128)(2,1)} %get-tuple-element.115.after_ref.refs_6_, ...), custom_call_target="tpu_custom_call" | custom-call | flops 10267656192 | bytes 9437184 | tf_op jit(solution)/shard_map/run_expert/pallas_call | solution.py:987
  198.1 10.7 %expert_grad_inner.1.refs_0_ = bf16[16,384,768]{2,1,0:T(8,128)(2,1)} custom-call(bf16[272,1536]{1,0:T(8,128)(2,1)} %copy-done.1, bf16[272,1536]{1,0:T(8,128)(2,1)} %get-tuple-element.109.refs_0_.refs_1_.refs_2_, bf16[272,1536]{1,0:T(8,128)(2,1)} %copy-done.3, bf16[272,1536]{1,0:T(8,128)(2,1)} %get-tuple-element.112.refs_0_.refs_3_.refs_4_, ...), custom_call_target="tpu_custom_call" | custom-call | flops 5133828096 | bytes 9437184 | tf_op jit(solution)/shard_map/expert_grad_inner/pallas_call | solution.py:1052
  208.8 6.2 %collective-permute-done.6.refs_1_ = bf16[272,1536]{1,0:T(8,128)(2,1)S(1)} collective-permute-done((bf16[272,1536]{1,0:T(8,128)(2,1)}, bf16[272,1536]{1,0:T(8,128)(2,1)S(1)}, u32[]{:S(2)}, u32[]{:S(2)}) %collective-permute-start.6) | collective-permute-done | bytes 835616 | tf_op jit(solution)/shard_map/ppermute | solution.py:1291
  215.8 10.7 %expert_grad_outer.1.after_ref = bf16[16,384,768]{2,1,0:T(8,128)(2,1)} custom-call(bf16[16,384,768]{2,1,0:T(8,128)(2,1)} %expert_grad_inner.1.refs_0_, bf16[272,1536]{1,0:T(8,128)(2,1)} %copy-done.2, bf16[272,1536]{1,0:T(8,128)(2,1)} %get-tuple-element.109.refs_0_.refs_1_.refs_2_, bf16[272,1536]{1,0:T(8,128)(2,1)} %copy-done.3, ...), custom_call_target="tpu_custom_call", output_to_operand_aliasing={{}: (0, {})} | custom-call | flops 5133828096 | bytes 9437184 | tf_op jit(solution)/shard_map/expert_grad_outer/pallas_call | solution.py:1052
  231.5 8.7 %second_back.2 = (bf16[2,512,768]{2,1,0:T(8,128)(2,1)}, f32[512,768]{1,0:T(8,128)}, bf16[512,768]{1,0:T(8,128)(2,1)}, f32[1,768]{1,0:T(1,128)}, f32[128,768]{1,0...) custom-call(s32[1]{0:T(128)} %bitcast.me_ref, bf16[2,512,544]{2,1,0:T(8,128)(2,1)} %get-tuple-element.96.back_ref, ...), custom_call_target="tpu_custom_call" | custom-call | flops 1811939328 | bytes 4718592 | tf_op jit(solution)/shard_map/second_back/pallas_call | solution.py:417
  241.5 8.6 %second_back.3 = (bf16[2,512,768]{2,1,0:T(8,128)(2,1)}, f32[512,768]{1,0:T(8,128)}, bf16[512,768]{1,0:T(8,128)(2,1)}, f32[1,768]{1,0:T(1,128)}, f32[128,768]{1,0...) custom-call(s32[1]{0:T(128)} %bitcast.me_ref, ...), custom_call_target="tpu_custom_call", output_to_operand_aliasing={{0}: (13, {})} | custom-call | flops 1811939328 | bytes 4718592 | tf_op jit(solution)/shard_map/second_back/pallas_call | solution.py:417
  259.5 17.2 %attend_back.2 = (bf16[1024,1152]{1,0:T(8,128)(2,1)}, f32[6,3,128,384]{3,2,1,0:T(8,128)}, f32[6,2,128,128]{3,2,1,0:T(8,128)}) custom-call(bf16[6,1024,1024]{2,1,0:T(8,128)(2,1)} %get-tuple-element.133.probs_ref, bf16[1024,384]{1,0:T(8,128)(2,1)} %get-tuple-element.102.joined_ref.out_ref, f32[1024,384]{1,0:T(8,128)} %get-tuple-element.134.inv_ref, ...), custom_call_target="tpu_custom_call" | custom-call | flops 12884901888 | bytes 12582912 | tf_op jit(solution)/shard_map/attend_back/pallas_call | solution.py:842
  279.3 17.9 %attend_back.3 = (bf16[1024,1152]{1,0:T(8,128)(2,1)}, f32[6,3,128,384]{3,2,1,0:T(8,128)}, f32[6,2,128,128]{3,2,1,0:T(8,128)}) custom-call(bf16[6,1024,1024]{2,1,0:T(8,128)(2,1)} %get-tuple-element.126.probs_ref, bf16[1024,384]{1,0:T(8,128)(2,1)} %get-tuple-element.103.joined_ref.after_ref.out_ref, ...), custom_call_target="tpu_custom_call", output_to_operand_aliasing={{1}: (10, {}), {2}: (11, {})} | custom-call | flops 12884901888 | bytes 12582912 | tf_op jit(solution)/shard_map/attend_back/pallas_call | solution.py:842
  304.2 8.8 %dense_grad.3 = (bf16[16,144,384]{2,1,0:T(8,128)(2,1)}, f32[768,1]{1,0:T(8,128)}) custom-call(bf16[4,96,384]{2,1,0:T(8,128)(2,1)} %collective-permute-done.10.after_ref.refs_5_, bf16[1024,768]{1,0:T(8,128)(2,1)} %get-tuple-element.139.refs_0_, bf16[1024,768]{1,0:T(8,128)(2,1)} %get-tuple-element.140.refs_1_, ...), custom_call_target="tpu_custom_call" | custom-call | flops 3623878656 | bytes 3145728 | tf_op jit(solution)/shard_map/dense_grad/pallas_call | solution.py:581
  322.0 6.3 %first_back.3 = (f32[512,768]{1,0:T(8,128)}, bf16[512,768]{1,0:T(8,128)(2,1)}) custom-call(bf16[1024,1152]{1,0:T(8,128)(2,1)} %get-tuple-element.141.refs_2_.grads_ref, bf16[16,256,384]{2,1,0:T(8,128)(2,1)} %get-tuple-element.98.weight_ref.refs_4_, s32[2,512,2]{2,1,0:T(8,128)} %get-tuple-element.97.place_ref.offset_ref, bf16[4,2,144,384]{3,2,1,0:T(8,128)(2,1)} %copy.132.after_ref), custom_call_target="tpu_custom_call" | custom-call | flops 1811939328 | bytes 6291456 | tf_op jit(solution)/shard_map/first_back/pallas_call | solution.py:496
  332.8 6.3 %first_back.2 = (f32[512,768]{1,0:T(8,128)}, bf16[512,768]{1,0:T(8,128)(2,1)}) custom-call(bf16[1024,1152]{1,0:T(8,128)(2,1)} %get-tuple-element.138.refs_3_.grads_ref, bf16[16,256,384]{2,1,0:T(8,128)(2,1)} %get-tuple-element.98.weight_ref.refs_4_, s32[2,512,2]{2,1,0:T(8,128)} %get-tuple-element.97.place_ref.offset_ref, bf16[4,144,384]{2,1,0:T(8,128)(2,1)} %copy-done.12), custom_call_target="tpu_custom_call" | custom-call | flops 1811939328 | bytes 6291456 | tf_op jit(solution)/shard_map/first_back/pallas_call | solution.py:496
  353.9 11.4 %collective-permute-done.13.refs_0_ = bf16[512,768]{1,0:T(8,128)(2,1)S(1)} collective-permute-done((bf16[512,768]{1,0:T(8,128)(2,1)}, bf16[512,768]{1,0:T(8,128)(2,1)S(1)}, u32[]{:S(2)}, u32[]{:S(2)}) %collective-permute-start.13) | collective-permute-done | bytes 786464 | tf_op jit(solution)/shard_map/ppermute | solution.py:1449
  373.8 4.5 %collective-permute-done.17 = bf16[256,384]{1,0:T(8,128)(2,1)S(1)} collective-permute-done((bf16[256,384]{1,0:T(8,128)(2,1)}, bf16[256,384]{1,0:T(8,128)(2,1)S(1)}, u32[]{:S(2)}, u32[]{:S(2)}) %collective-permute-start.17) | collective-permute-done | bytes 196640 | tf_op jit(solution)/shard_map/ppermute | solution.py:1502
  (218 shorter events, 114.9 us)
Async XLA Ops:
  7.2 54.7 %all-gather.5.cloned.1.call-start = ((), (), s32[]{:S(2)}) async-start(), calls=%async_computation.4 | async-start | bytes 3342336 | tf_op jit(solution)/shard_map/all_gather | solution.py:1153
  13.6 146.1 %all-gather.7.cloned.1.call-start = ((), (), s32[]{:S(2)}) async-start(), calls=%async_computation.5 | async-start | bytes 10027008 | tf_op jit(solution)/shard_map/all_gather | solution.py:1160
  13.6 37.6 %collective-permute-start = (bf16[2,512,768]{2,1,0:T(8,128)(2,1)}, bf16[2,512,768]{2,1,0:T(8,128)(2,1)S(1)}, u32[]{:S(2)}, u32[]{:S(2)}) collective-permute-start(bf16[2,512,768]{2,1,0:T(8,128)(2,1)} %rows_ref.7), channel_id=1, source_target_pairs={{0,1},{1,0},{2,3},{3,2},{4,5},{5,4},{6,7},{7,6},{8,9},{9,8},{10,11... | collective-permute-start | bytes 4718600 | tf_op jit(solution)/shard_map/ppermute | solution.py:1129
  20.2 31.0 %copy-start.7 = (bf16[384,768]{1,0:T(8,128)(2,1)}, bf16[384,768]{1,0:T(8,128)(2,1)S(1)}, u32[]{:S(2)}) copy-start(bf16[384,768]{1,0:T(8,128)(2,1)S(1)} %bitcast_dynamic-update-slice_fusion.carried_ref) | copy-start | bytes 1769476
  56.9 288.4 %reduce-scatter.3.cloned.1.call-start = ((), (), s32[]{:S(2)}) async-start(), calls=%async_computation.2 | async-start | bytes 10027008 | tf_op jit(solution)/shard_map/reduce_scatter | solution.py:1333
  66.2 34.9 %copy-start.22 = (bf16[2,8,16,384]{3,1,2,0:T(8,128)(2,1)}, bf16[2,8,16,384]{3,1,2,0:T(8,128)(2,1)S(1)}, u32[]{:S(2)}) copy-start(bf16[2,8,16,384]{3,1,2,0:T(8,128)(2,1)S(1)} %copy.150) | copy-start | bytes 589828
  98.1 11.7 %collective-permute-start.1 = (bf16[512,384]{1,0:T(8,128)(2,1)S(1)}, bf16[512,384]{1,0:T(8,128)(2,1)S(1)}, u32[]{:S(2)}, u32[]{:S(2)}) collective-permute-start(bf16[512,384]{1,0:T(8,128)(2,1)S(1)} %broadcast_select_fusion.3), channel_id=1, source_target_pairs={{0,1},{1,0},{2,3},{3,2},{4,5},{5,4},{6,7},{7,6},{8,9},{9,8},{10,11... | collective-permute-start | bytes 1179656 | tf_op jit(solution)/shard_map/ppermute | solution.py:1222
  129.7 12.0 %collective-permute-start.2 = (bf16[512,384]{1,0:T(8,128)(2,1)S(1)}, bf16[512,384]{1,0:T(8,128)(2,1)S(1)}, u32[]{:S(2)}, u32[]{:S(2)}) collective-permute-start(bf16[512,384]{1,0:T(8,128)(2,1)S(1)} %broadcast_select_fusion.2), channel_id=1, source_target_pairs={{0,1},{1,0},{2,3},{3,2},{4,5},{5,4},{6,7},{7,6},{8,9},{9,8},{10,11... | collective-permute-start | bytes 1179656 | tf_op jit(solution)/shard_map/ppermute | solution.py:1222
  137.2 22.4 %collective-permute-start.3 = (bf16[272,1536]{1,0:T(8,128)(2,1)}, bf16[272,1536]{1,0:T(8,128)(2,1)S(1)}, u32[]{:S(2)}, u32[]{:S(2)}) collective-permute-start(bf16[272,1536]{1,0:T(8,128)(2,1)} %get-tuple-element.110), channel_id=1, source_target_pairs={{0,1},{1,0},{2,3},{3,2},{4,5},{5,4},{6,7},{7,6},{8,9},{9,8},{10,11... | collective-permute-start | bytes 2506760 | tf_op jit(solution)/shard_map/ppermute | solution.py:1271
  148.8 29.1 %collective-permute-start.5 = (bf16[272,1536]{1,0:T(8,128)(2,1)}, bf16[272,1536]{1,0:T(8,128)(2,1)S(1)}, u32[]{:S(2)}, u32[]{:S(2)}) collective-permute-start(bf16[272,1536]{1,0:T(8,128)(2,1)} %get-tuple-element.113), channel_id=1, source_target_pairs={{0,1},{1,0},{2,3},{3,2},{4,5},{5,4},{6,7},{7,6},{8,9},{9,8},{10,11... | collective-permute-start | bytes 2506760 | tf_op jit(solution)/shard_map/ppermute | solution.py:1271
  177.6 19.6 %collective-permute-start.4 = (bf16[272,1536]{1,0:T(8,128)(2,1)}, bf16[272,1536]{1,0:T(8,128)(2,1)S(1)}, u32[]{:S(2)}, u32[]{:S(2)}) collective-permute-start(bf16[272,1536]{1,0:T(8,128)(2,1)} %get-tuple-element.111), channel_id=1, source_target_pairs={{0,1},{1,0},{2,3},{3,2},{4,5},{5,4},{6,7},{7,6},{8,9},{9,8},{10,11... | collective-permute-start | bytes 2506760 | tf_op jit(solution)/shard_map/ppermute | solution.py:1291
  195.5 19.4 %collective-permute-start.6 = (bf16[272,1536]{1,0:T(8,128)(2,1)}, bf16[272,1536]{1,0:T(8,128)(2,1)S(1)}, u32[]{:S(2)}, u32[]{:S(2)}) collective-permute-start(bf16[272,1536]{1,0:T(8,128)(2,1)} %get-tuple-element.117), channel_id=1, source_target_pairs={{0,1},{1,0},{2,3},{3,2},{4,5},{5,4},{6,7},{7,6},{8,9},{9,8},{10,11... | collective-permute-start | bytes 2506760 | tf_op jit(solution)/shard_map/ppermute | solution.py:1291
  226.5 144.9 %reduce-scatter.5.cloned.1.call-start = ((), (), s32[]{:S(2)}) async-start(), calls=%async_computation.3 | async-start | bytes 983040 | tf_op jit(solution)/shard_map/reduce_scatter | solution.py:1494
  240.2 12.6 %collective-permute-start.7 = (bf16[512,384]{1,0:T(8,128)(2,1)}, bf16[512,384]{1,0:T(8,128)(2,1)S(1)}, u32[]{:S(2)}, u32[]{:S(2)}) collective-permute-start(bf16[512,384]{1,0:T(8,128)(2,1)} %get-tuple-element.128), channel_id=1, source_target_pairs={{0,1},{1,0},{2,3},{3,2},{4,5},{5,4},{6,7},{7,6},{8,9},{9,8},{10,11... | collective-permute-start | bytes 1179656 | tf_op jit(solution)/shard_map/ppermute | solution.py:1387
  250.1 28.5 %collective-permute-start.9 = (bf16[512,384]{1,0:T(8,128)(2,1)}, bf16[512,384]{1,0:T(8,128)(2,1)S(1)}, u32[]{:S(2)}, u32[]{:S(2)}) collective-permute-start(bf16[512,384]{1,0:T(8,128)(2,1)} %get-tuple-element.132), channel_id=1, source_target_pairs={{0,1},{1,0},{2,3},{3,2},{4,5},{5,4},{6,7},{7,6},{8,9},{9,8},{10,11... | collective-permute-start | bytes 1179656 | tf_op jit(solution)/shard_map/ppermute | solution.py:1387
  259.4 17.2 %collective-permute-start.8 = (bf16[4,2,96,384]{3,2,0,1:T(8,128)(2,1)S(1)}, bf16[4,2,96,384]{3,2,0,1:T(8,128)(2,1)S(1)}, u32[]{:S(2)}, u32[]{:S(2)}) collective-permute-start(bf16[4,2,96,384]{3,2,0,1:T(8,128)(2,1)S(1)} %get-tuple-element.227), channel_id=1, source_target_pairs={{0,2},{2,0},{4,6},{6,4},{8,10},{10,8},{12,14},{14,12},{16,18},{18,... | collective-permute-start | bytes 1769480 | tf_op jit(solution)/shard_map/ppermute | solution.py:1343
  277.7 26.5 %collective-permute-start.10 = (bf16[4,96,384]{2,1,0:T(8,128)(2,1)}, bf16[4,96,384]{2,1,0:T(8,128)(2,1)}, u32[]{:S(2)}, u32[]{:S(2)}) collective-permute-start(bf16[4,96,384]{2,1,0:T(8,128)(2,1)} %get-tuple-element.225), channel_id=1, source_target_pairs={{0,4},{2,6},{4,0},{6,2},{8,12},{10,14},{12,8},{14,10},{16,20},{18,... | collective-permute-start | bytes 884744 | tf_op jit(solution)/shard_map/ppermute | solution.py:1354
  315.1 2.7 collective-permute-start.11
  318.9 13.1 %collective-permute-start.12 = (bf16[4,144,384]{2,1,0:T(8,128)(2,1)S(1)}, bf16[4,144,384]{2,1,0:T(8,128)(2,1)S(1)}, u32[]{:S(2)}, u32[]{:S(2)}) collective-permute-start(bf16[4,144,384]{2,1,0:T(8,128)(2,1)S(1)} %get-tuple-element.211), channel_id=1, source_target_pairs={{0,4},{2,6},{4,0},{6,2},{8,12},{10,14},{12,8},{14,10},{16,20},{18,... | collective-permute-start | bytes 1327112 | tf_op jit(solution)/shard_map/ppermute | solution.py:1354
  320.9 19.6 %collective-permute-start.15 = (bf16[4,2,16,384]{3,2,0,1:T(8,128)(2,1)S(1)}, bf16[4,2,16,384]{3,2,0,1:T(8,128)(2,1)S(1)}, u32[]{:S(2)}, u32[]{:S(2)}) collective-permute-start(bf16[4,2,16,384]{3,2,0,1:T(8,128)(2,1)S(1)} %get-tuple-element.253), channel_id=1, source_target_pairs={{0,2},{2,0},{4,6},{6,4},{8,10},{10,8},{12,14},{14,12},{16,18},{18,... | collective-permute-start | bytes 294920 | tf_op jit(solution)/shard_map/ppermute | solution.py:1343
  328.3 20.5 %collective-permute-start.14 = (bf16[512,768]{1,0:T(8,128)(2,1)}, bf16[512,768]{1,0:T(8,128)(2,1)S(1)}, u32[]{:S(2)}, u32[]{:S(2)}) collective-permute-start(bf16[512,768]{1,0:T(8,128)(2,1)} %get-tuple-element.148), channel_id=1, source_target_pairs={{0,1},{1,0},{2,3},{3,2},{4,5},{5,4},{6,7},{7,6},{8,9},{9,8},{10,11... | collective-permute-start | bytes 2359304 | tf_op jit(solution)/shard_map/ppermute | solution.py:1449
  339.1 26.2 %collective-permute-start.13 = (bf16[512,768]{1,0:T(8,128)(2,1)}, bf16[512,768]{1,0:T(8,128)(2,1)S(1)}, u32[]{:S(2)}, u32[]{:S(2)}) collective-permute-start(bf16[512,768]{1,0:T(8,128)(2,1)} %get-tuple-element.145), channel_id=1, source_target_pairs={{0,1},{1,0},{2,3},{3,2},{4,5},{5,4},{6,7},{7,6},{8,9},{9,8},{10,11... | collective-permute-start | bytes 2359304 | tf_op jit(solution)/shard_map/ppermute | solution.py:1449
  341.2 4.1 %collective-permute-start.16 = (bf16[4,16,384]{2,1,0:T(8,128)(2,1)S(1)}, bf16[4,16,384]{2,1,0:T(8,128)(2,1)S(1)}, u32[]{:S(2)}, u32[]{:S(2)}) collective-permute-start(bf16[4,16,384]{2,1,0:T(8,128)(2,1)S(1)} %get-tuple-element.250), channel_id=1, source_target_pairs={{0,4},{2,6},{4,0},{6,2},{8,12},{10,14},{12,8},{14,10},{16,20},{18,... | collective-permute-start | bytes 147464 | tf_op jit(solution)/shard_map/ppermute | solution.py:1354
  371.4 6.9 %collective-permute-start.17 = (bf16[256,384]{1,0:T(8,128)(2,1)}, bf16[256,384]{1,0:T(8,128)(2,1)S(1)}, u32[]{:S(2)}, u32[]{:S(2)}) collective-permute-start(bf16[256,384]{1,0:T(8,128)(2,1)} %bitcast.97), channel_id=1, source_target_pairs={{0,1},{1,0},{2,3},{3,2},{4,5},{5,4},{6,7},{7,6},{8,9},{9,8},{10,11... | collective-permute-start | bytes 589832 | tf_op jit(solution)/shard_map/ppermute | solution.py:1502
  (30 other events, 86.8 us)
Sparse Core Ops, SparseCore 0:
  13.7 48.1 all-gather.4
  64.7 80.2 all-gather.6
  226.6 109.9 reduce-scatter.2
  348.5 22.3 reduce-scatter.4

commit v6 on v5

--- a/solution.py
+++ b/solution.py
@@ -515,7 +515,7 @@
     return outs[0], list(outs[1:])
 
 
-def finish_kernel(received, own_ref, rows_ref, gain_ref, mid_ref, *refs):
+def finish_kernel(received, own_ref, rows_ref, gain_ref, mid_ref, after_ref, *refs):
     total = own_ref[...]
     for ref in refs[:received]:
         total = total + ref[...].astype(float32)
@@ -523,15 +523,16 @@
     refs[-1][0] = mid_ref[...] + grad
 
 
-def finish(batch, own, received, rows, gain, mid, buffer):
+def finish(batch, own, received, rows, gain, mid, buffer, after):
     batches, count, width = rows.shape
     row_spec = pl.BlockSpec((1, count, width), lambda i: (batch, 0, 0))
 
     def full(array):
         return pl.BlockSpec(array.shape, lambda i: (0,) * array.ndim)
 
-    operands = [own, rows, gain, mid] + received
-    in_specs = [full(own), row_spec, full(gain), full(mid)] + [full(part) for part in received]
+    operands = [own, rows, gain, mid, after] + received
+    in_specs = [full(own), row_spec, full(gain), full(mid), pl.BlockSpec(memory_space=pl.ANY)]
+    in_specs = in_specs + [full(part) for part in received]
     aliases = {}
     if buffer is not None:
         aliases = {len(operands): 0}
@@ -549,7 +550,8 @@
     )(*operands)
 
 
-def dense_kernel(batches, weighted, blocks, after_ref, *refs):
+def dense_kernel(skipped, batches, weighted, blocks, *refs):
+    refs = refs[skipped:]
     out_ref = refs[2 * batches + weighted]
     left = jnp.concatenate([ref[...] for ref in refs[:batches]], axis=0)
     right = jnp.concatenate([ref[...] for ref in refs[batches : 2 * batches]], axis=0)
@@ -568,7 +570,7 @@
         refs[-1][...] = jnp.sum(term, axis=1, keepdims=True)
 
 
-def dense_grad(left, right, lanes, shards, direct, after, packed=None):
+def dense_grad(left, right, lanes, shards, direct, afters, packed=None):
     batches = len(left)
     count, width = left[0].shape
     columns = right[0].shape[1]
@@ -579,9 +581,9 @@
     inner = depth if direct else width
     weighted = 0 if packed is None else 1
     outs = pl.pallas_call(
-        functools.partial(dense_kernel, batches, weighted, blocks),
+        functools.partial(dense_kernel, len(afters), batches, weighted, blocks),
         grid=(steps,),
-        in_specs=[pl.BlockSpec(memory_space=pl.ANY)]
+        in_specs=[pl.BlockSpec(memory_space=pl.ANY)] * len(afters)
         + [pl.BlockSpec((count, width // steps), lambda i: (0, i))] * batches
         + [pl.BlockSpec((count, columns), lambda i: (0, 0))] * batches
         + [pl.BlockSpec((outer, blocks * inner, lanes), lambda i: (i, 0, 0))] * weighted,
@@ -596,7 +598,7 @@
             transcendentals=0,
         ),
         name="dense_grad",
-    )(after, *left, *right, *([packed] if weighted else []))
+    )(*afters, *left, *right, *([packed] if weighted else []))
     out = outs[0]
     if not direct:
         out = jnp.transpose(out.reshape(blocks, shards, depth, lanes), (1, 0, 2, 3))
@@ -870,7 +872,8 @@
     )(probs, outs, inverse, qkv, qkv, qkv, offsets, after, *grads, *sums)
 
 
-def add_kernel(after_ref, *refs):
+def add_kernel(skipped, *refs):
+    refs = refs[skipped:]
     out_ref = refs[-1]
     start = 0
     for left_ref, right_ref in zip(refs[:-1:2], refs[1:-1:2]):
@@ -881,18 +884,18 @@
         start += rows
 
 
-def add_after(after, *operands):
+def add_after(afters, *operands):
     vmem = pl.BlockSpec(memory_space=pltpu.VMEM)
     outer, _, lanes = operands[0].shape
     rows = sum(operand.shape[1] for operand in operands[::2])
     return pl.pallas_call(
-        add_kernel,
-        in_specs=[pl.BlockSpec(memory_space=pl.ANY)] + [vmem] * len(operands),
+        functools.partial(add_kernel, len(afters)),
+        in_specs=[pl.BlockSpec(memory_space=pl.ANY)] * len(afters) + [vmem] * len(operands),
         out_specs=vmem,
         out_shape=jax.ShapeDtypeStruct((outer, rows, lanes), bfloat),
         compiler_params=params(),
         name="add_after",
-    )(after, *operands)
+    )(*afters, *operands)
 
 
 def order_kernel(count, place_ref, *refs):
@@ -1232,6 +1235,7 @@
     normed_two = []
     router_probs = []
     blocks = []
+    after = table
     for batch in range(batches):
         normed, packed_rows = project(batch, ordered_in, gain_one, packed, pairs, scale)
         normed_one.append(normed)
@@ -1241,7 +1245,7 @@
             ends[batch],
             bias,
             far,
-            arrived_heads[-1][-1] if arrived_heads else table,
+            after,
             head_dim,
             members,
         )
@@ -1249,11 +1253,10 @@
         outs.append(joined)
         inverses.append(inverse)
         arrived_heads.append(send_rows(batch, joined))
-    for batch in range(batches):
         mid, normed, chances, outgoing = middle(
             batch,
             me_row,
-            outs[batch],
+            joined,
             arrived_heads[batch],
             offsets,
             output_w,
@@ -1263,8 +1266,9 @@
             router_wide,
             routes,
             dispatch,
-            outs[-1],
-        )
+            blocks[-1][-1] if blocks else table,
+        )
+        after = outgoing[-1]
         blocks.append(
             [outgoing[0]]
             + [
@@ -1311,7 +1315,7 @@
             True,
             buffer_shape,
             pl.BlockSpec((group, depth_out, width), lambda i: (i, 1, 0)),
-            returned[-1][-1],
+            returned[0][-1],
             buffer,
         )
     else:
@@ -1405,12 +1409,26 @@
         for batch in range(batches)
     ]
     early_core = by_core(
-        dense_grad(attended, grad_attn, lanes, shards, direct, grad_heads[0][-1])
+        dense_grad(attended, grad_attn, lanes, shards, direct, [grad_heads[0][-1]])
     )
     early = by_y(early_core)
     grad_qkv = []
     sums = []
+    own_rows = []
+    received_rows = []
+    sent_last = buffer
+
+    def first_part(batch, after):
+        own, sent = first_back(batch, grad_qkv[batch], packed, pairs, width, offsets, after)
+        own_rows.append(own)
+        received_rows.append(
+            [lax.ppermute(rows, "expert", around(-step)) for step, rows in enumerate(sent, 1)]
+        )
+        return sent[-1]
+
     for batch in range(batches):
+        if batch > 0:
+            sent_last = first_part(batch - 1, buffer)
         grads, *sums = attend_back(
             batch,
             probs[batch],
@@ -1419,7 +1437,7 @@
             inverses[batch],
             qkv[batch],
             offsets,
-            buffer if batch == 0 else early_core[1],
+            sent_last,
             sums,
             head_dim,
             members,
@@ -1428,29 +1446,18 @@
         grad_qkv.append(grads)
     grad_bias, grad_far = sums
     grad_dense, weighted = dense_grad(
-        normed_one, grad_qkv, lanes, shards, direct, early[1], packed
+        normed_one,
+        grad_qkv,
+        lanes,
+        shards,
+        direct,
+        [early[1]] + [rows[-1] for rows in received_rows],
+        packed,
     )
     grad_gain_one = weighted[:, 0] / gain_one[0]
     late_core = by_core(grad_dense)
     late = by_y(late_core)
-
-    in_grad = None
-    for batch in range(batches):
-        own_rows, sent = first_back(
-            batch,
-            grad_qkv[batch],
-            packed,
-            pairs,
-            width,
-            offsets,
-            late_core[1] if batch == 0 else late[1],
-        )
-        received = [
-            lax.ppermute(rows, "expert", around(-step)) for step, rows in enumerate(sent, 1)
-        ]
-        in_grad = finish(
-            batch, own_rows, received, hidden_in, gain_one, grad_mid[batch], in_grad
-        )
+    sent_last = first_part(batches - 1, late_core[1])
 
     steps = 2 * members - 1
     reach = near_shift(tiles)
@@ -1491,8 +1498,21 @@
     small_grad = jnp.pad(small_grad, ((0, 0), (0, small_pad * lanes - small_used)))
     small_grad = small_grad.astype(bfloat).reshape(shards, small_pad, lanes)
     little = by_y(by_core(small_grad))
+    dense_added = add_after([expert_sum, sent_last], *late, *little, *early)
+    in_grad = None
+    for batch in range(batches):
+        in_grad = finish(
+            batch,
+            own_rows[batch],
+            received_rows[batch],
+            hidden_in,
+            gain_one,
+            grad_mid[batch],
+            in_grad,
+            buffer if batch < batches - 1 else dense_added,
+        )
     dense_part = lax.psum_scatter(
-        add_after(expert_sum, *late, *little, *early),
+        dense_added,
         "dp",
         scatter_dimension=0,
         tiled=False,

time: 395 us -> 397 us (level)
    ppermute x2, waiting for transfers between devices: 10.5 us -> 0.8 us  [on_device(): lax.ppermute(outgoing[step], 'expert', around(step))]
    reduce_scatter x1, waiting for transfers between devices: 0.01 us -> 6.07 us  [on_device(): lax.psum_scatter(dense_added, 'dp', scatter_dimension=0, tiled=False, axi...]
    ppermute x2, waiting for transfers between devices: 11.8 us -> 5.79 us  [first_part(): lax.ppermute(rows, 'expert', around(-step))]
    ppermute x2, waiting for transfers between devices: 3.64 us -> 9.2 us  [send_rows(): arrived.append(lax.ppermute(rows, 'expert', around(step)))]
    ppermute x3, waiting for transfers between devices: 5.29 us -> 10.8 us  [by_y(): lax.ppermute(sent, 'dp', [(idx, idx ^ 2) for idx in range(shards)])]
    unnamed x82 -> x84, local copies, waits for them, and re-layouts: 18.3 us -> 18.2 us
  transfers between devices with their start and end apart: 22 -> 22, of which waited for: 11 -> 12; matrix products, arithmetic and copies ran while one was open for 10% -> 10% of each run, Pallas kernels for 53% -> 49%
where the time goes in v6:
time: 397 us; the launch traced here: 393 us
  Pallas kernels  216 us (54%)
  waiting for transfers between devices  79.4 us (20%)
  local copies, waits for them, and re-layouts  37.1 us (9%)
  other arithmetic  23.7 us (6%)
  starting transfers between devices  18.4 us (5%)
  between operations  14.8 us (4%)
    pallas_call x2, Pallas kernels, attend_back(): pl.pallas_call(functools.partial(attend_back_kernel, stride, head_dim, he...  35.4 us
    pallas_call x2, Pallas kernels, attend(): pl.pallas_call(functools.partial(attend_kernel, stride, head_dim), grid=(...  35.3 us
    pallas_call x2, Pallas kernels, run_expert(): pl.pallas_call(functools.partial(expert_kernel, count, slots, width), gri...  33.6 us
    ppermute x1, waiting for transfers between devices, on_device(): lax.ppermute(hidden_in, 'expert', around(step))  31 us
    pallas_call x2, Pallas kernels, expert_grad(): pl.pallas_call(body, grid=(turns,), in_specs=in_specs, out_specs=out_spec...  21.4 us
    unnamed x84, local copies, waits for them, and re-layouts  18.2 us
    pallas_call x2, Pallas kernels, second_back(): pl.pallas_call(functools.partial(second_kernel, members, members, aliased...  16.4 us
    pallas_call x2, Pallas kernels, dense_grad(): pl.pallas_call(functools.partial(dense_kernel, len(afters), batches, weig...  13.1 us
  transfers between devices with their start and end apart: 22, of which 12 were waited for; matrix products, arithmetic and copies ran while one was open for 10% of the time, Pallas kernels for 49%

profile of v6, /device:TPU:0, one launch (start us, length us, event | category | flops | bytes accessed | tf_op | source)
XLA Modules:
  0.0 393.0 jit_solution(4742432834717521963)
XLA Ops:
  20.2 31.0 %collective-permute-done.after_ref.refs_1_ = bf16[2,512,768]{2,1,0:T(8,128)(2,1)S(1)} collective-permute-done((bf16[2,512,768]{2,1,0:T(8,128)(2,1)}, bf16[2,512,768]{2,1,0:T(8,128)(2,1)S(1)}, u32[]{:S(2)}, u32[]{:S(2)}) %collective-permute-start) | collective-permute-done | bytes 1572896 | tf_op jit(solution)/shard_map/ppermute | solution.py:1132
  67.9 5.0 %bias_tiles.1.bias_ref = f32[6,3,128,384]{3,2,1,0:T(8,128)} custom-call(f32[6,128]{1,0:T(8,128)} %pad.22.clone.table_ref), custom_call_target="tpu_custom_call" | custom-call | tf_op jit(solution)/shard_map/bias_tiles/pallas_call | solution.py:79
  73.5 5.8 %project.3 = (bf16[1024,768]{1,0:T(8,128)(2,1)}, bf16[1024,1152]{1,0:T(8,128)(2,1)}) custom-call(bf16[2,1024,768]{2,1,0:T(8,128)(2,1)} %bitcast.106, f32[1,768]{1,0:T(1,128)} %reshape.333.gain_ref, bf16[16,256,384]{2,1,0:T(8,128)(2,1)} %get-tuple-element.98.weight_ref.refs_6_), custom_call_target="tpu_custom_call" | custom-call | flops 1811939328 | bytes 4718592 | tf_op jit(solution)/shard_map/project/pallas_call | solution.py:108
  79.3 17.7 %attend.2 = (bf16[6,1024,1024]{2,1,0:T(8,128)(2,1)}, bf16[1024,384]{1,0:T(8,128)(2,1)}, f32[1024,384]{1,0:T(8,128)}) custom-call(f32[2,6]{1,0:T(2,128)} %pad_maximum_fusion.4.far_ref, s32[1]{0:T(128)} %bitcast.13.ends_ref, bf16[1024,1152]{1,0:T(8,128)(2,1)} %get-tuple-element.101.q_ref.k_ref.v_ref, bf16[1024,1152]{1,0:T(8,128)(2,1)} %get-tuple-element.101.q_ref.k_ref.v_ref, ...), custom_call_target="tpu_custom_call" | custom-call | flops 6442450944 | bytes 12582912 | tf_op jit(solution)/shard_map/attend/pallas_call | solution.py:720
  104.0 6.1 %project.2 = (bf16[1024,768]{1,0:T(8,128)(2,1)}, bf16[1024,1152]{1,0:T(8,128)(2,1)}) custom-call(bf16[2,1024,768]{2,1,0:T(8,128)(2,1)} %bitcast.107, f32[1,768]{1,0:T(1,128)} %reshape.333.gain_ref, bf16[16,256,384]{2,1,0:T(8,128)(2,1)} %get-tuple-element.98.weight_ref.refs_6_), custom_call_target="tpu_custom_call" | custom-call | flops 1811939328 | bytes 4718592 | tf_op jit(solution)/shard_map/project/pallas_call | solution.py:108
  110.9 6.2 %middle.2 = (f32[512,768]{1,0:T(8,128)}, bf16[512,768]{1,0:T(8,128)(2,1)}, f32[512,128]{1,0:T(8,128)}, bf16[272,1536]{1,0:T(8,128)(2,1)}, bf16[272,1536]{1,0:T(8,128)(2,1)}) custom-call(s32[1]{0:T(128)} %bitcast.me_ref, bf16[1024,384]{1,0:T(8,128)(2,1)} %get-tuple-element.102.joined_ref.out_ref, s32[2,512,2]{2,1,0:T(8,128)} %get-tuple-element.97.place_ref.offset_ref, ...), custom_call_target="tpu_custom_call" | custom-call | flops 14495514624 | bytes 4718592 | tf_op jit(solution)/shard_map/middle/pallas_call | solution.py:297
  118.0 17.6 %attend.3 = (bf16[6,1024,1024]{2,1,0:T(8,128)(2,1)}, bf16[1024,384]{1,0:T(8,128)(2,1)}, f32[1024,384]{1,0:T(8,128)}) custom-call(f32[2,6]{1,0:T(2,128)} %pad_maximum_fusion.4.far_ref, s32[1]{0:T(128)} %bitcast.10.ends_ref, bf16[1024,1152]{1,0:T(8,128)(2,1)} %get-tuple-element.100.q_ref.k_ref.v_ref, bf16[1024,1152]{1,0:T(8,128)(2,1)} %get-tuple-element.100.q_ref.k_ref.v_ref, ...), custom_call_target="tpu_custom_call" | custom-call | flops 6442450944 | bytes 12582912 | tf_op jit(solution)/shard_map/attend/pallas_call | solution.py:720
  138.1 9.2 %collective-permute-done.3.refs_0_ = bf16[512,384]{1,0:T(8,128)(2,1)S(1)} collective-permute-done((bf16[512,384]{1,0:T(8,128)(2,1)S(1)}, bf16[512,384]{1,0:T(8,128)(2,1)S(1)}, u32[]{:S(2)}, u32[]{:S(2)}) %collective-permute-start.3) | collective-permute-done | bytes 393248 | tf_op jit(solution)/shard_map/ppermute | solution.py:1225
  148.9 6.2 %middle.3 = (f32[512,768]{1,0:T(8,128)}, bf16[512,768]{1,0:T(8,128)(2,1)}, f32[512,128]{1,0:T(8,128)}, bf16[272,1536]{1,0:T(8,128)(2,1)}, bf16[272,1536]{1,0:T(8,128)(2,1)}) custom-call(s32[1]{0:T(128)} %bitcast.me_ref, bf16[1024,384]{1,0:T(8,128)(2,1)} %get-tuple-element.105.joined_ref.out_ref, s32[2,512,2]{2,1,0:T(8,128)} %get-tuple-element.97.place_ref.offset_ref, ...), custom_call_target="tpu_custom_call" | custom-call | flops 14495514624 | bytes 4718592 | tf_op jit(solution)/shard_map/middle/pallas_call | solution.py:297
  156.9 17.1 %run_expert.2 = (bf16[272,1536]{1,0:T(8,128)(2,1)}, bf16[272,1536]{1,0:T(8,128)(2,1)}, bf16[544,3072]{1,0:T(8,128)(2,1)}, bf16[544,3072]{1,0:T(8,128)(2,1)}) custom-call(bf16[16,384,768]{2,1,0:T(8,128)(2,1)} %bitcast.102, bf16[16,384,768]{2,1,0:T(8,128)(2,1)} %bitcast.103, bf16[32,12]{1,0:T(8,128)(2,1)} %copy-done.26, ...), custom_call_target="tpu_custom_call" | custom-call | flops 10267656192 | bytes 9437184 | tf_op jit(solution)/shard_map/run_expert/pallas_call | solution.py:990
  176.0 16.6 %run_expert.3 = (bf16[272,1536]{1,0:T(8,128)(2,1)}, bf16[272,1536]{1,0:T(8,128)(2,1)}, bf16[544,3072]{1,0:T(8,128)(2,1)}, bf16[544,3072]{1,0:T(8,128)(2,1)}) custom-call(bf16[16,384,768]{2,1,0:T(8,128)(2,1)} %bitcast.104, bf16[16,384,768]{2,1,0:T(8,128)(2,1)} %bitcast.105, bf16[544,3072]{1,0:T(8,128)(2,1)} %get-tuple-element.115.after_ref.refs_6_, ...), custom_call_target="tpu_custom_call" | custom-call | flops 10267656192 | bytes 9437184 | tf_op jit(solution)/shard_map/run_expert/pallas_call | solution.py:990
  194.4 10.7 %expert_grad_inner.1.refs_0_ = bf16[16,384,768]{2,1,0:T(8,128)(2,1)} custom-call(bf16[272,1536]{1,0:T(8,128)(2,1)} %copy-done, bf16[272,1536]{1,0:T(8,128)(2,1)} %get-tuple-element.110.refs_0_.refs_1_.refs_2_, bf16[272,1536]{1,0:T(8,128)(2,1)} %copy-done.2, bf16[272,1536]{1,0:T(8,128)(2,1)} %get-tuple-element.112.refs_0_.refs_3_.refs_4_, ...), custom_call_target="tpu_custom_call" | custom-call | flops 5133828096 | bytes 9437184 | tf_op jit(solution)/shard_map/expert_grad_inner/pallas_call | solution.py:1055
  205.1 10.7 %expert_grad_outer.1.after_ref = bf16[16,384,768]{2,1,0:T(8,128)(2,1)} custom-call(bf16[16,384,768]{2,1,0:T(8,128)(2,1)} %expert_grad_inner.1.refs_0_, bf16[272,1536]{1,0:T(8,128)(2,1)} %copy-done, bf16[272,1536]{1,0:T(8,128)(2,1)} %get-tuple-element.110.refs_0_.refs_1_.refs_2_, bf16[272,1536]{1,0:T(8,128)(2,1)} %copy-done.2, ...), custom_call_target="tpu_custom_call", output_to_operand_aliasing={{}: (0, {})} | custom-call | flops 5133828096 | bytes 9437184 | tf_op jit(solution)/shard_map/expert_grad_outer/pallas_call | solution.py:1055
  222.4 8.6 %second_back.2 = (bf16[2,512,768]{2,1,0:T(8,128)(2,1)}, f32[512,768]{1,0:T(8,128)}, bf16[512,768]{1,0:T(8,128)(2,1)}, f32[1,768]{1,0:T(1,128)}, f32[128,768]{1,0...) custom-call(s32[1]{0:T(128)} %bitcast.me_ref, bf16[2,512,544]{2,1,0:T(8,128)(2,1)} %get-tuple-element.96.back_ref, ...), custom_call_target="tpu_custom_call" | custom-call | flops 1811939328 | bytes 4718592 | tf_op jit(solution)/shard_map/second_back/pallas_call | solution.py:417
  231.5 8.5 %collective-permute-done.6.refs_1_ = bf16[272,1536]{1,0:T(8,128)(2,1)S(1)} collective-permute-done((bf16[272,1536]{1,0:T(8,128)(2,1)}, bf16[272,1536]{1,0:T(8,128)(2,1)S(1)}, u32[]{:S(2)}, u32[]{:S(2)}) %collective-permute-start.6) | collective-permute-done | bytes 835616 | tf_op jit(solution)/shard_map/ppermute | solution.py:1295
  240.9 7.8 %second_back.3 = (bf16[2,512,768]{2,1,0:T(8,128)(2,1)}, f32[512,768]{1,0:T(8,128)}, bf16[512,768]{1,0:T(8,128)(2,1)}, f32[1,768]{1,0:T(1,128)}, f32[128,768]{1,0...) custom-call(s32[1]{0:T(128)} %bitcast.me_ref, ...), custom_call_target="tpu_custom_call", output_to_operand_aliasing={{0}: (13, {})} | custom-call | flops 1811939328 | bytes 4718592 | tf_op jit(solution)/shard_map/second_back/pallas_call | solution.py:417
  259.6 17.2 %attend_back.2 = (bf16[1024,1152]{1,0:T(8,128)(2,1)}, f32[6,3,128,384]{3,2,1,0:T(8,128)}, f32[6,2,128,128]{3,2,1,0:T(8,128)}) custom-call(bf16[6,1024,1024]{2,1,0:T(8,128)(2,1)} %get-tuple-element.128.probs_ref, bf16[1024,384]{1,0:T(8,128)(2,1)} %get-tuple-element.102.joined_ref.out_ref, f32[1024,384]{1,0:T(8,128)} %get-tuple-element.129.inv_ref, ...), custom_call_target="tpu_custom_call" | custom-call | flops 12884901888 | bytes 12582912 | tf_op jit(solution)/shard_map/attend_back/pallas_call | solution.py:844
  276.8 6.2 %first_back.2 = (f32[512,768]{1,0:T(8,128)}, bf16[512,768]{1,0:T(8,128)(2,1)}) custom-call(bf16[1024,1152]{1,0:T(8,128)(2,1)} %get-tuple-element.132.grads_ref.refs_4_, bf16[16,256,384]{2,1,0:T(8,128)(2,1)} %get-tuple-element.98.weight_ref.refs_6_, s32[2,512,2]{2,1,0:T(8,128)} %get-tuple-element.97.place_ref.offset_ref, ...), custom_call_target="tpu_custom_call" | custom-call | flops 1811939328 | bytes 6291456 | tf_op jit(solution)/shard_map/first_back/pallas_call | solution.py:496
  284.3 18.2 %attend_back.3 = (bf16[1024,1152]{1,0:T(8,128)(2,1)}, f32[6,3,128,384]{3,2,1,0:T(8,128)}, f32[6,2,128,128]{3,2,1,0:T(8,128)}) custom-call(bf16[6,1024,1024]{2,1,0:T(8,128)(2,1)} %get-tuple-element.126.probs_ref, bf16[1024,384]{1,0:T(8,128)(2,1)} %get-tuple-element.105.joined_ref.out_ref, ...), custom_call_target="tpu_custom_call", output_to_operand_aliasing={{1}: (10, {}), {2}: (11, {})} | custom-call | flops 12884901888 | bytes 12582912 | tf_op jit(solution)/shard_map/attend_back/pallas_call | solution.py:844
  311.5 8.4 %collective-permute-done.10.refs_0_.refs_7_ = bf16[4,96,384]{2,1,0:T(8,128)(2,1)S(1)} collective-permute-done((bf16[4,96,384]{2,1,0:T(8,128)(2,1)S(1)}, bf16[4,96,384]{2,1,0:T(8,128)(2,1)S(1)}, u32[]{:S(2)}, u32[]{:S(2)}) %collective-permute-start.10) | collective-permute-done | bytes 294944 | tf_op jit(solution)/shard_map/ppermute | solution.py:1358
  320.6 8.7 %dense_grad.3 = (bf16[16,144,384]{2,1,0:T(8,128)(2,1)}, f32[768,1]{1,0:T(8,128)}) custom-call(bf16[4,96,384]{2,1,0:T(8,128)(2,1)} %copy-done.19, bf16[512,768]{1,0:T(8,128)(2,1)} %copy-done.9, bf16[1024,768]{1,0:T(8,128)(2,1)} %get-tuple-element.141.refs_2_, bf16[1024,768]{1,0:T(8,128)(2,1)} %get-tuple-element.142.refs_3_, ...), custom_call_target="tpu_custom_call" | custom-call | flops 3623878656 | bytes 3145728 | tf_op jit(solution)/shard_map/dense_grad/pallas_call | solution.py:583
  336.0 6.3 %first_back.3 = (f32[512,768]{1,0:T(8,128)}, bf16[512,768]{1,0:T(8,128)(2,1)}) custom-call(bf16[1024,1152]{1,0:T(8,128)(2,1)} %get-tuple-element.138.refs_5_.grads_ref, bf16[16,256,384]{2,1,0:T(8,128)(2,1)} %get-tuple-element.98.weight_ref.refs_6_, s32[2,512,2]{2,1,0:T(8,128)} %get-tuple-element.97.place_ref.offset_ref, bf16[4,2,144,384]{3,2,1,0:T(8,128)(2,1)} %copy.127.after_ref), custom_call_target="tpu_custom_call" | custom-call | flops 1811939328 | bytes 6291456 | tf_op jit(solution)/shard_map/first_back/pallas_call | solution.py:496
  356.0 5.8 %collective-permute-done.16.refs_0_ = bf16[512,768]{1,0:T(8,128)(2,1)S(1)} collective-permute-done((bf16[512,768]{1,0:T(8,128)(2,1)}, bf16[512,768]{1,0:T(8,128)(2,1)S(1)}, u32[]{:S(2)}, u32[]{:S(2)}) %collective-permute-start.16) | collective-permute-done | bytes 786464 | tf_op jit(solution)/shard_map/ppermute | solution.py:1425
  367.9 6.1 %reduce-scatter.5.cloned.1.call-done = bf16[1,256,384]{2,1,0:T(8,128)(2,1)} async-done(((bf16[4,256,384]{2,1,0:T(8,128)(2,1)}), bf16[1,256,384]{2,1,0:T(8,128)(2,1)}) %reduce-scatter.5.cloned.1.call-update) | async-done | bytes 196624 | tf_op jit(solution)/shard_map/reduce_scatter | solution.py:1514
  (219 shorter events, 116.4 us)
Async XLA Ops:
  7.2 54.7 %all-gather.5.cloned.1.call-start = ((), (), s32[]{:S(2)}) async-start(), calls=%async_computation.4 | async-start | bytes 3342336 | tf_op jit(solution)/shard_map/all_gather | solution.py:1156
  13.6 143.3 %all-gather.7.cloned.1.call-start = ((), (), s32[]{:S(2)}) async-start(), calls=%async_computation.5 | async-start | bytes 10027008 | tf_op jit(solution)/shard_map/all_gather | solution.py:1163
  13.6 37.6 %collective-permute-start = (bf16[2,512,768]{2,1,0:T(8,128)(2,1)}, bf16[2,512,768]{2,1,0:T(8,128)(2,1)S(1)}, u32[]{:S(2)}, u32[]{:S(2)}) collective-permute-start(bf16[2,512,768]{2,1,0:T(8,128)(2,1)} %rows_ref.7), channel_id=1, source_target_pairs={{0,1},{1,0},{2,3},{3,2},{4,5},{5,4},{6,7},{7,6},{8,9},{9,8},{10,11... | collective-permute-start | bytes 4718600 | tf_op jit(solution)/shard_map/ppermute | solution.py:1132
  20.2 31.0 %copy-start.6 = (bf16[384,768]{1,0:T(8,128)(2,1)}, bf16[384,768]{1,0:T(8,128)(2,1)S(1)}, u32[]{:S(2)}) copy-start(bf16[384,768]{1,0:T(8,128)(2,1)S(1)} %bitcast_dynamic-update-slice_fusion.carried_ref) | copy-start | bytes 1769476
  56.9 291.6 %reduce-scatter.3.cloned.1.call-start = ((), (), s32[]{:S(2)}) async-start(), calls=%async_computation.2 | async-start | bytes 10027008 | tf_op jit(solution)/shard_map/reduce_scatter | solution.py:1337
  66.2 35.0 %copy-start.23 = (bf16[2,8,16,384]{3,1,2,0:T(8,128)(2,1)}, bf16[2,8,16,384]{3,1,2,0:T(8,128)(2,1)S(1)}, u32[]{:S(2)}) copy-start(bf16[2,8,16,384]{3,1,2,0:T(8,128)(2,1)S(1)} %copy.145) | copy-start | bytes 589828
  98.2 11.9 %collective-permute-start.1 = (bf16[512,384]{1,0:T(8,128)(2,1)S(1)}, bf16[512,384]{1,0:T(8,128)(2,1)S(1)}, u32[]{:S(2)}, u32[]{:S(2)}) collective-permute-start(bf16[512,384]{1,0:T(8,128)(2,1)S(1)} %broadcast_select_fusion.3), channel_id=1, source_target_pairs={{0,1},{1,0},{2,3},{3,2},{4,5},{5,4},{6,7},{7,6},{8,9},{9,8},{10,11... | collective-permute-start | bytes 1179656 | tf_op jit(solution)/shard_map/ppermute | solution.py:1225
  117.2 30.2 %collective-permute-start.2 = (bf16[272,1536]{1,0:T(8,128)(2,1)}, bf16[272,1536]{1,0:T(8,128)(2,1)S(1)}, u32[]{:S(2)}, u32[]{:S(2)}) collective-permute-start(bf16[272,1536]{1,0:T(8,128)(2,1)} %get-tuple-element.104.after_ref), channel_id=1, source_target_pairs={{0,1},{1,0},{2,3},{3,2},{4,5},{5,4},{6,7},{7,6},{8,9},{9,8},{10,11... | collective-permute-start | bytes 2506760 | tf_op jit(solution)/shard_map/ppermute | solution.py:1275
  136.9 10.4 %collective-permute-start.3 = (bf16[512,384]{1,0:T(8,128)(2,1)S(1)}, bf16[512,384]{1,0:T(8,128)(2,1)S(1)}, u32[]{:S(2)}, u32[]{:S(2)}) collective-permute-start(bf16[512,384]{1,0:T(8,128)(2,1)S(1)} %broadcast_select_fusion.2), channel_id=1, source_target_pairs={{0,1},{1,0},{2,3},{3,2},{4,5},{5,4},{6,7},{7,6},{8,9},{9,8},{10,11... | collective-permute-start | bytes 1179656 | tf_op jit(solution)/shard_map/ppermute | solution.py:1225
  155.2 19.9 %collective-permute-start.5 = (bf16[272,1536]{1,0:T(8,128)(2,1)}, bf16[272,1536]{1,0:T(8,128)(2,1)S(1)}, u32[]{:S(2)}, u32[]{:S(2)}) collective-permute-start(bf16[272,1536]{1,0:T(8,128)(2,1)} %get-tuple-element.113), channel_id=1, source_target_pairs={{0,1},{1,0},{2,3},{3,2},{4,5},{5,4},{6,7},{7,6},{8,9},{9,8},{10,11... | collective-permute-start | bytes 2506760 | tf_op jit(solution)/shard_map/ppermute | solution.py:1275
  174.0 19.5 %collective-permute-start.4 = (bf16[272,1536]{1,0:T(8,128)(2,1)}, bf16[272,1536]{1,0:T(8,128)(2,1)S(1)}, u32[]{:S(2)}, u32[]{:S(2)}) collective-permute-start(bf16[272,1536]{1,0:T(8,128)(2,1)} %get-tuple-element.111), channel_id=1, source_target_pairs={{0,1},{1,0},{2,3},{3,2},{4,5},{5,4},{6,7},{7,6},{8,9},{9,8},{10,11... | collective-permute-start | bytes 2506760 | tf_op jit(solution)/shard_map/ppermute | solution.py:1295
  215.9 158.2 %reduce-scatter.5.cloned.1.call-start = ((), (), s32[]{:S(2)}) async-start(), calls=%async_computation.3 | async-start | bytes 983040 | tf_op jit(solution)/shard_map/reduce_scatter | solution.py:1514
  218.3 21.7 %collective-permute-start.6 = (bf16[272,1536]{1,0:T(8,128)(2,1)}, bf16[272,1536]{1,0:T(8,128)(2,1)S(1)}, u32[]{:S(2)}, u32[]{:S(2)}) collective-permute-start(bf16[272,1536]{1,0:T(8,128)(2,1)} %get-tuple-element.119), channel_id=1, source_target_pairs={{0,1},{1,0},{2,3},{3,2},{4,5},{5,4},{6,7},{7,6},{8,9},{9,8},{10,11... | collective-permute-start | bytes 2506760 | tf_op jit(solution)/shard_map/ppermute | solution.py:1295
  231.0 21.2 %collective-permute-start.7 = (bf16[512,384]{1,0:T(8,128)(2,1)}, bf16[512,384]{1,0:T(8,128)(2,1)S(1)}, u32[]{:S(2)}, u32[]{:S(2)}) collective-permute-start(bf16[512,384]{1,0:T(8,128)(2,1)} %get-tuple-element.131), channel_id=1, source_target_pairs={{0,1},{1,0},{2,3},{3,2},{4,5},{5,4},{6,7},{7,6},{8,9},{9,8},{10,11... | collective-permute-start | bytes 1179656 | tf_op jit(solution)/shard_map/ppermute | solution.py:1391
  248.7 34.8 %collective-permute-start.8 = (bf16[512,384]{1,0:T(8,128)(2,1)}, bf16[512,384]{1,0:T(8,128)(2,1)S(1)}, u32[]{:S(2)}, u32[]{:S(2)}) collective-permute-start(bf16[512,384]{1,0:T(8,128)(2,1)} %get-tuple-element.135), channel_id=1, source_target_pairs={{0,1},{1,0},{2,3},{3,2},{4,5},{5,4},{6,7},{7,6},{8,9},{9,8},{10,11... | collective-permute-start | bytes 1179656 | tf_op jit(solution)/shard_map/ppermute | solution.py:1391
  259.6 49.3 %collective-permute-start.9 = (bf16[4,2,96,384]{3,2,0,1:T(8,128)(2,1)}, bf16[4,2,96,384]{3,2,0,1:T(8,128)(2,1)}, u32[]{:S(2)}, u32[]{:S(2)}) collective-permute-start(bf16[4,2,96,384]{3,2,0,1:T(8,128)(2,1)} %get-tuple-element.227), channel_id=1, source_target_pairs={{0,2},{2,0},{4,6},{6,4},{8,10},{10,8},{12,14},{14,12},{16,18},{18,... | collective-permute-start | bytes 1769480 | tf_op jit(solution)/shard_map/ppermute | solution.py:1347
  283.0 28.4 %collective-permute-start.11 = (bf16[512,768]{1,0:T(8,128)(2,1)}, bf16[512,768]{1,0:T(8,128)(2,1)S(1)}, u32[]{:S(2)}, u32[]{:S(2)}) collective-permute-start(bf16[512,768]{1,0:T(8,128)(2,1)} %get-tuple-element.133.after_ref), channel_id=1, source_target_pairs={{0,1},{1,0},{2,3},{3,2},{4,5},{5,4},{6,7},{7,6},{8,9},{9,8},{10,11... | collective-permute-start | bytes 2359304 | tf_op jit(solution)/shard_map/ppermute | solution.py:1425
  310.8 9.1 %collective-permute-start.10 = (bf16[4,96,384]{2,1,0:T(8,128)(2,1)S(1)}, bf16[4,96,384]{2,1,0:T(8,128)(2,1)S(1)}, u32[]{:S(2)}, u32[]{:S(2)}) collective-permute-start(bf16[4,96,384]{2,1,0:T(8,128)(2,1)S(1)} %get-tuple-element.225), channel_id=1, source_target_pairs={{0,4},{2,6},{4,0},{6,2},{8,12},{10,14},{12,8},{14,10},{16,20},{18,... | collective-permute-start | bytes 884744 | tf_op jit(solution)/shard_map/ppermute | solution.py:1358
  331.2 2.5 collective-permute-start.12
  333.1 10.7 %collective-permute-start.14 = (bf16[4,2,16,384]{3,2,0,1:T(8,128)(2,1)S(1)}, bf16[4,2,16,384]{3,2,0,1:T(8,128)(2,1)S(1)}, u32[]{:S(2)}, u32[]{:S(2)}) collective-permute-start(bf16[4,2,16,384]{3,2,0,1:T(8,128)(2,1)S(1)} %get-tuple-element.253), channel_id=1, source_target_pairs={{0,2},{2,0},{4,6},{6,4},{8,10},{10,8},{12,14},{14,12},{16,18},{18,... | collective-permute-start | bytes 294920 | tf_op jit(solution)/shard_map/ppermute | solution.py:1347
  334.7 13.8 %collective-permute-start.13 = (bf16[4,144,384]{2,1,0:T(8,128)(2,1)S(1)}, bf16[4,144,384]{2,1,0:T(8,128)(2,1)S(1)}, u32[]{:S(2)}, u32[]{:S(2)}) collective-permute-start(bf16[4,144,384]{2,1,0:T(8,128)(2,1)S(1)} %get-tuple-element.210), channel_id=1, source_target_pairs={{0,4},{2,6},{4,0},{6,2},{8,12},{10,14},{12,8},{14,10},{16,20},{18,... | collective-permute-start | bytes 1327112 | tf_op jit(solution)/shard_map/ppermute | solution.py:1358
  342.3 19.5 %collective-permute-start.16 = (bf16[512,768]{1,0:T(8,128)(2,1)}, bf16[512,768]{1,0:T(8,128)(2,1)S(1)}, u32[]{:S(2)}, u32[]{:S(2)}) collective-permute-start(bf16[512,768]{1,0:T(8,128)(2,1)} %get-tuple-element.146.refs_1_), channel_id=1, source_target_pairs={{0,1},{1,0},{2,3},{3,2},{4,5},{5,4},{6,7},{7,6},{8,9},{9,8},{10,11... | collective-permute-start | bytes 2359304 | tf_op jit(solution)/shard_map/ppermute | solution.py:1425
  344.4 4.1 %collective-permute-start.15 = (bf16[4,16,384]{2,1,0:T(8,128)(2,1)S(1)}, bf16[4,16,384]{2,1,0:T(8,128)(2,1)S(1)}, u32[]{:S(2)}, u32[]{:S(2)}) collective-permute-start(bf16[4,16,384]{2,1,0:T(8,128)(2,1)S(1)} %get-tuple-element.250), channel_id=1, source_target_pairs={{0,4},{2,6},{4,0},{6,2},{8,12},{10,14},{12,8},{14,10},{16,20},{18,... | collective-permute-start | bytes 147464 | tf_op jit(solution)/shard_map/ppermute | solution.py:1358
  374.0 5.9 %collective-permute-start.17 = (bf16[256,384]{1,0:T(8,128)(2,1)}, bf16[256,384]{1,0:T(8,128)(2,1)S(1)}, u32[]{:S(2)}, u32[]{:S(2)}) collective-permute-start(bf16[256,384]{1,0:T(8,128)(2,1)} %bitcast.97), channel_id=1, source_target_pairs={{0,1},{1,0},{2,3},{3,2},{4,5},{5,4},{6,7},{7,6},{8,9},{9,8},{10,11... | collective-permute-start | bytes 589832 | tf_op jit(solution)/shard_map/ppermute | solution.py:1522
  (31 other events, 98.3 us)
Sparse Core Ops, SparseCore 0:
  13.7 48.1 all-gather.4
  64.7 80.2 all-gather.6
  216.0 109.9 reduce-scatter.2
  351.9 22.0 reduce-scatter.4

commit v7 on v6

--- a/solution.py
+++ b/solution.py
@@ -550,8 +550,8 @@
     )(*operands)
 
 
-def dense_kernel(skipped, batches, weighted, blocks, *refs):
-    refs = refs[skipped:]
+def dense_kernel(skipped, handed, batches, weighted, blocks, *refs):
+    refs = refs[skipped : len(refs) - handed]
     out_ref = refs[2 * batches + weighted]
     left = jnp.concatenate([ref[...] for ref in refs[:batches]], axis=0)
     right = jnp.concatenate([ref[...] for ref in refs[batches : 2 * batches]], axis=0)
@@ -570,7 +570,8 @@
         refs[-1][...] = jnp.sum(term, axis=1, keepdims=True)
 
 
-def dense_grad(left, right, lanes, shards, direct, afters, packed=None):
+def dense_grad(left, right, lanes, shards, direct, afters, packed=None, handed=()):
+    afters = list(handed) + list(afters)
     batches = len(left)
     count, width = left[0].shape
     columns = right[0].shape[1]
@@ -581,16 +582,19 @@
     inner = depth if direct else width
     weighted = 0 if packed is None else 1
     outs = pl.pallas_call(
-        functools.partial(dense_kernel, len(afters), batches, weighted, blocks),
+        functools.partial(dense_kernel, len(afters), len(handed), batches, weighted, blocks),
         grid=(steps,),
         in_specs=[pl.BlockSpec(memory_space=pl.ANY)] * len(afters)
         + [pl.BlockSpec((count, width // steps), lambda i: (0, i))] * batches
         + [pl.BlockSpec((count, columns), lambda i: (0, 0))] * batches
         + [pl.BlockSpec((outer, blocks * inner, lanes), lambda i: (i, 0, 0))] * weighted,
         out_specs=[pl.BlockSpec((outer, blocks * inner, lanes), lambda i: (i, 0, 0))]
-        + [pl.BlockSpec((width // steps, 1), lambda i: (i, 0))] * weighted,
+        + [pl.BlockSpec((width // steps, 1), lambda i: (i, 0))] * weighted
+        + [pl.BlockSpec(memory_space=pl.ANY)] * len(handed),
         out_shape=[jax.ShapeDtypeStruct((outer * steps, blocks * inner, lanes), bfloat)]
-        + [jax.ShapeDtypeStruct((width, 1), float32)] * weighted,
+        + [jax.ShapeDtypeStruct((width, 1), float32)] * weighted
+        + [jax.ShapeDtypeStruct(array.shape, array.dtype) for array in handed],
+        input_output_aliases={idx: 1 + weighted + idx for idx in range(len(handed))},
         compiler_params=params(),
         cost_estimate=pl.CostEstimate(
             flops=2 * batches * count * width * columns,
@@ -603,7 +607,7 @@
     if not direct:
         out = jnp.transpose(out.reshape(blocks, shards, depth, lanes), (1, 0, 2, 3))
         out = out.reshape(shards, blocks * depth, lanes)
-    return (out, outs[1]) if weighted else out
+    return (out,) + tuple(outs[1:])
 
 
 def segment_of(positions, ends):
@@ -752,6 +756,7 @@
     head_dim,
     scale,
     carried,
+    skipped,
     probs_ref,
     out_ref,
     inv_ref,
@@ -759,9 +764,9 @@
     k_ref,
     v_ref,
     offset_ref,
-    after_ref,
     *refs,
 ):
+    refs = refs[skipped:]
     grad_refs = refs[:stride]
     dqkv_ref, dbias_ref, dfar_ref, ds_ref, grads_ref = refs[-5:]
     rows_all = q_ref.shape[0]
@@ -828,7 +833,7 @@
 
 
 def attend_back(
-    batch, probs, grads, outs, inverse, qkv, offsets, after, sums, head_dim, stride, bias_shape
+    batch, probs, grads, outs, inverse, qkv, offsets, afters, sums, head_dim, stride, bias_shape
 ):
     rows_all, span = outs.shape
     per = tile // head_dim
@@ -840,15 +845,17 @@
         pl.BlockSpec((per, 2, tile, tile), lambda i: (i, 0, 0, 0)),
     ]
     carried = len(sums) > 0
-    first = 8 + stride
+    first = 7 + len(afters) + stride
     return pl.pallas_call(
-        functools.partial(attend_back_kernel, stride, head_dim, head_dim ** (-0.5), carried),
+        functools.partial(
+            attend_back_kernel, stride, head_dim, head_dim ** (-0.5), carried, len(afters)
+        ),
         grid=(span // tile,),
         in_specs=[pl.BlockSpec((per, rows_all, rows_all), lambda i: (i, 0, 0))]
         + [row_spec] * 2
         + kind_specs(rows_all)
         + [pl.BlockSpec((1,) + offsets.shape[1:], lambda i: (batch, 0, 0))]
-        + [pl.BlockSpec(memory_space=pl.ANY)]
+        + [pl.BlockSpec(memory_space=pl.ANY)] * len(afters)
         + [part_spec] * stride
         + (sum_specs if carried else []),
         out_specs=[pl.BlockSpec((rows_all, 3 * tile), lambda i: (0, i))] + sum_specs,
@@ -869,7 +876,7 @@
             transcendentals=0,
         ),
         name="attend_back",
-    )(probs, outs, inverse, qkv, qkv, qkv, offsets, after, *grads, *sums)
+    )(probs, outs, inverse, qkv, qkv, qkv, offsets, *afters, *grads, *sums)
 
 
 def add_kernel(skipped, *refs):
@@ -1030,7 +1037,7 @@
     out_ref[...] = total.astype(bfloat).reshape(out_ref.shape)
 
 
-def expert_grad(groups, wide, width, second, out_shape, out_spec, after, buffer=None):
+def expert_grad(groups, wide, width, second, out_shape, out_spec, afters, buffer=None):
     batches = len(groups)
     count = len(groups[0])
     slots = groups[0][0].shape[0]
@@ -1041,9 +1048,9 @@
     in_specs = in_specs + [pl.BlockSpec((total, width), lambda i: (0, i))] * batches
     operands = [block for group in groups for block in group] + list(wide)
     aliases = {}
-    carried = [after]
+    carried = list(afters)
     if buffer is not None:
-        carried = [buffer, after]
+        carried = [buffer] + carried
         aliases = {0: 0}
     skipped = len(carried)
     in_specs = [pl.BlockSpec(memory_space=pl.ANY)] * skipped + in_specs
@@ -1297,73 +1304,14 @@
             ]
         )
 
-    if direct:
-        buffer_shape = (shards, turns * depth + depth_out, width)
-        buffer = expert_grad(
-            blocks,
-            grad_pre,
-            width,
-            False,
-            buffer_shape,
-            pl.BlockSpec((shards, depth, width), lambda i: (0, i, 0)),
-            returned[0][-1],
-        )
-        buffer = expert_grad(
-            blocks,
-            hidden,
-            width,
-            True,
-            buffer_shape,
-            pl.BlockSpec((group, depth_out, width), lambda i: (i, 1, 0)),
-            returned[0][-1],
-            buffer,
-        )
-    else:
-        plain_shape = (turns, width, width)
-        inner_g = expert_grad(
-            blocks, grad_pre, width, False, plain_shape, plain, returned[0][-1]
-        )
-        outer_g = expert_grad(
-            blocks, hidden, width, True, plain_shape, plain, returned[0][-1]
-        )
-        inner_g = jnp.transpose(inner_g.reshape(turns, shards, depth, width), (1, 0, 2, 3))
-        buffer = jnp.concatenate(
-            [
-                inner_g.reshape(shards, turns * depth, width),
-                outer_g.reshape(shards, depth_out, width),
-            ],
-            axis=1,
-        )
-    expert_sum = lax.psum_scatter(buffer, "dp", scatter_dimension=0, tiled=False)
-
-    line = shards // 4
-    my_shard = lax.axis_index("dp")
-
-    def by_core(dense):
-        dense = dense.reshape((line, 2, 2) + dense.shape[1:])
-        odd = my_shard % 2 == 1
-        sent = jnp.where(odd, dense[:, :, 0], dense[:, :, 1])
-        held = jnp.where(odd, dense[:, :, 1], dense[:, :, 0])
-        return held, lax.ppermute(sent, "dp", [(idx, idx ^ 1) for idx in range(shards)])
-
-    def by_y(core_parts):
-        held, got = core_parts
-        odd = (my_shard // 2) % 2 == 1
-
-        def half(idx):
-            return held[:, idx].astype(float32) + got[:, idx].astype(float32)
-
-        sent = jnp.where(odd, half(0), half(1)).astype(bfloat)
-        kept = jnp.where(odd, half(1), half(0)).astype(bfloat)
-        return kept, lax.ppermute(sent, "dp", [(idx, idx ^ 2) for idx in range(shards)])
-
-    layer = None
+    layer_rows = [None]
     grad_mid = []
     grad_attn = []
     grad_heads = []
-    grad_gain_two = 0.0
-    grad_router = 0.0
-    for batch in range(batches):
+    gain_two_terms = []
+    router_terms_all = []
+
+    def norm_part(batch, after):
         layer, mid, attn, gain_terms, router_terms, parts = second_back(
             batch,
             batches,
@@ -1380,18 +1328,86 @@
             output_w,
             members,
             span,
-            buffer,
-            layer,
+            after,
+            layer_rows[-1],
         )
         grad_mid.append(mid)
         grad_attn.append(attn)
-        grad_gain_two = grad_gain_two + gain_terms
-        grad_router = grad_router + router_terms[:experts]
+        layer_rows.append(layer)
+        gain_two_terms.append(gain_terms)
+        router_terms_all.append(router_terms[:experts])
         from_members = [parts[0]] + [
             lax.ppermute(parts[members - step], "expert", around(step))
             for step in range(1, members)
         ]
         grad_heads.append(from_members)
+
+    if direct:
+        buffer_shape = (shards, turns * depth + depth_out, width)
+        buffer = expert_grad(
+            blocks,
+            grad_pre,
+            width,
+            False,
+            buffer_shape,
+            pl.BlockSpec((shards, depth, width), lambda i: (0, i, 0)),
+            [returned[0][-1]],
+        )
+        norm_part(0, table)
+        buffer = expert_grad(
+            blocks,
+            hidden,
+            width,
+            True,
+            buffer_shape,
+            pl.BlockSpec((group, depth_out, width), lambda i: (i, 1, 0)),
+            [returned[-1][-1], grad_attn[0]],
+            buffer,
+        )
+    else:
+        plain_shape = (turns, width, width)
+        inner_g = expert_grad(
+            blocks, grad_pre, width, False, plain_shape, plain, [returned[0][-1]]
+        )
+        norm_part(0, table)
+        outer_g = expert_grad(
+            blocks, hidden, width, True, plain_shape, plain, [returned[-1][-1]]
+        )
+        inner_g = jnp.transpose(inner_g.reshape(turns, shards, depth, width), (1, 0, 2, 3))
+        buffer = jnp.concatenate(
+            [
+                inner_g.reshape(shards, turns * depth, width),
+                outer_g.reshape(shards, depth_out, width),
+            ],
+            axis=1,
+        )
+    expert_sum = lax.psum_scatter(buffer, "dp", scatter_dimension=0, tiled=False)
+    for batch in range(1, batches):
+        norm_part(batch, buffer)
+    layer = layer_rows[-1]
+    grad_gain_two = sum(gain_two_terms)
+    grad_router = sum(router_terms_all)
+
+    line = shards // 4
+    my_shard = lax.axis_index("dp")
+
+    def by_core(dense):
+        dense = dense.reshape((line, 2, 2) + dense.shape[1:])
+        odd = my_shard % 2 == 1
+        sent = jnp.where(odd, dense[:, :, 0], dense[:, :, 1])
+        held = jnp.where(odd, dense[:, :, 1], dense[:, :, 0])
+        return held, lax.ppermute(sent, "dp", [(idx, idx ^ 1) for idx in range(shards)])
+
+    def by_y(core_parts):
+        held, got = core_parts
+        odd = (my_shard // 2) % 2 == 1
+
+        def half(idx):
+            return held[:, idx].astype(float32) + got[:, idx].astype(float32)
+
+        sent = jnp.where(odd, half(0), half(1)).astype(bfloat)
+        kept = jnp.where(odd, half(1), half(0)).astype(bfloat)
+        return kept, lax.ppermute(sent, "dp", [(idx, idx ^ 2) for idx in range(shards)])
 
     def own_rows_of(batch):
         joined = outs[batch]
@@ -1409,7 +1425,7 @@
         for batch in range(batches)
     ]
     early_core = by_core(
-        dense_grad(attended, grad_attn, lanes, shards, direct, [grad_heads[0][-1]])
+        dense_grad(attended, grad_attn, lanes, shards, direct, [grad_heads[0][-1]])[0]
     )
     early = by_y(early_core)
     grad_qkv = []
@@ -1437,15 +1453,14 @@
             inverses[batch],
             qkv[batch],
             offsets,
-            sent_last,
+            [buffer] if batch == 0 else [sent_last, early_core[1]],
             sums,
             head_dim,
             members,
             bias.shape,
         )
         grad_qkv.append(grads)
-    grad_bias, grad_far = sums
-    grad_dense, weighted = dense_grad(
+    grad_dense, weighted, grad_bias, grad_far = dense_grad(
         normed_one,
         grad_qkv,
         lanes,
@@ -1453,6 +1468,7 @@
         direct,
         [early[1]] + [rows[-1] for rows in received_rows],
         packed,
+        sums,
     )
     grad_gain_one = weighted[:, 0] / gain_one[0]
     late_core = by_core(grad_dense)

time: 397 us -> 384 us (0.967)
  waiting for transfers between devices: 79.4 us -> 63.8 us
    ppermute x2, waiting for transfers between devices: 9.37 us -> 0.01 us  [on_device(): lax.ppermute(results[step], 'expert', around(-step))]
    ppermute x3, waiting for transfers between devices: 10.8 us -> 3.83 us  [by_y(): lax.ppermute(sent, 'dp', [(idx, idx ^ 2) for idx in range(shards)])]
    unnamed x84 -> x88, local copies, waits for them, and re-layouts: 18.2 us -> 18.8 us
  transfers between devices with their start and end apart: 22 -> 22, of which waited for: 12 -> 9; matrix products, arithmetic and copies ran while one was open for 10% -> 11% of each run, Pallas kernels for 49% -> 54%
where the time goes in v7:
time: 384 us; the launch traced here: 380 us
  Pallas kernels  216 us (56%)
  waiting for transfers between devices  63.8 us (17%)
  local copies, waits for them, and re-layouts  39.9 us (10%)
  other arithmetic  20.7 us (5%)
  starting transfers between devices  20.1 us (5%)
  between operations  14.7 us (4%)
  matrix products  5.31 us (1%)
    pallas_call x2, Pallas kernels, attend(): pl.pallas_call(functools.partial(attend_kernel, stride, head_dim), grid=(...  35.2 us
    pallas_call x2, Pallas kernels, attend_back(): pl.pallas_call(functools.partial(attend_back_kernel, stride, head_dim, he...  35.1 us
    pallas_call x2, Pallas kernels, run_expert(): pl.pallas_call(functools.partial(expert_kernel, count, slots, width), gri...  33.8 us
    ppermute x1, waiting for transfers between devices, on_device(): lax.ppermute(hidden_in, 'expert', around(step))  31 us
    pallas_call x2, Pallas kernels, expert_grad(): pl.pallas_call(body, grid=(turns,), in_specs=in_specs, out_specs=out_spec...  21.4 us
    unnamed x88, local copies, waits for them, and re-layouts  18.8 us
    pallas_call x2, Pallas kernels, second_back(): pl.pallas_call(functools.partial(second_kernel, members, members, aliased...  16.4 us
    pallas_call x2, Pallas kernels, dense_grad(): pl.pallas_call(functools.partial(dense_kernel, len(afters), len(handed),...  13.3 us
  transfers between devices with their start and end apart: 22, of which 9 were waited for; matrix products, arithmetic and copies ran while one was open for 11% of the time, Pallas kernels for 54%

profile of v7, /device:TPU:0, one launch (start us, length us, event | category | flops | bytes accessed | tf_op | source)
XLA Modules:
  0.0 380.3 jit_solution(17582585889576785457)
XLA Ops:
  20.2 31.0 %collective-permute-done.after_ref.refs_1_ = bf16[2,512,768]{2,1,0:T(8,128)(2,1)S(1)} collective-permute-done((bf16[2,512,768]{2,1,0:T(8,128)(2,1)}, bf16[2,512,768]{2,1,0:T(8,128)(2,1)S(1)}, u32[]{:S(2)}, u32[]{:S(2)}) %collective-permute-start) | collective-permute-done | bytes 1572896 | tf_op jit(solution)/shard_map/ppermute | solution.py:1139
  52.4 4.6 %row_tables.1 = (bf16[2,544,512]{2,1,0:T(8,128)(2,1)}, bf16[2,512,544]{2,1,0:T(8,128)(2,1)}, s32[2,512,2]{2,1,0:T(8,128)}, bf16[384,768]{1,0:T(8,128)(2,1)}) custom-call(s32[1]{0:T(128)} %bitcast.me_ref, s32[2,1,512]{2,1,0:T(1,128)} %bitcast.100, s32[2,512,1]{2,1,0:T(8,128)} %copy.121.column_ref.route_ref, ...), custom_call_target="tpu_custom_call", output_to_operand_aliasing={{3}: (5, {})} | custom-call | tf_op jit(solution)/shard_map/row_tables/pallas_call | solution.py:190
  67.9 5.0 %bias_tiles.1.bias_ref = f32[6,3,128,384]{3,2,1,0:T(8,128)} custom-call(f32[6,128]{1,0:T(8,128)} %pad.22.clone.table_ref), custom_call_target="tpu_custom_call" | custom-call | tf_op jit(solution)/shard_map/bias_tiles/pallas_call | solution.py:79
  73.5 5.8 %project.3 = (bf16[1024,768]{1,0:T(8,128)(2,1)}, bf16[1024,1152]{1,0:T(8,128)(2,1)}) custom-call(bf16[2,1024,768]{2,1,0:T(8,128)(2,1)} %bitcast.106, f32[1,768]{1,0:T(1,128)} %reshape.333.gain_ref, bf16[16,256,384]{2,1,0:T(8,128)(2,1)} %get-tuple-element.100.weight_ref.refs_8_), custom_call_target="tpu_custom_call" | custom-call | flops 1811939328 | bytes 4718592 | tf_op jit(solution)/shard_map/project/pallas_call | solution.py:108
  79.3 17.6 %attend.2 = (bf16[6,1024,1024]{2,1,0:T(8,128)(2,1)}, bf16[1024,384]{1,0:T(8,128)(2,1)}, f32[1024,384]{1,0:T(8,128)}) custom-call(f32[2,6]{1,0:T(2,128)} %pad_maximum_fusion.4.far_ref, s32[1]{0:T(128)} %bitcast.13.ends_ref, bf16[1024,1152]{1,0:T(8,128)(2,1)} %get-tuple-element.103.q_ref.k_ref.v_ref, bf16[1024,1152]{1,0:T(8,128)(2,1)} %get-tuple-element.103.q_ref.k_ref.v_ref, ...), custom_call_target="tpu_custom_call" | custom-call | flops 6442450944 | bytes 12582912 | tf_op jit(solution)/shard_map/attend/pallas_call | solution.py:724
  104.0 6.1 %project.2 = (bf16[1024,768]{1,0:T(8,128)(2,1)}, bf16[1024,1152]{1,0:T(8,128)(2,1)}) custom-call(bf16[2,1024,768]{2,1,0:T(8,128)(2,1)} %bitcast.107, f32[1,768]{1,0:T(1,128)} %reshape.333.gain_ref, bf16[16,256,384]{2,1,0:T(8,128)(2,1)} %get-tuple-element.100.weight_ref.refs_8_), custom_call_target="tpu_custom_call" | custom-call | flops 1811939328 | bytes 4718592 | tf_op jit(solution)/shard_map/project/pallas_call | solution.py:108
  110.9 6.2 %middle.2 = (f32[512,768]{1,0:T(8,128)}, bf16[512,768]{1,0:T(8,128)(2,1)}, f32[512,128]{1,0:T(8,128)}, bf16[272,1536]{1,0:T(8,128)(2,1)}, bf16[272,1536]{1,0:T(8,128)(2,1)}) custom-call(s32[1]{0:T(128)} %bitcast.me_ref, bf16[1024,384]{1,0:T(8,128)(2,1)} %get-tuple-element.104.joined_ref.out_ref, s32[2,512,2]{2,1,0:T(8,128)} %get-tuple-element.99.place_ref.offset_ref, ...), custom_call_target="tpu_custom_call" | custom-call | flops 14495514624 | bytes 4718592 | tf_op jit(solution)/shard_map/middle/pallas_call | solution.py:297
  118.0 17.6 %attend.3 = (bf16[6,1024,1024]{2,1,0:T(8,128)(2,1)}, bf16[1024,384]{1,0:T(8,128)(2,1)}, f32[1024,384]{1,0:T(8,128)}) custom-call(f32[2,6]{1,0:T(2,128)} %pad_maximum_fusion.4.far_ref, s32[1]{0:T(128)} %bitcast.10.ends_ref, bf16[1024,1152]{1,0:T(8,128)(2,1)} %get-tuple-element.102.q_ref.k_ref.v_ref, bf16[1024,1152]{1,0:T(8,128)(2,1)} %get-tuple-element.102.q_ref.k_ref.v_ref, ...), custom_call_target="tpu_custom_call" | custom-call | flops 6442450944 | bytes 12582912 | tf_op jit(solution)/shard_map/attend/pallas_call | solution.py:724
  138.1 9.2 %collective-permute-done.3.refs_0_ = bf16[512,384]{1,0:T(8,128)(2,1)S(1)} collective-permute-done((bf16[512,384]{1,0:T(8,128)(2,1)S(1)}, bf16[512,384]{1,0:T(8,128)(2,1)S(1)}, u32[]{:S(2)}, u32[]{:S(2)}) %collective-permute-start.3) | collective-permute-done | bytes 393248 | tf_op jit(solution)/shard_map/ppermute | solution.py:1232
  149.0 6.2 %middle.3 = (f32[512,768]{1,0:T(8,128)}, bf16[512,768]{1,0:T(8,128)(2,1)}, f32[512,128]{1,0:T(8,128)}, bf16[272,1536]{1,0:T(8,128)(2,1)}, bf16[272,1536]{1,0:T(8,128)(2,1)}) custom-call(s32[1]{0:T(128)} %bitcast.me_ref, bf16[1024,384]{1,0:T(8,128)(2,1)} %get-tuple-element.107.joined_ref.out_ref, s32[2,512,2]{2,1,0:T(8,128)} %get-tuple-element.99.place_ref.offset_ref, ...), custom_call_target="tpu_custom_call" | custom-call | flops 14495514624 | bytes 4718592 | tf_op jit(solution)/shard_map/middle/pallas_call | solution.py:297
  157.0 17.2 %run_expert.2 = (bf16[272,1536]{1,0:T(8,128)(2,1)}, bf16[272,1536]{1,0:T(8,128)(2,1)}, bf16[544,3072]{1,0:T(8,128)(2,1)}, bf16[544,3072]{1,0:T(8,128)(2,1)}) custom-call(bf16[16,384,768]{2,1,0:T(8,128)(2,1)} %bitcast.102, bf16[16,384,768]{2,1,0:T(8,128)(2,1)} %bitcast.103, bf16[32,12]{1,0:T(8,128)(2,1)} %copy-done.26, ...), custom_call_target="tpu_custom_call" | custom-call | flops 10267656192 | bytes 9437184 | tf_op jit(solution)/shard_map/run_expert/pallas_call | solution.py:997
  176.0 16.6 %run_expert.3 = (bf16[272,1536]{1,0:T(8,128)(2,1)}, bf16[272,1536]{1,0:T(8,128)(2,1)}, bf16[544,3072]{1,0:T(8,128)(2,1)}, bf16[544,3072]{1,0:T(8,128)(2,1)}) custom-call(bf16[16,384,768]{2,1,0:T(8,128)(2,1)} %bitcast.104, bf16[16,384,768]{2,1,0:T(8,128)(2,1)} %bitcast.105, bf16[544,3072]{1,0:T(8,128)(2,1)} %get-tuple-element.117.after_ref.refs_7_, ...), custom_call_target="tpu_custom_call" | custom-call | flops 10267656192 | bytes 9437184 | tf_op jit(solution)/shard_map/run_expert/pallas_call | solution.py:997
  196.6 7.8 %second_back.2 = (bf16[2,512,768]{2,1,0:T(8,128)(2,1)}, f32[512,768]{1,0:T(8,128)}, bf16[512,768]{1,0:T(8,128)(2,1)}, f32[1,768]{1,0:T(1,128)}, f32[128,768]{1,0...) custom-call(s32[1]{0:T(128)} %bitcast.me_ref, bf16[2,512,544]{2,1,0:T(8,128)(2,1)} %get-tuple-element.98.back_ref, ...), custom_call_target="tpu_custom_call" | custom-call | flops 1811939328 | bytes 4718592 | tf_op jit(solution)/shard_map/second_back/pallas_call | solution.py:417
  204.4 10.8 %expert_grad_inner.1.refs_0_ = bf16[16,384,768]{2,1,0:T(8,128)(2,1)} custom-call(bf16[272,1536]{1,0:T(8,128)(2,1)} %copy-done.2, bf16[272,1536]{1,0:T(8,128)(2,1)} %get-tuple-element.112.refs_0_.refs_1_.refs_3_, bf16[272,1536]{1,0:T(8,128)(2,1)} %copy-done.4, bf16[272,1536]{1,0:T(8,128)(2,1)} %get-tuple-element.114.refs_0_.refs_3_.refs_5_, ...), custom_call_target="tpu_custom_call" | custom-call | flops 5133828096 | bytes 9437184 | tf_op jit(solution)/shard_map/expert_grad_inner/pallas_call | solution.py:1062
  216.0 10.7 %expert_grad_outer.1.after_ref.refs_0_ = bf16[16,384,768]{2,1,0:T(8,128)(2,1)} custom-call(bf16[16,384,768]{2,1,0:T(8,128)(2,1)} %expert_grad_inner.1.refs_0_, bf16[272,1536]{1,0:T(8,128)(2,1)} %copy-done.3, bf16[512,768]{1,0:T(8,128)(2,1)} %get-tuple-element.124.refs_2_.refs_3_, ...), custom_call_target="tpu_custom_call", output_to_operand_aliasing={{}: (0, {})} | custom-call | flops 5133828096 | bytes 9437184 | tf_op jit(solution)/shard_map/expert_grad_outer/pallas_call | solution.py:1062
  232.1 8.7 %second_back.3 = (bf16[2,512,768]{2,1,0:T(8,128)(2,1)}, f32[512,768]{1,0:T(8,128)}, bf16[512,768]{1,0:T(8,128)(2,1)}, f32[1,768]{1,0:T(1,128)}, f32[128,768]{1,0...) custom-call(s32[1]{0:T(128)} %bitcast.me_ref, ...), custom_call_target="tpu_custom_call", output_to_operand_aliasing={{0}: (13, {})} | custom-call | flops 1811939328 | bytes 4718592 | tf_op jit(solution)/shard_map/second_back/pallas_call | solution.py:417
  251.3 17.2 %attend_back.2 = (bf16[1024,1152]{1,0:T(8,128)(2,1)}, f32[6,3,128,384]{3,2,1,0:T(8,128)}, f32[6,2,128,128]{3,2,1,0:T(8,128)}) custom-call(bf16[6,1024,1024]{2,1,0:T(8,128)(2,1)} %get-tuple-element.131.probs_ref, bf16[1024,384]{1,0:T(8,128)(2,1)} %get-tuple-element.104.joined_ref.out_ref, f32[1024,384]{1,0:T(8,128)} %get-tuple-element.132.inv_ref, ...), custom_call_target="tpu_custom_call" | custom-call | flops 12884901888 | bytes 12582912 | tf_op jit(solution)/shard_map/attend_back/pallas_call | solution.py:849
  268.5 6.2 %first_back.2 = (f32[512,768]{1,0:T(8,128)}, bf16[512,768]{1,0:T(8,128)(2,1)}) custom-call(bf16[1024,1152]{1,0:T(8,128)(2,1)} %get-tuple-element.135.grads_ref.refs_6_, bf16[16,256,384]{2,1,0:T(8,128)(2,1)} %get-tuple-element.100.weight_ref.refs_8_, s32[2,512,2]{2,1,0:T(8,128)} %get-tuple-element.99.place_ref.offset_ref, ...), custom_call_target="tpu_custom_call" | custom-call | flops 1811939328 | bytes 6291456 | tf_op jit(solution)/shard_map/first_back/pallas_call | solution.py:496
  277.5 17.9 %attend_back.3 = (bf16[1024,1152]{1,0:T(8,128)(2,1)}, f32[6,3,128,384]{3,2,1,0:T(8,128)}, f32[6,2,128,128]{3,2,1,0:T(8,128)}) custom-call(bf16[6,1024,1024]{2,1,0:T(8,128)(2,1)} %get-tuple-element.129.probs_ref, bf16[1024,384]{1,0:T(8,128)(2,1)} %get-tuple-element.107.joined_ref.out_ref, ...), custom_call_target="tpu_custom_call", output_to_operand_aliasing={{1}: (11, {}), {2}: (12, {})} | custom-call | flops 12884901888 | bytes 12582912 | tf_op jit(solution)/shard_map/attend_back/pallas_call | solution.py:849
  296.4 9.0 %dense_grad.3 = (bf16[16,144,384]{2,1,0:T(8,128)(2,1)}, f32[768,1]{1,0:T(8,128)}, f32[6,3,128,384]{3,2,1,0:T(8,128)}, f32[6,2,128,128]{3,2,1,0:T(8,128)}) custom-call(f32[6,3,128,384]{3,2,1,0:T(8,128)} %get-tuple-element.143.refs_0_, f32[6,2,128,128]{3,2,1,0:T(8,128)} %get-tuple-element.144.refs_1_, ...), custom_call_target="tpu_custom_call", output_to_operand_aliasing={{2}: (0, {}), {3}: (1, {})} | custom-call | flops 3623878656 | bytes 3145728 | tf_op jit(solution)/shard_map/dense_grad/pallas_call | solution.py:584
  310.7 5.3 %fusion.3 = f32[32,6]{0,1:T(8,128)S(1)} fusion(bf16[6,3,128,384]{3,2,1,0:T(8,128)(2,1)} %convert_element_type.282, s32[3,128,384]{2,0,1:T(4,128)} %copy.136), kind=kOutput, calls=%fused_computation.5 | convolution fusion | flops 61341696 | bytes 2360064 | tf_op jit(solution)/shard_map/hsab,ksab->kh/dot_general | solution.py:1495
  322.3 6.3 %first_back.3 = (f32[512,768]{1,0:T(8,128)}, bf16[512,768]{1,0:T(8,128)(2,1)}) custom-call(bf16[1024,1152]{1,0:T(8,128)(2,1)} %get-tuple-element.142.refs_7_.grads_ref, bf16[16,256,384]{2,1,0:T(8,128)(2,1)} %get-tuple-element.100.weight_ref.refs_8_, s32[2,512,2]{2,1,0:T(8,128)} %get-tuple-element.99.place_ref.offset_ref, ...), custom_call_target="tpu_custom_call" | custom-call | flops 1811939328 | bytes 6291456 | tf_op jit(solution)/shard_map/first_back/pallas_call | solution.py:496
  342.7 6.0 %collective-permute-done.16.refs_0_ = bf16[512,768]{1,0:T(8,128)(2,1)S(1)} collective-permute-done((bf16[512,768]{1,0:T(8,128)(2,1)}, bf16[512,768]{1,0:T(8,128)(2,1)S(1)}, u32[]{:S(2)}, u32[]{:S(2)}) %collective-permute-start.16) | collective-permute-done | bytes 786464 | tf_op jit(solution)/shard_map/ppermute | solution.py:1441
  354.8 6.7 %reduce-scatter.5.cloned.1.call-done = bf16[1,256,384]{2,1,0:T(8,128)(2,1)} async-done(((bf16[4,256,384]{2,1,0:T(8,128)(2,1)}), bf16[1,256,384]{2,1,0:T(8,128)(2,1)}) %reduce-scatter.5.cloned.1.call-update) | async-done | bytes 196624 | tf_op jit(solution)/shard_map/reduce_scatter | solution.py:1530
  (224 shorter events, 110.1 us)
Async XLA Ops:
  7.2 54.7 %all-gather.5.cloned.1.call-start = ((), (), s32[]{:S(2)}) async-start(), calls=%async_computation.4 | async-start | bytes 3342336 | tf_op jit(solution)/shard_map/all_gather | solution.py:1163
  13.6 143.4 %all-gather.7.cloned.1.call-start = ((), (), s32[]{:S(2)}) async-start(), calls=%async_computation.5 | async-start | bytes 10027008 | tf_op jit(solution)/shard_map/all_gather | solution.py:1170
  13.6 37.6 %collective-permute-start = (bf16[2,512,768]{2,1,0:T(8,128)(2,1)}, bf16[2,512,768]{2,1,0:T(8,128)(2,1)S(1)}, u32[]{:S(2)}, u32[]{:S(2)}) collective-permute-start(bf16[2,512,768]{2,1,0:T(8,128)(2,1)} %rows_ref.7), channel_id=1, source_target_pairs={{0,1},{1,0},{2,3},{3,2},{4,5},{5,4},{6,7},{7,6},{8,9},{9,8},{10,11... | collective-permute-start | bytes 4718600 | tf_op jit(solution)/shard_map/ppermute | solution.py:1139
  20.2 31.0 %copy-start.10 = (bf16[384,768]{1,0:T(8,128)(2,1)}, bf16[384,768]{1,0:T(8,128)(2,1)S(1)}, u32[]{:S(2)}) copy-start(bf16[384,768]{1,0:T(8,128)(2,1)S(1)} %bitcast_dynamic-update-slice_fusion.carried_ref) | copy-start | bytes 1769476
  57.0 278.8 %reduce-scatter.3.cloned.1.call-start = ((), (), s32[]{:S(2)}) async-start(), calls=%async_computation.2 | async-start | bytes 10027008 | tf_op jit(solution)/shard_map/reduce_scatter | solution.py:1384
  66.3 34.9 %copy-start.24 = (bf16[2,8,16,384]{3,1,2,0:T(8,128)(2,1)}, bf16[2,8,16,384]{3,1,2,0:T(8,128)(2,1)S(1)}, u32[]{:S(2)}) copy-start(bf16[2,8,16,384]{3,1,2,0:T(8,128)(2,1)S(1)} %copy.152) | copy-start | bytes 589828
  98.1 11.9 %collective-permute-start.1 = (bf16[512,384]{1,0:T(8,128)(2,1)S(1)}, bf16[512,384]{1,0:T(8,128)(2,1)S(1)}, u32[]{:S(2)}, u32[]{:S(2)}) collective-permute-start(bf16[512,384]{1,0:T(8,128)(2,1)S(1)} %broadcast_select_fusion.3), channel_id=1, source_target_pairs={{0,1},{1,0},{2,3},{3,2},{4,5},{5,4},{6,7},{7,6},{8,9},{9,8},{10,11... | collective-permute-start | bytes 1179656 | tf_op jit(solution)/shard_map/ppermute | solution.py:1232
  117.1 30.2 %collective-permute-start.2 = (bf16[272,1536]{1,0:T(8,128)(2,1)}, bf16[272,1536]{1,0:T(8,128)(2,1)S(1)}, u32[]{:S(2)}, u32[]{:S(2)}) collective-permute-start(bf16[272,1536]{1,0:T(8,128)(2,1)} %get-tuple-element.106.after_ref), channel_id=1, source_target_pairs={{0,1},{1,0},{2,3},{3,2},{4,5},{5,4},{6,7},{7,6},{8,9},{9,8},{10,11... | collective-permute-start | bytes 2506760 | tf_op jit(solution)/shard_map/ppermute | solution.py:1282
  136.9 10.4 %collective-permute-start.3 = (bf16[512,384]{1,0:T(8,128)(2,1)S(1)}, bf16[512,384]{1,0:T(8,128)(2,1)S(1)}, u32[]{:S(2)}, u32[]{:S(2)}) collective-permute-start(bf16[512,384]{1,0:T(8,128)(2,1)S(1)} %broadcast_select_fusion.2), channel_id=1, source_target_pairs={{0,1},{1,0},{2,3},{3,2},{4,5},{5,4},{6,7},{7,6},{8,9},{9,8},{10,11... | collective-permute-start | bytes 1179656 | tf_op jit(solution)/shard_map/ppermute | solution.py:1232
  155.2 19.8 %collective-permute-start.5 = (bf16[272,1536]{1,0:T(8,128)(2,1)}, bf16[272,1536]{1,0:T(8,128)(2,1)S(1)}, u32[]{:S(2)}, u32[]{:S(2)}) collective-permute-start(bf16[272,1536]{1,0:T(8,128)(2,1)} %get-tuple-element.115), channel_id=1, source_target_pairs={{0,1},{1,0},{2,3},{3,2},{4,5},{5,4},{6,7},{7,6},{8,9},{9,8},{10,11... | collective-permute-start | bytes 2506760 | tf_op jit(solution)/shard_map/ppermute | solution.py:1282
  174.2 21.5 %collective-permute-start.4 = (bf16[272,1536]{1,0:T(8,128)(2,1)}, bf16[272,1536]{1,0:T(8,128)(2,1)S(1)}, u32[]{:S(2)}, u32[]{:S(2)}) collective-permute-start(bf16[272,1536]{1,0:T(8,128)(2,1)} %get-tuple-element.113), channel_id=1, source_target_pairs={{0,1},{1,0},{2,3},{3,2},{4,5},{5,4},{6,7},{7,6},{8,9},{9,8},{10,11... | collective-permute-start | bytes 2506760 | tf_op jit(solution)/shard_map/ppermute | solution.py:1302
  192.6 22.6 %collective-permute-start.6 = (bf16[272,1536]{1,0:T(8,128)(2,1)}, bf16[272,1536]{1,0:T(8,128)(2,1)S(1)}, u32[]{:S(2)}, u32[]{:S(2)}) collective-permute-start(bf16[272,1536]{1,0:T(8,128)(2,1)} %get-tuple-element.119), channel_id=1, source_target_pairs={{0,1},{1,0},{2,3},{3,2},{4,5},{5,4},{6,7},{7,6},{8,9},{9,8},{10,11... | collective-permute-start | bytes 2506760 | tf_op jit(solution)/shard_map/ppermute | solution.py:1302
  226.8 134.8 %reduce-scatter.5.cloned.1.call-start = ((), (), s32[]{:S(2)}) async-start(), calls=%async_computation.3 | async-start | bytes 983040 | tf_op jit(solution)/shard_map/reduce_scatter | solution.py:1530
  232.1 12.6 %collective-permute-start.7 = (bf16[512,384]{1,0:T(8,128)(2,1)S(1)}, bf16[512,384]{1,0:T(8,128)(2,1)S(1)}, u32[]{:S(2)}, u32[]{:S(2)}) collective-permute-start(bf16[512,384]{1,0:T(8,128)(2,1)S(1)} %copy-done.33), channel_id=1, source_target_pairs={{0,1},{1,0},{2,3},{3,2},{4,5},{5,4},{6,7},{7,6},{8,9},{9,8},{10,11... | collective-permute-start | bytes 1179656 | tf_op jit(solution)/shard_map/ppermute | solution.py:1340
  240.8 36.0 %collective-permute-start.9 = (bf16[512,384]{1,0:T(8,128)(2,1)}, bf16[512,384]{1,0:T(8,128)(2,1)S(1)}, u32[]{:S(2)}, u32[]{:S(2)}) collective-permute-start(bf16[512,384]{1,0:T(8,128)(2,1)} %get-tuple-element.139), channel_id=1, source_target_pairs={{0,1},{1,0},{2,3},{3,2},{4,5},{5,4},{6,7},{7,6},{8,9},{9,8},{10,11... | collective-permute-start | bytes 1179656 | tf_op jit(solution)/shard_map/ppermute | solution.py:1340
  251.2 23.7 %collective-permute-start.8 = (bf16[4,2,96,384]{3,2,0,1:T(8,128)(2,1)S(1)}, bf16[4,2,96,384]{3,2,0,1:T(8,128)(2,1)S(1)}, u32[]{:S(2)}, u32[]{:S(2)}) collective-permute-start(bf16[4,2,96,384]{3,2,0,1:T(8,128)(2,1)S(1)} %get-tuple-element.231), channel_id=1, source_target_pairs={{0,2},{2,0},{4,6},{6,4},{8,10},{10,8},{12,14},{14,12},{16,18},{18,... | collective-permute-start | bytes 1769480 | tf_op jit(solution)/shard_map/ppermute | solution.py:1399
  274.7 20.6 %collective-permute-start.11 = (bf16[512,768]{1,0:T(8,128)(2,1)}, bf16[512,768]{1,0:T(8,128)(2,1)S(1)}, u32[]{:S(2)}, u32[]{:S(2)}) collective-permute-start(bf16[512,768]{1,0:T(8,128)(2,1)} %get-tuple-element.136.refs_0_), channel_id=1, source_target_pairs={{0,1},{1,0},{2,3},{3,2},{4,5},{5,4},{6,7},{7,6},{8,9},{9,8},{10,11... | collective-permute-start | bytes 2359304 | tf_op jit(solution)/shard_map/ppermute | solution.py:1441
  275.8 19.6 %collective-permute-start.10 = (bf16[4,96,384]{2,1,0:T(8,128)(2,1)S(1)}, bf16[4,96,384]{2,1,0:T(8,128)(2,1)S(1)}, u32[]{:S(2)}, u32[]{:S(2)}) collective-permute-start(bf16[4,96,384]{2,1,0:T(8,128)(2,1)S(1)} %get-tuple-element.229), channel_id=1, source_target_pairs={{0,4},{2,6},{4,0},{6,2},{8,12},{10,14},{12,8},{14,10},{16,20},{18,... | collective-permute-start | bytes 884744 | tf_op jit(solution)/shard_map/ppermute | solution.py:1410
  307.2 11.3 %collective-permute-start.12 = (bf16[4,2,144,384]{3,2,0,1:T(8,128)(2,1)S(1)}, bf16[4,2,144,384]{3,2,0,1:T(8,128)(2,1)S(1)}, u32[]{:S(2)}, u32[]{:S(2)}) collective-permute-start(bf16[4,2,144,384]{3,2,0,1:T(8,128)(2,1)S(1)} %get-tuple-element.217), channel_id=1, source_target_pairs={{0,2},{2,0},{4,6},{6,4},{8,10},{10,8},{12,14},{14,12},{16,18},{18,... | collective-permute-start | bytes 2654216 | tf_op jit(solution)/shard_map/ppermute | solution.py:1399
  318.0 12.5 %collective-permute-start.14 = (bf16[4,2,16,384]{3,2,0,1:T(8,128)(2,1)S(1)}, bf16[4,2,16,384]{3,2,0,1:T(8,128)(2,1)S(1)}, u32[]{:S(2)}, u32[]{:S(2)}) collective-permute-start(bf16[4,2,16,384]{3,2,0,1:T(8,128)(2,1)S(1)} %get-tuple-element.257), channel_id=1, source_target_pairs={{0,2},{2,0},{4,6},{6,4},{8,10},{10,8},{12,14},{14,12},{16,18},{18,... | collective-permute-start | bytes 294920 | tf_op jit(solution)/shard_map/ppermute | solution.py:1399
  319.5 15.7 %collective-permute-start.13 = (bf16[4,144,384]{2,1,0:T(8,128)(2,1)S(1)}, bf16[4,144,384]{2,1,0:T(8,128)(2,1)S(1)}, u32[]{:S(2)}, u32[]{:S(2)}) collective-permute-start(bf16[4,144,384]{2,1,0:T(8,128)(2,1)S(1)} %get-tuple-element.214), channel_id=1, source_target_pairs={{0,4},{2,6},{4,0},{6,2},{8,12},{10,14},{12,8},{14,10},{16,20},{18,... | collective-permute-start | bytes 1327112 | tf_op jit(solution)/shard_map/ppermute | solution.py:1410
  328.5 20.1 %collective-permute-start.16 = (bf16[512,768]{1,0:T(8,128)(2,1)}, bf16[512,768]{1,0:T(8,128)(2,1)S(1)}, u32[]{:S(2)}, u32[]{:S(2)}) collective-permute-start(bf16[512,768]{1,0:T(8,128)(2,1)} %get-tuple-element.150.refs_1_), channel_id=1, source_target_pairs={{0,1},{1,0},{2,3},{3,2},{4,5},{5,4},{6,7},{7,6},{8,9},{9,8},{10,11... | collective-permute-start | bytes 2359304 | tf_op jit(solution)/shard_map/ppermute | solution.py:1441
  331.2 4.1 %collective-permute-start.15 = (bf16[4,16,384]{2,1,0:T(8,128)(2,1)S(1)}, bf16[4,16,384]{2,1,0:T(8,128)(2,1)S(1)}, u32[]{:S(2)}, u32[]{:S(2)}) collective-permute-start(bf16[4,16,384]{2,1,0:T(8,128)(2,1)S(1)} %get-tuple-element.254), channel_id=1, source_target_pairs={{0,4},{2,6},{4,0},{6,2},{8,12},{10,14},{12,8},{14,10},{16,20},{18,... | collective-permute-start | bytes 147464 | tf_op jit(solution)/shard_map/ppermute | solution.py:1410
  361.5 5.9 %collective-permute-start.17 = (bf16[256,384]{1,0:T(8,128)(2,1)}, bf16[256,384]{1,0:T(8,128)(2,1)S(1)}, u32[]{:S(2)}, u32[]{:S(2)}) collective-permute-start(bf16[256,384]{1,0:T(8,128)(2,1)} %bitcast.97), channel_id=1, source_target_pairs={{0,1},{1,0},{2,3},{3,2},{4,5},{5,4},{6,7},{7,6},{8,9},{9,8},{10,11... | collective-permute-start | bytes 589832 | tf_op jit(solution)/shard_map/ppermute | solution.py:1538
  (33 other events, 96.4 us)
Sparse Core Ops, SparseCore 0:
  13.7 48.1 all-gather.4
  64.7 80.2 all-gather.6
  226.9 108.8 reduce-scatter.2
  338.6 22.8 reduce-scatter.4

commit v8 on v7

--- a/solution.py
+++ b/solution.py
@@ -60,16 +60,33 @@
 
 
 def bias_kernel(stride, reach, table_ref, out_ref):
-    row = lax.broadcasted_iota(jnp.int32, (tile, tile), 0)
-    lane = lax.broadcasted_iota(jnp.int32, (tile, tile), 1)
+    part = 16
+    row = lax.broadcasted_iota(jnp.int32, (part, tile), 0)
+    lane = lax.broadcasted_iota(jnp.int32, (part, tile), 1)
     heads = out_ref.shape[0]
+    edge = bucket_edges[-1]
     for shift in range(-reach, reach + 1):
+        columns = slice((shift + reach) * tile, (shift + reach + 1) * tile)
         for step in range(2 * stride - 1):
-            ids = bucket_of(stride * (tile * shift + lane - row) + step - (stride - 1))
-            columns = slice((shift + reach) * tile, (shift + reach + 1) * tile)
-            for head in range(heads):
-                values = jnp.broadcast_to(table_ref[head : head + 1, :], (tile, tile))
-                out_ref[head, step, :, columns] = jnp.take_along_axis(values, ids, axis=1)
+            for start in range(0, tile, part):
+                base = stride * (tile * shift - start) + step - (stride - 1)
+                rows = slice(start, start + part)
+                far = None
+                if base - stride * (part - 1) >= edge:
+                    far = 2 * levels_all - 1
+                elif base + stride * (tile - 1) <= -edge:
+                    far = levels_all - 1
+                else:
+                    ids = bucket_of(base + stride * (lane - row))
+                for head in range(heads):
+                    if far is None:
+                        values = jnp.broadcast_to(table_ref[head : head + 1, :], (part, tile))
+                        values = jnp.take_along_axis(values, ids, axis=1)
+                    else:
+                        values = jnp.broadcast_to(
+                            table_ref[head : head + 1, far : far + 1], (part, tile)
+                        )
+                    out_ref[head, step, rows, columns] = values
 
 
 def bias_tiles(table, stride, tiles):

time: 384 us -> 385 us (level)
  no operation moved by 1% of the time
where the time goes in v8:
time: 385 us; the launch traced here: 380 us
  Pallas kernels  216 us (56%)
  waiting for transfers between devices  64.5 us (17%)
  local copies, waits for them, and re-layouts  39.9 us (10%)
  other arithmetic  20.7 us (5%)
  starting transfers between devices  19.8 us (5%)
  between operations  14.6 us (4%)
  matrix products  5.31 us (1%)
    pallas_call x2, Pallas kernels, attend(): pl.pallas_call(functools.partial(attend_kernel, stride, head_dim), grid=(...  35.7 us
    pallas_call x2, Pallas kernels, attend_back(): pl.pallas_call(functools.partial(attend_back_kernel, stride, head_dim, he...  35 us
    pallas_call x2, Pallas kernels, run_expert(): pl.pallas_call(functools.partial(expert_kernel, count, slots, width), gri...  33.5 us
    ppermute x1, waiting for transfers between devices, on_device(): lax.ppermute(hidden_in, 'expert', around(step))  31 us
    pallas_call x2, Pallas kernels, expert_grad(): pl.pallas_call(body, grid=(turns,), in_specs=in_specs, out_specs=out_spec...  21.4 us
    unnamed x88, local copies, waits for them, and re-layouts  18.7 us
    pallas_call x2, Pallas kernels, second_back(): pl.pallas_call(functools.partial(second_kernel, members, members, aliased...  16.5 us
    pallas_call x2, Pallas kernels, dense_grad(): pl.pallas_call(functools.partial(dense_kernel, len(afters), len(handed),...  13.7 us
  transfers between devices with their start and end apart: 22, of which 9 were waited for; matrix products, arithmetic and copies ran while one was open for 11% of the time, Pallas kernels for 54%

profile of v8, /device:TPU:0, one launch (start us, length us, event | category | flops | bytes accessed | tf_op | source)
XLA Modules:
  0.0 380.3 jit_solution(720328833914726102)
XLA Ops:
  20.2 31.0 %collective-permute-done.after_ref.refs_1_ = bf16[2,512,768]{2,1,0:T(8,128)(2,1)S(1)} collective-permute-done((bf16[2,512,768]{2,1,0:T(8,128)(2,1)}, bf16[2,512,768]{2,1,0:T(8,128)(2,1)S(1)}, u32[]{:S(2)}, u32[]{:S(2)}) %collective-permute-start) | collective-permute-done | bytes 1572896 | tf_op jit(solution)/shard_map/ppermute | solution.py:1156
  52.4 4.6 %row_tables.1 = (bf16[2,544,512]{2,1,0:T(8,128)(2,1)}, bf16[2,512,544]{2,1,0:T(8,128)(2,1)}, s32[2,512,2]{2,1,0:T(8,128)}, bf16[384,768]{1,0:T(8,128)(2,1)}) custom-call(s32[1]{0:T(128)} %bitcast.me_ref, s32[2,1,512]{2,1,0:T(1,128)} %bitcast.100, s32[2,512,1]{2,1,0:T(8,128)} %copy.121.column_ref.route_ref, ...), custom_call_target="tpu_custom_call", output_to_operand_aliasing={{3}: (5, {})} | custom-call | tf_op jit(solution)/shard_map/row_tables/pallas_call | solution.py:207
  72.7 5.8 %project.3 = (bf16[1024,768]{1,0:T(8,128)(2,1)}, bf16[1024,1152]{1,0:T(8,128)(2,1)}) custom-call(bf16[2,1024,768]{2,1,0:T(8,128)(2,1)} %bitcast.106, f32[1,768]{1,0:T(1,128)} %reshape.333.gain_ref, bf16[16,256,384]{2,1,0:T(8,128)(2,1)} %get-tuple-element.100.weight_ref.refs_8_), custom_call_target="tpu_custom_call" | custom-call | flops 1811939328 | bytes 4718592 | tf_op jit(solution)/shard_map/project/pallas_call | solution.py:125
  78.5 17.6 %attend.2 = (bf16[6,1024,1024]{2,1,0:T(8,128)(2,1)}, bf16[1024,384]{1,0:T(8,128)(2,1)}, f32[1024,384]{1,0:T(8,128)}) custom-call(f32[2,6]{1,0:T(2,128)} %pad_maximum_fusion.4.far_ref, s32[1]{0:T(128)} %bitcast.13.ends_ref, bf16[1024,1152]{1,0:T(8,128)(2,1)} %get-tuple-element.103.q_ref.k_ref.v_ref, bf16[1024,1152]{1,0:T(8,128)(2,1)} %get-tuple-element.103.q_ref.k_ref.v_ref, ...), custom_call_target="tpu_custom_call" | custom-call | flops 6442450944 | bytes 12582912 | tf_op jit(solution)/shard_map/attend/pallas_call | solution.py:741
  103.5 5.9 %project.2 = (bf16[1024,768]{1,0:T(8,128)(2,1)}, bf16[1024,1152]{1,0:T(8,128)(2,1)}) custom-call(bf16[2,1024,768]{2,1,0:T(8,128)(2,1)} %bitcast.107, f32[1,768]{1,0:T(1,128)} %reshape.333.gain_ref, bf16[16,256,384]{2,1,0:T(8,128)(2,1)} %get-tuple-element.100.weight_ref.refs_8_), custom_call_target="tpu_custom_call" | custom-call | flops 1811939328 | bytes 4718592 | tf_op jit(solution)/shard_map/project/pallas_call | solution.py:125
  110.1 6.2 %middle.2 = (f32[512,768]{1,0:T(8,128)}, bf16[512,768]{1,0:T(8,128)(2,1)}, f32[512,128]{1,0:T(8,128)}, bf16[272,1536]{1,0:T(8,128)(2,1)}, bf16[272,1536]{1,0:T(8,128)(2,1)}) custom-call(s32[1]{0:T(128)} %bitcast.me_ref, bf16[1024,384]{1,0:T(8,128)(2,1)} %get-tuple-element.104.joined_ref.out_ref, s32[2,512,2]{2,1,0:T(8,128)} %get-tuple-element.99.place_ref.offset_ref, ...), custom_call_target="tpu_custom_call" | custom-call | flops 14495514624 | bytes 4718592 | tf_op jit(solution)/shard_map/middle/pallas_call | solution.py:314
  117.3 18.2 %attend.3 = (bf16[6,1024,1024]{2,1,0:T(8,128)(2,1)}, bf16[1024,384]{1,0:T(8,128)(2,1)}, f32[1024,384]{1,0:T(8,128)}) custom-call(f32[2,6]{1,0:T(2,128)} %pad_maximum_fusion.4.far_ref, s32[1]{0:T(128)} %bitcast.10.ends_ref, bf16[1024,1152]{1,0:T(8,128)(2,1)} %get-tuple-element.102.q_ref.k_ref.v_ref, bf16[1024,1152]{1,0:T(8,128)(2,1)} %get-tuple-element.102.q_ref.k_ref.v_ref, ...), custom_call_target="tpu_custom_call" | custom-call | flops 6442450944 | bytes 12582912 | tf_op jit(solution)/shard_map/attend/pallas_call | solution.py:741
  138.0 9.1 %collective-permute-done.3.refs_0_ = bf16[512,384]{1,0:T(8,128)(2,1)S(1)} collective-permute-done((bf16[512,384]{1,0:T(8,128)(2,1)S(1)}, bf16[512,384]{1,0:T(8,128)(2,1)S(1)}, u32[]{:S(2)}, u32[]{:S(2)}) %collective-permute-start.3) | collective-permute-done | bytes 393248 | tf_op jit(solution)/shard_map/ppermute | solution.py:1249
  148.7 6.2 %middle.3 = (f32[512,768]{1,0:T(8,128)}, bf16[512,768]{1,0:T(8,128)(2,1)}, f32[512,128]{1,0:T(8,128)}, bf16[272,1536]{1,0:T(8,128)(2,1)}, bf16[272,1536]{1,0:T(8,128)(2,1)}) custom-call(s32[1]{0:T(128)} %bitcast.me_ref, bf16[1024,384]{1,0:T(8,128)(2,1)} %get-tuple-element.107.joined_ref.out_ref, s32[2,512,2]{2,1,0:T(8,128)} %get-tuple-element.99.place_ref.offset_ref, ...), custom_call_target="tpu_custom_call" | custom-call | flops 14495514624 | bytes 4718592 | tf_op jit(solution)/shard_map/middle/pallas_call | solution.py:314
  156.4 16.7 %run_expert.2 = (bf16[272,1536]{1,0:T(8,128)(2,1)}, bf16[272,1536]{1,0:T(8,128)(2,1)}, bf16[544,3072]{1,0:T(8,128)(2,1)}, bf16[544,3072]{1,0:T(8,128)(2,1)}) custom-call(bf16[16,384,768]{2,1,0:T(8,128)(2,1)} %bitcast.102, bf16[16,384,768]{2,1,0:T(8,128)(2,1)} %bitcast.103, bf16[32,12]{1,0:T(8,128)(2,1)} %copy-done.26, ...), custom_call_target="tpu_custom_call" | custom-call | flops 10267656192 | bytes 9437184 | tf_op jit(solution)/shard_map/run_expert/pallas_call | solution.py:1014
  175.3 16.7 %run_expert.3 = (bf16[272,1536]{1,0:T(8,128)(2,1)}, bf16[272,1536]{1,0:T(8,128)(2,1)}, bf16[544,3072]{1,0:T(8,128)(2,1)}, bf16[544,3072]{1,0:T(8,128)(2,1)}) custom-call(bf16[16,384,768]{2,1,0:T(8,128)(2,1)} %bitcast.104, bf16[16,384,768]{2,1,0:T(8,128)(2,1)} %bitcast.105, bf16[544,3072]{1,0:T(8,128)(2,1)} %get-tuple-element.117.after_ref.refs_7_, ...), custom_call_target="tpu_custom_call" | custom-call | flops 10267656192 | bytes 9437184 | tf_op jit(solution)/shard_map/run_expert/pallas_call | solution.py:1014
  196.1 7.8 %second_back.2 = (bf16[2,512,768]{2,1,0:T(8,128)(2,1)}, f32[512,768]{1,0:T(8,128)}, bf16[512,768]{1,0:T(8,128)(2,1)}, f32[1,768]{1,0:T(1,128)}, f32[128,768]{1,0...) custom-call(s32[1]{0:T(128)} %bitcast.me_ref, bf16[2,512,544]{2,1,0:T(8,128)(2,1)} %get-tuple-element.98.back_ref, ...), custom_call_target="tpu_custom_call" | custom-call | flops 1811939328 | bytes 4718592 | tf_op jit(solution)/shard_map/second_back/pallas_call | solution.py:434
  203.9 10.8 %expert_grad_inner.1.refs_0_ = bf16[16,384,768]{2,1,0:T(8,128)(2,1)} custom-call(bf16[272,1536]{1,0:T(8,128)(2,1)} %copy-done.2, bf16[272,1536]{1,0:T(8,128)(2,1)} %get-tuple-element.112.refs_0_.refs_1_.refs_3_, bf16[272,1536]{1,0:T(8,128)(2,1)} %copy-done.4, bf16[272,1536]{1,0:T(8,128)(2,1)} %get-tuple-element.114.refs_0_.refs_3_.refs_5_, ...), custom_call_target="tpu_custom_call" | custom-call | flops 5133828096 | bytes 9437184 | tf_op jit(solution)/shard_map/expert_grad_inner/pallas_call | solution.py:1079
  215.5 10.7 %expert_grad_outer.1.after_ref.refs_0_ = bf16[16,384,768]{2,1,0:T(8,128)(2,1)} custom-call(bf16[16,384,768]{2,1,0:T(8,128)(2,1)} %expert_grad_inner.1.refs_0_, bf16[272,1536]{1,0:T(8,128)(2,1)} %copy-done.3, bf16[512,768]{1,0:T(8,128)(2,1)} %get-tuple-element.124.refs_2_.refs_3_, ...), custom_call_target="tpu_custom_call", output_to_operand_aliasing={{}: (0, {})} | custom-call | flops 5133828096 | bytes 9437184 | tf_op jit(solution)/shard_map/expert_grad_outer/pallas_call | solution.py:1079
  231.3 8.7 %second_back.3 = (bf16[2,512,768]{2,1,0:T(8,128)(2,1)}, f32[512,768]{1,0:T(8,128)}, bf16[512,768]{1,0:T(8,128)(2,1)}, f32[1,768]{1,0:T(1,128)}, f32[128,768]{1,0...) custom-call(s32[1]{0:T(128)} %bitcast.me_ref, ...), custom_call_target="tpu_custom_call", output_to_operand_aliasing={{0}: (13, {})} | custom-call | flops 1811939328 | bytes 4718592 | tf_op jit(solution)/shard_map/second_back/pallas_call | solution.py:434
  244.8 4.6 %dense_grad.2 = bf16[16,96,384]{2,1,0:T(8,128)(2,1)} custom-call(bf16[512,384]{1,0:T(8,128)(2,1)} %copy-done.19, bf16[512,768]{1,0:T(8,128)(2,1)} %pad_maximum_fusion.1.refs_1_, bf16[512,768]{1,0:T(8,128)(2,1)} %pad_maximum_fusion.2.refs_2_, bf16[512,768]{1,0:T(8,128)(2,1)} %get-tuple-element.124.refs_2_.refs_3_, bf16[512,768]{1,0:T(8,128)(2,1)} %get-tuple-element.137.refs_4_), custom_call_target="tpu_custom_call" | custom-call | flops 1207959552 | bytes 1572864 | tf_op jit(solution)/shard_map/dense_grad/pallas_call | solution.py:601
  250.9 17.2 %attend_back.2 = (bf16[1024,1152]{1,0:T(8,128)(2,1)}, f32[6,3,128,384]{3,2,1,0:T(8,128)}, f32[6,2,128,128]{3,2,1,0:T(8,128)}) custom-call(bf16[6,1024,1024]{2,1,0:T(8,128)(2,1)} %get-tuple-element.131.probs_ref, bf16[1024,384]{1,0:T(8,128)(2,1)} %get-tuple-element.104.joined_ref.out_ref, f32[1024,384]{1,0:T(8,128)} %get-tuple-element.132.inv_ref, ...), custom_call_target="tpu_custom_call" | custom-call | flops 12884901888 | bytes 12582912 | tf_op jit(solution)/shard_map/attend_back/pallas_call | solution.py:866
  268.1 6.2 %first_back.2 = (f32[512,768]{1,0:T(8,128)}, bf16[512,768]{1,0:T(8,128)(2,1)}) custom-call(bf16[1024,1152]{1,0:T(8,128)(2,1)} %get-tuple-element.135.grads_ref.refs_6_, bf16[16,256,384]{2,1,0:T(8,128)(2,1)} %get-tuple-element.100.weight_ref.refs_8_, s32[2,512,2]{2,1,0:T(8,128)} %get-tuple-element.99.place_ref.offset_ref, ...), custom_call_target="tpu_custom_call" | custom-call | flops 1811939328 | bytes 6291456 | tf_op jit(solution)/shard_map/first_back/pallas_call | solution.py:513
  277.2 17.9 %attend_back.3 = (bf16[1024,1152]{1,0:T(8,128)(2,1)}, f32[6,3,128,384]{3,2,1,0:T(8,128)}, f32[6,2,128,128]{3,2,1,0:T(8,128)}) custom-call(bf16[6,1024,1024]{2,1,0:T(8,128)(2,1)} %get-tuple-element.129.probs_ref, bf16[1024,384]{1,0:T(8,128)(2,1)} %get-tuple-element.107.joined_ref.out_ref, ...), custom_call_target="tpu_custom_call", output_to_operand_aliasing={{1}: (11, {}), {2}: (12, {})} | custom-call | flops 12884901888 | bytes 12582912 | tf_op jit(solution)/shard_map/attend_back/pallas_call | solution.py:866
  296.1 9.1 %dense_grad.3 = (bf16[16,144,384]{2,1,0:T(8,128)(2,1)}, f32[768,1]{1,0:T(8,128)}, f32[6,3,128,384]{3,2,1,0:T(8,128)}, f32[6,2,128,128]{3,2,1,0:T(8,128)}) custom-call(f32[6,3,128,384]{3,2,1,0:T(8,128)} %get-tuple-element.143.refs_0_, f32[6,2,128,128]{3,2,1,0:T(8,128)} %get-tuple-element.144.refs_1_, ...), custom_call_target="tpu_custom_call", output_to_operand_aliasing={{2}: (0, {}), {3}: (1, {})} | custom-call | flops 3623878656 | bytes 3145728 | tf_op jit(solution)/shard_map/dense_grad/pallas_call | solution.py:601
  310.6 5.3 %fusion.3 = f32[32,6]{0,1:T(8,128)S(1)} fusion(bf16[6,3,128,384]{3,2,1,0:T(8,128)(2,1)} %convert_element_type.282, s32[3,128,384]{2,0,1:T(4,128)} %copy.136), kind=kOutput, calls=%fused_computation.5 | convolution fusion | flops 61341696 | bytes 2360064 | tf_op jit(solution)/shard_map/hsab,ksab->kh/dot_general | solution.py:1512
  321.9 6.3 %first_back.3 = (f32[512,768]{1,0:T(8,128)}, bf16[512,768]{1,0:T(8,128)(2,1)}) custom-call(bf16[1024,1152]{1,0:T(8,128)(2,1)} %get-tuple-element.142.refs_7_.grads_ref, bf16[16,256,384]{2,1,0:T(8,128)(2,1)} %get-tuple-element.100.weight_ref.refs_8_, s32[2,512,2]{2,1,0:T(8,128)} %get-tuple-element.99.place_ref.offset_ref, ...), custom_call_target="tpu_custom_call" | custom-call | flops 1811939328 | bytes 6291456 | tf_op jit(solution)/shard_map/first_back/pallas_call | solution.py:513
  342.6 5.8 %collective-permute-done.16.refs_0_ = bf16[512,768]{1,0:T(8,128)(2,1)S(1)} collective-permute-done((bf16[512,768]{1,0:T(8,128)(2,1)}, bf16[512,768]{1,0:T(8,128)(2,1)S(1)}, u32[]{:S(2)}, u32[]{:S(2)}) %collective-permute-start.16) | collective-permute-done | bytes 786464 | tf_op jit(solution)/shard_map/ppermute | solution.py:1458
  354.5 7.1 %reduce-scatter.5.cloned.1.call-done = bf16[1,256,384]{2,1,0:T(8,128)(2,1)} async-done(((bf16[4,256,384]{2,1,0:T(8,128)(2,1)}), bf16[1,256,384]{2,1,0:T(8,128)(2,1)}) %reduce-scatter.5.cloned.1.call-update) | async-done | bytes 196624 | tf_op jit(solution)/shard_map/reduce_scatter | solution.py:1547
  (224 shorter events, 110.4 us)
Async XLA Ops:
  7.2 54.7 %all-gather.5.cloned.1.call-start = ((), (), s32[]{:S(2)}) async-start(), calls=%async_computation.4 | async-start | bytes 3342336 | tf_op jit(solution)/shard_map/all_gather | solution.py:1180
  13.6 142.8 %all-gather.7.cloned.1.call-start = ((), (), s32[]{:S(2)}) async-start(), calls=%async_computation.5 | async-start | bytes 10027008 | tf_op jit(solution)/shard_map/all_gather | solution.py:1187
  13.6 37.6 %collective-permute-start = (bf16[2,512,768]{2,1,0:T(8,128)(2,1)}, bf16[2,512,768]{2,1,0:T(8,128)(2,1)S(1)}, u32[]{:S(2)}, u32[]{:S(2)}) collective-permute-start(bf16[2,512,768]{2,1,0:T(8,128)(2,1)} %rows_ref.7), channel_id=1, source_target_pairs={{0,1},{1,0},{2,3},{3,2},{4,5},{5,4},{6,7},{7,6},{8,9},{9,8},{10,11... | collective-permute-start | bytes 4718600 | tf_op jit(solution)/shard_map/ppermute | solution.py:1156
  20.2 31.0 %copy-start.10 = (bf16[384,768]{1,0:T(8,128)(2,1)}, bf16[384,768]{1,0:T(8,128)(2,1)S(1)}, u32[]{:S(2)}) copy-start(bf16[384,768]{1,0:T(8,128)(2,1)S(1)} %bitcast_dynamic-update-slice_fusion.carried_ref) | copy-start | bytes 1769476
  57.0 278.9 %reduce-scatter.3.cloned.1.call-start = ((), (), s32[]{:S(2)}) async-start(), calls=%async_computation.2 | async-start | bytes 10027008 | tf_op jit(solution)/shard_map/reduce_scatter | solution.py:1401
  66.5 34.1 %copy-start.24 = (bf16[2,8,16,384]{3,1,2,0:T(8,128)(2,1)}, bf16[2,8,16,384]{3,1,2,0:T(8,128)(2,1)S(1)}, u32[]{:S(2)}) copy-start(bf16[2,8,16,384]{3,1,2,0:T(8,128)(2,1)S(1)} %copy.152) | copy-start | bytes 589828
  97.3 12.0 %collective-permute-start.1 = (bf16[512,384]{1,0:T(8,128)(2,1)S(1)}, bf16[512,384]{1,0:T(8,128)(2,1)S(1)}, u32[]{:S(2)}, u32[]{:S(2)}) collective-permute-start(bf16[512,384]{1,0:T(8,128)(2,1)S(1)} %broadcast_select_fusion.3), channel_id=1, source_target_pairs={{0,1},{1,0},{2,3},{3,2},{4,5},{5,4},{6,7},{7,6},{8,9},{9,8},{10,11... | collective-permute-start | bytes 1179656 | tf_op jit(solution)/shard_map/ppermute | solution.py:1249
  116.4 30.6 %collective-permute-start.2 = (bf16[272,1536]{1,0:T(8,128)(2,1)}, bf16[272,1536]{1,0:T(8,128)(2,1)S(1)}, u32[]{:S(2)}, u32[]{:S(2)}) collective-permute-start(bf16[272,1536]{1,0:T(8,128)(2,1)} %get-tuple-element.106.after_ref), channel_id=1, source_target_pairs={{0,1},{1,0},{2,3},{3,2},{4,5},{5,4},{6,7},{7,6},{8,9},{9,8},{10,11... | collective-permute-start | bytes 2506760 | tf_op jit(solution)/shard_map/ppermute | solution.py:1299
  136.7 10.3 %collective-permute-start.3 = (bf16[512,384]{1,0:T(8,128)(2,1)S(1)}, bf16[512,384]{1,0:T(8,128)(2,1)S(1)}, u32[]{:S(2)}, u32[]{:S(2)}) collective-permute-start(bf16[512,384]{1,0:T(8,128)(2,1)S(1)} %broadcast_select_fusion.2), channel_id=1, source_target_pairs={{0,1},{1,0},{2,3},{3,2},{4,5},{5,4},{6,7},{7,6},{8,9},{9,8},{10,11... | collective-permute-start | bytes 1179656 | tf_op jit(solution)/shard_map/ppermute | solution.py:1249
  154.9 19.4 %collective-permute-start.5 = (bf16[272,1536]{1,0:T(8,128)(2,1)}, bf16[272,1536]{1,0:T(8,128)(2,1)S(1)}, u32[]{:S(2)}, u32[]{:S(2)}) collective-permute-start(bf16[272,1536]{1,0:T(8,128)(2,1)} %get-tuple-element.115), channel_id=1, source_target_pairs={{0,1},{1,0},{2,3},{3,2},{4,5},{5,4},{6,7},{7,6},{8,9},{9,8},{10,11... | collective-permute-start | bytes 2506760 | tf_op jit(solution)/shard_map/ppermute | solution.py:1299
  173.1 22.0 %collective-permute-start.4 = (bf16[272,1536]{1,0:T(8,128)(2,1)}, bf16[272,1536]{1,0:T(8,128)(2,1)S(1)}, u32[]{:S(2)}, u32[]{:S(2)}) collective-permute-start(bf16[272,1536]{1,0:T(8,128)(2,1)} %get-tuple-element.113), channel_id=1, source_target_pairs={{0,1},{1,0},{2,3},{3,2},{4,5},{5,4},{6,7},{7,6},{8,9},{9,8},{10,11... | collective-permute-start | bytes 2506760 | tf_op jit(solution)/shard_map/ppermute | solution.py:1319
  192.0 22.6 %collective-permute-start.6 = (bf16[272,1536]{1,0:T(8,128)(2,1)}, bf16[272,1536]{1,0:T(8,128)(2,1)S(1)}, u32[]{:S(2)}, u32[]{:S(2)}) collective-permute-start(bf16[272,1536]{1,0:T(8,128)(2,1)} %get-tuple-element.119), channel_id=1, source_target_pairs={{0,1},{1,0},{2,3},{3,2},{4,5},{5,4},{6,7},{7,6},{8,9},{9,8},{10,11... | collective-permute-start | bytes 2506760 | tf_op jit(solution)/shard_map/ppermute | solution.py:1319
  226.3 135.3 %reduce-scatter.5.cloned.1.call-start = ((), (), s32[]{:S(2)}) async-start(), calls=%async_computation.3 | async-start | bytes 983040 | tf_op jit(solution)/shard_map/reduce_scatter | solution.py:1547
  231.3 12.7 %collective-permute-start.7 = (bf16[512,384]{1,0:T(8,128)(2,1)S(1)}, bf16[512,384]{1,0:T(8,128)(2,1)S(1)}, u32[]{:S(2)}, u32[]{:S(2)}) collective-permute-start(bf16[512,384]{1,0:T(8,128)(2,1)S(1)} %copy-done.33), channel_id=1, source_target_pairs={{0,1},{1,0},{2,3},{3,2},{4,5},{5,4},{6,7},{7,6},{8,9},{9,8},{10,11... | collective-permute-start | bytes 1179656 | tf_op jit(solution)/shard_map/ppermute | solution.py:1357
  240.0 36.4 %collective-permute-start.9 = (bf16[512,384]{1,0:T(8,128)(2,1)}, bf16[512,384]{1,0:T(8,128)(2,1)S(1)}, u32[]{:S(2)}, u32[]{:S(2)}) collective-permute-start(bf16[512,384]{1,0:T(8,128)(2,1)} %get-tuple-element.139), channel_id=1, source_target_pairs={{0,1},{1,0},{2,3},{3,2},{4,5},{5,4},{6,7},{7,6},{8,9},{9,8},{10,11... | collective-permute-start | bytes 1179656 | tf_op jit(solution)/shard_map/ppermute | solution.py:1357
  250.9 23.5 %collective-permute-start.8 = (bf16[4,2,96,384]{3,2,0,1:T(8,128)(2,1)S(1)}, bf16[4,2,96,384]{3,2,0,1:T(8,128)(2,1)S(1)}, u32[]{:S(2)}, u32[]{:S(2)}) collective-permute-start(bf16[4,2,96,384]{3,2,0,1:T(8,128)(2,1)S(1)} %get-tuple-element.231), channel_id=1, source_target_pairs={{0,2},{2,0},{4,6},{6,4},{8,10},{10,8},{12,14},{14,12},{16,18},{18,... | collective-permute-start | bytes 1769480 | tf_op jit(solution)/shard_map/ppermute | solution.py:1416
  274.3 20.8 %collective-permute-start.11 = (bf16[512,768]{1,0:T(8,128)(2,1)}, bf16[512,768]{1,0:T(8,128)(2,1)S(1)}, u32[]{:S(2)}, u32[]{:S(2)}) collective-permute-start(bf16[512,768]{1,0:T(8,128)(2,1)} %get-tuple-element.136.refs_0_), channel_id=1, source_target_pairs={{0,1},{1,0},{2,3},{3,2},{4,5},{5,4},{6,7},{7,6},{8,9},{9,8},{10,11... | collective-permute-start | bytes 2359304 | tf_op jit(solution)/shard_map/ppermute | solution.py:1458
  275.3 19.8 %collective-permute-start.10 = (bf16[4,96,384]{2,1,0:T(8,128)(2,1)S(1)}, bf16[4,96,384]{2,1,0:T(8,128)(2,1)S(1)}, u32[]{:S(2)}, u32[]{:S(2)}) collective-permute-start(bf16[4,96,384]{2,1,0:T(8,128)(2,1)S(1)} %get-tuple-element.229), channel_id=1, source_target_pairs={{0,4},{2,6},{4,0},{6,2},{8,12},{10,14},{12,8},{14,10},{16,20},{18,... | collective-permute-start | bytes 884744 | tf_op jit(solution)/shard_map/ppermute | solution.py:1427
  307.1 11.0 %collective-permute-start.12 = (bf16[4,2,144,384]{3,2,0,1:T(8,128)(2,1)S(1)}, bf16[4,2,144,384]{3,2,0,1:T(8,128)(2,1)S(1)}, u32[]{:S(2)}, u32[]{:S(2)}) collective-permute-start(bf16[4,2,144,384]{3,2,0,1:T(8,128)(2,1)S(1)} %get-tuple-element.217), channel_id=1, source_target_pairs={{0,2},{2,0},{4,6},{6,4},{8,10},{10,8},{12,14},{14,12},{16,18},{18,... | collective-permute-start | bytes 2654216 | tf_op jit(solution)/shard_map/ppermute | solution.py:1416
  317.9 12.3 %collective-permute-start.14 = (bf16[4,2,16,384]{3,2,0,1:T(8,128)(2,1)S(1)}, bf16[4,2,16,384]{3,2,0,1:T(8,128)(2,1)S(1)}, u32[]{:S(2)}, u32[]{:S(2)}) collective-permute-start(bf16[4,2,16,384]{3,2,0,1:T(8,128)(2,1)S(1)} %get-tuple-element.257), channel_id=1, source_target_pairs={{0,2},{2,0},{4,6},{6,4},{8,10},{10,8},{12,14},{14,12},{16,18},{18,... | collective-permute-start | bytes 294920 | tf_op jit(solution)/shard_map/ppermute | solution.py:1416
  319.2 15.8 %collective-permute-start.13 = (bf16[4,144,384]{2,1,0:T(8,128)(2,1)S(1)}, bf16[4,144,384]{2,1,0:T(8,128)(2,1)S(1)}, u32[]{:S(2)}, u32[]{:S(2)}) collective-permute-start(bf16[4,144,384]{2,1,0:T(8,128)(2,1)S(1)} %get-tuple-element.214), channel_id=1, source_target_pairs={{0,4},{2,6},{4,0},{6,2},{8,12},{10,14},{12,8},{14,10},{16,20},{18,... | collective-permute-start | bytes 1327112 | tf_op jit(solution)/shard_map/ppermute | solution.py:1427
  328.2 20.2 %collective-permute-start.16 = (bf16[512,768]{1,0:T(8,128)(2,1)}, bf16[512,768]{1,0:T(8,128)(2,1)S(1)}, u32[]{:S(2)}, u32[]{:S(2)}) collective-permute-start(bf16[512,768]{1,0:T(8,128)(2,1)} %get-tuple-element.150.refs_1_), channel_id=1, source_target_pairs={{0,1},{1,0},{2,3},{3,2},{4,5},{5,4},{6,7},{7,6},{8,9},{9,8},{10,11... | collective-permute-start | bytes 2359304 | tf_op jit(solution)/shard_map/ppermute | solution.py:1458
  330.9 4.1 %collective-permute-start.15 = (bf16[4,16,384]{2,1,0:T(8,128)(2,1)S(1)}, bf16[4,16,384]{2,1,0:T(8,128)(2,1)S(1)}, u32[]{:S(2)}, u32[]{:S(2)}) collective-permute-start(bf16[4,16,384]{2,1,0:T(8,128)(2,1)S(1)} %get-tuple-element.254), channel_id=1, source_target_pairs={{0,4},{2,6},{4,0},{6,2},{8,12},{10,14},{12,8},{14,10},{16,20},{18,... | collective-permute-start | bytes 147464 | tf_op jit(solution)/shard_map/ppermute | solution.py:1427
  361.6 5.9 %collective-permute-start.17 = (bf16[256,384]{1,0:T(8,128)(2,1)}, bf16[256,384]{1,0:T(8,128)(2,1)S(1)}, u32[]{:S(2)}, u32[]{:S(2)}) collective-permute-start(bf16[256,384]{1,0:T(8,128)(2,1)} %bitcast.97), channel_id=1, source_target_pairs={{0,1},{1,0},{2,3},{3,2},{4,5},{5,4},{6,7},{7,6},{8,9},{9,8},{10,11... | collective-permute-start | bytes 589832 | tf_op jit(solution)/shard_map/ppermute | solution.py:1555
  (33 other events, 95.2 us)
Sparse Core Ops, SparseCore 0:
  13.7 48.1 all-gather.4
  64.7 80.3 all-gather.6
  226.4 109.5 reduce-scatter.2
  338.5 23.0 reduce-scatter.4
